TPU v7x, 32 devices: a whole 2x2x4 slice. The times are simulated.
32 devices in a mesh: pipe: 2 (over x), expert: 16 (over z, y, core).
Axes of the slice: x: 2, y: 2, z: 4, core: 2. Of those that a mesh axis runs over, the one named last changes fastest.
Arguments:
- tokens: bfloat16 [2, 128, 3584], P(None, ('pipe', 'expert')), may hold values from -6 to 6
- cotangent: bfloat16 [2, 128, 3584], P(None, ('pipe', 'expert')), may hold values from -6 to 6
- expert_ids: int32 [2, 128, 2], P(None, ('pipe', 'expert')), may hold values from 0 to 3, all different within a row; in each aligned block of 4 rows (0 to 3, 4 to 7, ..., all dimensions but the last counted through in order) at most 3 rows name the same one
- gate_values: bfloat16 [2, 128, 2], P(None, ('pipe', 'expert')), may hold values from 0.19921875 to 1.5
- w_gate: bfloat16 [3584, 8192], P('pipe', 'expert'), may hold values from -0.09375 to 0.09375
- w_up: bfloat16 [3584, 8192], P('pipe', 'expert'), may hold values from -0.09375 to 0.09375
- w_down_t: bfloat16 [3584, 8192], P('pipe', 'expert'), may hold values from -0.125 to 0.125
Outputs:
- d_tokens: bfloat16 [2, 128, 3584], P(None, ('pipe', 'expert'))
- gate_weight_gradient: float32 [2, 128, 2], P(None, ('pipe', 'expert'))
- dw_gate: bfloat16 [3584, 8192], P('pipe', 'expert')
- dw_up: bfloat16 [3584, 8192], P('pipe', 'expert')
- dw_down_t: bfloat16 [3584, 8192], P('pipe', 'expert')
Inputs may be any that keep to these rules, and one draw needn't show every extreme that they name: `expert_ids`: within each micro-batch, the 4 tokens of one device route to one expert at most 3 times; a token's 2 experts differ.
All inputs are finite; a program needn't handle non-finite values.
Results may differ from a plain program's by a relative error of at most 0.014.
Values may be sent and summed in bfloat16 or wider, within the bound.
No kernel may reach another device: no remote copies, remote signals or barrier semaphores. Data moves between devices by JAX's collectives and lax.ppermute only.
A program may use at most 64 MiB of HBM per device.

v0:
```python
import math

import jax
import jax.numpy as jnp
from jax import lax
from jax.sharding import PartitionSpec as P

EXPERTS = 4
CAP = 3


def partner(x, axis, stride):
    return lax.ppermute(x, axis, [(i, i ^ 1 << stride) for i in range(lax.axis_size(axis))])


def route_table(expert_ids, expert_total, capacity):
    micro_count, tok_count, top_count = expert_ids.shape
    flat_ids = expert_ids.reshape(micro_count, tok_count * top_count)
    onehot = (
        flat_ids[:, :, None] == jnp.arange(expert_total, dtype=jnp.int32)[None, None, :]
    ).astype(jnp.int32)
    earlier = jnp.cumsum(onehot, axis=1) - onehot
    position = jnp.sum(earlier * onehot, axis=2)
    slot_index = flat_ids * capacity + position
    slot_ids = jnp.arange(expert_total * capacity, dtype=jnp.int32)
    return (slot_index[:, None, :] == slot_ids[None, :, None]).astype(jnp.float32)


def on_device(tokens, cotangent, expert_ids, gate_values, w_gate, w_up, w_down_t):
    micro_count, tok_count, d_model = tokens.shape
    top_count = expert_ids.shape[2]
    pipe_size = lax.axis_size("pipe")
    expert_size = lax.axis_size("expert")
    group_size = expert_size // EXPERTS
    bit_total = group_size.bit_length() - 1
    capacity = CAP
    slot_total = EXPERTS * capacity
    highest_precision = lax.Precision.HIGHEST
    member = lax.axis_index("expert") % group_size
    gate_full, up_full, down_full = (
        lax.all_gather(w_gate, "pipe", axis=0, tiled=True),
        lax.all_gather(w_up, "pipe", axis=0, tiled=True),
        lax.all_gather(w_down_t, "pipe", axis=0, tiled=True),
    )
    routing_table = route_table(expert_ids, EXPERTS, capacity)
    routing_table_bfloat16 = routing_table.astype(jnp.bfloat16)
    token_replica = jnp.repeat(tokens, top_count, axis=1)
    cotangent_replica = jnp.repeat(cotangent, top_count, axis=1)
    flattened_gate = gate_values.reshape(micro_count, tok_count * top_count)
    send_tok = jnp.einsum(
        "egf,efh->egh", routing_table_bfloat16, token_replica, preferred_element_type=jnp.float32
    ).astype(jnp.bfloat16)
    send_cot = jnp.einsum(
        "egf,efh->egh",
        routing_table_bfloat16,
        cotangent_replica,
        preferred_element_type=jnp.float32,
    ).astype(jnp.bfloat16)
    send_gate = jnp.einsum(
        "wkx,wx->wk", routing_table_bfloat16, flattened_gate, preferred_element_type=jnp.float32
    ).astype(jnp.bfloat16)
    send_tok = send_tok.reshape(micro_count, EXPERTS, capacity, d_model)
    send_cot = send_cot.reshape(micro_count, EXPERTS, capacity, d_model)
    gate_blocks = jnp.broadcast_to(
        send_gate.reshape(micro_count, EXPERTS, 1, capacity),
        (micro_count, EXPERTS, group_size, capacity),
    ).reshape(micro_count, expert_size, capacity)
    share = d_model // group_size
    tok_blocks = jnp.swapaxes(
        send_tok.reshape(micro_count, EXPERTS, capacity, group_size, share), 2, 3
    ).reshape(micro_count, expert_size, capacity, share)
    cot_blocks = jnp.swapaxes(
        send_cot.reshape(micro_count, EXPERTS, capacity, group_size, share), 2, 3
    ).reshape(micro_count, expert_size, capacity, share)
    recv_tok, recv_cot, recv_gate = (
        lax.all_to_all(tok_blocks, "expert", split_axis=1, concat_axis=1, tiled=True),
        lax.all_to_all(cot_blocks, "expert", split_axis=1, concat_axis=1, tiled=True),
        lax.all_to_all(gate_blocks, "expert", split_axis=1, concat_axis=1, tiled=True),
    )
    for bit_index in range(bit_total):
        their_tok, their_cot = partner((recv_tok, recv_cot), "expert", bit_index)
        low_side = member // (1 << bit_index) % 2 == 0
        recv_tok = jnp.where(
            low_side,
            jnp.concatenate([recv_tok, their_tok], 3),
            jnp.concatenate([their_tok, recv_tok], 3),
        )
        recv_cot = jnp.where(
            low_side,
            jnp.concatenate([recv_cot, their_cot], 3),
            jnp.concatenate([their_cot, recv_cot], 3),
        )
    row_count = micro_count * expert_size * capacity
    tok_rows = recv_tok.reshape(row_count, d_model)
    cot_rows = recv_cot.reshape(row_count, d_model)
    gate_rows = recv_gate.reshape(row_count, 1).astype(jnp.float32)
    pre_gate = jnp.dot(tok_rows, gate_full, preferred_element_type=jnp.float32)
    pre_up = jnp.dot(tok_rows, up_full, preferred_element_type=jnp.float32)
    back_proj = jnp.dot(cot_rows, down_full, preferred_element_type=jnp.float32)
    sigmoid_gate = jax.nn.sigmoid(pre_gate)
    activated = pre_gate * sigmoid_gate
    hidden = activated * pre_up
    gate_part = jnp.sum(back_proj * hidden, axis=1)
    scaled_hidden = (gate_rows * hidden).astype(jnp.bfloat16)
    d_hidden = gate_rows * back_proj
    d_pre_gate = (
        d_hidden * pre_up * sigmoid_gate * (1.0 + pre_gate * (1.0 - sigmoid_gate))
    ).astype(jnp.bfloat16)
    d_pre_up = (d_hidden * activated).astype(jnp.bfloat16)
    input_part = jnp.dot(d_pre_gate, gate_full.T, preferred_element_type=jnp.float32)
    input_part = input_part + jnp.dot(d_pre_up, up_full.T, preferred_element_type=jnp.float32)
    tokens_total = tok_count * pipe_size * expert_size
    grad_scale = 1.0 / math.sqrt(micro_count * tokens_total * top_count / EXPERTS)
    contract = (((0,), (0,)), ((), ()))
    part_gate = lax.dot_general(tok_rows, d_pre_gate, contract, preferred_element_type=jnp.float32)
    part_up = lax.dot_general(tok_rows, d_pre_up, contract, preferred_element_type=jnp.float32)
    part_down = lax.dot_general(
        cot_rows, scaled_hidden, contract, preferred_element_type=jnp.float32
    )
    summed = lax.psum_scatter(
        (jnp.concatenate([part_gate, part_up, part_down], 1) * grad_scale).astype(jnp.bfloat16),
        "pipe",
        scatter_dimension=0,
        tiled=True,
    ).astype(jnp.float32)
    hidden_width = gate_full.shape[1]
    dw_gate = summed[:, :hidden_width].astype(jnp.bfloat16)
    dw_up = summed[:, hidden_width : 2 * hidden_width].astype(jnp.bfloat16)
    dw_down_t = summed[:, 2 * hidden_width :].astype(jnp.bfloat16)
    input_blocks = input_part.reshape(micro_count, expert_size, capacity, d_model)
    gate_sums = gate_part.reshape(micro_count, expert_size, capacity)
    back_rows, back_gate = (
        lax.all_to_all(
            input_blocks.astype(jnp.bfloat16), "expert", split_axis=1, concat_axis=1, tiled=True
        ).astype(input_blocks.dtype),
        lax.all_to_all(
            gate_sums.astype(jnp.bfloat16), "expert", split_axis=1, concat_axis=1, tiled=True
        ).astype(gate_sums.dtype),
    )
    slot_input = jnp.sum(
        back_rows.reshape(micro_count, EXPERTS, group_size, capacity, d_model), axis=2
    )
    gate_per_slot = jnp.sum(back_gate.reshape(micro_count, EXPERTS, group_size, capacity), axis=2)
    slot_input = slot_input.reshape(micro_count, slot_total, d_model)
    gate_per_slot = gate_per_slot.reshape(micro_count, slot_total)
    token_table = jnp.sum(
        routing_table.reshape(micro_count, slot_total, tok_count, top_count), axis=3
    )
    d_tokens = jnp.einsum(
        "msc,msd->mcd", token_table, slot_input, precision=highest_precision
    ).astype(jnp.bfloat16)
    gate_weight_gradient = jnp.einsum(
        "kxw,kx->kw", routing_table, gate_per_slot, precision=highest_precision
    ).reshape(micro_count, tok_count, top_count)
    return (d_tokens, gate_weight_gradient, dw_gate, dw_up, dw_down_t)


def solution(mesh):
    return jax.shard_map(
        on_device,
        mesh=mesh,
        in_specs=(
            P(None, ("pipe", "expert"), None),
            P(None, ("pipe", "expert"), None),
            P(None, ("pipe", "expert"), None),
            P(None, ("pipe", "expert"), None),
            P("pipe", "expert"),
            P("pipe", "expert"),
            P("pipe", "expert"),
        ),
        out_specs=(
            P(None, ("pipe", "expert"), None),
            P(None, ("pipe", "expert"), None),
            P("pipe", "expert"),
            P("pipe", "expert"),
            P("pipe", "expert"),
        ),
        check_vma=False,
    )
```

profile of v0, /device:TPU:0, one launch (start us, length us, event | category | flops | bytes accessed | tf_op | source)
XLA Modules:
  0.0 330.3 jit_solution(16616396827548589065)
XLA Ops:
  11.4 7.4 %all-to-all-start.1 = ((bf16[2,16,3,896]{3,0,2,1:T(2,128)(2,1)}), bf16[2,16,3,896]{3,0,2,1:T(2,128)(2,1)S(1)}, u32[]{:S(2)}, u32[]{:S(2)}) async-start(bf16[2,16,3,896]{3,0,2,1:T(2,128)(2,1)} %bitcast.5), calls=%async_computation.1 | async-start | bytes 344064 | tf_op jit(solution)/shard_map/all_to_all | solution.py:77
  19.3 0.8 copy.139
  20.1 7.3 %all-to-all-done.1 = bf16[2,16,3,896]{3,0,2,1:T(2,128)(2,1)S(1)} async-done(((bf16[2,16,3,896]{3,0,2,1:T(2,128)(2,1)}), bf16[2,16,3,896]{3,0,2,1:T(2,128)(2,1)S(1)}, u32[]{:S(2)}, u32[]{:S(2)}) %all-to-all-start.1) | async-done | bytes 172064 | tf_op jit(solution)/shard_map/all_to_all | solution.py:77
  27.4 3.5 %all-to-all-start.2 = ((bf16[2,16,3,896]{3,0,2,1:T(2,128)(2,1)}), bf16[2,16,3,896]{3,0,2,1:T(2,128)(2,1)S(1)}, u32[]{:S(2)}, u32[]{:S(2)}) async-start(bf16[2,16,3,896]{3,0,2,1:T(2,128)(2,1)} %bitcast.8), calls=%async_computation.2 | async-start | bytes 344064 | tf_op jit(solution)/shard_map/all_to_all | solution.py:76
  31.4 8.1 %all-to-all-done.2 = bf16[2,16,3,896]{3,0,2,1:T(2,128)(2,1)S(1)} async-done(((bf16[2,16,3,896]{3,0,2,1:T(2,128)(2,1)}), bf16[2,16,3,896]{3,0,2,1:T(2,128)(2,1)S(1)}, u32[]{:S(2)}, u32[]{:S(2)}) %all-to-all-start.2) | async-done | bytes 172064 | tf_op jit(solution)/shard_map/all_to_all | solution.py:76
  40.4 3.5 %all-to-all-start = ((bf16[2,16,3]{2,0,1:T(2,128)(2,1)}), bf16[2,16,3]{2,0,1:T(2,128)(2,1)S(1)}, u32[]{:S(2)}, u32[]{:S(2)}) async-start(bf16[2,16,3]{2,0,1:T(2,128)(2,1)} %bitcast.2), calls=%async_computation | async-start | bytes 16384 | tf_op jit(solution)/shard_map/all_to_all | solution.py:78
  44.0 6.2 %all-to-all-done = bf16[2,16,3]{2,0,1:T(2,128)(2,1)S(1)} async-done(((bf16[2,16,3]{2,0,1:T(2,128)(2,1)}), bf16[2,16,3]{2,0,1:T(2,128)(2,1)S(1)}, u32[]{:S(2)}, u32[]{:S(2)}) %all-to-all-start) | async-done | bytes 224 | tf_op jit(solution)/shard_map/all_to_all | solution.py:78
  52.9 1.6 collective-permute-start.3
  54.9 7.9 %collective-permute-done.1 = bf16[2,16,3,1792]{3,0,2,1:T(2,128)(2,1)S(1)} collective-permute-done((bf16[2,16,3,1792]{3,0,2,1:T(2,128)(2,1)S(1)}, bf16[2,16,3,1792]{3,0,2,1:T(2,128)(2,1)S(1)}, u32[]{:S(2)}, u32[]{:S(2)}) %collective-permute-start.1) | collective-permute-done | bytes 344096 | tf_op jit(solution)/shard_map/ppermute | solution.py:13
  63.3 5.7 %collective-permute-done.3 = bf16[2,16,3,1792]{3,0,2,1:T(2,128)(2,1)S(1)} collective-permute-done((bf16[2,16,3,1792]{3,0,2,1:T(2,128)(2,1)S(1)}, bf16[2,16,3,1792]{3,0,2,1:T(2,128)(2,1)S(1)}, u32[]{:S(2)}, u32[]{:S(2)}) %collective-permute-start.3) | collective-permute-done | bytes 344096 | tf_op jit(solution)/shard_map/ppermute | solution.py:13
  69.5 3.1 fusion.20
  72.6 43.0 %all-gather.6.cloned.1.call-done = bf16[3584,512]{1,0:T(8,128)(2,1)} async-done(((bf16[1792,512]{1,0:T(8,128)(2,1)}), bf16[3584,512]{1,0:T(8,128)(2,1)}) %all-gather.6.cloned.1.call-update) | async-done | bytes 3670032 | tf_op jit(solution)/shard_map/all_gather | solution.py:42
  115.6 2.7 fusion.21
  118.3 4.2 %fusion.4 = f32[3584,512]{0,1:T(8,128)} fusion(bf16[96,1792]{1,0:T(8,128)(2,1)S(1)} %concatenate.61, bf16[96,1792]{1,0:T(8,128)(2,1)S(1)} %maximum_select_fusion.2, pred[]{:T(512)S(6)} %eq.55, f32[96]{0:T(128)S(1)} %reshape.110, f32[96,512]{1,0:T(8,128)S(1)} %fusion.21, f32[96,512]{1,0:T(8,128)S(1)} %fusion.20), kind=kOutput, calls=%fused_computation.21 | convolution fusion | flops 355762176 | bytes 8421761 | tf_op jit(solution)/shard_map/dot_general | solution.py:117
  122.5 45.5 %all-gather.4.cloned.1.call-done = bf16[3584,512]{1,0:T(8,128)(2,1)} async-done(((bf16[1792,512]{1,0:T(8,128)(2,1)}), bf16[3584,512]{1,0:T(8,128)(2,1)}) %all-gather.4.cloned.1.call-update) | async-done | bytes 3670032 | tf_op jit(solution)/shard_map/all_gather | solution.py:43
  168.0 2.9 multiply_reduce_fusion
  170.9 1.2 fusion.19
  172.0 1.2 fusion.18
  173.2 1.1 slice-done.1
  174.3 7.0 %fusion = bf16[3584,1536]{0,1:T(8,128)(2,1)} fusion(f32[3584,512]{0,1:T(8,128)S(1)} %bitcast.33, f32[3584,512]{0,1:T(8,128)S(1)} %fusion.18, f32[3584,512]{0,1:T(8,128)S(1)} %fusion.19), kind=kLoop, calls=%fused_computation.1 | loop fusion | flops 22020096 | bytes 33030144 | tf_op jit(solution)/shard_map/convert_element_type | solution.py:121
  182.0 5.6 %all-to-all-start.4 = ((bf16[2,16,3]{2,0,1:T(2,128)(2,1)}), bf16[2,16,3]{2,0,1:T(2,128)(2,1)S(1)}, u32[]{:S(2)}, u32[]{:S(2)}) async-start(bf16[2,16,3]{2,0,1:T(2,128)(2,1)} %copy.147), calls=%async_computation.4 | async-start | bytes 16384 | tf_op jit(solution)/shard_map/all_to_all | solution.py:136
  187.7 3.6 %fusion.23 = f32[96,3584]{1,0:T(8,128)S(1)} fusion(bf16[96,512]{1,0:T(8,128)(2,1)S(1)} %get-tuple-element.39, bf16[3584,512]{1,0:T(8,128)(2,1)} %all-gather.8.cloned.1.call-done), kind=kOutput, calls=%fused_computation.47 | convolution fusion | flops 352321536 | bytes 5144576 | tf_op jit(solution)/shard_map/dot_general | solution.py:110
  191.3 1.2 fusion.1
  193.0 1.7 copy.143
  194.7 6.0 %all-to-all-start.3 = ((bf16[2,16,3,3584]{3,0,2,1:T(2,128)(2,1)}), bf16[2,16,3,3584]{3,0,2,1:T(2,128)(2,1)S(1)}, u32[]{:S(2)}, u32[]{:S(2)}) async-start(bf16[2,16,3,3584]{3,0,2,1:T(2,128)(2,1)} %copy.143), calls=%async_computation.3 | async-start | bytes 1376256 | tf_op jit(solution)/shard_map/all_to_all | solution.py:133
  202.4 15.4 %all-to-all-done.3 = bf16[2,16,3,3584]{3,0,2,1:T(2,128)(2,1)S(1)} async-done(((bf16[2,16,3,3584]{3,0,2,1:T(2,128)(2,1)}), bf16[2,16,3,3584]{3,0,2,1:T(2,128)(2,1)S(1)}, u32[]{:S(2)}, u32[]{:S(2)}) %all-to-all-start.3) | async-done | bytes 688160 | tf_op jit(solution)/shard_map/all_to_all | solution.py:133
  218.5 1.0 convolution_convert_fusion.2
  219.5 89.5 %reduce-scatter.2.cloned.1.call-done = bf16[1792,1536]{0,1:T(8,128)(2,1)} async-done(((bf16[3584,1536]{0,1:T(8,128)(2,1)}), bf16[1792,1536]{0,1:T(8,128)(2,1)}) %reduce-scatter.2.cloned.1.call-update) | async-done | bytes 5505040 | tf_op jit(solution)/shard_map/reduce_scatter | solution.py:120
  309.0 4.8 %fusion.22 = (bf16[1792,512]{0,1:T(8,128)(2,1)}, bf16[1792,512]{0,1:T(8,128)(2,1)}, bf16[1792,512]{0,1:T(8,128)(2,1)S(1)}) fusion(bf16[1792,1536]{0,1:T(8,128)(2,1)} %reduce-scatter.2.cloned.1.call-done), kind=kLoop, calls=%fused_computation.46 | loop fusion | bytes 11010048 | tf_op jit(solution)/shard_map/slice | solution.py:129
  313.8 3.8 %copy.153 = bf16[1792,512]{1,0:T(8,128)(2,1)} copy(bf16[1792,512]{0,1:T(8,128)(2,1)} %get-tuple-element.35) | data formatting | bytes 3670016
  317.6 3.8 %copy.152 = bf16[1792,512]{1,0:T(8,128)(2,1)} copy(bf16[1792,512]{0,1:T(8,128)(2,1)} %get-tuple-element.36) | data formatting | bytes 3670016
  321.4 2.3 copy.151
  (86 shorter events, 13.6 us)
Async XLA Ops:
  7.2 62.3 %all-gather.8.cloned.1.call-start = ((), (), s32[]{:S(2)}) async-start(), calls=%async_computation.8 | async-start | bytes 5505024 | tf_op jit(solution)/shard_map/all_gather | solution.py:41
  7.9 1.5 copy-start.3
  7.9 1.7 copy-start.1
  7.9 107.6 %all-gather.6.cloned.1.call-start = ((), (), s32[]{:S(2)}) async-start(), calls=%async_computation.7 | async-start | bytes 5505024 | tf_op jit(solution)/shard_map/all_gather | solution.py:42
  8.7 10.1 %copy-start.2 = (bf16[2,4,3584]{2,1,0:T(4,128)(2,1)S(1)}, bf16[2,4,3584]{2,1,0:T(4,128)(2,1)}, u32[]{:S(2)}) copy-start(bf16[2,4,3584]{2,1,0:T(4,128)(2,1)} %param.7) | copy-start | bytes 172036
  8.7 159.3 %all-gather.4.cloned.1.call-start = ((), (), s32[]{:S(2)}) async-start(), calls=%async_computation.6 | async-start | bytes 5505024 | tf_op jit(solution)/shard_map/all_gather | solution.py:43
  9.6 21.3 %copy-start.4 = (bf16[2,4,2]{1,2,0:T(2,128)(2,1)S(1)}, bf16[2,4,2]{1,2,0:T(2,128)(2,1)}, u32[]{:S(2)}) copy-start(bf16[2,4,2]{1,2,0:T(2,128)(2,1)} %param.10) | copy-start | bytes 100
  11.4 16.0 %all-to-all-start.1 = ((bf16[2,16,3,896]{3,0,2,1:T(2,128)(2,1)}), bf16[2,16,3,896]{3,0,2,1:T(2,128)(2,1)S(1)}, u32[]{:S(2)}, u32[]{:S(2)}) async-start(bf16[2,16,3,896]{3,0,2,1:T(2,128)(2,1)} %bitcast.5), calls=%async_computation.1 | async-start | bytes 344064 | tf_op jit(solution)/shard_map/all_to_all | solution.py:77
  27.4 12.1 %all-to-all-start.2 = ((bf16[2,16,3,896]{3,0,2,1:T(2,128)(2,1)}), bf16[2,16,3,896]{3,0,2,1:T(2,128)(2,1)S(1)}, u32[]{:S(2)}, u32[]{:S(2)}) async-start(bf16[2,16,3,896]{3,0,2,1:T(2,128)(2,1)} %bitcast.8), calls=%async_computation.2 | async-start | bytes 344064 | tf_op jit(solution)/shard_map/all_to_all | solution.py:76
  31.1 20.1 %collective-permute-start = (bf16[2,16,3,896]{3,0,2,1:T(2,128)(2,1)S(1)}, bf16[2,16,3,896]{3,0,2,1:T(2,128)(2,1)S(1)}, u32[]{:S(2)}, u32[]{:S(2)}) collective-permute-start(bf16[2,16,3,896]{3,0,2,1:T(2,128)(2,1)S(1)} %all-to-all-done.1), channel_id=1, source_target_pairs={{0,1},{1,0},{2,3},{3,2},{4,5},{5,4},{6,7},{7,6},{8,9},{9,8},{10,11... | collective-permute-start | bytes 516104 | tf_op jit(solution)/shard_map/ppermute | solution.py:13
  39.5 11.5 %collective-permute-start.2 = (bf16[2,16,3,896]{3,0,2,1:T(2,128)(2,1)S(1)}, bf16[2,16,3,896]{3,0,2,1:T(2,128)(2,1)S(1)}, u32[]{:S(2)}, u32[]{:S(2)}) collective-permute-start(bf16[2,16,3,896]{3,0,2,1:T(2,128)(2,1)S(1)} %all-to-all-done.2), channel_id=1, source_target_pairs={{0,1},{1,0},{2,3},{3,2},{4,5},{5,4},{6,7},{7,6},{8,9},{9,8},{10,11... | collective-permute-start | bytes 516104 | tf_op jit(solution)/shard_map/ppermute | solution.py:13
  40.4 9.8 %all-to-all-start = ((bf16[2,16,3]{2,0,1:T(2,128)(2,1)}), bf16[2,16,3]{2,0,1:T(2,128)(2,1)S(1)}, u32[]{:S(2)}, u32[]{:S(2)}) async-start(bf16[2,16,3]{2,0,1:T(2,128)(2,1)} %bitcast.2), calls=%async_computation | async-start | bytes 16384 | tf_op jit(solution)/shard_map/all_to_all | solution.py:78
  43.8 265.1 %reduce-scatter.2.cloned.1.call-start = ((), (), s32[]{:S(2)}) async-start(), calls=%async_computation.9 | async-start | bytes 16515072 | tf_op jit(solution)/shard_map/reduce_scatter | solution.py:120
  51.8 11.0 %collective-permute-start.1 = (bf16[2,16,3,1792]{3,0,2,1:T(2,128)(2,1)S(1)}, bf16[2,16,3,1792]{3,0,2,1:T(2,128)(2,1)S(1)}, u32[]{:S(2)}, u32[]{:S(2)}) collective-permute-start(bf16[2,16,3,1792]{3,0,2,1:T(2,128)(2,1)S(1)} %broadcast_select_fusion.1), channel_id=1, source_target_pairs={{0,2},{1,3},{2,0},{3,1},{4,6},{5,7},{6,4},{7,5},{8,10},{9,11},{10,... | collective-permute-start | bytes 1032200 | tf_op jit(solution)/shard_map/ppermute | solution.py:13
  52.9 16.1 %collective-permute-start.3 = (bf16[2,16,3,1792]{3,0,2,1:T(2,128)(2,1)S(1)}, bf16[2,16,3,1792]{3,0,2,1:T(2,128)(2,1)S(1)}, u32[]{:S(2)}, u32[]{:S(2)}) collective-permute-start(bf16[2,16,3,1792]{3,0,2,1:T(2,128)(2,1)S(1)} %broadcast_select_fusion), channel_id=1, source_target_pairs={{0,2},{1,3},{2,0},{3,1},{4,6},{5,7},{6,4},{7,5},{8,10},{9,11},{10,... | collective-permute-start | bytes 1032200 | tf_op jit(solution)/shard_map/ppermute | solution.py:13
  170.9 2.3 slice-start
  172.0 2.2 slice-start.1
  182.0 12.6 %all-to-all-start.4 = ((bf16[2,16,3]{2,0,1:T(2,128)(2,1)}), bf16[2,16,3]{2,0,1:T(2,128)(2,1)S(1)}, u32[]{:S(2)}, u32[]{:S(2)}) async-start(bf16[2,16,3]{2,0,1:T(2,128)(2,1)} %copy.147), calls=%async_computation.4 | async-start | bytes 16384 | tf_op jit(solution)/shard_map/all_to_all | solution.py:136
  187.7 3.6 %copy-start = (bf16[3584,512]{1,0:T(8,128)(2,1)S(1)}, bf16[3584,512]{1,0:T(8,128)(2,1)}, u32[]{:S(2)}) copy-start(bf16[3584,512]{1,0:T(8,128)(2,1)} %all-gather.6.cloned.1.call-done) | copy-start | bytes 11010052
  194.7 23.1 %all-to-all-start.3 = ((bf16[2,16,3,3584]{3,0,2,1:T(2,128)(2,1)}), bf16[2,16,3,3584]{3,0,2,1:T(2,128)(2,1)S(1)}, u32[]{:S(2)}, u32[]{:S(2)}) async-start(bf16[2,16,3,3584]{3,0,2,1:T(2,128)(2,1)} %copy.143), calls=%async_computation.3 | async-start | bytes 1376256 | tf_op jit(solution)/shard_map/all_to_all | solution.py:133
Sparse Core Ops, SparseCore 0:
  9.5 53.5 all-gather.7
  64.7 50.8 all-gather.5
  117.1 50.8 all-gather.3
  181.4 127.5 reduce-scatter.1
where the time goes:
time: 331 us; the launch traced here: 330 us
  waiting for transfers between devices  231 us (70%)
  starting transfers between devices  28.6 us (9%)
  local copies, waits for them, and re-layouts  25.2 us (8%)
  matrix products  22.1 us (7%)
  between operations  14.2 us (4%)
  other arithmetic  9.56 us (3%)
    reduce_scatter x1, waiting for transfers between devices, on_device(): lax.psum_scatter((jnp.concatenate([part_gate, part_up, part_down], 1) * g...  89.5 us
    all_gather x1, waiting for transfers between devices, on_device(): lax.all_gather(w_down_t, 'pipe', axis=0, tiled=True)  45.5 us
    all_gather x1, waiting for transfers between devices, on_device(): lax.all_gather(w_up, 'pipe', axis=0, tiled=True)  43 us
    all_to_all x1, waiting for transfers between devices, on_device(): lax.all_to_all(input_blocks.astype(jnp.bfloat16), 'expert', split_axis=1,...  15.4 us
    ppermute x4, waiting for transfers between devices, partner(): lax.ppermute(x, axis, [(i, i ^ 1 << stride) for i in range(lax.axis_size(...  13.6 us
    unnamed x21, local copies, waits for them, and re-layouts  11.9 us
    all_to_all x1, waiting for transfers between devices, on_device(): lax.all_to_all(tok_blocks, 'expert', split_axis=1, concat_axis=1, tiled=T...  8.06 us
    all_to_all x1, starting transfers between devices, on_device(): lax.all_to_all(cot_blocks, 'expert', split_axis=1, concat_axis=1, tiled=T...  7.39 us
  transfers between devices with their start and end apart: 13, of which 9 were waited for; matrix products, arithmetic and copies ran while one was open for 9% of the time, Pallas kernels for 0%

commit v1 on v0

v1 whole, which is shorter than its diff:
```python
import functools
import math

import jax
import jax.numpy as jnp
from jax import lax
from jax.experimental import pallas as pl
from jax.experimental.pallas import tpu as pltpu
from jax.sharding import PartitionSpec as P

EXPERTS = 4
CAP = 3
LANES = 128
VMEM_LIMIT = 48 * 1024 * 1024
f32, bf16 = jnp.float32, jnp.bfloat16


def swap(x, axis, bit):
    return lax.ppermute(x, axis, [(i, i ^ bit) for i in range(lax.axis_size(axis))])


def compact_kernel(tok_count, me_ref, rows_ref, slots_ref, place_ref):
    row_count = rows_ref.shape[0]
    slot_count = slots_ref.shape[0]
    width = rows_ref.shape[1] - LANES
    me = me_ref[0].astype(f32)
    extras = rows_ref[:, width:].astype(f32)
    first, second = extras[:, 0:1] == me, extras[:, 1:2] == me
    gate = jnp.where(first, extras[:, 2:3], 0.0) + jnp.where(second, extras[:, 3:4], 0.0)
    routed = jnp.where(first | second, 1.0, 0.0)
    row = lax.broadcasted_iota(jnp.int32, (row_count, row_count), 0)
    other = lax.broadcasted_iota(jnp.int32, (row_count, row_count), 1)
    earlier = ((other < row) & (other // tok_count == row // tok_count)).astype(bf16)
    position = jnp.dot(
        earlier, jnp.broadcast_to(routed, (row_count, LANES)).astype(bf16), preferred_element_type=f32
    )[:, 0:1]
    block = lax.broadcasted_iota(jnp.int32, (row_count, 1), 0) // tok_count
    slot = block.astype(f32) * CAP + position
    lane = lax.broadcasted_iota(jnp.int32, (row_count, slot_count), 1).astype(f32)
    place = jnp.where((lane == slot) & (routed > 0.0), 1.0, 0.0).astype(bf16)
    place_ref[...] = place
    contract = (((0,), (0,)), ((), ()))
    slots_ref[:, :width] = lax.dot_general(
        place, rows_ref[:, :width], contract, preferred_element_type=f32
    ).astype(bf16)
    slots_ref[:, width:] = lax.dot_general(
        place,
        jnp.broadcast_to(gate, (row_count, LANES)).astype(bf16),
        contract,
        preferred_element_type=f32,
    ).astype(bf16)


def hidden_kernel(
    d_part, gate_ref, own_g, own_u, own_b, got_g, got_u, got_b, w_gate, w_up, d_gate, d_up, scaled, back
):
    gate = gate_ref[:, 0:1].astype(f32)
    pre_gate = own_g[...] + got_g[...].astype(f32)
    pre_up = own_u[...] + got_u[...].astype(f32)
    back_proj = own_b[...] + got_b[...].astype(f32)
    sig = jax.nn.sigmoid(pre_gate)
    activated = pre_gate * sig
    hidden = activated * pre_up
    share = jnp.sum(back_proj * hidden, axis=1, keepdims=True)
    scaled[...] = (gate * hidden).astype(bf16)
    d_hidden = gate * back_proj
    d_gate[...] = (d_hidden * pre_up * sig * (1.0 + pre_gate * (1.0 - sig))).astype(bf16)
    d_up[...] = (d_hidden * activated).astype(bf16)
    contract = (((1,), (1,)), ((), ()))
    back[:, :d_part] = (
        lax.dot_general(d_gate[...], w_gate[...], contract, preferred_element_type=f32)
        + lax.dot_general(d_up[...], w_up[...], contract, preferred_element_type=f32)
    ).astype(bf16)
    high = share.astype(bf16)
    low = (share - high.astype(f32)).astype(bf16)
    lane = lax.broadcasted_iota(jnp.int32, (share.shape[0], LANES), 1)
    back[:, d_part:] = jnp.where(lane == 0, high, jnp.where(lane == 1, low, jnp.zeros_like(low)))


def expand_kernel(place_ref, a_ref, b_ref, out_ref):
    total = (a_ref[...].astype(f32) + b_ref[...].astype(f32)).astype(bf16)
    out_ref[...] = jnp.dot(place_ref[...], total, preferred_element_type=f32).astype(bf16)


def call(kernel, out_shape, in_specs, name, flops=0, bytes_accessed=0):
    return pl.pallas_call(
        kernel,
        out_shape=out_shape,
        in_specs=in_specs,
        out_specs=jax.tree.map(lambda _: pl.BlockSpec(memory_space=pltpu.VMEM), out_shape),
        compiler_params=pltpu.CompilerParams(vmem_limit_bytes=VMEM_LIMIT),
        cost_estimate=pl.CostEstimate(flops=flops, bytes_accessed=bytes_accessed, transcendentals=0),
        name=name,
    )


def on_device(tokens, cotangent, expert_ids, gate_values, w_gate, w_up, w_down_t):
    micro_count, tok_count, d_model = tokens.shape
    top_count = expert_ids.shape[2]
    pipe_size = lax.axis_size("pipe")
    expert_size = lax.axis_size("expert")
    group_size = expert_size // EXPERTS
    bits = [1 << i for i in reversed(range(group_size.bit_length() - 1))]
    d_part, f_part = w_gate.shape
    seg = -(-d_part // LANES) * LANES
    width = 2 * seg + LANES
    own_rows = micro_count * tok_count
    expert = lax.axis_index("expert") // group_size

    def shares(x):
        x = x.reshape(own_rows, pipe_size, d_part)
        return jnp.pad(x, ((0, 0), (0, 0), (0, seg - d_part)))

    ids = expert_ids.reshape(own_rows, top_count)
    extras = jnp.concatenate([ids.astype(bf16), gate_values.reshape(own_rows, top_count)], 1)
    extras = jnp.pad(extras, ((0, 0), (0, LANES - 2 * top_count)))
    extras = jnp.broadcast_to(extras[:, None], (own_rows, pipe_size, LANES))
    send = jnp.concatenate([shares(tokens), shares(cotangent), extras], 2)
    send = jnp.swapaxes(send, 0, 1)

    layer_rows = lax.all_to_all(send, "pipe", split_axis=0, concat_axis=0, tiled=True)
    layer_rows = layer_rows.reshape(pipe_size * own_rows, width)
    rows = jnp.concatenate(
        [layer_rows] + [swap(layer_rows, "expert", k * group_size) for k in range(1, EXPERTS)], 0
    )
    row_count = rows.shape[0]
    slot_count = row_count // tok_count * CAP
    vmem = pl.BlockSpec(memory_space=pltpu.VMEM)
    smem = pl.BlockSpec(memory_space=pltpu.SMEM)
    slots, place = call(
        functools.partial(compact_kernel, tok_count),
        (
            jax.ShapeDtypeStruct((slot_count, width), bf16),
            jax.ShapeDtypeStruct((row_count, slot_count), bf16),
        ),
        [smem, vmem],
        "compact",
    )(expert.reshape(1).astype(jnp.int32), rows)

    for bit in bits:
        slots = jnp.concatenate([slots, swap(slots, "expert", bit)], 0)
    total = slots.shape[0]
    tok_rows, cot_rows = slots[:, :d_part], slots[:, seg : seg + d_part]
    gate_col = slots[:, 2 * seg :]

    own, got = [], []
    for left, weight in ((tok_rows, w_gate), (tok_rows, w_up), (cot_rows, w_down_t)):
        part = jnp.dot(left, weight, preferred_element_type=f32)
        bit = pipe_size // 2
        while bit > 1:
            part = part + swap(part.astype(bf16), "pipe", bit).astype(f32)
            bit //= 2
        own.append(part)
        got.append(swap(part.astype(bf16), "pipe", 1) if pipe_size > 1 else jnp.zeros_like(part, bf16))

    hidden_shape = jax.ShapeDtypeStruct((total, f_part), bf16)
    d_gate, d_up, scaled, back = call(
        functools.partial(hidden_kernel, d_part),
        (hidden_shape,) * 3 + (jax.ShapeDtypeStruct((total, d_part + LANES), bf16),),
        [vmem] * 9,
        "hidden",
    )(gate_col, *own, *got, w_gate, w_up)

    tokens_total = own_rows * pipe_size * expert_size
    scale = 1.0 / math.sqrt(tokens_total * top_count / EXPERTS)
    contract = (((0,), (0,)), ((), ()))

    def weight_grad(left, right):
        return (lax.dot_general(left, right, contract, preferred_element_type=f32) * scale).astype(bf16)

    dw_gate = weight_grad(tok_rows, d_gate)
    dw_up = weight_grad(tok_rows, d_up)
    dw_down_t = weight_grad(cot_rows, scaled)

    for bit in reversed(bits[1:]):
        half = back.shape[0] // 2
        back = (back[:half].astype(f32) + swap(back[half:], "expert", bit).astype(f32)).astype(bf16)
    half = back.shape[0] // 2
    got_back = swap(back[half:], "expert", bits[0])
    rows_back = call(
        expand_kernel,
        jax.ShapeDtypeStruct((row_count, d_part + LANES), bf16),
        [vmem] * 3,
        "expand",
    )(place, back[:half], got_back)

    block = pipe_size * own_rows
    pieces = [rows_back[:block]] + [
        swap(rows_back[k * block : (k + 1) * block], "expert", k * group_size) for k in range(1, EXPERTS)
    ]
    summed = sum(piece[:, :d_part].astype(f32) for piece in pieces).astype(bf16)
    summed = summed.reshape(pipe_size, own_rows, d_part)
    d_tokens = lax.all_to_all(summed, "pipe", split_axis=0, concat_axis=0, tiled=True)
    d_tokens = jnp.swapaxes(d_tokens, 0, 1).reshape(micro_count, tok_count, d_model)
    start = lax.axis_index("pipe") * own_rows
    gate_grad = jnp.zeros((own_rows, top_count), f32)
    for k, piece in enumerate(pieces):
        share = lax.dynamic_slice_in_dim(piece[:, d_part : d_part + 2].astype(f32), start, own_rows, 0)
        gate_grad = gate_grad + jnp.where(ids == (expert ^ k), share[:, 0:1] + share[:, 1:2], 0.0)
    gate_weight_gradient = gate_grad.reshape(micro_count, tok_count, top_count)
    return (d_tokens, gate_weight_gradient, dw_gate, dw_up, dw_down_t)


def solution(mesh):
    rows = P(None, ("pipe", "expert"), None)
    weights = P("pipe", "expert")
    return jax.shard_map(
        on_device,
        mesh=mesh,
        in_specs=(rows, rows, rows, rows, weights, weights, weights),
        out_specs=(rows, rows, weights, weights, weights),
        check_vma=False,
    )
```

time: 331 us -> 89.3 us (0.27)
  waiting for transfers between devices: 231 us -> 39.9 us
  local copies, waits for them, and re-layouts: 25.2 us -> 6.41 us
  between operations: 14.2 us -> 0.86 us
  matrix products: 22.1 us -> 9.36 us
  starting transfers between devices: 28.6 us -> 16.9 us
  blocking collectives: 0 us -> 8.41 us
  other arithmetic: 9.56 us -> 2.92 us
  Pallas kernels: 0 us -> 4.07 us
    reduce_scatter x1 -> x0, waiting for transfers between devices: 89.5 us -> none  [on_device(): lax.psum_scatter((jnp.concatenate([part_gate, part_up, part_down], 1) * g...]
    all_gather x3 -> x0, waiting for transfers between devices: 88.6 us -> none  [the longest x1 45.5 us: on_device(): lax.all_gather(w_down_t, 'pipe', axis=0, tiled=True)]
    all_to_all x5 -> x1, waiting for transfers between devices: 36.9 us -> 3.46 us  [on_device(): lax.all_to_all(summed, 'pipe', split_axis=0, concat_axis=0, tiled=True)]
    ppermute x4 -> x13, waiting for transfers between devices: 13.6 us -> 36.4 us  [swap(): lax.ppermute(x, axis, [(i, i ^ bit) for i in range(lax.axis_size(axis))])]
    all_to_all x5 -> x1, starting transfers between devices: 26 us -> 3.29 us  [on_device(): lax.all_to_all(summed, 'pipe', split_axis=0, concat_axis=0, tiled=True)]
    dot_general x13 -> x6, matrix products: 22.1 us -> 9.36 us  [the longest x3 5.71 us: weight_grad(): lax.dot_general(left, right, contract, preferred_element_type=f32) * scale]
    ppermute x4 -> x13, starting transfers between devices: 2.44 us -> 13.6 us  [swap(): lax.ppermute(x, axis, [(i, i ^ bit) for i in range(lax.axis_size(axis))])]
    unnamed x21 -> x18, local copies, waits for them, and re-layouts: 11.9 us -> 2.5 us
  transfers between devices with their start and end apart: 13 -> 14, of which waited for: 9 -> 12; matrix products, arithmetic and copies ran while one was open for 9% -> 11% of each run, Pallas kernels for 0% -> 0%
where the time goes in v1:
time: 89.3 us; the launch traced here: 88.8 us
  waiting for transfers between devices  39.9 us (45%)
  starting transfers between devices  16.9 us (19%)
  matrix products  9.36 us (10%)
  blocking collectives  8.41 us (9%)
  local copies, waits for them, and re-layouts  6.41 us (7%)
  Pallas kernels  4.07 us (5%)
  other arithmetic  2.92 us (3%)
    ppermute x13, waiting for transfers between devices, swap(): lax.ppermute(x, axis, [(i, i ^ bit) for i in range(lax.axis_size(axis))])  36.4 us
    ppermute x13, starting transfers between devices, swap(): lax.ppermute(x, axis, [(i, i ^ bit) for i in range(lax.axis_size(axis))])  13.6 us
    all_to_all x1, blocking collectives, on_device(): lax.all_to_all(send, 'pipe', split_axis=0, concat_axis=0, tiled=True)  8.41 us
    dot_general x3, matrix products, weight_grad(): lax.dot_general(left, right, contract, preferred_element_type=f32) * scale  5.71 us
    dot_general x3, matrix products, on_device(): part = jnp.dot(left, weight, preferred_element_type=f32)  3.65 us
    all_to_all x1, waiting for transfers between devices, on_device(): lax.all_to_all(summed, 'pipe', split_axis=0, concat_axis=0, tiled=True)  3.46 us
    all_to_all x1, starting transfers between devices, on_device(): lax.all_to_all(summed, 'pipe', split_axis=0, concat_axis=0, tiled=True)  3.29 us
    pallas_call x1, Pallas kernels, on_device(): call(functools.partial(hidden_kernel, d_part), (hidden_shape,) * 3 + (jax...  3.21 us
  transfers between devices with their start and end apart: 14, of which 12 were waited for; matrix products, arithmetic and copies ran while one was open for 11% of the time, Pallas kernels for 0%

profile of v1, /device:TPU:0, one launch (start us, length us, event | category | flops | bytes accessed | tf_op | source)
XLA Modules:
  0.0 88.8 jit_solution(4829821307781458707)
XLA Ops:
  0.6 0.8 copy.19
  2.4 0.8 reshape.56
  3.3 0.8 reshape.57
  4.2 8.4 %all_to_all.10 = bf16[2,8,3712]{2,1,0:T(8,128)(2,1)S(1)} all-to-all(bf16[2,8,3712]{2,1,0:T(8,128)(2,1)S(1)} %maximum_bitcast_fusion), channel_id=1, replica_groups=mesh['pipe'=2,'expert'=16] {'pipe'}, dimensions={0} | all-to-all | bytes 237568 | tf_op jit(solution)/shard_map/all_to_all | solution.py:121
  12.6 3.6 %collective-permute-start.2 = (bf16[16,3712]{1,0:T(8,128)(2,1)S(1)}, bf16[16,3712]{1,0:T(8,128)(2,1)S(1)}, u32[]{:S(2)}, u32[]{:S(2)}) collective-permute-start(bf16[16,3712]{1,0:T(8,128)(2,1)S(1)} %bitcast.17), channel_id=1, source_target_pairs={{0,12},{1,13},{2,14},{3,15},{4,8},{5,9},{6,10},{7,11},{8,4},{9,5},... | collective-permute-start | bytes 356360 | tf_op jit(solution)/shard_map/ppermute | solution.py:19
  16.2 0.8 collective-permute-start
  17.0 2.9 %collective-permute-done.2 = bf16[16,3712]{1,0:T(8,128)(2,1)S(1)} collective-permute-done((bf16[16,3712]{1,0:T(8,128)(2,1)S(1)}, bf16[16,3712]{1,0:T(8,128)(2,1)S(1)}, u32[]{:S(2)}, u32[]{:S(2)}) %collective-permute-start.2) | collective-permute-done | bytes 118816 | tf_op jit(solution)/shard_map/ppermute | solution.py:19
  19.9 5.0 %collective-permute-done.1 = bf16[16,3712]{1,0:T(8,128)(2,1)S(1)} collective-permute-done((bf16[16,3712]{1,0:T(8,128)(2,1)S(1)}, bf16[16,3712]{1,0:T(8,128)(2,1)S(1)}, u32[]{:S(2)}, u32[]{:S(2)}) %collective-permute-start.1) | collective-permute-done | bytes 118816 | tf_op jit(solution)/shard_map/ppermute | solution.py:19
  25.6 1.6 %collective-permute-start.3 = (bf16[48,3712]{1,0:T(8,128)(2,1)S(1)}, bf16[48,3712]{1,0:T(8,128)(2,1)S(1)}, u32[]{:S(2)}, u32[]{:S(2)}) collective-permute-start(bf16[48,3712]{1,0:T(8,128)(2,1)S(1)} %get-tuple-element.12), channel_id=1, source_target_pairs={{0,2},{1,3},{2,0},{3,1},{4,6},{5,7},{6,4},{7,5},{8,10},{9,11},{10,... | collective-permute-start | bytes 1069064 | tf_op jit(solution)/shard_map/ppermute | solution.py:19
  27.2 7.8 %collective-permute-done.3 = bf16[48,3712]{1,0:T(8,128)(2,1)S(1)} collective-permute-done((bf16[48,3712]{1,0:T(8,128)(2,1)S(1)}, bf16[48,3712]{1,0:T(8,128)(2,1)S(1)}, u32[]{:S(2)}, u32[]{:S(2)}) %collective-permute-start.3) | collective-permute-done | bytes 356384 | tf_op jit(solution)/shard_map/ppermute | solution.py:19
  35.2 2.1 %collective-permute-done.4 = bf16[96,3712]{1,0:T(8,128)(2,1)S(1)} collective-permute-done((bf16[96,3712]{1,0:T(8,128)(2,1)S(1)}, bf16[96,3712]{1,0:T(8,128)(2,1)S(1)}, u32[]{:S(2)}, u32[]{:S(2)}) %collective-permute-start.4) | collective-permute-done | bytes 712736 | tf_op jit(solution)/shard_map/ppermute | solution.py:19
  37.4 1.2 %fusion.16 = (bf16[192,512]{1,0:T(8,128)(2,1)}, f32[192,512]{1,0:T(8,128)S(1)}) fusion(bf16[1792,512]{1,0:T(8,128)(2,1)S(1)} %copy-done.3, bf16[192,3712]{1,0:T(8,128)(2,1)S(1)} %constant_dynamic-update-slice_fusion), kind=kOutput, calls=%fused_computation.40 | convolution fusion | flops 352419840 | bytes 3112960 | tf_op jit(solution)/shard_map/dot_general | solution.py:148
  38.9 1.2 %fusion.17 = (bf16[192,512]{1,0:T(8,128)(2,1)}, f32[192,512]{1,0:T(8,128)S(1)}) fusion(bf16[1792,512]{1,0:T(8,128)(2,1)S(1)} %copy-done, bf16[192,3712]{1,0:T(8,128)(2,1)S(1)} %constant_dynamic-update-slice_fusion), kind=kOutput, calls=%fused_computation.41 | convolution fusion | flops 352419840 | bytes 3112960 | tf_op jit(solution)/shard_map/dot_general | solution.py:148
  40.1 1.7 %collective-permute-start.7 = (bf16[192,512]{1,0:T(8,128)(2,1)}, bf16[192,512]{1,0:T(8,128)(2,1)S(1)}, u32[]{:S(2)}, u32[]{:S(2)}) collective-permute-start(bf16[192,512]{1,0:T(8,128)(2,1)} %get-tuple-element.26), channel_id=1, source_target_pairs={{0,16},{16,0},{1,17},{17,1},{2,18},{18,2},{3,19},{19,3},{4,20},{20... | collective-permute-start | bytes 589832 | tf_op jit(solution)/shard_map/ppermute | solution.py:19
  41.9 1.2 %fusion.15 = (bf16[192,512]{1,0:T(8,128)(2,1)}, f32[192,512]{1,0:T(8,128)S(1)}) fusion(bf16[1792,512]{1,0:T(8,128)(2,1)S(1)} %copy-done.1, bf16[192,3712]{1,0:T(8,128)(2,1)S(1)} %constant_dynamic-update-slice_fusion), kind=kOutput, calls=%fused_computation.39 | convolution fusion | flops 352419840 | bytes 3112960 | tf_op jit(solution)/shard_map/dot_general | solution.py:148
  43.4 0.8 slice.107.gate_ref
  44.2 2.4 %collective-permute-done.6.got_u = bf16[192,512]{1,0:T(8,128)(2,1)S(1)} collective-permute-done((bf16[192,512]{1,0:T(8,128)(2,1)}, bf16[192,512]{1,0:T(8,128)(2,1)S(1)}, u32[]{:S(2)}, u32[]{:S(2)}) %collective-permute-start.6) | collective-permute-done | bytes 196640 | tf_op jit(solution)/shard_map/ppermute | solution.py:19
  46.6 4.2 %collective-permute-done.7.got_b = bf16[192,512]{1,0:T(8,128)(2,1)S(1)} collective-permute-done((bf16[192,512]{1,0:T(8,128)(2,1)}, bf16[192,512]{1,0:T(8,128)(2,1)S(1)}, u32[]{:S(2)}, u32[]{:S(2)}) %collective-permute-start.7) | collective-permute-done | bytes 196640 | tf_op jit(solution)/shard_map/ppermute | solution.py:19
  50.8 3.5 %collective-permute-done.5.got_g = bf16[192,512]{1,0:T(8,128)(2,1)} collective-permute-done((bf16[192,512]{1,0:T(8,128)(2,1)}, bf16[192,512]{1,0:T(8,128)(2,1)}, u32[]{:S(2)}, u32[]{:S(2)}) %collective-permute-start.5) | collective-permute-done | bytes 196640 | tf_op jit(solution)/shard_map/ppermute | solution.py:19
  54.3 1.5 %copy-done.2 = bf16[1792,512]{1,0:T(8,128)(2,1)S(1)} copy-done((bf16[1792,512]{1,0:T(8,128)(2,1)S(1)}, bf16[1792,512]{1,0:T(8,128)(2,1)}, u32[]{:S(2)}) %copy-start.2) | copy-done | bytes 1835032
  55.8 3.2 %hidden.1 = (bf16[192,512]{1,0:T(8,128)(2,1)S(1)}, bf16[192,512]{1,0:T(8,128)(2,1)S(1)}, bf16[192,512]{1,0:T(8,128)(2,1)S(1)}, bf16[192,1920]{1,0:T(8,128)(2,1)S(1)}) custom-call(bf16[192,128]{1,0:T(8,128)(2,1)S(1)} %slice.107.gate_ref, f32[192,512]{1,0:T(8,128)S(1)} %get-tuple-element.23.own_g, f32[192,512]{1,0:T(8,128)S(1)} %get-tuple-element.25.own_u, ...), custom_call_target="tpu_custom_call" | custom-call | tf_op jit(solution)/shard_map/hidden/pallas_call | solution.py:157
  59.1 1.9 %multiply_convert_fusion.2 = bf16[1792,512]{1,0:T(8,128)(2,1)} fusion(bf16[192,512]{1,0:T(8,128)(2,1)S(1)} %get-tuple-element.14, bf16[192,3712]{1,0:T(8,128)(2,1)S(1)} %copy-done.5), kind=kOutput, calls=%fused_computation.2 | convolution fusion | flops 354156544 | bytes 2719744 | tf_op jit(solution)/shard_map/dot_general | solution.py:169
  61.0 1.9 %multiply_convert_fusion.1 = bf16[1792,512]{1,0:T(8,128)(2,1)} fusion(bf16[192,512]{1,0:T(8,128)(2,1)S(1)} %get-tuple-element.15, bf16[192,3712]{1,0:T(8,128)(2,1)S(1)} %copy-done.5), kind=kOutput, calls=%fused_computation.1 | convolution fusion | flops 354156544 | bytes 2719744 | tf_op jit(solution)/shard_map/dot_general | solution.py:169
  63.1 1.6 %collective-permute-start.9 = (bf16[48,1920]{1,0:T(8,128)(2,1)S(1)}, bf16[48,1920]{1,0:T(8,128)(2,1)S(1)}, u32[]{:S(2)}, u32[]{:S(2)}) collective-permute-start(bf16[48,1920]{1,0:T(8,128)(2,1)S(1)} %get-tuple-element.17), channel_id=1, source_target_pairs={{0,2},{1,3},{2,0},{3,1},{4,6},{5,7},{6,4},{7,5},{8,10},{9,11},{10,... | collective-permute-start | bytes 552968 | tf_op jit(solution)/shard_map/ppermute | solution.py:19
  64.7 1.9 %multiply_convert_fusion = bf16[1792,512]{1,0:T(8,128)(2,1)} fusion(bf16[192,512]{1,0:T(8,128)(2,1)S(1)} %get-tuple-element.16, bf16[192,3712]{1,0:T(8,128)(2,1)S(1)} %copy-done.5), kind=kOutput, calls=%fused_computation | convolution fusion | flops 354156544 | bytes 2719744 | tf_op jit(solution)/shard_map/dot_general | solution.py:169
  66.6 3.6 %collective-permute-done.9.b_ref = bf16[48,1920]{1,0:T(8,128)(2,1)S(1)} collective-permute-done((bf16[48,1920]{1,0:T(8,128)(2,1)S(1)}, bf16[48,1920]{1,0:T(8,128)(2,1)S(1)}, u32[]{:S(2)}, u32[]{:S(2)}) %collective-permute-start.9) | collective-permute-done | bytes 184352 | tf_op jit(solution)/shard_map/ppermute | solution.py:19
  70.8 1.0 %collective-permute-start.12 = (bf16[16,1920]{1,0:T(8,128)(2,1)S(1)}, bf16[16,1920]{1,0:T(8,128)(2,1)S(1)}, u32[]{:S(2)}, u32[]{:S(2)}) collective-permute-start(bf16[16,1920]{1,0:T(8,128)(2,1)S(1)} %get-tuple-element.20), channel_id=1, source_target_pairs={{0,12},{1,13},{2,14},{3,15},{4,8},{5,9},{6,10},{7,11},{8,4},{9,5},... | collective-permute-start | bytes 184328 | tf_op jit(solution)/shard_map/ppermute | solution.py:19
  71.8 2.5 %collective-permute-start.11 = (bf16[16,1920]{1,0:T(8,128)(2,1)S(1)}, bf16[16,1920]{1,0:T(8,128)(2,1)S(1)}, u32[]{:S(2)}, u32[]{:S(2)}) collective-permute-start(bf16[16,1920]{1,0:T(8,128)(2,1)S(1)} %get-tuple-element.21), channel_id=1, source_target_pairs={{0,8},{1,9},{2,10},{3,11},{4,12},{5,13},{6,14},{7,15},{8,0},{9,1},... | collective-permute-start | bytes 184328 | tf_op jit(solution)/shard_map/ppermute | solution.py:19
  75.0 2.0 %collective-permute-done.12 = bf16[16,1920]{1,0:T(8,128)(2,1)S(1)} collective-permute-done((bf16[16,1920]{1,0:T(8,128)(2,1)S(1)}, bf16[16,1920]{1,0:T(8,128)(2,1)S(1)}, u32[]{:S(2)}, u32[]{:S(2)}) %collective-permute-start.12) | collective-permute-done | bytes 61472 | tf_op jit(solution)/shard_map/ppermute | solution.py:19
  77.0 2.5 %collective-permute-done.11 = bf16[16,1920]{1,0:T(8,128)(2,1)S(1)} collective-permute-done((bf16[16,1920]{1,0:T(8,128)(2,1)S(1)}, bf16[16,1920]{1,0:T(8,128)(2,1)S(1)}, u32[]{:S(2)}, u32[]{:S(2)}) %collective-permute-start.11) | collective-permute-done | bytes 61472 | tf_op jit(solution)/shard_map/ppermute | solution.py:19
  80.7 3.3 %all-to-all-start.1 = ((bf16[2,8,1792]{2,1,0:T(8,128)(2,1)}), bf16[2,8,1792]{2,1,0:T(8,128)(2,1)S(1)}, u32[]{:S(2)}, u32[]{:S(2)}) async-start(bf16[2,8,1792]{2,1,0:T(8,128)(2,1)} %fusion.9), calls=%async_computation.1 | async-start | bytes 114688 | tf_op jit(solution)/shard_map/all_to_all | solution.py:193
  84.6 3.5 %all-to-all-done.1 = bf16[2,8,1792]{2,1,0:T(8,128)(2,1)S(1)} async-done(((bf16[2,8,1792]{2,1,0:T(8,128)(2,1)}), bf16[2,8,1792]{2,1,0:T(8,128)(2,1)S(1)}, u32[]{:S(2)}, u32[]{:S(2)}) %all-to-all-start.1) | async-done | bytes 57376 | tf_op jit(solution)/shard_map/all_to_all | solution.py:193
  (63 shorter events, 6.7 us)
Async XLA Ops:
  0.6 38.3 %copy-start = (bf16[1792,512]{1,0:T(8,128)(2,1)S(1)}, bf16[1792,512]{1,0:T(8,128)(2,1)}, u32[]{:S(2)}) copy-start(bf16[1792,512]{1,0:T(8,128)(2,1)} %param.13) | copy-start | bytes 5505028
  12.6 7.3 %collective-permute-start.2 = (bf16[16,3712]{1,0:T(8,128)(2,1)S(1)}, bf16[16,3712]{1,0:T(8,128)(2,1)S(1)}, u32[]{:S(2)}, u32[]{:S(2)}) collective-permute-start(bf16[16,3712]{1,0:T(8,128)(2,1)S(1)} %bitcast.17), channel_id=1, source_target_pairs={{0,12},{1,13},{2,14},{3,15},{4,8},{5,9},{6,10},{7,11},{8,4},{9,5},... | collective-permute-start | bytes 356360 | tf_op jit(solution)/shard_map/ppermute | solution.py:19
  16.2 8.7 %collective-permute-start.1 = (bf16[16,3712]{1,0:T(8,128)(2,1)S(1)}, bf16[16,3712]{1,0:T(8,128)(2,1)S(1)}, u32[]{:S(2)}, u32[]{:S(2)}) collective-permute-start(bf16[16,3712]{1,0:T(8,128)(2,1)S(1)} %bitcast.18), channel_id=1, source_target_pairs={{0,8},{1,9},{2,10},{3,11},{4,12},{5,13},{6,14},{7,15},{8,0},{9,1},... | collective-permute-start | bytes 356360 | tf_op jit(solution)/shard_map/ppermute | solution.py:19
  16.2 8.7 %collective-permute-start = (bf16[16,3712]{1,0:T(8,128)(2,1)S(1)}, bf16[16,3712]{1,0:T(8,128)(2,1)S(1)}, u32[]{:S(2)}, u32[]{:S(2)}) collective-permute-start(bf16[16,3712]{1,0:T(8,128)(2,1)S(1)} %bitcast.19), channel_id=1, source_target_pairs={{0,4},{1,5},{2,6},{3,7},{4,0},{5,1},{6,2},{7,3},{8,12},{9,13},{10,... | collective-permute-start | bytes 356360 | tf_op jit(solution)/shard_map/ppermute | solution.py:19
  25.6 11.8 %copy-start.3 = (bf16[1792,512]{1,0:T(8,128)(2,1)S(1)}, bf16[1792,512]{1,0:T(8,128)(2,1)}, u32[]{:S(2)}) copy-start(bf16[1792,512]{1,0:T(8,128)(2,1)} %w_up.1) | copy-start | bytes 5505028
  25.6 9.4 %collective-permute-start.3 = (bf16[48,3712]{1,0:T(8,128)(2,1)S(1)}, bf16[48,3712]{1,0:T(8,128)(2,1)S(1)}, u32[]{:S(2)}, u32[]{:S(2)}) collective-permute-start(bf16[48,3712]{1,0:T(8,128)(2,1)S(1)} %get-tuple-element.12), channel_id=1, source_target_pairs={{0,2},{1,3},{2,0},{3,1},{4,6},{5,7},{6,4},{7,5},{8,10},{9,11},{10,... | collective-permute-start | bytes 1069064 | tf_op jit(solution)/shard_map/ppermute | solution.py:19
  35.0 2.2 %collective-permute-start.4 = (bf16[96,3712]{1,0:T(8,128)(2,1)S(1)}, bf16[96,3712]{1,0:T(8,128)(2,1)S(1)}, u32[]{:S(2)}, u32[]{:S(2)}) collective-permute-start(bf16[96,3712]{1,0:T(8,128)(2,1)S(1)} %pad_maximum_fusion), channel_id=1, source_target_pairs={{0,1},{1,0},{2,3},{3,2},{4,5},{5,4},{6,7},{7,6},{8,9},{9,8},{10,11... | collective-permute-start | bytes 2138120 | tf_op jit(solution)/shard_map/ppermute | solution.py:19
  37.4 4.5 %copy-start.4 = (bf16[192,3712]{1,0:T(8,128)(2,1)}, bf16[192,3712]{1,0:T(8,128)(2,1)S(1)}, u32[]{:S(2)}) copy-start(bf16[192,3712]{1,0:T(8,128)(2,1)S(1)} %constant_dynamic-update-slice_fusion) | copy-start | bytes 4276228
  38.6 3.3 %copy-start.1 = (bf16[1792,512]{1,0:T(8,128)(2,1)S(1)}, bf16[1792,512]{1,0:T(8,128)(2,1)}, u32[]{:S(2)}) copy-start(bf16[1792,512]{1,0:T(8,128)(2,1)} %w_gate.1) | copy-start | bytes 5505028
  38.6 8.0 %collective-permute-start.6 = (bf16[192,512]{1,0:T(8,128)(2,1)}, bf16[192,512]{1,0:T(8,128)(2,1)S(1)}, u32[]{:S(2)}, u32[]{:S(2)}) collective-permute-start(bf16[192,512]{1,0:T(8,128)(2,1)} %get-tuple-element.24), channel_id=1, source_target_pairs={{0,16},{16,0},{1,17},{17,1},{2,18},{18,2},{3,19},{19,3},{4,20},{20... | collective-permute-start | bytes 589832 | tf_op jit(solution)/shard_map/ppermute | solution.py:19
  40.1 10.7 %collective-permute-start.7 = (bf16[192,512]{1,0:T(8,128)(2,1)}, bf16[192,512]{1,0:T(8,128)(2,1)S(1)}, u32[]{:S(2)}, u32[]{:S(2)}) collective-permute-start(bf16[192,512]{1,0:T(8,128)(2,1)} %get-tuple-element.26), channel_id=1, source_target_pairs={{0,16},{16,0},{1,17},{17,1},{2,18},{18,2},{3,19},{19,3},{4,20},{20... | collective-permute-start | bytes 589832 | tf_op jit(solution)/shard_map/ppermute | solution.py:19
  43.1 11.2 %collective-permute-start.5 = (bf16[192,512]{1,0:T(8,128)(2,1)}, bf16[192,512]{1,0:T(8,128)(2,1)}, u32[]{:S(2)}, u32[]{:S(2)}) collective-permute-start(bf16[192,512]{1,0:T(8,128)(2,1)} %get-tuple-element.22), channel_id=1, source_target_pairs={{0,16},{16,0},{1,17},{17,1},{2,18},{18,2},{3,19},{19,3},{4,20},{20... | collective-permute-start | bytes 589832 | tf_op jit(solution)/shard_map/ppermute | solution.py:19
  54.3 1.5 %copy-start.2 = (bf16[1792,512]{1,0:T(8,128)(2,1)S(1)}, bf16[1792,512]{1,0:T(8,128)(2,1)}, u32[]{:S(2)}) copy-start(bf16[1792,512]{1,0:T(8,128)(2,1)} %w_gate.1) | copy-start | bytes 5505028
  55.8 3.3 %copy-start.5 = (bf16[192,3712]{1,0:T(8,128)(2,1)S(1)}, bf16[192,3712]{1,0:T(8,128)(2,1)}, u32[]{:S(2)}) copy-start(bf16[192,3712]{1,0:T(8,128)(2,1)} %copy-done.4) | copy-start | bytes 4276228
  59.0 3.9 %collective-permute-start.8 = (bf16[96,1920]{1,0:T(8,128)(2,1)S(1)}, bf16[96,1920]{1,0:T(8,128)(2,1)S(1)}, u32[]{:S(2)}, u32[]{:S(2)}) collective-permute-start(bf16[96,1920]{1,0:T(8,128)(2,1)S(1)} %slice.85), channel_id=1, source_target_pairs={{0,1},{1,0},{2,3},{3,2},{4,5},{5,4},{6,7},{7,6},{8,9},{9,8},{10,11... | collective-permute-start | bytes 1105928 | tf_op jit(solution)/shard_map/ppermute | solution.py:19
  63.1 7.1 %collective-permute-start.9 = (bf16[48,1920]{1,0:T(8,128)(2,1)S(1)}, bf16[48,1920]{1,0:T(8,128)(2,1)S(1)}, u32[]{:S(2)}, u32[]{:S(2)}) collective-permute-start(bf16[48,1920]{1,0:T(8,128)(2,1)S(1)} %get-tuple-element.17), channel_id=1, source_target_pairs={{0,2},{1,3},{2,0},{3,1},{4,6},{5,7},{6,4},{7,5},{8,10},{9,11},{10,... | collective-permute-start | bytes 552968 | tf_op jit(solution)/shard_map/ppermute | solution.py:19
  64.7 19.3 %copy-start.6 = (s32[2,4,2]{1,2,0:T(2,128)S(1)}, s32[2,4,2]{1,2,0:T(2,128)}, u32[]{:S(2)}) copy-start(s32[2,4,2]{1,2,0:T(2,128)} %param.9) | copy-start | bytes 196
  70.4 4.3 %collective-permute-start.10 = (bf16[16,1920]{1,0:T(8,128)(2,1)S(1)}, bf16[16,1920]{1,0:T(8,128)(2,1)S(1)}, u32[]{:S(2)}, u32[]{:S(2)}) collective-permute-start(bf16[16,1920]{1,0:T(8,128)(2,1)S(1)} %get-tuple-element.19), channel_id=1, source_target_pairs={{0,4},{1,5},{2,6},{3,7},{4,0},{5,1},{6,2},{7,3},{8,12},{9,13},{10,... | collective-permute-start | bytes 184328 | tf_op jit(solution)/shard_map/ppermute | solution.py:19
  70.8 6.2 %collective-permute-start.12 = (bf16[16,1920]{1,0:T(8,128)(2,1)S(1)}, bf16[16,1920]{1,0:T(8,128)(2,1)S(1)}, u32[]{:S(2)}, u32[]{:S(2)}) collective-permute-start(bf16[16,1920]{1,0:T(8,128)(2,1)S(1)} %get-tuple-element.20), channel_id=1, source_target_pairs={{0,12},{1,13},{2,14},{3,15},{4,8},{5,9},{6,10},{7,11},{8,4},{9,5},... | collective-permute-start | bytes 184328 | tf_op jit(solution)/shard_map/ppermute | solution.py:19
  71.8 7.7 %collective-permute-start.11 = (bf16[16,1920]{1,0:T(8,128)(2,1)S(1)}, bf16[16,1920]{1,0:T(8,128)(2,1)S(1)}, u32[]{:S(2)}, u32[]{:S(2)}) collective-permute-start(bf16[16,1920]{1,0:T(8,128)(2,1)S(1)} %get-tuple-element.21), channel_id=1, source_target_pairs={{0,8},{1,9},{2,10},{3,11},{4,12},{5,13},{6,14},{7,15},{8,0},{9,1},... | collective-permute-start | bytes 184328 | tf_op jit(solution)/shard_map/ppermute | solution.py:19
  80.7 7.4 %all-to-all-start.1 = ((bf16[2,8,1792]{2,1,0:T(8,128)(2,1)}), bf16[2,8,1792]{2,1,0:T(8,128)(2,1)S(1)}, u32[]{:S(2)}, u32[]{:S(2)}) async-start(bf16[2,8,1792]{2,1,0:T(8,128)(2,1)} %fusion.9), calls=%async_computation.1 | async-start | bytes 114688 | tf_op jit(solution)/shard_map/all_to_all | solution.py:193

commit v2 on v1

v2 whole, which is shorter than its diff:
```python
import functools
import math

import jax
import jax.numpy as jnp
from jax import lax
from jax.experimental import pallas as pl
from jax.experimental.pallas import tpu as pltpu
from jax.sharding import PartitionSpec as P

EXPERTS = 4
CAP = 3
GROUPS = 2
LANES = 128
f32, bf16, i32 = jnp.float32, jnp.bfloat16, jnp.int32
ROWS_BY_ROWS = (((0,), (0,)), ((), ()))
COLUMNS_BY_COLUMNS = (((1,), (1,)), ((), ()))


def swap(x, axis, bit):
    return lax.ppermute(x, axis, [(i, i ^ bit) for i in range(lax.axis_size(axis))])


def prep_kernel(d_part, tok_ref, cot_ref, ids_ref, gate_ref, out_ref):
    micro_count = tok_ref.shape[0]
    seg = out_ref.shape[2] - LANES

    def flat(ref):
        return jnp.concatenate([ref[m].astype(f32) for m in range(micro_count)], 0)

    ids, gates = flat(ids_ref), flat(gate_ref)
    lane = lax.broadcasted_iota(i32, (ids.shape[0], LANES), 1)
    extras = jnp.zeros((ids.shape[0], LANES), f32)
    for k in range(ids.shape[1]):
        extras = jnp.where(lane == k, ids[:, k : k + 1], extras)
        extras = jnp.where(lane == ids.shape[1] + k, gates[:, k : k + 1], extras)
    both = jnp.concatenate([flat(tok_ref), flat(cot_ref)], 0).astype(bf16)
    extras = jnp.concatenate([extras, extras], 0).astype(bf16)
    for p in range(out_ref.shape[0]):
        out_ref[p, :, :d_part] = both[:, p * d_part : (p + 1) * d_part]
        if seg > d_part:
            out_ref[p, :, d_part:seg] = jnp.zeros((both.shape[0], seg - d_part), bf16)
        out_ref[p, :, seg:] = extras


def pack_kernel(tok_count, top_count, me_ref, rows_ref, *out_refs):
    slot_refs, place_ref, info_ref = out_refs[:EXPERTS], out_refs[EXPERTS], out_refs[EXPERTS + 1]
    pipe_size, both_rows, width = rows_ref.shape
    own_rows = both_rows // 2
    total = pipe_size * both_rows
    slot_count = slot_refs[0].shape[0] // 2
    me = me_ref[0]
    rows = jnp.concatenate([rows_ref[p] for p in range(pipe_size)], 0)
    extras = rows[:, width - LANES :].astype(f32)
    row = lax.broadcasted_iota(i32, (total, total), 0)
    other = lax.broadcasted_iota(i32, (total, total), 1)
    earlier = ((other < row) & (other // tok_count == row // tok_count)).astype(bf16)
    at = (lax.broadcasted_iota(i32, (total, LANES), 1) ^ me).astype(f32)
    routed = jnp.zeros((total, LANES), f32)
    for k in range(top_count):
        routed = jnp.where(extras[:, k : k + 1] == at, 1.0, routed)
    position = jnp.dot(earlier, routed.astype(bf16), preferred_element_type=f32)
    index = lax.broadcasted_iota(i32, (total, 1), 0)
    within = index % both_rows
    kind = within // own_rows
    block = index // both_rows * (own_rows // tok_count) + within % own_rows // tok_count
    base = (kind * slot_count + block * CAP).astype(f32)
    lane = lax.broadcasted_iota(i32, (total, 2 * slot_count), 1).astype(f32)
    for k in range(EXPERTS):
        chosen = (lane == base + position[:, k : k + 1]) & (routed[:, k : k + 1] > 0.0)
        place = jnp.where(chosen, 1.0, 0.0)
        slot_refs[k][...] = lax.dot_general(
            place.astype(bf16), rows, ROWS_BY_ROWS, preferred_element_type=f32
        ).astype(bf16)
        for p in range(pipe_size):
            start = p * both_rows
            place_ref[k, p * own_rows : (p + 1) * own_rows, :] = place[start : start + own_rows, :slot_count]
    for p in range(pipe_size):
        start = p * both_rows
        info_ref[p * own_rows : (p + 1) * own_rows, :] = extras[start : start + own_rows]


def hidden_kernel(d_part, top_count, me_ref, *refs):
    groups = [refs[7 * g : 7 * (g + 1)] for g in range(GROUPS)]
    w_gate, w_up, d_gate, d_up, scaled, low_back, high_back = refs[7 * GROUPS :]
    me = me_ref[0].astype(f32)
    shares = []
    for g, (info, own_g, own_u, own_b, got_g, got_u, got_b) in enumerate(groups):
        count = info.shape[0]
        extras = info[...].astype(f32)
        gate = jnp.zeros((count, 1), f32)
        for k in range(top_count):
            gate = gate + jnp.where(
                extras[:, k : k + 1] == me, extras[:, top_count + k : top_count + k + 1], 0.0
            )
        pre_gate = own_g[...] + got_g[...].astype(f32)
        pre_up = own_u[...] + got_u[...].astype(f32)
        back_proj = own_b[...] + got_b[...].astype(f32)
        sig = jax.nn.sigmoid(pre_gate)
        activated = pre_gate * sig
        hidden = activated * pre_up
        shares.append(jnp.sum(back_proj * hidden, axis=1, keepdims=True))
        d_hidden = gate * back_proj
        here = slice(g * count, (g + 1) * count)
        scaled[here] = (gate * hidden).astype(bf16)
        d_gate[here] = (d_hidden * pre_up * sig * (1.0 + pre_gate * (1.0 - sig))).astype(bf16)
        d_up[here] = (d_hidden * activated).astype(bf16)
    back = lax.dot_general(
        d_gate[...], w_gate[...], COLUMNS_BY_COLUMNS, preferred_element_type=f32
    ) + lax.dot_general(d_up[...], w_up[...], COLUMNS_BY_COLUMNS, preferred_element_type=f32)
    share = jnp.concatenate(shares, 0)
    high = share.astype(bf16).astype(f32)
    lane = lax.broadcasted_iota(i32, (share.shape[0], LANES), 1)
    tail = jnp.where(lane == 0, high, jnp.where(lane == 1, share - high, 0.0))
    half, rows = low_back.shape[0], low_back.shape[1] // GROUPS
    for member in range(2 * half):
        out = low_back if member < half else high_back
        starts = [g * 2 * half * rows + member * rows for g in range(GROUPS)]
        out[member % half, :, :d_part] = jnp.concatenate([back[s : s + rows] for s in starts], 0).astype(bf16)
        out[member % half, :, d_part:] = jnp.concatenate([tail[s : s + rows] for s in starts], 0).astype(bf16)


def owner_kernel(d_part, top_count, me_ref, place_ref, info_ref, *refs):
    slot_refs, rows_ref, grad_ref = refs[:EXPERTS], refs[EXPERTS], refs[EXPERTS + 1]
    total = jnp.zeros((info_ref.shape[0], d_part), f32)
    grad = jnp.zeros((info_ref.shape[0], LANES), f32)
    lane = lax.broadcasted_iota(i32, grad.shape, 1)
    for k in range(EXPERTS):
        rows = jnp.dot(place_ref[k].astype(bf16), slot_refs[k][...], preferred_element_type=f32)
        total = total + rows[:, :d_part]
        share = rows[:, d_part : d_part + 1] + rows[:, d_part + 1 : d_part + 2]
        expert = (me_ref[0] ^ k).astype(f32)
        grad = jnp.where((info_ref[...] == expert) & (lane < top_count), share, grad)
    pipe_size, own_rows = rows_ref.shape[0], rows_ref.shape[1]
    for p in range(pipe_size):
        rows_ref[p] = total[p * own_rows : (p + 1) * own_rows].astype(bf16)
        grad_ref[p] = grad[p * own_rows : (p + 1) * own_rows]


def call(kernel, out_shape, operand_count, name, smem=1, mib=8, flops=0, bytes_accessed=0):
    vmem = pl.BlockSpec(memory_space=pltpu.VMEM)
    return pl.pallas_call(
        kernel,
        out_shape=out_shape,
        in_specs=[pl.BlockSpec(memory_space=pltpu.SMEM)] * smem + [vmem] * operand_count,
        out_specs=jax.tree.map(lambda _: vmem, out_shape),
        compiler_params=pltpu.CompilerParams(vmem_limit_bytes=mib << 20),
        cost_estimate=pl.CostEstimate(flops=flops, bytes_accessed=bytes_accessed, transcendentals=0),
        name=name,
    )


def pipe_exchange(blocks):
    pipe_size = blocks.shape[0]
    if pipe_size != 2:
        return lax.all_to_all(blocks, "pipe", split_axis=0, concat_axis=0, tiled=True)
    first = lax.axis_index("pipe") == 0
    got = swap(jnp.where(first, blocks[1], blocks[0]), "pipe", 1)
    return jnp.where(first, jnp.stack([blocks[0], got]), jnp.stack([got, blocks[1]]))


def on_device(tokens, cotangent, expert_ids, gate_values, w_gate, w_up, w_down_t):
    micro_count, tok_count, d_model = tokens.shape
    top_count = expert_ids.shape[2]
    pipe_size = lax.axis_size("pipe")
    expert_size = lax.axis_size("expert")
    group_size = expert_size // EXPERTS
    bits = [1 << i for i in reversed(range(group_size.bit_length() - 1))]
    d_part, f_part = w_gate.shape
    width = -(-d_part // LANES) * LANES + LANES
    own_rows = micro_count * tok_count
    slot_count = pipe_size * micro_count * CAP
    expert = (lax.axis_index("expert") // group_size).astype(i32)
    me = expert.reshape(1)
    shape = jax.ShapeDtypeStruct

    send = call(
        functools.partial(prep_kernel, d_part), shape((pipe_size, 2 * own_rows, width), bf16), 4, "prep", smem=0
    )(tokens, cotangent, expert_ids, gate_values)
    layer_rows = pipe_exchange(send)
    *slots, place, info = call(
        functools.partial(pack_kernel, tok_count, top_count),
        tuple(shape((2 * slot_count, width), bf16) for _ in range(EXPERTS))
        + (
            shape((EXPERTS, pipe_size * own_rows, slot_count), f32),
            shape((pipe_size * own_rows, LANES), f32),
        ),
        1,
        "pack",
    )(me, layer_rows)

    gathered = [slots[0]] + [swap(slots[k], "expert", k * group_size) for k in range(1, EXPERTS)]
    per_group = EXPERTS // GROUPS
    operands, tok_groups, cot_groups = [], [], []
    for g in range(GROUPS):
        blocks = gathered[g * per_group : (g + 1) * per_group]
        rows = jnp.stack(
            [jnp.concatenate([b[a * slot_count : (a + 1) * slot_count] for b in blocks], 0) for a in range(2)]
        )
        for bit in bits:
            rows = jnp.concatenate([rows, swap(rows, "expert", bit)], 1)
        tok_rows, cot_rows = rows[0, :, :d_part], rows[1, :, :d_part]
        tok_groups.append(tok_rows)
        cot_groups.append(cot_rows)
        own, got = [], []
        for left, weight in ((tok_rows, w_gate), (tok_rows, w_up), (cot_rows, w_down_t)):
            part = jnp.dot(left, weight, preferred_element_type=f32)
            bit = pipe_size // 2
            while bit > 1:
                part = part + swap(part.astype(bf16), "pipe", bit).astype(f32)
                bit //= 2
            own.append(part)
            got.append(swap(part.astype(bf16), "pipe", 1) if pipe_size > 1 else jnp.zeros_like(part, bf16))
        operands += [rows[0, :, width - LANES :]] + own + got

    total = GROUPS * operands[0].shape[0]
    hidden_shape = shape((total, f_part), bf16)
    half_shape = shape((group_size // 2, EXPERTS * slot_count, d_part + LANES), bf16)
    moved = total * f_part * 4 * 5 + total * d_part * 8 + 4 * d_part * f_part
    d_gate, d_up, scaled, low, high = call(
        functools.partial(hidden_kernel, d_part, top_count),
        (hidden_shape,) * 3 + (half_shape,) * 2,
        7 * GROUPS + 2,
        "hidden",
        mib=min(52, 8 + 2 * moved // (1 << 20)),
        flops=4 * total * d_part * f_part,
        bytes_accessed=moved,
    )(me, *operands, w_gate, w_up)

    back = None
    for bit in reversed(bits):
        if back is not None:
            half = back.shape[0] // 2
            low, high = back[:half], back[half:]
        back = (low.astype(f32) + swap(high, "expert", bit).astype(f32)).astype(bf16)
    back = back[0]
    pieces = [back[k * slot_count : (k + 1) * slot_count] for k in range(EXPERTS)]
    pieces = [pieces[0]] + [swap(pieces[k], "expert", k * group_size) for k in range(1, EXPERTS)]

    tokens_total = own_rows * pipe_size * expert_size
    scale = 1.0 / math.sqrt(tokens_total * top_count / EXPERTS)
    tok_all, cot_all = jnp.concatenate(tok_groups, 0), jnp.concatenate(cot_groups, 0)

    def weight_grad(left, right):
        return (lax.dot_general(left, right, ROWS_BY_ROWS, preferred_element_type=f32) * scale).astype(bf16)

    dw_gate = weight_grad(tok_all, d_gate)
    dw_up = weight_grad(tok_all, d_up)
    dw_down_t = weight_grad(cot_all, scaled)

    summed, grads = call(
        functools.partial(owner_kernel, d_part, top_count),
        (shape((pipe_size, own_rows, d_part), bf16), shape((pipe_size, own_rows, LANES), f32)),
        2 + EXPERTS,
        "owner",
    )(me, place, info, *pieces)
    d_tokens = jnp.swapaxes(pipe_exchange(summed), 0, 1).reshape(micro_count, tok_count, d_model)
    grads = lax.dynamic_index_in_dim(grads, lax.axis_index("pipe"), 0, keepdims=False)
    gate_weight_gradient = grads[:, :top_count].reshape(micro_count, tok_count, top_count)
    return (d_tokens, gate_weight_gradient, dw_gate, dw_up, dw_down_t)


def solution(mesh):
    rows = P(None, ("pipe", "expert"), None)
    weights = P("pipe", "expert")
    return jax.shard_map(
        on_device,
        mesh=mesh,
        in_specs=(rows, rows, rows, rows, weights, weights, weights),
        out_specs=(rows, rows, weights, weights, weights),
        check_vma=False,
    )
```

time: 89.3 us -> 75.5 us (0.85)
  waiting for transfers between devices: 39.9 us -> 30.3 us
  blocking collectives: 8.41 us -> 0 us
  starting transfers between devices: 16.9 us -> 24.4 us
  other arithmetic: 2.92 us -> 1.54 us
  Pallas kernels: 4.07 us -> 2.7 us
    ppermute x13 -> x20, starting transfers between devices: 13.6 us -> 24.4 us  [swap(): lax.ppermute(x, axis, [(i, i ^ bit) for i in range(lax.axis_size(axis))])]
    all_to_all x1 -> x0, blocking collectives: 8.41 us -> none  [on_device(): lax.all_to_all(send, 'pipe', split_axis=0, concat_axis=0, tiled=True)]
    ppermute x13 -> x20, waiting for transfers between devices: 36.4 us -> 30.3 us  [swap(): lax.ppermute(x, axis, [(i, i ^ bit) for i in range(lax.axis_size(axis))])]
    all_to_all x1 -> x0, waiting for transfers between devices: 3.46 us -> none  [on_device(): lax.all_to_all(summed, 'pipe', split_axis=0, concat_axis=0, tiled=True)]
    all_to_all x1 -> x0, starting transfers between devices: 3.29 us -> none  [on_device(): lax.all_to_all(summed, 'pipe', split_axis=0, concat_axis=0, tiled=True)]
    unnamed x18 -> x21, local copies, waits for them, and re-layouts: 2.5 us -> 5.06 us
    reshape x6 -> x1, local copies, waits for them, and re-layouts: 2.46 us -> 0.66 us  [on_device(): jnp.swapaxes(pipe_exchange(summed), 0, 1)]
    pallas_call x3 -> x4, Pallas kernels: 4.07 us -> 2.7 us  [the longest x1 1.69 us: on_device(): call(functools.partial(hidden_kernel, d_part, top_count), (hidden_shape,)...]
  transfers between devices with their start and end apart: 14 -> 20, of which waited for: 12 -> 14; matrix products, arithmetic and copies ran while one was open for 11% -> 12% of each run, Pallas kernels for 0% -> 0%
where the time goes in v2:
time: 75.5 us; the launch traced here: 75.2 us
  waiting for transfers between devices  30.3 us (40%)
  starting transfers between devices  24.4 us (32%)
  matrix products  9.42 us (12%)
  local copies, waits for them, and re-layouts  5.89 us (8%)
  Pallas kernels  2.7 us (4%)
  other arithmetic  1.54 us (2%)
  between operations  0.92 us (1%)
    ppermute x20, waiting for transfers between devices, swap(): lax.ppermute(x, axis, [(i, i ^ bit) for i in range(lax.axis_size(axis))])  30.3 us
    ppermute x20, starting transfers between devices, swap(): lax.ppermute(x, axis, [(i, i ^ bit) for i in range(lax.axis_size(axis))])  24.4 us
    dot_general x3, matrix products, weight_grad(): lax.dot_general(left, right, ROWS_BY_ROWS, preferred_element_type=f32)  6.86 us
    unnamed x21, local copies, waits for them, and re-layouts  5.06 us
    dot_general x6, matrix products, on_device(): part = jnp.dot(left, weight, preferred_element_type=f32)  2.56 us
    pallas_call x1, Pallas kernels, on_device(): call(functools.partial(hidden_kernel, d_part, top_count), (hidden_shape,)...  1.69 us
  transfers between devices with their start and end apart: 20, of which 14 were waited for; matrix products, arithmetic and copies ran while one was open for 12% of the time, Pallas kernels for 0%

profile of v2, /device:TPU:0, one launch (start us, length us, event | category | flops | bytes accessed | tf_op | source)
XLA Modules:
  0.0 75.2 jit_solution(15448849547620204394)
XLA Ops:
  0.7 0.9 %copy.16.gate_ref = bf16[2,4,2]{2,1,0:T(4,128)(2,1)S(1)} copy(bf16[2,4,2]{1,2,0:T(2,128)(2,1)} %param.10) | data formatting | bytes 64 | tf_op args[3]
  4.1 3.0 %collective-permute-start = (bf16[16,1920]{1,0:T(8,128)(2,1)S(1)}, bf16[16,1920]{1,0:T(8,128)(2,1)S(1)}, u32[]{:S(2)}, u32[]{:S(2)}) collective-permute-start(bf16[16,1920]{1,0:T(8,128)(2,1)S(1)} %get-tuple-element.50), channel_id=1, source_target_pairs={{0,16},{16,0},{1,17},{17,1},{2,18},{18,2},{3,19},{19,3},{4,20},{20... | collective-permute-start | bytes 184328 | tf_op jit(solution)/shard_map/ppermute | solution.py:21
  7.1 2.2 %collective-permute-done = bf16[16,1920]{1,0:T(8,128)(2,1)S(1)} collective-permute-done((bf16[16,1920]{1,0:T(8,128)(2,1)S(1)}, bf16[16,1920]{1,0:T(8,128)(2,1)S(1)}, u32[]{:S(2)}, u32[]{:S(2)}) %collective-permute-start) | collective-permute-done | bytes 61472 | tf_op jit(solution)/shard_map/ppermute | solution.py:21
  9.9 2.2 %collective-permute-start.1 = (bf16[24,1920]{1,0:T(8,128)(2,1)S(1)}, bf16[24,1920]{1,0:T(8,128)(2,1)S(1)}, u32[]{:S(2)}, u32[]{:S(2)}) collective-permute-start(bf16[24,1920]{1,0:T(8,128)(2,1)S(1)} %get-tuple-element.21), channel_id=1, source_target_pairs={{0,4},{1,5},{2,6},{3,7},{4,0},{5,1},{6,2},{7,3},{8,12},{9,13},{10,... | collective-permute-start | bytes 276488 | tf_op jit(solution)/shard_map/ppermute | solution.py:21
  12.1 2.6 %collective-permute-start.7 = (bf16[24,1920]{1,0:T(8,128)(2,1)S(1)}, bf16[24,1920]{1,0:T(8,128)(2,1)S(1)}, u32[]{:S(2)}, u32[]{:S(2)}) collective-permute-start(bf16[24,1920]{1,0:T(8,128)(2,1)S(1)} %get-tuple-element.22), channel_id=1, source_target_pairs={{0,8},{1,9},{2,10},{3,11},{4,12},{5,13},{6,14},{7,15},{8,0},{9,1},... | collective-permute-start | bytes 276488 | tf_op jit(solution)/shard_map/ppermute | solution.py:21
  14.7 5.2 %collective-permute-done.7 = bf16[24,1920]{1,0:T(8,128)(2,1)S(1)} collective-permute-done((bf16[24,1920]{1,0:T(8,128)(2,1)S(1)}, bf16[24,1920]{1,0:T(8,128)(2,1)S(1)}, u32[]{:S(2)}, u32[]{:S(2)}) %collective-permute-start.7) | collective-permute-done | bytes 92192 | tf_op jit(solution)/shard_map/ppermute | solution.py:21
  19.9 1.2 %collective-permute-done.8 = bf16[24,1920]{1,0:T(8,128)(2,1)S(1)} collective-permute-done((bf16[24,1920]{1,0:T(8,128)(2,1)S(1)}, bf16[24,1920]{1,0:T(8,128)(2,1)S(1)}, u32[]{:S(2)}, u32[]{:S(2)}) %collective-permute-start.8) | collective-permute-done | bytes 92192 | tf_op jit(solution)/shard_map/ppermute | solution.py:21
  21.2 1.6 %collective-permute-start.9 = (bf16[2,24,1920]{2,1,0:T(8,128)(2,1)S(1)}, bf16[2,24,1920]{2,1,0:T(8,128)(2,1)S(1)}, u32[]{:S(2)}, u32[]{:S(2)}) collective-permute-start(bf16[2,24,1920]{2,1,0:T(8,128)(2,1)S(1)} %pad_maximum_fusion.12), channel_id=1, source_target_pairs={{0,2},{1,3},{2,0},{3,1},{4,6},{5,7},{6,4},{7,5},{8,10},{9,11},{10,... | collective-permute-start | bytes 552968 | tf_op jit(solution)/shard_map/ppermute | solution.py:21
  23.5 4.1 %collective-permute-done.9 = bf16[2,24,1920]{2,1,0:T(8,128)(2,1)S(1)} collective-permute-done((bf16[2,24,1920]{2,1,0:T(8,128)(2,1)S(1)}, bf16[2,24,1920]{2,1,0:T(8,128)(2,1)S(1)}, u32[]{:S(2)}, u32[]{:S(2)}) %collective-permute-start.9) | collective-permute-done | bytes 184352 | tf_op jit(solution)/shard_map/ppermute | solution.py:21
  27.8 1.9 %collective-permute-done.2 = bf16[2,24,1920]{2,1,0:T(8,128)(2,1)S(1)} collective-permute-done((bf16[2,24,1920]{2,1,0:T(8,128)(2,1)S(1)}, bf16[2,24,1920]{2,1,0:T(8,128)(2,1)S(1)}, u32[]{:S(2)}, u32[]{:S(2)}) %collective-permute-start.2) | collective-permute-done | bytes 184352 | tf_op jit(solution)/shard_map/ppermute | solution.py:21
  30.3 1.0 %copy-done.1 = bf16[1792,512]{1,0:T(8,128)(2,1)S(1)} copy-done((bf16[1792,512]{1,0:T(8,128)(2,1)S(1)}, bf16[1792,512]{1,0:T(8,128)(2,1)}, u32[]{:S(2)}) %copy-start.1) | copy-done | bytes 1835032
  33.1 1.6 %collective-permute-start.13 = (bf16[96,512]{1,0:T(8,128)(2,1)S(1)}, bf16[96,512]{1,0:T(8,128)(2,1)S(1)}, u32[]{:S(2)}, u32[]{:S(2)}) collective-permute-start(bf16[96,512]{1,0:T(8,128)(2,1)S(1)} %get-tuple-element.73), channel_id=1, source_target_pairs={{0,16},{16,0},{1,17},{17,1},{2,18},{18,2},{3,19},{19,3},{4,20},{20... | collective-permute-start | bytes 294920 | tf_op jit(solution)/shard_map/ppermute | solution.py:21
  35.2 1.5 %collective-permute-start.11 = (bf16[96,512]{1,0:T(8,128)(2,1)S(1)}, bf16[96,512]{1,0:T(8,128)(2,1)S(1)}, u32[]{:S(2)}, u32[]{:S(2)}) collective-permute-start(bf16[96,512]{1,0:T(8,128)(2,1)S(1)} %get-tuple-element.69), channel_id=1, source_target_pairs={{0,16},{16,0},{1,17},{17,1},{2,18},{18,2},{3,19},{19,3},{4,20},{20... | collective-permute-start | bytes 294920 | tf_op jit(solution)/shard_map/ppermute | solution.py:21
  37.8 1.5 %collective-permute-start.5 = (bf16[96,512]{1,0:T(8,128)(2,1)S(1)}, bf16[96,512]{1,0:T(8,128)(2,1)S(1)}, u32[]{:S(2)}, u32[]{:S(2)}) collective-permute-start(bf16[96,512]{1,0:T(8,128)(2,1)S(1)} %get-tuple-element.65), channel_id=1, source_target_pairs={{0,16},{16,0},{1,17},{17,1},{2,18},{18,2},{3,19},{19,3},{4,20},{20... | collective-permute-start | bytes 294920 | tf_op jit(solution)/shard_map/ppermute | solution.py:21
  39.3 1.1 %collective-permute-start.4 = (bf16[96,512]{1,0:T(8,128)(2,1)S(1)}, bf16[96,512]{1,0:T(8,128)(2,1)S(1)}, u32[]{:S(2)}, u32[]{:S(2)}) collective-permute-start(bf16[96,512]{1,0:T(8,128)(2,1)S(1)} %get-tuple-element.63), channel_id=1, source_target_pairs={{0,16},{16,0},{1,17},{17,1},{2,18},{18,2},{3,19},{19,3},{4,20},{20... | collective-permute-start | bytes 294920 | tf_op jit(solution)/shard_map/ppermute | solution.py:21
  40.9 2.1 %collective-permute-done.11.refs_11_ = bf16[96,512]{1,0:T(8,128)(2,1)S(1)} collective-permute-done((bf16[96,512]{1,0:T(8,128)(2,1)S(1)}, bf16[96,512]{1,0:T(8,128)(2,1)S(1)}, u32[]{:S(2)}, u32[]{:S(2)}) %collective-permute-start.11) | collective-permute-done | bytes 98336 | tf_op jit(solution)/shard_map/ppermute | solution.py:21
  43.0 2.1 %collective-permute-done.6.refs_6_ = bf16[96,512]{1,0:T(8,128)(2,1)S(1)} collective-permute-done((bf16[96,512]{1,0:T(8,128)(2,1)S(1)}, bf16[96,512]{1,0:T(8,128)(2,1)S(1)}, u32[]{:S(2)}, u32[]{:S(2)}) %collective-permute-start.6) | collective-permute-done | bytes 98336 | tf_op jit(solution)/shard_map/ppermute | solution.py:21
  45.1 2.1 %collective-permute-done.5.refs_5_ = bf16[96,512]{1,0:T(8,128)(2,1)S(1)} collective-permute-done((bf16[96,512]{1,0:T(8,128)(2,1)S(1)}, bf16[96,512]{1,0:T(8,128)(2,1)S(1)}, u32[]{:S(2)}, u32[]{:S(2)}) %collective-permute-start.5) | collective-permute-done | bytes 98336 | tf_op jit(solution)/shard_map/ppermute | solution.py:21
  47.2 1.1 %collective-permute-done.4.refs_4_ = bf16[96,512]{1,0:T(8,128)(2,1)S(1)} collective-permute-done((bf16[96,512]{1,0:T(8,128)(2,1)S(1)}, bf16[96,512]{1,0:T(8,128)(2,1)S(1)}, u32[]{:S(2)}, u32[]{:S(2)}) %collective-permute-start.4) | collective-permute-done | bytes 98336 | tf_op jit(solution)/shard_map/ppermute | solution.py:21
  48.4 1.7 %hidden.1 = (bf16[192,512]{1,0:T(8,128)(2,1)S(1)}, bf16[192,512]{1,0:T(8,128)(2,1)S(1)}, bf16[192,512]{1,0:T(8,128)(2,1)S(1)}, bf16[2,48,1920]{2,1,0:T(8,128)(2,1)S(1)}, bf16[2,48,1920]{2,1,0:T(8,128)(2,1)S(1)}) custom-call(s32[1]{0:T(128)} %bitcast.me_ref, bf16[96,128]{1,0:T(8,128)(2,1)S(1)} %maximum_bitcast_fusion.7.refs_0_, ...), custom_call_target="tpu_custom_call" | custom-call | flops 704643072 | bytes 8388608 | tf_op jit(solution)/shard_map/hidden/pallas_call | solution.py:220
  50.2 3.0 %multiply_convert_fusion = bf16[1792,512]{1,0:T(8,128)(2,1)} fusion(bf16[192,512]{1,0:T(8,128)(2,1)S(1)} %get-tuple-element.30, bf16[96,1792]{1,0:T(8,128)(2,1)} %copy-done.7, bf16[96,1792]{1,0:T(8,128)(2,1)} %copy-done.8), kind=kOutput, calls=%fused_computation | convolution fusion | flops 355532800 | bytes 2719744 | tf_op jit(solution)/shard_map/dot_general | solution.py:245
  53.2 1.1 %add_convert_fusion = bf16[2,48,1920]{2,1,0:T(8,128)(2,1)S(1)} fusion(bf16[2,48,1920]{2,1,0:T(8,128)(2,1)} %collective-permute-done.14, bf16[2,48,1920]{2,1,0:T(8,128)(2,1)S(1)} %get-tuple-element.24), kind=kLoop, calls=%fused_computation.3 | loop fusion | flops 737280 | bytes 1105920 | tf_op jit(solution)/shard_map/convert_element_type | solution.py:235
  54.3 1.6 %collective-permute-start.15 = (bf16[1,48,1920]{2,1,0:T(8,128)(2,1)S(1)}, bf16[1,48,1920]{2,1,0:T(8,128)(2,1)S(1)}, u32[]{:S(2)}, u32[]{:S(2)}) collective-permute-start(bf16[1,48,1920]{2,1,0:T(8,128)(2,1)S(1)} %slice.129), channel_id=1, source_target_pairs={{0,2},{1,3},{2,0},{3,1},{4,6},{5,7},{6,4},{7,5},{8,10},{9,11},{10,... | collective-permute-start | bytes 552968 | tf_op jit(solution)/shard_map/ppermute | solution.py:21
  55.9 1.9 %multiply_convert_fusion.2 = bf16[1792,512]{1,0:T(8,128)(2,1)} fusion(bf16[192,512]{1,0:T(8,128)(2,1)S(1)} %get-tuple-element.28, bf16[96,1792]{1,0:T(8,128)(2,1)S(1)} %get-tuple-element.42, bf16[96,1792]{1,0:T(8,128)(2,1)S(1)} %copy-done.6), kind=kOutput, calls=%fused_computation.2 | convolution fusion | flops 355532800 | bytes 2719744 | tf_op jit(solution)/shard_map/dot_general | solution.py:245
  57.8 3.6 %collective-permute-done.15 = bf16[1,48,1920]{2,1,0:T(8,128)(2,1)S(1)} collective-permute-done((bf16[1,48,1920]{2,1,0:T(8,128)(2,1)S(1)}, bf16[1,48,1920]{2,1,0:T(8,128)(2,1)S(1)}, u32[]{:S(2)}, u32[]{:S(2)}) %collective-permute-start.15) | collective-permute-done | bytes 184352 | tf_op jit(solution)/shard_map/ppermute | solution.py:21
  61.5 1.7 %collective-permute-start.18 = (bf16[12,1920]{1,0:T(8,128)(2,1)S(1)}, bf16[12,1920]{1,0:T(8,128)(2,1)S(1)}, u32[]{:S(2)}, u32[]{:S(2)}) collective-permute-start(bf16[12,1920]{1,0:T(8,128)(2,1)S(1)} %get-tuple-element.45), channel_id=1, source_target_pairs={{0,12},{1,13},{2,14},{3,15},{4,8},{5,9},{6,10},{7,11},{8,4},{9,5},... | collective-permute-start | bytes 138248 | tf_op jit(solution)/shard_map/ppermute | solution.py:21
  63.2 0.9 %collective-permute-start.17 = (bf16[12,1920]{1,0:T(8,128)(2,1)S(1)}, bf16[12,1920]{1,0:T(8,128)(2,1)S(1)}, u32[]{:S(2)}, u32[]{:S(2)}) collective-permute-start(bf16[12,1920]{1,0:T(8,128)(2,1)S(1)} %get-tuple-element.46), channel_id=1, source_target_pairs={{0,8},{1,9},{2,10},{3,11},{4,12},{5,13},{6,14},{7,15},{8,0},{9,1},... | collective-permute-start | bytes 138248 | tf_op jit(solution)/shard_map/ppermute | solution.py:21
  64.1 1.9 %collective-permute-start.16 = (bf16[12,1920]{1,0:T(8,128)(2,1)S(1)}, bf16[12,1920]{1,0:T(8,128)(2,1)S(1)}, u32[]{:S(2)}, u32[]{:S(2)}) collective-permute-start(bf16[12,1920]{1,0:T(8,128)(2,1)S(1)} %get-tuple-element.47), channel_id=1, source_target_pairs={{0,4},{1,5},{2,6},{3,7},{4,0},{5,1},{6,2},{7,3},{8,12},{9,13},{10,... | collective-permute-start | bytes 138248 | tf_op jit(solution)/shard_map/ppermute | solution.py:21
  66.0 1.9 %multiply_convert_fusion.1 = bf16[1792,512]{1,0:T(8,128)(2,1)} fusion(bf16[192,512]{1,0:T(8,128)(2,1)S(1)} %get-tuple-element.29, bf16[96,1792]{1,0:T(8,128)(2,1)S(1)} %get-tuple-element.42, bf16[96,1792]{1,0:T(8,128)(2,1)S(1)} %copy-done.6), kind=kOutput, calls=%fused_computation.1 | convolution fusion | flops 355532800 | bytes 2719744 | tf_op jit(solution)/shard_map/dot_general | solution.py:245
  68.4 1.8 %collective-permute-done.17.refs_2_ = bf16[12,1920]{1,0:T(8,128)(2,1)S(1)} collective-permute-done((bf16[12,1920]{1,0:T(8,128)(2,1)S(1)}, bf16[12,1920]{1,0:T(8,128)(2,1)S(1)}, u32[]{:S(2)}, u32[]{:S(2)}) %collective-permute-start.17) | collective-permute-done | bytes 46112 | tf_op jit(solution)/shard_map/ppermute | solution.py:21
  70.5 1.5 %collective-permute-start.19 = (bf16[8,1792]{1,0:T(8,128)(2,1)S(1)}, bf16[8,1792]{1,0:T(8,128)(2,1)S(1)}, u32[]{:S(2)}, u32[]{:S(2)}) collective-permute-start(bf16[8,1792]{1,0:T(8,128)(2,1)S(1)} %get-tuple-element.61), channel_id=1, source_target_pairs={{0,16},{16,0},{1,17},{17,1},{2,18},{18,2},{3,19},{19,3},{4,20},{20... | collective-permute-start | bytes 86024 | tf_op jit(solution)/shard_map/ppermute | solution.py:21
  72.7 1.8 %collective-permute-done.19 = bf16[8,1792]{1,0:T(8,128)(2,1)S(1)} collective-permute-done((bf16[8,1792]{1,0:T(8,128)(2,1)S(1)}, bf16[8,1792]{1,0:T(8,128)(2,1)S(1)}, u32[]{:S(2)}, u32[]{:S(2)}) %collective-permute-start.19) | collective-permute-done | bytes 28704 | tf_op jit(solution)/shard_map/ppermute | solution.py:21
  (67 shorter events, 10.9 us)
Async XLA Ops:
  0.6 32.1 %copy-start = (bf16[1792,512]{1,0:T(8,128)(2,1)S(1)}, bf16[1792,512]{1,0:T(8,128)(2,1)}, u32[]{:S(2)}) copy-start(bf16[1792,512]{1,0:T(8,128)(2,1)} %param.13) | copy-start | bytes 5505028
  2.3 0.8 %copy-start.3 = (bf16[2,4,3584]{2,1,0:T(4,128)(2,1)S(1)}, bf16[2,4,3584]{2,1,0:T(4,128)(2,1)}, u32[]{:S(2)}) copy-start(bf16[2,4,3584]{2,1,0:T(4,128)(2,1)} %tok_ref.1) | copy-start | bytes 172036
  3.2 0.8 %copy-start.4 = (bf16[2,4,3584]{2,1,0:T(4,128)(2,1)S(1)}, bf16[2,4,3584]{2,1,0:T(4,128)(2,1)}, u32[]{:S(2)}) copy-start(bf16[2,4,3584]{2,1,0:T(4,128)(2,1)} %cot_ref.1) | copy-start | bytes 172036
  4.1 5.2 %collective-permute-start = (bf16[16,1920]{1,0:T(8,128)(2,1)S(1)}, bf16[16,1920]{1,0:T(8,128)(2,1)S(1)}, u32[]{:S(2)}, u32[]{:S(2)}) collective-permute-start(bf16[16,1920]{1,0:T(8,128)(2,1)S(1)} %get-tuple-element.50), channel_id=1, source_target_pairs={{0,16},{16,0},{1,17},{17,1},{2,18},{18,2},{3,19},{19,3},{4,20},{20... | collective-permute-start | bytes 184328 | tf_op jit(solution)/shard_map/ppermute | solution.py:21
  9.9 12.9 %collective-permute-start.1 = (bf16[24,1920]{1,0:T(8,128)(2,1)S(1)}, bf16[24,1920]{1,0:T(8,128)(2,1)S(1)}, u32[]{:S(2)}, u32[]{:S(2)}) collective-permute-start(bf16[24,1920]{1,0:T(8,128)(2,1)S(1)} %get-tuple-element.21), channel_id=1, source_target_pairs={{0,4},{1,5},{2,6},{3,7},{4,0},{5,1},{6,2},{7,3},{8,12},{9,13},{10,... | collective-permute-start | bytes 276488 | tf_op jit(solution)/shard_map/ppermute | solution.py:21
  12.1 7.8 %collective-permute-start.7 = (bf16[24,1920]{1,0:T(8,128)(2,1)S(1)}, bf16[24,1920]{1,0:T(8,128)(2,1)S(1)}, u32[]{:S(2)}, u32[]{:S(2)}) collective-permute-start(bf16[24,1920]{1,0:T(8,128)(2,1)S(1)} %get-tuple-element.22), channel_id=1, source_target_pairs={{0,8},{1,9},{2,10},{3,11},{4,12},{5,13},{6,14},{7,15},{8,0},{9,1},... | collective-permute-start | bytes 276488 | tf_op jit(solution)/shard_map/ppermute | solution.py:21
  14.7 6.5 %collective-permute-start.8 = (bf16[24,1920]{1,0:T(8,128)(2,1)S(1)}, bf16[24,1920]{1,0:T(8,128)(2,1)S(1)}, u32[]{:S(2)}, u32[]{:S(2)}) collective-permute-start(bf16[24,1920]{1,0:T(8,128)(2,1)S(1)} %get-tuple-element.23), channel_id=1, source_target_pairs={{0,12},{1,13},{2,14},{3,15},{4,8},{5,9},{6,10},{7,11},{8,4},{9,5},... | collective-permute-start | bytes 276488 | tf_op jit(solution)/shard_map/ppermute | solution.py:21
  21.2 6.4 %collective-permute-start.9 = (bf16[2,24,1920]{2,1,0:T(8,128)(2,1)S(1)}, bf16[2,24,1920]{2,1,0:T(8,128)(2,1)S(1)}, u32[]{:S(2)}, u32[]{:S(2)}) collective-permute-start(bf16[2,24,1920]{2,1,0:T(8,128)(2,1)S(1)} %pad_maximum_fusion.12), channel_id=1, source_target_pairs={{0,2},{1,3},{2,0},{3,1},{4,6},{5,7},{6,4},{7,5},{8,10},{9,11},{10,... | collective-permute-start | bytes 552968 | tf_op jit(solution)/shard_map/ppermute | solution.py:21
  22.8 7.0 %copy-start.2 = (bf16[1792,512]{1,0:T(8,128)(2,1)S(1)}, bf16[1792,512]{1,0:T(8,128)(2,1)}, u32[]{:S(2)}) copy-start(bf16[1792,512]{1,0:T(8,128)(2,1)} %refs_15_.1) | copy-start | bytes 5505028
  22.9 6.7 %collective-permute-start.2 = (bf16[2,24,1920]{2,1,0:T(8,128)(2,1)S(1)}, bf16[2,24,1920]{2,1,0:T(8,128)(2,1)S(1)}, u32[]{:S(2)}, u32[]{:S(2)}) collective-permute-start(bf16[2,24,1920]{2,1,0:T(8,128)(2,1)S(1)} %pad_maximum_fusion.11), channel_id=1, source_target_pairs={{0,2},{1,3},{2,0},{3,1},{4,6},{5,7},{6,4},{7,5},{8,10},{9,11},{10,... | collective-permute-start | bytes 552968 | tf_op jit(solution)/shard_map/ppermute | solution.py:21
  27.7 2.1 %collective-permute-start.10 = (bf16[2,48,1920]{2,1,0:T(8,128)(2,1)S(1)}, bf16[2,48,1920]{2,1,0:T(8,128)(2,1)S(1)}, u32[]{:S(2)}, u32[]{:S(2)}) collective-permute-start(bf16[2,48,1920]{2,1,0:T(8,128)(2,1)S(1)} %pad_maximum_fusion.4), channel_id=1, source_target_pairs={{0,1},{1,0},{2,3},{3,2},{4,5},{5,4},{6,7},{7,6},{8,9},{9,8},{10,11... | collective-permute-start | bytes 1105928 | tf_op jit(solution)/shard_map/ppermute | solution.py:21
  29.7 1.6 %copy-start.1 = (bf16[1792,512]{1,0:T(8,128)(2,1)S(1)}, bf16[1792,512]{1,0:T(8,128)(2,1)}, u32[]{:S(2)}) copy-start(bf16[1792,512]{1,0:T(8,128)(2,1)} %refs_14_.1) | copy-start | bytes 5505028
  29.7 2.0 %collective-permute-start.3 = (bf16[2,48,1920]{2,1,0:T(8,128)(2,1)S(1)}, bf16[2,48,1920]{2,1,0:T(8,128)(2,1)S(1)}, u32[]{:S(2)}, u32[]{:S(2)}) collective-permute-start(bf16[2,48,1920]{2,1,0:T(8,128)(2,1)S(1)} %pad_maximum_fusion.3), channel_id=1, source_target_pairs={{0,1},{1,0},{2,3},{3,2},{4,5},{5,4},{6,7},{7,6},{8,9},{9,8},{10,11... | collective-permute-start | bytes 1105928 | tf_op jit(solution)/shard_map/ppermute | solution.py:21
  29.8 2.9 %copy-start.7 = (bf16[96,1792]{1,0:T(8,128)(2,1)}, bf16[96,1792]{1,0:T(8,128)(2,1)S(1)}, u32[]{:S(2)}) copy-start(bf16[96,1792]{1,0:T(8,128)(2,1)S(1)} %get-tuple-element.41) | copy-start | bytes 1032196
  31.8 0.9 %copy-start.5 = (bf16[96,1792]{1,0:T(8,128)(2,1)}, bf16[96,1792]{1,0:T(8,128)(2,1)S(1)}, u32[]{:S(2)}) copy-start(bf16[96,1792]{1,0:T(8,128)(2,1)S(1)} %get-tuple-element.44) | copy-start | bytes 1032196
  31.8 4.9 %copy-start.8 = (bf16[96,1792]{1,0:T(8,128)(2,1)}, bf16[96,1792]{1,0:T(8,128)(2,1)S(1)}, u32[]{:S(2)}) copy-start(bf16[96,1792]{1,0:T(8,128)(2,1)S(1)} %get-tuple-element.43) | copy-start | bytes 1032196
  33.1 6.1 %collective-permute-start.13 = (bf16[96,512]{1,0:T(8,128)(2,1)S(1)}, bf16[96,512]{1,0:T(8,128)(2,1)S(1)}, u32[]{:S(2)}, u32[]{:S(2)}) collective-permute-start(bf16[96,512]{1,0:T(8,128)(2,1)S(1)} %get-tuple-element.73), channel_id=1, source_target_pairs={{0,16},{16,0},{1,17},{17,1},{2,18},{18,2},{3,19},{19,3},{4,20},{20... | collective-permute-start | bytes 294920 | tf_op jit(solution)/shard_map/ppermute | solution.py:21
  34.7 6.2 %collective-permute-start.12 = (bf16[96,512]{1,0:T(8,128)(2,1)S(1)}, bf16[96,512]{1,0:T(8,128)(2,1)S(1)}, u32[]{:S(2)}, u32[]{:S(2)}) collective-permute-start(bf16[96,512]{1,0:T(8,128)(2,1)S(1)} %get-tuple-element.71), channel_id=1, source_target_pairs={{0,16},{16,0},{1,17},{17,1},{2,18},{18,2},{3,19},{19,3},{4,20},{20... | collective-permute-start | bytes 294920 | tf_op jit(solution)/shard_map/ppermute | solution.py:21
  35.2 7.8 %collective-permute-start.11 = (bf16[96,512]{1,0:T(8,128)(2,1)S(1)}, bf16[96,512]{1,0:T(8,128)(2,1)S(1)}, u32[]{:S(2)}, u32[]{:S(2)}) collective-permute-start(bf16[96,512]{1,0:T(8,128)(2,1)S(1)} %get-tuple-element.69), channel_id=1, source_target_pairs={{0,16},{16,0},{1,17},{17,1},{2,18},{18,2},{3,19},{19,3},{4,20},{20... | collective-permute-start | bytes 294920 | tf_op jit(solution)/shard_map/ppermute | solution.py:21
  37.2 8.0 %collective-permute-start.6 = (bf16[96,512]{1,0:T(8,128)(2,1)S(1)}, bf16[96,512]{1,0:T(8,128)(2,1)S(1)}, u32[]{:S(2)}, u32[]{:S(2)}) collective-permute-start(bf16[96,512]{1,0:T(8,128)(2,1)S(1)} %get-tuple-element.67), channel_id=1, source_target_pairs={{0,16},{16,0},{1,17},{17,1},{2,18},{18,2},{3,19},{19,3},{4,20},{20... | collective-permute-start | bytes 294920 | tf_op jit(solution)/shard_map/ppermute | solution.py:21
  37.8 9.5 %collective-permute-start.5 = (bf16[96,512]{1,0:T(8,128)(2,1)S(1)}, bf16[96,512]{1,0:T(8,128)(2,1)S(1)}, u32[]{:S(2)}, u32[]{:S(2)}) collective-permute-start(bf16[96,512]{1,0:T(8,128)(2,1)S(1)} %get-tuple-element.65), channel_id=1, source_target_pairs={{0,16},{16,0},{1,17},{17,1},{2,18},{18,2},{3,19},{19,3},{4,20},{20... | collective-permute-start | bytes 294920 | tf_op jit(solution)/shard_map/ppermute | solution.py:21
  39.3 9.1 %collective-permute-start.4 = (bf16[96,512]{1,0:T(8,128)(2,1)S(1)}, bf16[96,512]{1,0:T(8,128)(2,1)S(1)}, u32[]{:S(2)}, u32[]{:S(2)}) collective-permute-start(bf16[96,512]{1,0:T(8,128)(2,1)S(1)} %get-tuple-element.63), channel_id=1, source_target_pairs={{0,16},{16,0},{1,17},{17,1},{2,18},{18,2},{3,19},{19,3},{4,20},{20... | collective-permute-start | bytes 294920 | tf_op jit(solution)/shard_map/ppermute | solution.py:21
  50.1 3.1 %collective-permute-start.14 = (bf16[2,48,1920]{2,1,0:T(8,128)(2,1)S(1)}, bf16[2,48,1920]{2,1,0:T(8,128)(2,1)}, u32[]{:S(2)}, u32[]{:S(2)}) collective-permute-start(bf16[2,48,1920]{2,1,0:T(8,128)(2,1)S(1)} %get-tuple-element.25), channel_id=1, source_target_pairs={{0,1},{1,0},{2,3},{3,2},{4,5},{5,4},{6,7},{7,6},{8,9},{9,8},{10,11... | collective-permute-start | bytes 1105928 | tf_op jit(solution)/shard_map/ppermute | solution.py:21
  50.1 5.8 %copy-start.6 = (bf16[96,1792]{1,0:T(8,128)(2,1)S(1)}, bf16[96,1792]{1,0:T(8,128)(2,1)}, u32[]{:S(2)}) copy-start(bf16[96,1792]{1,0:T(8,128)(2,1)} %copy-done.5) | copy-start | bytes 1032196
  54.3 7.1 %collective-permute-start.15 = (bf16[1,48,1920]{2,1,0:T(8,128)(2,1)S(1)}, bf16[1,48,1920]{2,1,0:T(8,128)(2,1)S(1)}, u32[]{:S(2)}, u32[]{:S(2)}) collective-permute-start(bf16[1,48,1920]{2,1,0:T(8,128)(2,1)S(1)} %slice.129), channel_id=1, source_target_pairs={{0,2},{1,3},{2,0},{3,1},{4,6},{5,7},{6,4},{7,5},{8,10},{9,11},{10,... | collective-permute-start | bytes 552968 | tf_op jit(solution)/shard_map/ppermute | solution.py:21
  61.5 6.8 %collective-permute-start.18 = (bf16[12,1920]{1,0:T(8,128)(2,1)S(1)}, bf16[12,1920]{1,0:T(8,128)(2,1)S(1)}, u32[]{:S(2)}, u32[]{:S(2)}) collective-permute-start(bf16[12,1920]{1,0:T(8,128)(2,1)S(1)} %get-tuple-element.45), channel_id=1, source_target_pairs={{0,12},{1,13},{2,14},{3,15},{4,8},{5,9},{6,10},{7,11},{8,4},{9,5},... | collective-permute-start | bytes 138248 | tf_op jit(solution)/shard_map/ppermute | solution.py:21
  63.2 6.9 %collective-permute-start.17 = (bf16[12,1920]{1,0:T(8,128)(2,1)S(1)}, bf16[12,1920]{1,0:T(8,128)(2,1)S(1)}, u32[]{:S(2)}, u32[]{:S(2)}) collective-permute-start(bf16[12,1920]{1,0:T(8,128)(2,1)S(1)} %get-tuple-element.46), channel_id=1, source_target_pairs={{0,8},{1,9},{2,10},{3,11},{4,12},{5,13},{6,14},{7,15},{8,0},{9,1},... | collective-permute-start | bytes 138248 | tf_op jit(solution)/shard_map/ppermute | solution.py:21
  64.1 6.1 %collective-permute-start.16 = (bf16[12,1920]{1,0:T(8,128)(2,1)S(1)}, bf16[12,1920]{1,0:T(8,128)(2,1)S(1)}, u32[]{:S(2)}, u32[]{:S(2)}) collective-permute-start(bf16[12,1920]{1,0:T(8,128)(2,1)S(1)} %get-tuple-element.47), channel_id=1, source_target_pairs={{0,4},{1,5},{2,6},{3,7},{4,0},{5,1},{6,2},{7,3},{8,12},{9,13},{10,... | collective-permute-start | bytes 138248 | tf_op jit(solution)/shard_map/ppermute | solution.py:21
  70.5 3.9 %collective-permute-start.19 = (bf16[8,1792]{1,0:T(8,128)(2,1)S(1)}, bf16[8,1792]{1,0:T(8,128)(2,1)S(1)}, u32[]{:S(2)}, u32[]{:S(2)}) collective-permute-start(bf16[8,1792]{1,0:T(8,128)(2,1)S(1)} %get-tuple-element.61), channel_id=1, source_target_pairs={{0,16},{16,0},{1,17},{17,1},{2,18},{18,2},{3,19},{19,3},{4,20},{20... | collective-permute-start | bytes 86024 | tf_op jit(solution)/shard_map/ppermute | solution.py:21

commit v3 on v2

v3 whole, which is shorter than its diff:
```python
import functools
import math

import jax
import jax.numpy as jnp
from jax import lax
from jax.experimental import pallas as pl
from jax.experimental.pallas import tpu as pltpu
from jax.sharding import PartitionSpec as P

EXPERTS = 4
CAP = 3
GROUPS = 2
PER_GROUP = EXPERTS // GROUPS
LANES = 128
ROWS = 8
PREP_MIB = 56
f32, bf16, i32 = jnp.float32, jnp.bfloat16, jnp.int32
ROWS_BY_ROWS = (((0,), (0,)), ((), ()))
COLUMNS_BY_COLUMNS = (((1,), (1,)), ((), ()))
shape = jax.ShapeDtypeStruct


def swap(x, axis, bit):
    return lax.ppermute(x, axis, [(i, i ^ bit) for i in range(lax.axis_size(axis))])


def swap_both(x, bit):
    count = lax.axis_size("expert")
    pairs = [(p * count + e, (p ^ 1) * count + (e ^ bit)) for p in range(2) for e in range(count)]
    return lax.ppermute(x, ("pipe", "expert"), pairs)


def prep_kernel(d_part, tok_hbm, cot_hbm, ids_hbm, gate_hbm, out_ref, tok_ref, cot_ref, ids_ref, gate_ref, sems):
    pairs = ((tok_hbm, tok_ref), (cot_hbm, cot_ref), (ids_hbm, ids_ref), (gate_hbm, gate_ref))
    copies = [pltpu.make_async_copy(src, dst, sems.at[i]) for i, (src, dst) in enumerate(pairs)]
    for copy in copies:
        copy.start()
    for copy in copies:
        copy.wait()
    micro_count, tok_count = tok_ref.shape[:2]
    top_count = ids_ref.shape[1]
    seg = out_ref.shape[2] - LANES

    def flat(ref):
        return jnp.concatenate([ref[m].astype(f32) for m in range(micro_count)], 0)

    lane = lax.broadcasted_iota(i32, (tok_count, LANES), 1)
    diagonal = lax.broadcasted_iota(i32, (tok_count, tok_count), 0) == lax.broadcasted_iota(
        i32, (tok_count, tok_count), 1
    )
    blocks = []
    for m in range(micro_count):
        block = jnp.zeros((tok_count, LANES), f32)
        for at, ref in enumerate((ids_ref, gate_ref)):
            values = ref[m].astype(f32)
            for k in range(top_count):
                row = jnp.broadcast_to(values[k : k + 1], (tok_count, tok_count))
                column = jnp.sum(jnp.where(diagonal, row, 0.0), axis=1, keepdims=True)
                block = jnp.where(lane == at * top_count + k, column, block)
        blocks.append(block)
    extras = jnp.concatenate(blocks + blocks, 0).astype(bf16)
    both = jnp.concatenate([flat(tok_ref), flat(cot_ref)], 0).astype(bf16)
    for p in range(out_ref.shape[0]):
        out_ref[p, :, :d_part] = both[:, p * d_part : (p + 1) * d_part]
        if seg > d_part:
            out_ref[p, :, d_part:seg] = jnp.zeros((both.shape[0], seg - d_part), bf16)
        out_ref[p, :, seg:] = extras


def pack_kernel(tok_count, top_count, where_ref, rows_ref, *out_refs):
    slot_refs, place_ref = out_refs[:EXPERTS], out_refs[EXPERTS]
    pipe_size, both_rows, width = rows_ref.shape
    own_rows = both_rows // 2
    total = pipe_size * both_rows
    slot_count = slot_refs[0].shape[0] // 2
    me = where_ref[0]
    rows = jnp.concatenate([rows_ref[p] for p in range(pipe_size)], 0)
    extras = rows[:, width - LANES :].astype(f32)
    row = lax.broadcasted_iota(i32, (total, total), 0)
    other = lax.broadcasted_iota(i32, (total, total), 1)
    earlier = ((other < row) & (other // tok_count == row // tok_count)).astype(bf16)
    at = (lax.broadcasted_iota(i32, (total, LANES), 1) ^ me).astype(f32)
    routed = jnp.zeros((total, LANES), f32)
    for k in range(top_count):
        routed = jnp.where(extras[:, k : k + 1] == at, 1.0, routed)
    position = jnp.dot(earlier, routed.astype(bf16), preferred_element_type=f32)
    index = lax.broadcasted_iota(i32, (total, 1), 0)
    within = index % both_rows
    block = within % own_rows // tok_count
    device = index // both_rows
    base = within // own_rows * slot_count + (device * (own_rows // tok_count) + block) * CAP
    lane = lax.broadcasted_iota(i32, (total, EXPERTS * 2 * slot_count), 1).astype(f32)
    chosen = jnp.zeros(lane.shape, f32)
    small_lane = lax.broadcasted_iota(i32, (total, LANES), 1).astype(f32)
    places = jnp.zeros((total, LANES), f32)
    for k in range(EXPERTS):
        here = routed[:, k : k + 1] > 0.0
        target = (k * 2 * slot_count + base).astype(f32) + position[:, k : k + 1]
        chosen = chosen + jnp.where((lane == target) & here, 1.0, 0.0)
        local = (k * ROWS + block * CAP).astype(f32) + position[:, k : k + 1]
        places = places + jnp.where((small_lane == local) & here, 1.0, 0.0)
    slots = lax.dot_general(chosen.astype(bf16), rows, ROWS_BY_ROWS, preferred_element_type=f32)
    for k in range(EXPERTS):
        slot_refs[k][...] = slots[2 * k * slot_count : 2 * (k + 1) * slot_count].astype(bf16)
    for p in range(pipe_size):
        start = p * both_rows
        place_ref[p, :, :LANES] = places[start : start + own_rows]
        place_ref[p, :, LANES:] = extras[start : start + own_rows]


def join_kernel(pipe_size, *refs):
    blocks, out_ref = [ref[...].astype(f32) for ref in refs[:PER_GROUP]], refs[-1]
    rows = blocks[0].shape[0] // 2 // pipe_size
    for a in range(2):
        starts = [(a * pipe_size + p) * rows for p in range(pipe_size)]
        out_ref[a] = jnp.concatenate([b[s : s + rows] for s in starts for b in blocks], 0).astype(bf16)


def hidden_kernel(d_part, top_count, pipe_size, where_ref, *refs):
    pieces = [refs[5 * i : 5 * (i + 1)] for i in range(2 * GROUPS)]
    w_gate, w_up = refs[10 * GROUPS : 10 * GROUPS + 2]
    d_gate, d_up, scaled, low_back, high_back = refs[-5:]
    me = where_ref[0].astype(f32)
    shares = []
    for i, (info, own_g, own_u, own_b, got) in enumerate(pieces):
        count = own_g.shape[0]
        extras = info[...].astype(f32)
        gate = jnp.zeros((count, 1), f32)
        for k in range(top_count):
            gate = gate + jnp.where(
                extras[:, k : k + 1] == me, extras[:, top_count + k : top_count + k + 1], 0.0
            )
        pre_gate = own_g[...] + got[0].astype(f32)
        pre_up = own_u[...] + got[1].astype(f32)
        back_proj = own_b[...] + got[2].astype(f32)
        sig = jax.nn.sigmoid(pre_gate)
        activated = pre_gate * sig
        hidden = activated * pre_up
        shares.append(jnp.sum(back_proj * hidden, axis=1, keepdims=True))
        d_hidden = gate * back_proj
        here = slice(i * count, (i + 1) * count)
        scaled[here] = (gate * hidden).astype(bf16)
        d_gate[here] = (d_hidden * pre_up * sig * (1.0 + pre_gate * (1.0 - sig))).astype(bf16)
        d_up[here] = (d_hidden * activated).astype(bf16)
    back = lax.dot_general(
        d_gate[...], w_gate[...], COLUMNS_BY_COLUMNS, preferred_element_type=f32
    ) + lax.dot_general(d_up[...], w_up[...], COLUMNS_BY_COLUMNS, preferred_element_type=f32)
    share = jnp.concatenate(shares, 0)
    high = share.astype(bf16).astype(f32)
    lane = lax.broadcasted_iota(i32, (share.shape[0], LANES), 1)
    tail = jnp.where(lane == 0, high, jnp.where(lane == 1, share - high, 0.0))
    members = low_back.shape[1] // pipe_size * 2
    used = count // members // pipe_size
    for h in range(2):
        for member in range(members):
            ref = low_back if member < members // 2 else high_back
            for p in range(pipe_size):
                starts = [(2 * g + h) * count + (member * pipe_size + p) * used for g in range(GROUPS)]
                at = member % (members // 2) * pipe_size + (p ^ where_ref[1] if pipe_size == 2 else p)
                for columns, values in ((slice(0, d_part), back), (slice(d_part, None), tail)):
                    block = jnp.concatenate([values[start : start + used] for start in starts], 0)
                    ref[h, at, :, columns] = block.astype(bf16)


def fold_kernel(a_ref, b_ref, *out_refs):
    for i, ref in enumerate(out_refs):
        here = i // a_ref.shape[1], i % a_ref.shape[1]
        ref[...] = (a_ref[here].astype(f32) + b_ref[here].astype(f32)).astype(bf16)


def fold_pairs_kernel(used, a_ref, b_ref, c_ref, d_ref, *out_refs):
    totals = (
        a_ref[...].astype(f32) + b_ref[...].astype(f32),
        c_ref[...].astype(f32) + d_ref[...].astype(f32),
    )
    for k, ref in enumerate(out_refs):
        for h, total in enumerate(totals):
            rows = total[k * used : (k + 1) * used]
            pad = jnp.zeros((ROWS - used, rows.shape[1]), f32)
            ref[h] = jnp.concatenate([rows, pad], 0).astype(bf16)


def owner_kernel(d_part, where_ref, place_ref, *refs):
    piece_refs, tok_ref, grad_ref = refs[:EXPERTS], refs[EXPERTS], refs[EXPERTS + 1]
    micro_count, tok_count = tok_ref.shape[:2]
    top_count = grad_ref.shape[1]
    pipe_size = piece_refs[0].shape[0]
    mine = place_ref[where_ref[1]]
    place = mine[:, : EXPERTS * ROWS].astype(bf16)
    ids = mine[:, LANES:]
    halves = []
    for h in range(pipe_size):
        rows = jnp.concatenate([ref[h].astype(f32) for ref in piece_refs], 0)
        halves.append(rows)
    sums = [jnp.dot(place, h.astype(bf16), preferred_element_type=f32)[:, :d_part] for h in halves]
    if pipe_size == 2:
        first = where_ref[1] == 0
        sums = [jnp.where(first, sums[0], sums[1]), jnp.where(first, sums[1], sums[0])]
    tail = halves[0][:, d_part:]
    shares = tail[:, 0:1] + tail[:, 1:2]
    slot_lane = lax.broadcasted_iota(i32, place.shape, 1)
    diagonal = lax.broadcasted_iota(i32, (tok_count, tok_count), 0) == lax.broadcasted_iota(
        i32, (tok_count, tok_count), 1
    )
    square = EXPERTS * ROWS
    eye = lax.broadcasted_iota(i32, (square, square), 0) == lax.broadcasted_iota(i32, (square, square), 1)
    share_row = jnp.sum(jnp.where(eye, jnp.broadcast_to(shares, (square, square)), 0.0), axis=0, keepdims=True)
    picked = mine[:, : EXPERTS * ROWS] * share_row
    expert_of = ((slot_lane // ROWS) ^ where_ref[0]).astype(f32)
    for k in range(top_count):
        grad = jnp.sum(jnp.where(expert_of == ids[:, k : k + 1], picked, 0.0), axis=1, keepdims=True)
        for m in range(micro_count):
            part = jnp.broadcast_to(grad[m * tok_count : (m + 1) * tok_count], (tok_count, tok_count))
            grad_ref[m, k : k + 1, :] = jnp.sum(jnp.where(diagonal, part, 0.0), axis=0, keepdims=True)
    for m in range(micro_count):
        for p in range(pipe_size):
            tok_ref[m, :, p * d_part : (p + 1) * d_part] = sums[p][m * tok_count : (m + 1) * tok_count].astype(bf16)


def flip_kernel(*refs):
    refs[-1][...] = jnp.concatenate([ref[...] for ref in refs[:-1]], 0).T


def weight_kernel(scale, block, tok_ref, cot_ref, d_gate, d_up, scaled, after, *refs):
    del after
    out_refs, held, sems = refs[:3], refs[3], refs[4]
    copies = []
    for i in range(tok_ref.shape[0] // block):
        here = slice(i * block, (i + 1) * block)
        for w, (left, right) in enumerate(((tok_ref, d_gate), (tok_ref, d_up), (cot_ref, scaled))):
            rows = jnp.dot(left[here], right[...], preferred_element_type=f32)
            held[w, here] = (rows * scale).astype(bf16)
            copies.append(pltpu.make_async_copy(held.at[w, here], out_refs[w].at[here], sems.at[w, i]))
            copies[-1].start()
    for copy in copies:
        copy.wait()


def tie_kernel(*refs):
    del refs


def call(kernel, out_shape, in_specs, name, mib=8, flops=0, moved=0, **more):
    specs = {"s": pl.BlockSpec(memory_space=pltpu.SMEM), "v": pl.BlockSpec(memory_space=pltpu.VMEM)}
    specs["a"] = pl.BlockSpec(memory_space=pl.ANY)
    specs["h"] = pl.BlockSpec(memory_space=pltpu.HBM)
    more.setdefault("out_specs", jax.tree.map(lambda _: specs["v"], out_shape))
    return pl.pallas_call(
        kernel,
        out_shape=out_shape,
        in_specs=[specs[c] for c in in_specs],
        compiler_params=pltpu.CompilerParams(vmem_limit_bytes=mib << 20),
        cost_estimate=pl.CostEstimate(flops=flops, bytes_accessed=moved, transcendentals=0),
        name=name,
        **more,
    )


def tie(values, after):
    return call(
        tie_kernel,
        [shape(v.shape, v.dtype) for v in values],
        "a" * (len(values) + 1),
        "tie",
        out_specs=[pl.BlockSpec(memory_space=pl.ANY)] * len(values),
        input_output_aliases={i: i for i in range(len(values))},
    )(*values, after)


def on_device(tokens, cotangent, expert_ids, gate_values, w_gate, w_up, w_down_t):
    micro_count, tok_count, d_model = tokens.shape
    top_count = expert_ids.shape[2]
    pipe_size = lax.axis_size("pipe")
    expert_size = lax.axis_size("expert")
    group_size = expert_size // EXPERTS
    bits = [1 << i for i in reversed(range(group_size.bit_length() - 1))]
    d_part, f_part = w_gate.shape
    width = -(-d_part // LANES) * LANES + LANES
    own_rows = micro_count * tok_count
    slots_here = micro_count * CAP
    slot_count = pipe_size * slots_here
    pipe = lax.axis_index("pipe")
    where = jnp.stack([lax.axis_index("expert") // group_size, pipe]).astype(i32)

    send = call(
        functools.partial(prep_kernel, d_part),
        shape((pipe_size, 2 * own_rows, width), bf16),
        "hhhh",
        "prep",
        scratch_shapes=[
            pltpu.VMEM(tokens.shape, bf16),
            pltpu.VMEM(tokens.shape, bf16),
            pltpu.VMEM((micro_count, top_count, tok_count), i32),
            pltpu.VMEM((micro_count, top_count, tok_count), bf16),
            pltpu.SemaphoreType.DMA((4,)),
        ],
        mib=PREP_MIB,
    )(tokens, cotangent, jnp.swapaxes(expert_ids, 1, 2), jnp.swapaxes(gate_values, 1, 2))
    if pipe_size == 2:
        first = pipe == 0
        got = swap(jnp.where(first, send[1], send[0]), "pipe", 1)
        layer_rows = jnp.where(first, jnp.stack([send[0], got]), jnp.stack([got, send[1]]))
    else:
        layer_rows = lax.all_to_all(send, "pipe", split_axis=0, concat_axis=0, tiled=True)
    *slots, place = call(
        functools.partial(pack_kernel, tok_count, top_count),
        tuple(shape((2 * slot_count, width), bf16) for _ in range(EXPERTS))
        + (shape((pipe_size, own_rows, 2 * LANES), f32),),
        "sv",
        "pack",
    )(where, layer_rows)

    gathered = [slots[0]] + [swap(slots[k], "expert", k * group_size) for k in range(1, EXPERTS)]
    groups, after = [], ()
    for g in range(GROUPS):
        joined = call(
            functools.partial(join_kernel, pipe_size),
            shape((2, PER_GROUP * slot_count, width), bf16),
            "v" * PER_GROUP + "a" * len(after),
            "join",
        )(*gathered[g * PER_GROUP : (g + 1) * PER_GROUP], *after)
        after = (joined,)
        sent = joined if g == 0 else tie([joined], groups[-1][1])[0]
        groups.append([joined, swap(sent, "expert", bits[0])])
    for halves in groups:
        for h in range(2):
            for bit in bits[1:]:
                halves[h] = jnp.concatenate([halves[h], swap(halves[h], "expert", bit)], 1)

    exchanged = []
    for halves in groups:
        for rows in halves:
            tok_rows, cot_rows = rows[0, :, :d_part], rows[1, :, :d_part]
            own = []
            for left, weight in ((tok_rows, w_gate), (tok_rows, w_up), (cot_rows, w_down_t)):
                own.append(jnp.dot(left, weight, preferred_element_type=f32))
            bit = pipe_size // 2
            while bit > 1:
                got = swap(jnp.stack([part.astype(bf16) for part in own]), "pipe", bit)
                own = [part + got[i].astype(f32) for i, part in enumerate(own)]
                bit //= 2
            got = swap(jnp.stack([part.astype(bf16) for part in own]), "pipe", 1)
            exchanged.append([rows[0, :, width - LANES :], *own, got])
    count = exchanged[0][0].shape[0]

    flipped = [
        call(flip_kernel, shape((d_part, 2 * GROUPS * count), bf16), "v" * (2 * GROUPS), "flip", mib=24)(
            *[rows[a, :, :d_part] for halves in groups for rows in halves]
        )
        for a in range(2)
    ]

    out_width = d_part + LANES
    total = 2 * GROUPS * count
    padded = EXPERTS * slots_here
    half_shape = shape((2, group_size // 4 * pipe_size, padded, out_width), bf16)
    moved = total * (f_part * 24 + d_part * 8) + 4 * d_part * f_part
    operands = [x for piece in exchanged for x in piece]
    *grads, low, high = call(
        functools.partial(hidden_kernel, d_part, top_count, pipe_size),
        (shape((total, f_part), bf16),) * 3 + (half_shape,) * 2,
        "s" + "v" * (len(operands) + 2) + "a" * len(flipped),
        "hidden",
        mib=min(52, 8 + 2 * moved // (1 << 20)),
    )(where, *operands, w_gate, w_up, *flipped)
    piece_shapes = [shape((pipe_size, ROWS, out_width), bf16) for _ in range(EXPERTS)]
    if pipe_size == 2 and group_size == 4:
        parts = call(fold_kernel, [shape((padded, out_width), bf16) for _ in range(4)], "vv", "fold")(
            low, swap(high, "expert", bits[1])
        )
        after = parts[0]
        got_both = swap_both(parts[3], bits[0])
        got_member = swap(parts[2], "expert", bits[0])
        got_pipe = swap(parts[1], "pipe", 1)
        pieces = call(functools.partial(fold_pairs_kernel, slots_here), piece_shapes, "vvvv", "fold_pairs")(
            parts[0], got_member, got_pipe, got_both
        )
    else:
        for bit in reversed(bits[1:]):
            sums = (low.astype(f32) + swap(high, "expert", bit).astype(f32)).astype(bf16)
            low, high = jnp.split(sums, 2, 1) if bit != bits[1] else (sums[0], sums[1])
        sums = (low.astype(f32) + swap(high, "expert", bits[0]).astype(f32)).astype(bf16)
        after = sums
        if pipe_size == 2:
            sums = jnp.stack([sums[0], swap(sums[1], "pipe", 1)])
        else:
            sums = lax.all_to_all(sums, "pipe", split_axis=0, concat_axis=0, tiled=True)
        pieces = [
            jnp.pad(sums[:, k * slots_here : (k + 1) * slots_here], ((0, 0), (0, ROWS - slots_here), (0, 0)))
            for k in range(EXPERTS)
        ]
    pieces = [swap(piece, "expert", k * group_size) if k else piece for k, piece in enumerate(pieces)]

    tokens_total = own_rows * pipe_size * expert_size
    scale = 1.0 / math.sqrt(tokens_total * top_count / EXPERTS)
    block = 256 if d_part % 256 == 0 else d_part
    dw_gate, dw_up, dw_down_t = call(
        functools.partial(weight_kernel, scale, block),
        [shape((d_part, f_part), bf16)] * 3,
        "vvvvva",
        "weight_grads",
        mib=min(52, 12 + (d_part * (total * 4 + f_part * 8) >> 20)),
        out_specs=[pl.BlockSpec(memory_space=pl.ANY)] * 3,
        scratch_shapes=[
            pltpu.VMEM((3, d_part, f_part), bf16),
            pltpu.SemaphoreType.DMA((3, d_part // block)),
        ],
    )(*flipped, *grads, after)

    d_tokens, gate_grads = call(
        functools.partial(owner_kernel, d_part),
        (shape(tokens.shape, bf16), shape((micro_count, top_count, tok_count), f32)),
        "sv" + "v" * EXPERTS,
        "owner",
    )(where, place, *pieces)
    return (d_tokens, jnp.swapaxes(gate_grads, 1, 2), dw_gate, dw_up, dw_down_t)


def solution(mesh):
    rows = P(None, ("pipe", "expert"), None)
    weights = P("pipe", "expert")
    return jax.shard_map(
        on_device,
        mesh=mesh,
        in_specs=(rows, rows, rows, rows, weights, weights, weights),
        out_specs=(rows, rows, weights, weights, weights),
        check_vma=False,
    )
```

time: 75.5 us -> 66.7 us (0.88)
  Pallas kernels: 2.7 us -> 10.2 us
  waiting for transfers between devices: 30.3 us -> 24.5 us
  local copies, waits for them, and re-layouts: 5.89 us -> 0.18 us
  matrix products: 9.42 us -> 4.98 us
    ppermute x20, waiting for transfers between devices: 30.3 us -> 21.9 us  [swap(): lax.ppermute(x, axis, [(i, i ^ bit) for i in range(lax.axis_size(axis))])]
    pallas_call x2 -> x10, Pallas kernels: 2.03 us -> 7.35 us  [the longest x1 2.8 us: on_device(): call(functools.partial(weight_kernel, scale, block), [shape((d_part, f_pa...]
    unnamed x21 -> x8, local copies, waits for them, and re-layouts: 5.06 us -> 0.06 us
    dot_general x9 -> x12, matrix products: 9.42 us -> 4.98 us  [on_device(): own.append(jnp.dot(left, weight, preferred_element_type=f32))]
    ppermute x0 -> x1, waiting for transfers between devices: none -> 2.52 us  [swap_both(): return lax.ppermute(x, ('pipe', 'expert'), pairs)]
    pallas_call x1, Pallas kernels: 0.08 us -> 1.75 us  [on_device(): call(functools.partial(prep_kernel, d_part), shape((pipe_size, 2 * own_ro...]
    ppermute x0 -> x1, starting transfers between devices: none -> 1.26 us  [swap_both(): return lax.ppermute(x, ('pipe', 'expert'), pairs)]
    ppermute x20, starting transfers between devices: 24.4 us -> 23.2 us  [swap(): lax.ppermute(x, axis, [(i, i ^ bit) for i in range(lax.axis_size(axis))])]
  transfers between devices with their start and end apart: 20 -> 21, of which waited for: 14 -> 16; matrix products, arithmetic and copies ran while one was open for 12% -> 8% of each run, Pallas kernels for 0% -> 5%
where the time goes in v3:
time: 66.7 us; the launch traced here: 66.5 us
  starting transfers between devices  24.5 us (37%)
  waiting for transfers between devices  24.5 us (37%)
  Pallas kernels  10.2 us (15%)
  matrix products  4.98 us (7%)
  other arithmetic  1.25 us (2%)
  between operations  0.95 us (1%)
    ppermute x20, starting transfers between devices, swap(): lax.ppermute(x, axis, [(i, i ^ bit) for i in range(lax.axis_size(axis))])  23.2 us
    ppermute x20, waiting for transfers between devices, swap(): lax.ppermute(x, axis, [(i, i ^ bit) for i in range(lax.axis_size(axis))])  21.9 us
    dot_general x12, matrix products, on_device(): own.append(jnp.dot(left, weight, preferred_element_type=f32))  4.98 us
    pallas_call x1, Pallas kernels, on_device(): call(functools.partial(weight_kernel, scale, block), [shape((d_part, f_pa...  2.8 us
    ppermute x1, waiting for transfers between devices, swap_both(): return lax.ppermute(x, ('pipe', 'expert'), pairs)  2.52 us
    pallas_call x1, Pallas kernels, on_device(): call(functools.partial(hidden_kernel, d_part, top_count, pipe_size), (sha...  2.28 us
    pallas_call x1, Pallas kernels, on_device(): call(functools.partial(prep_kernel, d_part), shape((pipe_size, 2 * own_ro...  1.75 us
    pallas_call x1, Pallas kernels, on_device(): call(functools.partial(owner_kernel, d_part), (shape(tokens.shape, bf16),...  1.37 us
  transfers between devices with their start and end apart: 21, of which 16 were waited for; matrix products, arithmetic and copies ran while one was open for 8% of the time, Pallas kernels for 5%

profile of v3, /device:TPU:0, one launch (start us, length us, event | category | flops | bytes accessed | tf_op | source)
XLA Modules:
  0.0 66.5 jit_solution(18058132508039567207)
XLA Ops:
  0.7 1.8 %prep.1 = bf16[2,16,1920]{2,1,0:T(8,128)(2,1)} custom-call(bf16[2,4,3584]{2,1,0:T(4,128)(2,1)} %tok_hbm.1, bf16[2,4,3584]{2,1,0:T(4,128)(2,1)} %cot_hbm.1, s32[2,2,4]{2,1,0:T(2,128)} %bitcast.81, bf16[2,2,4]{2,1,0:T(2,128)(2,1)} %bitcast.82), custom_call_target="tpu_custom_call" | custom-call | tf_op jit(solution)/shard_map/prep/pallas_call | solution.py:286
  2.4 0.9 %fusion.8 = (bf16[1,16,1920]{2,1,0:T(8,128)(2,1)S(1)}, bf16[16,1920]{1,0:T(8,128)(2,1)S(1)}, bf16[1,16,1920]{2,1,0:T(8,128)(2,1)S(1)}) fusion(bf16[2,16,1920]{2,1,0:T(8,128)(2,1)} %prep.1, pred[]{:T(512)S(6)} %eq.3), kind=kLoop, calls=%fused_computation.43 | loop fusion | flops 30720 | bytes 307201 | tf_op jit(solution)/shard_map/slice | solution.py:302
  3.3 3.0 %collective-permute-start = (bf16[16,1920]{1,0:T(8,128)(2,1)S(1)}, bf16[16,1920]{1,0:T(8,128)(2,1)S(1)}, u32[]{:S(2)}, u32[]{:S(2)}) collective-permute-start(bf16[16,1920]{1,0:T(8,128)(2,1)S(1)} %get-tuple-element.60), channel_id=1, source_target_pairs={{0,16},{16,0},{1,17},{17,1},{2,18},{18,2},{3,19},{19,3},{4,20},{20... | collective-permute-start | bytes 184328 | tf_op jit(solution)/shard_map/ppermute | solution.py:25
  6.4 2.1 %collective-permute-done = bf16[16,1920]{1,0:T(8,128)(2,1)S(1)} collective-permute-done((bf16[16,1920]{1,0:T(8,128)(2,1)S(1)}, bf16[16,1920]{1,0:T(8,128)(2,1)S(1)}, u32[]{:S(2)}, u32[]{:S(2)}) %collective-permute-start) | collective-permute-done | bytes 61472 | tf_op jit(solution)/shard_map/ppermute | solution.py:25
  8.5 1.1 %pack.1 = (bf16[24,1920]{1,0:T(8,128)(2,1)S(1)}, bf16[24,1920]{1,0:T(8,128)(2,1)S(1)}, bf16[24,1920]{1,0:T(8,128)(2,1)S(1)}, bf16[24,1920]{1,0:T(8,128)(2,1)S(1)}, f32[2,8,256]{2,1,0:T(8,128)S(1)}) custom-call(s32[2]{0:T(128)S(1)} %pad_add_fusion.where_ref, bf16[2,16,1920]{2,1,0:T(8,128)(2,1)S(1)} %maximum_select_fusion.rows_ref), custom_call_target="tpu_custom_call" | custom-call | tf_op jit(solution)/shard_map/pack/pallas_call | solution.py:306
  9.6 2.2 %collective-permute-start.1 = (bf16[24,1920]{1,0:T(8,128)(2,1)S(1)}, bf16[24,1920]{1,0:T(8,128)(2,1)S(1)}, u32[]{:S(2)}, u32[]{:S(2)}) collective-permute-start(bf16[24,1920]{1,0:T(8,128)(2,1)S(1)} %get-tuple-element.30), channel_id=1, source_target_pairs={{0,4},{1,5},{2,6},{3,7},{4,0},{5,1},{6,2},{7,3},{8,12},{9,13},{10,... | collective-permute-start | bytes 276488 | tf_op jit(solution)/shard_map/ppermute | solution.py:25
  11.8 2.6 %collective-permute-start.7 = (bf16[24,1920]{1,0:T(8,128)(2,1)S(1)}, bf16[24,1920]{1,0:T(8,128)(2,1)S(1)}, u32[]{:S(2)}, u32[]{:S(2)}) collective-permute-start(bf16[24,1920]{1,0:T(8,128)(2,1)S(1)} %get-tuple-element.31), channel_id=1, source_target_pairs={{0,8},{1,9},{2,10},{3,11},{4,12},{5,13},{6,14},{7,15},{8,0},{9,1},... | collective-permute-start | bytes 276488 | tf_op jit(solution)/shard_map/ppermute | solution.py:25
  14.4 0.9 %collective-permute-done.1.refs_1_ = bf16[24,1920]{1,0:T(8,128)(2,1)S(1)} collective-permute-done((bf16[24,1920]{1,0:T(8,128)(2,1)S(1)}, bf16[24,1920]{1,0:T(8,128)(2,1)S(1)}, u32[]{:S(2)}, u32[]{:S(2)}) %collective-permute-start.1) | collective-permute-done | bytes 92192 | tf_op jit(solution)/shard_map/ppermute | solution.py:25
  15.3 4.3 %collective-permute-done.7.refs_0_ = bf16[24,1920]{1,0:T(8,128)(2,1)S(1)} collective-permute-done((bf16[24,1920]{1,0:T(8,128)(2,1)S(1)}, bf16[24,1920]{1,0:T(8,128)(2,1)S(1)}, u32[]{:S(2)}, u32[]{:S(2)}) %collective-permute-start.7) | collective-permute-done | bytes 92192 | tf_op jit(solution)/shard_map/ppermute | solution.py:25
  19.6 1.2 %collective-permute-done.8.refs_1_ = bf16[24,1920]{1,0:T(8,128)(2,1)S(1)} collective-permute-done((bf16[24,1920]{1,0:T(8,128)(2,1)S(1)}, bf16[24,1920]{1,0:T(8,128)(2,1)S(1)}, u32[]{:S(2)}, u32[]{:S(2)}) %collective-permute-start.8) | collective-permute-done | bytes 92192 | tf_op jit(solution)/shard_map/ppermute | solution.py:25
  21.0 1.6 %collective-permute-start.4 = (bf16[2,24,1920]{2,1,0:T(8,128)(2,1)S(1)}, bf16[2,24,1920]{2,1,0:T(8,128)(2,1)S(1)}, u32[]{:S(2)}, u32[]{:S(2)}) collective-permute-start(bf16[2,24,1920]{2,1,0:T(8,128)(2,1)S(1)} %join.2.refs_2_), channel_id=1, source_target_pairs={{0,2},{1,3},{2,0},{3,1},{4,6},{5,7},{6,4},{7,5},{8,10},{9,11},{10,... | collective-permute-start | bytes 552968 | tf_op jit(solution)/shard_map/ppermute | solution.py:25
  25.4 1.6 %collective-permute-start.10 = (bf16[3,48,512]{2,1,0:T(8,128)(2,1)S(1)}, bf16[3,48,512]{2,1,0:T(8,128)(2,1)S(1)}, u32[]{:S(2)}, u32[]{:S(2)}) collective-permute-start(bf16[3,48,512]{2,1,0:T(8,128)(2,1)S(1)} %pad_maximum_fusion.4), channel_id=1, source_target_pairs={{0,16},{16,0},{1,17},{17,1},{2,18},{18,2},{3,19},{19,3},{4,20},{20... | collective-permute-start | bytes 442376 | tf_op jit(solution)/shard_map/ppermute | solution.py:25
  27.0 1.1 %collective-permute-done.4.refs_1_ = bf16[2,24,1920]{2,1,0:T(8,128)(2,1)S(1)} collective-permute-done((bf16[2,24,1920]{2,1,0:T(8,128)(2,1)S(1)}, bf16[2,24,1920]{2,1,0:T(8,128)(2,1)S(1)}, u32[]{:S(2)}, u32[]{:S(2)}) %collective-permute-start.4) | collective-permute-done | bytes 184352 | tf_op jit(solution)/shard_map/ppermute | solution.py:25
  28.1 1.5 %collective-permute-start.11 = (bf16[2,24,1920]{2,1,0:T(8,128)(2,1)S(1)}, bf16[2,24,1920]{2,1,0:T(8,128)(2,1)S(1)}, u32[]{:S(2)}, u32[]{:S(2)}) collective-permute-start(bf16[2,24,1920]{2,1,0:T(8,128)(2,1)S(1)} %tie.1), channel_id=1, source_target_pairs={{0,2},{1,3},{2,0},{3,1},{4,6},{5,7},{6,4},{7,5},{8,10},{9,11},{10,... | collective-permute-start | bytes 552968 | tf_op jit(solution)/shard_map/ppermute | solution.py:25
  30.1 1.6 %collective-permute-start.3 = (bf16[3,48,512]{2,1,0:T(8,128)(2,1)S(1)}, bf16[3,48,512]{2,1,0:T(8,128)(2,1)S(1)}, u32[]{:S(2)}, u32[]{:S(2)}) collective-permute-start(bf16[3,48,512]{2,1,0:T(8,128)(2,1)S(1)} %pad_maximum_fusion.2), channel_id=1, source_target_pairs={{0,16},{16,0},{1,17},{17,1},{2,18},{18,2},{3,19},{19,3},{4,20},{20... | collective-permute-start | bytes 442376 | tf_op jit(solution)/shard_map/ppermute | solution.py:25
  31.7 1.4 %collective-permute-done.5 = bf16[2,24,1920]{2,1,0:T(8,128)(2,1)S(1)} collective-permute-done((bf16[2,24,1920]{2,1,0:T(8,128)(2,1)S(1)}, bf16[2,24,1920]{2,1,0:T(8,128)(2,1)S(1)}, u32[]{:S(2)}, u32[]{:S(2)}) %collective-permute-start.5) | collective-permute-done | bytes 184352 | tf_op jit(solution)/shard_map/ppermute | solution.py:25
  35.1 1.4 %collective-permute-done.12 = bf16[2,24,1920]{2,1,0:T(8,128)(2,1)S(1)} collective-permute-done((bf16[2,24,1920]{2,1,0:T(8,128)(2,1)S(1)}, bf16[2,24,1920]{2,1,0:T(8,128)(2,1)S(1)}, u32[]{:S(2)}, u32[]{:S(2)}) %collective-permute-start.12) | collective-permute-done | bytes 184352 | tf_op jit(solution)/shard_map/ppermute | solution.py:25
  37.9 1.6 %collective-permute-start.13 = (bf16[3,48,512]{2,1,0:T(8,128)(2,1)S(1)}, bf16[3,48,512]{2,1,0:T(8,128)(2,1)S(1)}, u32[]{:S(2)}, u32[]{:S(2)}) collective-permute-start(bf16[3,48,512]{2,1,0:T(8,128)(2,1)S(1)} %pad_maximum_fusion.5), channel_id=1, source_target_pairs={{0,16},{16,0},{1,17},{17,1},{2,18},{18,2},{3,19},{19,3},{4,20},{20... | collective-permute-start | bytes 442376 | tf_op jit(solution)/shard_map/ppermute | solution.py:25
  40.4 3.4 %collective-permute-done.13.refs_19_ = bf16[3,48,512]{2,1,0:T(8,128)(2,1)S(1)} collective-permute-done((bf16[3,48,512]{2,1,0:T(8,128)(2,1)S(1)}, bf16[3,48,512]{2,1,0:T(8,128)(2,1)S(1)}, u32[]{:S(2)}, u32[]{:S(2)}) %collective-permute-start.13) | collective-permute-done | bytes 147488 | tf_op jit(solution)/shard_map/ppermute | solution.py:25
  43.8 2.3 %hidden.1 = (bf16[192,512]{1,0:T(8,128)(2,1)S(1)}, bf16[192,512]{1,0:T(8,128)(2,1)S(1)}, bf16[192,512]{1,0:T(8,128)(2,1)S(1)}, bf16[2,2,24,1920]{3,2,1,0:T(8,128)(2,1)S(1)}, bf16[2,2,24,1920]{3,2,1,0:T(8,128)(2,1)S(1)}) custom-call(s32[2]{0:T(128)S(1)} %pad_add_fusion.where_ref, bf16[48,128]{1,0:T(8,128)(2,1)S(1)} %maximum_bitcast_fusion.3.refs_0_, ...), custom_call_target="tpu_custom_call" | custom-call | tf_op jit(solution)/shard_map/hidden/pallas_call | solution.py:360
  46.2 1.7 %collective-permute-done.14.b_ref = bf16[2,2,24,1920]{3,2,1,0:T(8,128)(2,1)S(1)} collective-permute-done((bf16[2,2,24,1920]{3,2,1,0:T(8,128)(2,1)S(1)}, bf16[2,2,24,1920]{3,2,1,0:T(8,128)(2,1)S(1)}, u32[]{:S(2)}, u32[]{:S(2)}) %collective-permute-start.14) | collective-permute-done | bytes 368672 | tf_op jit(solution)/shard_map/ppermute | solution.py:25
  48.0 0.8 %collective-permute-start.15 = (bf16[24,1920]{1,0:T(8,128)(2,1)S(1)}, bf16[24,1920]{1,0:T(8,128)(2,1)S(1)}, u32[]{:S(2)}, u32[]{:S(2)}) collective-permute-start(bf16[24,1920]{1,0:T(8,128)(2,1)S(1)} %get-tuple-element.36), channel_id=1, source_target_pairs={{0,2},{1,3},{2,0},{3,1},{4,6},{5,7},{6,4},{7,5},{8,10},{9,11},{10,... | collective-permute-start | bytes 276488 | tf_op jit(solution)/shard_map/ppermute | solution.py:25
  48.8 1.5 %collective-permute-start.16 = (bf16[24,1920]{1,0:T(8,128)(2,1)S(1)}, bf16[24,1920]{1,0:T(8,128)(2,1)S(1)}, u32[]{:S(2)}, u32[]{:S(2)}) collective-permute-start(bf16[24,1920]{1,0:T(8,128)(2,1)S(1)} %get-tuple-element.37), channel_id=1, source_target_pairs={{0,16},{16,0},{1,17},{17,1},{2,18},{18,2},{3,19},{19,3},{4,20},{20... | collective-permute-start | bytes 276488 | tf_op jit(solution)/shard_map/ppermute | solution.py:25
  50.3 1.3 %collective-permute-start.17 = (bf16[24,1920]{1,0:T(8,128)(2,1)S(1)}, bf16[24,1920]{1,0:T(8,128)(2,1)S(1)}, u32[]{:S(2)}, u32[]{:S(2)}) collective-permute-start(bf16[24,1920]{1,0:T(8,128)(2,1)S(1)} %get-tuple-element.38), channel_id=1, source_target_pairs={{0,18},{1,19},{2,16},{3,17},{4,22},{5,23},{6,20},{7,21},{8,26},{9,... | collective-permute-start | bytes 276488 | tf_op jit(solution)/shard_map/ppermute | solution.py:31
  51.5 1.2 %collective-permute-done.15.b_ref = bf16[24,1920]{1,0:T(8,128)(2,1)S(1)} collective-permute-done((bf16[24,1920]{1,0:T(8,128)(2,1)S(1)}, bf16[24,1920]{1,0:T(8,128)(2,1)S(1)}, u32[]{:S(2)}, u32[]{:S(2)}) %collective-permute-start.15) | collective-permute-done | bytes 92192 | tf_op jit(solution)/shard_map/ppermute | solution.py:25
  53.5 2.5 %collective-permute-done.17.d_ref = bf16[24,1920]{1,0:T(8,128)(2,1)S(1)} collective-permute-done((bf16[24,1920]{1,0:T(8,128)(2,1)S(1)}, bf16[24,1920]{1,0:T(8,128)(2,1)S(1)}, u32[]{:S(2)}, u32[]{:S(2)}) %collective-permute-start.17) | collective-permute-done | bytes 92192 | tf_op jit(solution)/shard_map/ppermute | solution.py:31
  56.1 1.4 %collective-permute-start.18 = (bf16[2,8,1920]{2,1,0:T(8,128)(2,1)S(1)}, bf16[2,8,1920]{2,1,0:T(8,128)(2,1)S(1)}, u32[]{:S(2)}, u32[]{:S(2)}) collective-permute-start(bf16[2,8,1920]{2,1,0:T(8,128)(2,1)S(1)} %get-tuple-element.40), channel_id=1, source_target_pairs={{0,4},{1,5},{2,6},{3,7},{4,0},{5,1},{6,2},{7,3},{8,12},{9,13},{10,... | collective-permute-start | bytes 184328 | tf_op jit(solution)/shard_map/ppermute | solution.py:25
  57.5 1.5 %collective-permute-start.19 = (bf16[2,8,1920]{2,1,0:T(8,128)(2,1)S(1)}, bf16[2,8,1920]{2,1,0:T(8,128)(2,1)S(1)}, u32[]{:S(2)}, u32[]{:S(2)}) collective-permute-start(bf16[2,8,1920]{2,1,0:T(8,128)(2,1)S(1)} %get-tuple-element.41), channel_id=1, source_target_pairs={{0,8},{1,9},{2,10},{3,11},{4,12},{5,13},{6,14},{7,15},{8,0},{9,1},... | collective-permute-start | bytes 184328 | tf_op jit(solution)/shard_map/ppermute | solution.py:25
  59.0 1.6 %collective-permute-start.20 = (bf16[2,8,1920]{2,1,0:T(8,128)(2,1)S(1)}, bf16[2,8,1920]{2,1,0:T(8,128)(2,1)S(1)}, u32[]{:S(2)}, u32[]{:S(2)}) collective-permute-start(bf16[2,8,1920]{2,1,0:T(8,128)(2,1)S(1)} %get-tuple-element.42), channel_id=1, source_target_pairs={{0,12},{1,13},{2,14},{3,15},{4,8},{5,9},{6,10},{7,11},{8,4},{9,5},... | collective-permute-start | bytes 184328 | tf_op jit(solution)/shard_map/ppermute | solution.py:25
  60.6 2.8 %weight_grads.1 = (bf16[1792,512]{1,0:T(8,128)(2,1)}, bf16[1792,512]{1,0:T(8,128)(2,1)}, bf16[1792,512]{1,0:T(8,128)(2,1)}) custom-call(bf16[1792,192]{1,0:T(8,128)(2,1)S(1)} %flip.2.refs_22_.tok_ref, bf16[1792,192]{1,0:T(8,128)(2,1)S(1)} %flip.3.refs_23_.cot_ref, bf16[192,512]{1,0:T(8,128)(2,1)S(1)} %get-tuple-element.45.d_gate, ...), custom_call_target="tpu_custom_call" | custom-call | tf_op jit(solution)/shard_map/weight_grads/pallas_call | solution.py:398
  64.0 1.1 %collective-permute-done.20.refs_3_ = bf16[2,8,1920]{2,1,0:T(8,128)(2,1)S(1)} collective-permute-done((bf16[2,8,1920]{2,1,0:T(8,128)(2,1)S(1)}, bf16[2,8,1920]{2,1,0:T(8,128)(2,1)S(1)}, u32[]{:S(2)}, u32[]{:S(2)}) %collective-permute-start.20) | collective-permute-done | bytes 61472 | tf_op jit(solution)/shard_map/ppermute | solution.py:25
  65.1 1.4 %owner.1 = (bf16[2,4,3584]{2,1,0:T(4,128)(2,1)}, f32[2,2,4]{2,1,0:T(2,128)}) custom-call(s32[2]{0:T(128)S(1)} %pad_add_fusion.where_ref, f32[2,8,256]{2,1,0:T(8,128)S(1)} %get-tuple-element.28.place_ref, bf16[2,8,1920]{2,1,0:T(8,128)(2,1)S(1)} %get-tuple-element.39.refs_0_, bf16[2,8,1920]{2,1,0:T(8,128)(2,1)S(1)} %collective-permute-done.18.refs_1_, ...), custom_call_target="tpu_custom_call" | custom-call | tf_op jit(solution)/shard_map/owner/pallas_call | solution.py:411
  (67 shorter events, 9.5 us)
Async XLA Ops:
  0.6 24.3 %copy-start = (bf16[1792,512]{1,0:T(8,128)(2,1)S(1)}, bf16[1792,512]{1,0:T(8,128)(2,1)}, u32[]{:S(2)}) copy-start(bf16[1792,512]{1,0:T(8,128)(2,1)} %param.13) | copy-start | bytes 5505028
  3.3 5.2 %collective-permute-start = (bf16[16,1920]{1,0:T(8,128)(2,1)S(1)}, bf16[16,1920]{1,0:T(8,128)(2,1)S(1)}, u32[]{:S(2)}, u32[]{:S(2)}) collective-permute-start(bf16[16,1920]{1,0:T(8,128)(2,1)S(1)} %get-tuple-element.60), channel_id=1, source_target_pairs={{0,16},{16,0},{1,17},{17,1},{2,18},{18,2},{3,19},{19,3},{4,20},{20... | collective-permute-start | bytes 184328 | tf_op jit(solution)/shard_map/ppermute | solution.py:25
  6.3 16.5 %copy-start.2 = (bf16[1792,512]{1,0:T(8,128)(2,1)S(1)}, bf16[1792,512]{1,0:T(8,128)(2,1)}, u32[]{:S(2)}) copy-start(bf16[1792,512]{1,0:T(8,128)(2,1)} %refs_21_.1) | copy-start | bytes 5505028
  9.6 5.6 %collective-permute-start.1 = (bf16[24,1920]{1,0:T(8,128)(2,1)S(1)}, bf16[24,1920]{1,0:T(8,128)(2,1)S(1)}, u32[]{:S(2)}, u32[]{:S(2)}) collective-permute-start(bf16[24,1920]{1,0:T(8,128)(2,1)S(1)} %get-tuple-element.30), channel_id=1, source_target_pairs={{0,4},{1,5},{2,6},{3,7},{4,0},{5,1},{6,2},{7,3},{8,12},{9,13},{10,... | collective-permute-start | bytes 276488 | tf_op jit(solution)/shard_map/ppermute | solution.py:25
  11.8 7.8 %collective-permute-start.7 = (bf16[24,1920]{1,0:T(8,128)(2,1)S(1)}, bf16[24,1920]{1,0:T(8,128)(2,1)S(1)}, u32[]{:S(2)}, u32[]{:S(2)}) collective-permute-start(bf16[24,1920]{1,0:T(8,128)(2,1)S(1)} %get-tuple-element.31), channel_id=1, source_target_pairs={{0,8},{1,9},{2,10},{3,11},{4,12},{5,13},{6,14},{7,15},{8,0},{9,1},... | collective-permute-start | bytes 276488 | tf_op jit(solution)/shard_map/ppermute | solution.py:25
  14.4 6.5 %collective-permute-start.8 = (bf16[24,1920]{1,0:T(8,128)(2,1)S(1)}, bf16[24,1920]{1,0:T(8,128)(2,1)S(1)}, u32[]{:S(2)}, u32[]{:S(2)}) collective-permute-start(bf16[24,1920]{1,0:T(8,128)(2,1)S(1)} %get-tuple-element.32), channel_id=1, source_target_pairs={{0,12},{1,13},{2,14},{3,15},{4,8},{5,9},{6,10},{7,11},{8,4},{9,5},... | collective-permute-start | bytes 276488 | tf_op jit(solution)/shard_map/ppermute | solution.py:25
  15.3 8.0 %copy-start.1 = (bf16[1792,512]{1,0:T(8,128)(2,1)S(1)}, bf16[1792,512]{1,0:T(8,128)(2,1)}, u32[]{:S(2)}) copy-start(bf16[1792,512]{1,0:T(8,128)(2,1)} %refs_20_.1) | copy-start | bytes 5505028
  20.9 1.8 %collective-permute-start.9 = (bf16[2,24,1920]{2,1,0:T(8,128)(2,1)S(1)}, bf16[2,24,1920]{2,1,0:T(8,128)(2,1)S(1)}, u32[]{:S(2)}, u32[]{:S(2)}) collective-permute-start(bf16[2,24,1920]{2,1,0:T(8,128)(2,1)S(1)} %join.3.refs_0_), channel_id=1, source_target_pairs={{0,1},{1,0},{2,3},{3,2},{4,5},{5,4},{6,7},{7,6},{8,9},{9,8},{10,11... | collective-permute-start | bytes 552968 | tf_op jit(solution)/shard_map/ppermute | solution.py:25
  21.0 7.1 %collective-permute-start.4 = (bf16[2,24,1920]{2,1,0:T(8,128)(2,1)S(1)}, bf16[2,24,1920]{2,1,0:T(8,128)(2,1)S(1)}, u32[]{:S(2)}, u32[]{:S(2)}) collective-permute-start(bf16[2,24,1920]{2,1,0:T(8,128)(2,1)S(1)} %join.2.refs_2_), channel_id=1, source_target_pairs={{0,2},{1,3},{2,0},{3,1},{4,6},{5,7},{6,4},{7,5},{8,10},{9,11},{10,... | collective-permute-start | bytes 552968 | tf_op jit(solution)/shard_map/ppermute | solution.py:25
  22.6 1.4 %collective-permute-start.2 = (bf16[2,24,1920]{2,1,0:T(8,128)(2,1)S(1)}, bf16[2,24,1920]{2,1,0:T(8,128)(2,1)S(1)}, u32[]{:S(2)}, u32[]{:S(2)}) collective-permute-start(bf16[2,24,1920]{2,1,0:T(8,128)(2,1)S(1)} %join.2.refs_2_), channel_id=1, source_target_pairs={{0,1},{1,0},{2,3},{3,2},{4,5},{5,4},{6,7},{7,6},{8,9},{9,8},{10,11... | collective-permute-start | bytes 552968 | tf_op jit(solution)/shard_map/ppermute | solution.py:25
  25.4 14.7 %collective-permute-start.10 = (bf16[3,48,512]{2,1,0:T(8,128)(2,1)S(1)}, bf16[3,48,512]{2,1,0:T(8,128)(2,1)S(1)}, u32[]{:S(2)}, u32[]{:S(2)}) collective-permute-start(bf16[3,48,512]{2,1,0:T(8,128)(2,1)S(1)} %pad_maximum_fusion.4), channel_id=1, source_target_pairs={{0,16},{16,0},{1,17},{17,1},{2,18},{18,2},{3,19},{19,3},{4,20},{20... | collective-permute-start | bytes 442376 | tf_op jit(solution)/shard_map/ppermute | solution.py:25
  28.1 7.0 %collective-permute-start.11 = (bf16[2,24,1920]{2,1,0:T(8,128)(2,1)S(1)}, bf16[2,24,1920]{2,1,0:T(8,128)(2,1)S(1)}, u32[]{:S(2)}, u32[]{:S(2)}) collective-permute-start(bf16[2,24,1920]{2,1,0:T(8,128)(2,1)S(1)} %tie.1), channel_id=1, source_target_pairs={{0,2},{1,3},{2,0},{3,1},{4,6},{5,7},{6,4},{7,5},{8,10},{9,11},{10,... | collective-permute-start | bytes 552968 | tf_op jit(solution)/shard_map/ppermute | solution.py:25
  30.1 10.0 %collective-permute-start.3 = (bf16[3,48,512]{2,1,0:T(8,128)(2,1)S(1)}, bf16[3,48,512]{2,1,0:T(8,128)(2,1)S(1)}, u32[]{:S(2)}, u32[]{:S(2)}) collective-permute-start(bf16[3,48,512]{2,1,0:T(8,128)(2,1)S(1)} %pad_maximum_fusion.2), channel_id=1, source_target_pairs={{0,16},{16,0},{1,17},{17,1},{2,18},{18,2},{3,19},{19,3},{4,20},{20... | collective-permute-start | bytes 442376 | tf_op jit(solution)/shard_map/ppermute | solution.py:25
  31.6 1.4 %collective-permute-start.5 = (bf16[2,24,1920]{2,1,0:T(8,128)(2,1)S(1)}, bf16[2,24,1920]{2,1,0:T(8,128)(2,1)S(1)}, u32[]{:S(2)}, u32[]{:S(2)}) collective-permute-start(bf16[2,24,1920]{2,1,0:T(8,128)(2,1)S(1)} %collective-permute-done.4.refs_1_), channel_id=1, source_target_pairs={{0,1},{1,0},{2,3},{3,2},{4,5},{5,4},{6,7},{7,6},{8,9},{9,8},{10,11... | collective-permute-start | bytes 552968 | tf_op jit(solution)/shard_map/ppermute | solution.py:25
  34.4 6.0 %collective-permute-start.6 = (bf16[3,48,512]{2,1,0:T(8,128)(2,1)S(1)}, bf16[3,48,512]{2,1,0:T(8,128)(2,1)S(1)}, u32[]{:S(2)}, u32[]{:S(2)}) collective-permute-start(bf16[3,48,512]{2,1,0:T(8,128)(2,1)S(1)} %pad_maximum_fusion.3), channel_id=1, source_target_pairs={{0,16},{16,0},{1,17},{17,1},{2,18},{18,2},{3,19},{19,3},{4,20},{20... | collective-permute-start | bytes 442376 | tf_op jit(solution)/shard_map/ppermute | solution.py:25
  35.0 1.4 %collective-permute-start.12 = (bf16[2,24,1920]{2,1,0:T(8,128)(2,1)S(1)}, bf16[2,24,1920]{2,1,0:T(8,128)(2,1)S(1)}, u32[]{:S(2)}, u32[]{:S(2)}) collective-permute-start(bf16[2,24,1920]{2,1,0:T(8,128)(2,1)S(1)} %collective-permute-done.11), channel_id=1, source_target_pairs={{0,1},{1,0},{2,3},{3,2},{4,5},{5,4},{6,7},{7,6},{8,9},{9,8},{10,11... | collective-permute-start | bytes 552968 | tf_op jit(solution)/shard_map/ppermute | solution.py:25
  37.9 6.0 %collective-permute-start.13 = (bf16[3,48,512]{2,1,0:T(8,128)(2,1)S(1)}, bf16[3,48,512]{2,1,0:T(8,128)(2,1)S(1)}, u32[]{:S(2)}, u32[]{:S(2)}) collective-permute-start(bf16[3,48,512]{2,1,0:T(8,128)(2,1)S(1)} %pad_maximum_fusion.5), channel_id=1, source_target_pairs={{0,16},{16,0},{1,17},{17,1},{2,18},{18,2},{3,19},{19,3},{4,20},{20... | collective-permute-start | bytes 442376 | tf_op jit(solution)/shard_map/ppermute | solution.py:25
  46.1 1.8 %collective-permute-start.14 = (bf16[2,2,24,1920]{3,2,1,0:T(8,128)(2,1)S(1)}, bf16[2,2,24,1920]{3,2,1,0:T(8,128)(2,1)S(1)}, u32[]{:S(2)}, u32[]{:S(2)}) collective-permute-start(bf16[2,2,24,1920]{3,2,1,0:T(8,128)(2,1)S(1)} %get-tuple-element.34), channel_id=1, source_target_pairs={{0,1},{1,0},{2,3},{3,2},{4,5},{5,4},{6,7},{7,6},{8,9},{9,8},{10,11... | collective-permute-start | bytes 1105928 | tf_op jit(solution)/shard_map/ppermute | solution.py:25
  48.0 4.8 %collective-permute-start.15 = (bf16[24,1920]{1,0:T(8,128)(2,1)S(1)}, bf16[24,1920]{1,0:T(8,128)(2,1)S(1)}, u32[]{:S(2)}, u32[]{:S(2)}) collective-permute-start(bf16[24,1920]{1,0:T(8,128)(2,1)S(1)} %get-tuple-element.36), channel_id=1, source_target_pairs={{0,2},{1,3},{2,0},{3,1},{4,6},{5,7},{6,4},{7,5},{8,10},{9,11},{10,... | collective-permute-start | bytes 276488 | tf_op jit(solution)/shard_map/ppermute | solution.py:25
  48.8 4.7 %collective-permute-start.16 = (bf16[24,1920]{1,0:T(8,128)(2,1)S(1)}, bf16[24,1920]{1,0:T(8,128)(2,1)S(1)}, u32[]{:S(2)}, u32[]{:S(2)}) collective-permute-start(bf16[24,1920]{1,0:T(8,128)(2,1)S(1)} %get-tuple-element.37), channel_id=1, source_target_pairs={{0,16},{16,0},{1,17},{17,1},{2,18},{18,2},{3,19},{19,3},{4,20},{20... | collective-permute-start | bytes 276488 | tf_op jit(solution)/shard_map/ppermute | solution.py:25
  50.3 5.8 %collective-permute-start.17 = (bf16[24,1920]{1,0:T(8,128)(2,1)S(1)}, bf16[24,1920]{1,0:T(8,128)(2,1)S(1)}, u32[]{:S(2)}, u32[]{:S(2)}) collective-permute-start(bf16[24,1920]{1,0:T(8,128)(2,1)S(1)} %get-tuple-element.38), channel_id=1, source_target_pairs={{0,18},{1,19},{2,16},{3,17},{4,22},{5,23},{6,20},{7,21},{8,26},{9,... | collective-permute-start | bytes 276488 | tf_op jit(solution)/shard_map/ppermute | solution.py:31
  56.1 7.3 %collective-permute-start.18 = (bf16[2,8,1920]{2,1,0:T(8,128)(2,1)S(1)}, bf16[2,8,1920]{2,1,0:T(8,128)(2,1)S(1)}, u32[]{:S(2)}, u32[]{:S(2)}) collective-permute-start(bf16[2,8,1920]{2,1,0:T(8,128)(2,1)S(1)} %get-tuple-element.40), channel_id=1, source_target_pairs={{0,4},{1,5},{2,6},{3,7},{4,0},{5,1},{6,2},{7,3},{8,12},{9,13},{10,... | collective-permute-start | bytes 184328 | tf_op jit(solution)/shard_map/ppermute | solution.py:25
  57.5 6.6 %collective-permute-start.19 = (bf16[2,8,1920]{2,1,0:T(8,128)(2,1)S(1)}, bf16[2,8,1920]{2,1,0:T(8,128)(2,1)S(1)}, u32[]{:S(2)}, u32[]{:S(2)}) collective-permute-start(bf16[2,8,1920]{2,1,0:T(8,128)(2,1)S(1)} %get-tuple-element.41), channel_id=1, source_target_pairs={{0,8},{1,9},{2,10},{3,11},{4,12},{5,13},{6,14},{7,15},{8,0},{9,1},... | collective-permute-start | bytes 184328 | tf_op jit(solution)/shard_map/ppermute | solution.py:25
  59.0 6.1 %collective-permute-start.20 = (bf16[2,8,1920]{2,1,0:T(8,128)(2,1)S(1)}, bf16[2,8,1920]{2,1,0:T(8,128)(2,1)S(1)}, u32[]{:S(2)}, u32[]{:S(2)}) collective-permute-start(bf16[2,8,1920]{2,1,0:T(8,128)(2,1)S(1)} %get-tuple-element.42), channel_id=1, source_target_pairs={{0,12},{1,13},{2,14},{3,15},{4,8},{5,9},{6,10},{7,11},{8,4},{9,5},... | collective-permute-start | bytes 184328 | tf_op jit(solution)/shard_map/ppermute | solution.py:25

commit v4 on v3

--- a/solution.py
+++ b/solution.py
@@ -14,10 +14,10 @@
 PER_GROUP = EXPERTS // GROUPS
 LANES = 128
 ROWS = 8
-PREP_MIB = 56
+PIECES = 3
+JOIN_COST = dict(flops=4_000_000_000, moved=12_000_000)
 f32, bf16, i32 = jnp.float32, jnp.bfloat16, jnp.int32
 ROWS_BY_ROWS = (((0,), (0,)), ((), ()))
-COLUMNS_BY_COLUMNS = (((1,), (1,)), ((), ()))
 shape = jax.ShapeDtypeStruct
 
 
@@ -31,7 +31,8 @@
     return lax.ppermute(x, ("pipe", "expert"), pairs)
 
 
-def prep_kernel(d_part, tok_hbm, cot_hbm, ids_hbm, gate_hbm, out_ref, tok_ref, cot_ref, ids_ref, gate_ref, sems):
+def prep_kernel(d_part, tok_hbm, cot_hbm, ids_hbm, gate_hbm, *refs):
+    out_refs, (tok_ref, cot_ref, ids_ref, gate_ref, sems) = refs[:-5], refs[-5:]
     pairs = ((tok_hbm, tok_ref), (cot_hbm, cot_ref), (ids_hbm, ids_ref), (gate_hbm, gate_ref))
     copies = [pltpu.make_async_copy(src, dst, sems.at[i]) for i, (src, dst) in enumerate(pairs)]
     for copy in copies:
@@ -40,7 +41,7 @@
         copy.wait()
     micro_count, tok_count = tok_ref.shape[:2]
     top_count = ids_ref.shape[1]
-    seg = out_ref.shape[2] - LANES
+    seg = out_refs[0].shape[-1] - LANES
 
     def flat(ref):
         return jnp.concatenate([ref[m].astype(f32) for m in range(micro_count)], 0)
@@ -61,21 +62,24 @@
         blocks.append(block)
     extras = jnp.concatenate(blocks + blocks, 0).astype(bf16)
     both = jnp.concatenate([flat(tok_ref), flat(cot_ref)], 0).astype(bf16)
-    for p in range(out_ref.shape[0]):
-        out_ref[p, :, :d_part] = both[:, p * d_part : (p + 1) * d_part]
+    for p, ref in enumerate(out_refs):
+        ref[:, :d_part] = both[:, p * d_part : (p + 1) * d_part]
         if seg > d_part:
-            out_ref[p, :, d_part:seg] = jnp.zeros((both.shape[0], seg - d_part), bf16)
-        out_ref[p, :, seg:] = extras
-
-
-def pack_kernel(tok_count, top_count, where_ref, rows_ref, *out_refs):
-    slot_refs, place_ref = out_refs[:EXPERTS], out_refs[EXPERTS]
-    pipe_size, both_rows, width = rows_ref.shape
+            ref[:, d_part:seg] = jnp.zeros((both.shape[0], seg - d_part), bf16)
+        ref[:, seg:] = extras
+
+
+def pack_kernel(tok_count, top_count, pipe_size, where_ref, *refs):
+    blocks, slot_refs, place_ref = [ref[...] for ref in refs[:pipe_size]], refs[pipe_size:-1], refs[-1]
+    both_rows, width = blocks[0].shape
     own_rows = both_rows // 2
     total = pipe_size * both_rows
     slot_count = slot_refs[0].shape[0] // 2
     me = where_ref[0]
-    rows = jnp.concatenate([rows_ref[p] for p in range(pipe_size)], 0)
+    if pipe_size == 2:
+        first = where_ref[1] == 0
+        blocks = [jnp.where(first, blocks[0], blocks[1]), jnp.where(first, blocks[1], blocks[0])]
+    rows = jnp.concatenate(blocks, 0)
     extras = rows[:, width - LANES :].astype(f32)
     row = lax.broadcasted_iota(i32, (total, total), 0)
     other = lax.broadcasted_iota(i32, (total, total), 1)
@@ -118,12 +122,12 @@
 
 
 def hidden_kernel(d_part, top_count, pipe_size, where_ref, *refs):
-    pieces = [refs[5 * i : 5 * (i + 1)] for i in range(2 * GROUPS)]
-    w_gate, w_up = refs[10 * GROUPS : 10 * GROUPS + 2]
+    pieces = [refs[5 * i : 5 * (i + 1)] for i in range(PIECES)]
+    w_gate, w_up = refs[5 * PIECES : 5 * PIECES + 2]
     d_gate, d_up, scaled, low_back, high_back = refs[-5:]
     me = where_ref[0].astype(f32)
-    shares = []
-    for i, (info, own_g, own_u, own_b, got) in enumerate(pieces):
+    shares, base = [], 0
+    for info, own_g, own_u, own_b, got in pieces:
         count = own_g.shape[0]
         extras = info[...].astype(f32)
         gate = jnp.zeros((count, 1), f32)
@@ -139,13 +143,13 @@
         hidden = activated * pre_up
         shares.append(jnp.sum(back_proj * hidden, axis=1, keepdims=True))
         d_hidden = gate * back_proj
-        here = slice(i * count, (i + 1) * count)
+        here = slice(base, base + count)
+        base += count
         scaled[here] = (gate * hidden).astype(bf16)
         d_gate[here] = (d_hidden * pre_up * sig * (1.0 + pre_gate * (1.0 - sig))).astype(bf16)
         d_up[here] = (d_hidden * activated).astype(bf16)
-    back = lax.dot_general(
-        d_gate[...], w_gate[...], COLUMNS_BY_COLUMNS, preferred_element_type=f32
-    ) + lax.dot_general(d_up[...], w_up[...], COLUMNS_BY_COLUMNS, preferred_element_type=f32)
+    back = jnp.dot(d_gate[...], w_gate[...], preferred_element_type=f32)
+    back = back + jnp.dot(d_up[...], w_up[...], preferred_element_type=f32)
     share = jnp.concatenate(shares, 0)
     high = share.astype(bf16).astype(f32)
     lane = lax.broadcasted_iota(i32, (share.shape[0], LANES), 1)
@@ -156,7 +160,9 @@
         for member in range(members):
             ref = low_back if member < members // 2 else high_back
             for p in range(pipe_size):
-                starts = [(2 * g + h) * count + (member * pipe_size + p) * used for g in range(GROUPS)]
+                at_p = (member * pipe_size + p) * used
+                between = count + ((2 * member + 1 - h) * pipe_size + p) * used
+                starts = [at_p, between] if h == 0 else [between, 3 * count + at_p]
                 at = member % (members // 2) * pipe_size + (p ^ where_ref[1] if pipe_size == 2 else p)
                 for columns, values in ((slice(0, d_part), back), (slice(d_part, None), tail)):
                     block = jnp.concatenate([values[start : start + used] for start in starts], 0)
@@ -222,6 +228,11 @@
     refs[-1][...] = jnp.concatenate([ref[...] for ref in refs[:-1]], 0).T
 
 
+def flip_weight_kernel(weight_ref, after, out_ref):
+    del after
+    out_ref[...] = weight_ref[...].T
+
+
 def weight_kernel(scale, block, tok_ref, cot_ref, d_gate, d_up, scaled, after, *refs):
     del after
     out_refs, held, sems = refs[:3], refs[3], refs[4]
@@ -283,10 +294,11 @@
     pipe = lax.axis_index("pipe")
     where = jnp.stack([lax.axis_index("expert") // group_size, pipe]).astype(i32)
 
-    send = call(
+    inputs = (tokens, cotangent, jnp.swapaxes(expert_ids, 1, 2), jnp.swapaxes(gate_values, 1, 2))
+    blocks = call(
         functools.partial(prep_kernel, d_part),
-        shape((pipe_size, 2 * own_rows, width), bf16),
-        "hhhh",
+        [shape((2 * own_rows, width), bf16) for _ in range(pipe_size)],
+        "aaaa",
         "prep",
         scratch_shapes=[
             pltpu.VMEM(tokens.shape, bf16),
@@ -295,64 +307,80 @@
             pltpu.VMEM((micro_count, top_count, tok_count), bf16),
             pltpu.SemaphoreType.DMA((4,)),
         ],
-        mib=PREP_MIB,
-    )(tokens, cotangent, jnp.swapaxes(expert_ids, 1, 2), jnp.swapaxes(gate_values, 1, 2))
+    )(*[pltpu.with_memory_space_constraint(x, pltpu.HBM) for x in inputs])
     if pipe_size == 2:
         first = pipe == 0
-        got = swap(jnp.where(first, send[1], send[0]), "pipe", 1)
-        layer_rows = jnp.where(first, jnp.stack([send[0], got]), jnp.stack([got, send[1]]))
+        kept, sent = jnp.where(first, blocks[0], blocks[1]), jnp.where(first, blocks[1], blocks[0])
+        blocks = [kept, swap(sent, "pipe", 1)]
     else:
-        layer_rows = lax.all_to_all(send, "pipe", split_axis=0, concat_axis=0, tiled=True)
+        got = lax.all_to_all(jnp.stack(blocks), "pipe", split_axis=0, concat_axis=0, tiled=True)
+        blocks = [got[p] for p in range(pipe_size)]
     *slots, place = call(
-        functools.partial(pack_kernel, tok_count, top_count),
+        functools.partial(pack_kernel, tok_count, top_count, pipe_size),
         tuple(shape((2 * slot_count, width), bf16) for _ in range(EXPERTS))
         + (shape((pipe_size, own_rows, 2 * LANES), f32),),
-        "sv",
+        "s" + "v" * pipe_size,
         "pack",
-    )(where, layer_rows)
+    )(where, *blocks)
 
     gathered = [slots[0]] + [swap(slots[k], "expert", k * group_size) for k in range(1, EXPERTS)]
-    groups, after = [], ()
-    for g in range(GROUPS):
-        joined = call(
+    joined = [
+        call(
             functools.partial(join_kernel, pipe_size),
             shape((2, PER_GROUP * slot_count, width), bf16),
-            "v" * PER_GROUP + "a" * len(after),
+            "v" * PER_GROUP,
             "join",
-        )(*gathered[g * PER_GROUP : (g + 1) * PER_GROUP], *after)
-        after = (joined,)
-        sent = joined if g == 0 else tie([joined], groups[-1][1])[0]
-        groups.append([joined, swap(sent, "expert", bits[0])])
-    for halves in groups:
-        for h in range(2):
-            for bit in bits[1:]:
-                halves[h] = jnp.concatenate([halves[h], swap(halves[h], "expert", bit)], 1)
-
-    exchanged = []
-    for halves in groups:
-        for rows in halves:
-            tok_rows, cot_rows = rows[0, :, :d_part], rows[1, :, :d_part]
-            own = []
-            for left, weight in ((tok_rows, w_gate), (tok_rows, w_up), (cot_rows, w_down_t)):
-                own.append(jnp.dot(left, weight, preferred_element_type=f32))
-            bit = pipe_size // 2
-            while bit > 1:
-                got = swap(jnp.stack([part.astype(bf16) for part in own]), "pipe", bit)
-                own = [part + got[i].astype(f32) for i, part in enumerate(own)]
-                bit //= 2
-            got = swap(jnp.stack([part.astype(bf16) for part in own]), "pipe", 1)
-            exchanged.append([rows[0, :, width - LANES :], *own, got])
-    count = exchanged[0][0].shape[0]
+            **(JOIN_COST if g else {}),
+        )(*gathered[g * PER_GROUP : (g + 1) * PER_GROUP])
+        for g in range(GROUPS)
+    ]
+
+    def spread(rows):
+        for bit in bits[1:]:
+            rows = jnp.concatenate([rows, swap(rows, "expert", bit)], 1)
+        return rows
+
+    def project(rows):
+        tok_rows, cot_rows = rows[0, :, :d_part], rows[1, :, :d_part]
+        own = []
+        for left, weight in ((tok_rows, w_gate), (tok_rows, w_up), (cot_rows, w_down_t)):
+            own.append(jnp.dot(left, weight, preferred_element_type=f32))
+        return own
+
+    def exchange(rows, own):
+        bit = pipe_size // 2
+        while bit > 1:
+            got = swap(jnp.stack([part.astype(bf16) for part in own]), "pipe", bit)
+            own = [part + got[i].astype(f32) for i, part in enumerate(own)]
+            bit //= 2
+        got = swap(jnp.stack([part.astype(bf16) for part in own]), "pipe", 1)
+        return [rows[0, :, width - LANES :], *own, got]
+
+    there = swap(joined[0], "expert", bits[0])
+    later = tie([joined[1]], there)[0]
+    later_there = swap(later, "expert", bits[0])
+    first = spread(joined[0])
+    first_own = project(first)
+    middle = spread(jnp.concatenate([there, later], 1))
+    middle_own = project(middle)
+    last = spread(tie([later_there], middle_own[2])[0])
+    pieces, owns = [first, middle, last], [first_own, middle_own, project(last)]
+    exchanged = [exchange(rows, own) for rows, own in zip(pieces, owns)]
+    total = sum(piece[0].shape[0] for piece in exchanged)
 
     flipped = [
-        call(flip_kernel, shape((d_part, 2 * GROUPS * count), bf16), "v" * (2 * GROUPS), "flip", mib=24)(
-            *[rows[a, :, :d_part] for halves in groups for rows in halves]
+        call(flip_kernel, shape((d_part, total), bf16), "v" * len(pieces), "flip", mib=24)(
+            *[rows[a, :, :d_part] for rows in pieces]
         )
         for a in range(2)
     ]
 
+    flipped_weights = [
+        call(flip_weight_kernel, shape((f_part, d_part), bf16), "va", "flip_weight", mib=24)(w, exchanged[-1][3])
+        for w in (w_gate, w_up)
+    ]
+
     out_width = d_part + LANES
-    total = 2 * GROUPS * count
     padded = EXPERTS * slots_here
     half_shape = shape((2, group_size // 4 * pipe_size, padded, out_width), bf16)
     moved = total * (f_part * 24 + d_part * 8) + 4 * d_part * f_part
@@ -363,7 +391,7 @@
         "s" + "v" * (len(operands) + 2) + "a" * len(flipped),
         "hidden",
         mib=min(52, 8 + 2 * moved // (1 << 20)),
-    )(where, *operands, w_gate, w_up, *flipped)
+    )(where, *operands, *flipped_weights, *flipped)
     piece_shapes = [shape((pipe_size, ROWS, out_width), bf16) for _ in range(EXPERTS)]
     if pipe_size == 2 and group_size == 4:
         parts = call(fold_kernel, [shape((padded, out_width), bf16) for _ in range(4)], "vv", "fold")(
@@ -373,7 +401,7 @@
         got_both = swap_both(parts[3], bits[0])
         got_member = swap(parts[2], "expert", bits[0])
         got_pipe = swap(parts[1], "pipe", 1)
-        pieces = call(functools.partial(fold_pairs_kernel, slots_here), piece_shapes, "vvvv", "fold_pairs")(
+        contributions = call(functools.partial(fold_pairs_kernel, slots_here), piece_shapes, "vvvv", "fold_pairs")(
             parts[0], got_member, got_pipe, got_both
         )
     else:
@@ -386,11 +414,11 @@
             sums = jnp.stack([sums[0], swap(sums[1], "pipe", 1)])
         else:
             sums = lax.all_to_all(sums, "pipe", split_axis=0, concat_axis=0, tiled=True)
-        pieces = [
+        contributions = [
             jnp.pad(sums[:, k * slots_here : (k + 1) * slots_here], ((0, 0), (0, ROWS - slots_here), (0, 0)))
             for k in range(EXPERTS)
         ]
-    pieces = [swap(piece, "expert", k * group_size) if k else piece for k, piece in enumerate(pieces)]
+    contributions = [swap(x, "expert", k * group_size) if k else x for k, x in enumerate(contributions)]
 
     tokens_total = own_rows * pipe_size * expert_size
     scale = 1.0 / math.sqrt(tokens_total * top_count / EXPERTS)
@@ -413,7 +441,7 @@
         (shape(tokens.shape, bf16), shape((micro_count, top_count, tok_count), f32)),
         "sv" + "v" * EXPERTS,
         "owner",
-    )(where, place, *pieces)
+    )(where, place, *contributions)
     return (d_tokens, jnp.swapaxes(gate_grads, 1, 2), dw_gate, dw_up, dw_down_t)
 
 

time: 66.7 us -> 61.9 us (0.928)
  waiting for transfers between devices: 24.5 us -> 22 us
  matrix products: 4.98 us -> 3.76 us
  other arithmetic: 1.25 us -> 0.44 us
    ppermute x20 -> x18, waiting for transfers between devices: 21.9 us -> 20 us  [swap(): lax.ppermute(x, axis, [(i, i ^ bit) for i in range(lax.axis_size(axis))])]
    dot_general x12 -> x9, matrix products: 4.98 us -> 3.76 us  [project(): own.append(jnp.dot(left, weight, preferred_element_type=f32))]
    slice x1 -> x0, other arithmetic: 0.88 us -> none  [on_device(): got = swap(jnp.where(first, send[1], send[0]), 'pipe', 1)]
    pallas_call x4 -> x6, Pallas kernels: 3.45 us -> 3.85 us  [the longest x1 1.11 us: on_device(): call(functools.partial(pack_kernel, tok_count, top_count, pipe_size), tup...]
    ppermute x20 -> x18, starting transfers between devices: 23.2 us -> 23.4 us  [swap(): lax.ppermute(x, axis, [(i, i ^ bit) for i in range(lax.axis_size(axis))])]
  transfers between devices with their start and end apart: 21 -> 19, of which waited for: 16 -> 12; matrix products, arithmetic and copies ran while one was open for 8% -> 7% of each run, Pallas kernels for 5% -> 7%
where the time goes in v4:
time: 61.9 us; the launch traced here: 61.8 us
  starting transfers between devices  24.4 us (39%)
  waiting for transfers between devices  22 us (36%)
  Pallas kernels  10.2 us (16%)
  matrix products  3.76 us (6%)
  between operations  0.96 us (2%)
    ppermute x18, starting transfers between devices, swap(): lax.ppermute(x, axis, [(i, i ^ bit) for i in range(lax.axis_size(axis))])  23.4 us
    ppermute x18, waiting for transfers between devices, swap(): lax.ppermute(x, axis, [(i, i ^ bit) for i in range(lax.axis_size(axis))])  20 us
    dot_general x9, matrix products, project(): own.append(jnp.dot(left, weight, preferred_element_type=f32))  3.76 us
    pallas_call x1, Pallas kernels, on_device(): call(functools.partial(weight_kernel, scale, block), [shape((d_part, f_pa...  2.8 us
    ppermute x1, waiting for transfers between devices, swap_both(): return lax.ppermute(x, ('pipe', 'expert'), pairs)  1.97 us
    pallas_call x1, Pallas kernels, on_device(): call(functools.partial(hidden_kernel, d_part, top_count, pipe_size), (sha...  1.88 us
    pallas_call x1, Pallas kernels, on_device(): call(functools.partial(owner_kernel, d_part), (shape(tokens.shape, bf16),...  1.37 us
  transfers between devices with their start and end apart: 19, of which 12 were waited for; matrix products, arithmetic and copies ran while one was open for 7% of the time, Pallas kernels for 7%

profile of v4, /device:TPU:0, one launch (start us, length us, event | category | flops | bytes accessed | tf_op | source)
XLA Modules:
  0.0 61.8 jit_solution(14627935892460753036)
XLA Ops:
  0.7 1.1 %prep.1 = (bf16[16,1920]{1,0:T(8,128)(2,1)S(1)}, bf16[16,1920]{1,0:T(8,128)(2,1)S(1)}) custom-call(bf16[2,4,3584]{2,1,0:T(4,128)(2,1)} %tok_hbm.1, bf16[2,4,3584]{2,1,0:T(4,128)(2,1)} %cot_hbm.1, s32[2,2,4]{2,1,0:T(2,128)} %bitcast.59, bf16[2,2,4]{2,1,0:T(2,128)(2,1)} %bitcast.60), custom_call_target="tpu_custom_call" | custom-call | tf_op jit(solution)/shard_map/prep/pallas_call | solution.py:298
  1.8 3.0 %collective-permute-start = (bf16[16,1920]{1,0:T(8,128)(2,1)S(1)}, bf16[16,1920]{1,0:T(8,128)(2,1)S(1)}, u32[]{:S(2)}, u32[]{:S(2)}) collective-permute-start(bf16[16,1920]{1,0:T(8,128)(2,1)S(1)} %get-tuple-element.61), channel_id=1, source_target_pairs={{0,16},{16,0},{1,17},{17,1},{2,18},{18,2},{3,19},{19,3},{4,20},{20... | collective-permute-start | bytes 184328 | tf_op jit(solution)/shard_map/ppermute | solution.py:25
  4.9 2.1 %collective-permute-done.refs_1_ = bf16[16,1920]{1,0:T(8,128)(2,1)S(1)} collective-permute-done((bf16[16,1920]{1,0:T(8,128)(2,1)S(1)}, bf16[16,1920]{1,0:T(8,128)(2,1)S(1)}, u32[]{:S(2)}, u32[]{:S(2)}) %collective-permute-start) | collective-permute-done | bytes 61472 | tf_op jit(solution)/shard_map/ppermute | solution.py:25
  7.0 1.1 %pack.1 = (bf16[24,1920]{1,0:T(8,128)(2,1)S(1)}, bf16[24,1920]{1,0:T(8,128)(2,1)S(1)}, bf16[24,1920]{1,0:T(8,128)(2,1)S(1)}, bf16[24,1920]{1,0:T(8,128)(2,1)S(1)}, f32[2,8,256]{2,1,0:T(8,128)S(1)}) custom-call(s32[2]{0:T(128)S(1)} %pad_add_fusion.where_ref, bf16[16,1920]{1,0:T(8,128)(2,1)S(1)} %get-tuple-element.62.refs_0_, ...), custom_call_target="tpu_custom_call" | custom-call | tf_op jit(solution)/shard_map/pack/pallas_call | solution.py:318
  8.1 2.2 %collective-permute-start.1 = (bf16[24,1920]{1,0:T(8,128)(2,1)S(1)}, bf16[24,1920]{1,0:T(8,128)(2,1)S(1)}, u32[]{:S(2)}, u32[]{:S(2)}) collective-permute-start(bf16[24,1920]{1,0:T(8,128)(2,1)S(1)} %get-tuple-element.34), channel_id=1, source_target_pairs={{0,4},{1,5},{2,6},{3,7},{4,0},{5,1},{6,2},{7,3},{8,12},{9,13},{10,... | collective-permute-start | bytes 276488 | tf_op jit(solution)/shard_map/ppermute | solution.py:25
  10.3 2.6 %collective-permute-start.5 = (bf16[24,1920]{1,0:T(8,128)(2,1)S(1)}, bf16[24,1920]{1,0:T(8,128)(2,1)S(1)}, u32[]{:S(2)}, u32[]{:S(2)}) collective-permute-start(bf16[24,1920]{1,0:T(8,128)(2,1)S(1)} %get-tuple-element.35), channel_id=1, source_target_pairs={{0,8},{1,9},{2,10},{3,11},{4,12},{5,13},{6,14},{7,15},{8,0},{9,1},... | collective-permute-start | bytes 276488 | tf_op jit(solution)/shard_map/ppermute | solution.py:25
  12.9 0.9 %collective-permute-done.1.refs_1_ = bf16[24,1920]{1,0:T(8,128)(2,1)S(1)} collective-permute-done((bf16[24,1920]{1,0:T(8,128)(2,1)S(1)}, bf16[24,1920]{1,0:T(8,128)(2,1)S(1)}, u32[]{:S(2)}, u32[]{:S(2)}) %collective-permute-start.1) | collective-permute-done | bytes 92192 | tf_op jit(solution)/shard_map/ppermute | solution.py:25
  13.8 1.9 %collective-permute-start.4 = (bf16[2,24,1920]{2,1,0:T(8,128)(2,1)S(1)}, bf16[2,24,1920]{2,1,0:T(8,128)(2,1)S(1)}, u32[]{:S(2)}, u32[]{:S(2)}) collective-permute-start(bf16[2,24,1920]{2,1,0:T(8,128)(2,1)S(1)} %join.2), channel_id=1, source_target_pairs={{0,2},{1,3},{2,0},{3,1},{4,6},{5,7},{6,4},{7,5},{8,10},{9,11},{10,... | collective-permute-start | bytes 552968 | tf_op jit(solution)/shard_map/ppermute | solution.py:25
  15.8 2.3 %collective-permute-done.5.refs_0_ = bf16[24,1920]{1,0:T(8,128)(2,1)S(1)} collective-permute-done((bf16[24,1920]{1,0:T(8,128)(2,1)S(1)}, bf16[24,1920]{1,0:T(8,128)(2,1)S(1)}, u32[]{:S(2)}, u32[]{:S(2)}) %collective-permute-start.5) | collective-permute-done | bytes 92192 | tf_op jit(solution)/shard_map/ppermute | solution.py:25
  18.1 1.2 %collective-permute-done.6.refs_1_ = bf16[24,1920]{1,0:T(8,128)(2,1)S(1)} collective-permute-done((bf16[24,1920]{1,0:T(8,128)(2,1)S(1)}, bf16[24,1920]{1,0:T(8,128)(2,1)S(1)}, u32[]{:S(2)}, u32[]{:S(2)}) %collective-permute-start.6) | collective-permute-done | bytes 92192 | tf_op jit(solution)/shard_map/ppermute | solution.py:25
  19.4 1.9 %collective-permute-start.9 = (bf16[2,24,1920]{2,1,0:T(8,128)(2,1)S(1)}, bf16[2,24,1920]{2,1,0:T(8,128)(2,1)S(1)}, u32[]{:S(2)}, u32[]{:S(2)}) collective-permute-start(bf16[2,24,1920]{2,1,0:T(8,128)(2,1)S(1)} %tie.2), channel_id=1, source_target_pairs={{0,2},{1,3},{2,0},{3,1},{4,6},{5,7},{6,4},{7,5},{8,10},{9,11},{10,... | collective-permute-start | bytes 552968 | tf_op jit(solution)/shard_map/ppermute | solution.py:25
  22.8 1.6 %collective-permute-start.3 = (bf16[3,48,512]{2,1,0:T(8,128)(2,1)S(1)}, bf16[3,48,512]{2,1,0:T(8,128)(2,1)S(1)}, u32[]{:S(2)}, u32[]{:S(2)}) collective-permute-start(bf16[3,48,512]{2,1,0:T(8,128)(2,1)S(1)} %pad_maximum_fusion.6), channel_id=1, source_target_pairs={{0,16},{16,0},{1,17},{17,1},{2,18},{18,2},{3,19},{19,3},{4,20},{20... | collective-permute-start | bytes 442376 | tf_op jit(solution)/shard_map/ppermute | solution.py:25
  26.1 1.1 %collective-permute-start.8 = (bf16[3,96,512]{2,1,0:T(8,128)(2,1)S(1)}, bf16[3,96,512]{2,1,0:T(8,128)(2,1)S(1)}, u32[]{:S(2)}, u32[]{:S(2)}) collective-permute-start(bf16[3,96,512]{2,1,0:T(8,128)(2,1)S(1)} %pad_maximum_fusion.3), channel_id=1, source_target_pairs={{0,16},{16,0},{1,17},{17,1},{2,18},{18,2},{3,19},{19,3},{4,20},{20... | collective-permute-start | bytes 884744 | tf_op jit(solution)/shard_map/ppermute | solution.py:25
  28.6 1.2 %collective-permute-start.11 = (bf16[3,48,512]{2,1,0:T(8,128)(2,1)S(1)}, bf16[3,48,512]{2,1,0:T(8,128)(2,1)S(1)}, u32[]{:S(2)}, u32[]{:S(2)}) collective-permute-start(bf16[3,48,512]{2,1,0:T(8,128)(2,1)S(1)} %pad_maximum_fusion.7), channel_id=1, source_target_pairs={{0,16},{16,0},{1,17},{17,1},{2,18},{18,2},{3,19},{19,3},{4,20},{20... | collective-permute-start | bytes 442376 | tf_op jit(solution)/shard_map/ppermute | solution.py:25
  30.9 0.5 flip_weight.2.refs_15_
  31.4 4.6 %collective-permute-done.8.refs_9_ = bf16[3,96,512]{2,1,0:T(8,128)(2,1)S(1)} collective-permute-done((bf16[3,96,512]{2,1,0:T(8,128)(2,1)S(1)}, bf16[3,96,512]{2,1,0:T(8,128)(2,1)S(1)}, u32[]{:S(2)}, u32[]{:S(2)}) %collective-permute-start.8) | collective-permute-done | bytes 294944 | tf_op jit(solution)/shard_map/ppermute | solution.py:25
  36.0 2.6 %collective-permute-done.11.refs_14_ = bf16[3,48,512]{2,1,0:T(8,128)(2,1)S(1)} collective-permute-done((bf16[3,48,512]{2,1,0:T(8,128)(2,1)S(1)}, bf16[3,48,512]{2,1,0:T(8,128)(2,1)S(1)}, u32[]{:S(2)}, u32[]{:S(2)}) %collective-permute-start.11) | collective-permute-done | bytes 147488 | tf_op jit(solution)/shard_map/ppermute | solution.py:25
  38.6 1.9 %hidden.1 = (bf16[192,512]{1,0:T(8,128)(2,1)S(1)}, bf16[192,512]{1,0:T(8,128)(2,1)S(1)}, bf16[192,512]{1,0:T(8,128)(2,1)S(1)}, bf16[2,2,24,1920]{3,2,1,0:T(8,128)(2,1)S(1)}, bf16[2,2,24,1920]{3,2,1,0:T(8,128)(2,1)S(1)}) custom-call(s32[2]{0:T(128)S(1)} %pad_add_fusion.where_ref, bf16[48,128]{1,0:T(8,128)(2,1)S(1)} %maximum_bitcast_fusion.5.refs_0_, ...), custom_call_target="tpu_custom_call" | custom-call | tf_op jit(solution)/shard_map/hidden/pallas_call | solution.py:388
  40.6 1.7 %collective-permute-done.12.b_ref = bf16[2,2,24,1920]{3,2,1,0:T(8,128)(2,1)S(1)} collective-permute-done((bf16[2,2,24,1920]{3,2,1,0:T(8,128)(2,1)S(1)}, bf16[2,2,24,1920]{3,2,1,0:T(8,128)(2,1)S(1)}, u32[]{:S(2)}, u32[]{:S(2)}) %collective-permute-start.12) | collective-permute-done | bytes 368672 | tf_op jit(solution)/shard_map/ppermute | solution.py:25
  42.3 1.1 %collective-permute-start.13 = (bf16[24,1920]{1,0:T(8,128)(2,1)S(1)}, bf16[24,1920]{1,0:T(8,128)(2,1)S(1)}, u32[]{:S(2)}, u32[]{:S(2)}) collective-permute-start(bf16[24,1920]{1,0:T(8,128)(2,1)S(1)} %get-tuple-element.40), channel_id=1, source_target_pairs={{0,2},{1,3},{2,0},{3,1},{4,6},{5,7},{6,4},{7,5},{8,10},{9,11},{10,... | collective-permute-start | bytes 276488 | tf_op jit(solution)/shard_map/ppermute | solution.py:25
  43.4 1.5 %collective-permute-start.14 = (bf16[24,1920]{1,0:T(8,128)(2,1)S(1)}, bf16[24,1920]{1,0:T(8,128)(2,1)S(1)}, u32[]{:S(2)}, u32[]{:S(2)}) collective-permute-start(bf16[24,1920]{1,0:T(8,128)(2,1)S(1)} %get-tuple-element.41), channel_id=1, source_target_pairs={{0,16},{16,0},{1,17},{17,1},{2,18},{18,2},{3,19},{19,3},{4,20},{20... | collective-permute-start | bytes 276488 | tf_op jit(solution)/shard_map/ppermute | solution.py:25
  44.9 1.0 %collective-permute-start.15 = (bf16[24,1920]{1,0:T(8,128)(2,1)S(1)}, bf16[24,1920]{1,0:T(8,128)(2,1)S(1)}, u32[]{:S(2)}, u32[]{:S(2)}) collective-permute-start(bf16[24,1920]{1,0:T(8,128)(2,1)S(1)} %get-tuple-element.42), channel_id=1, source_target_pairs={{0,18},{1,19},{2,16},{3,17},{4,22},{5,23},{6,20},{7,21},{8,26},{9,... | collective-permute-start | bytes 276488 | tf_op jit(solution)/shard_map/ppermute | solution.py:31
  45.9 1.2 %collective-permute-done.13.b_ref = bf16[24,1920]{1,0:T(8,128)(2,1)S(1)} collective-permute-done((bf16[24,1920]{1,0:T(8,128)(2,1)S(1)}, bf16[24,1920]{1,0:T(8,128)(2,1)S(1)}, u32[]{:S(2)}, u32[]{:S(2)}) %collective-permute-start.13) | collective-permute-done | bytes 92192 | tf_op jit(solution)/shard_map/ppermute | solution.py:25
  47.1 1.3 %collective-permute-done.14.c_ref = bf16[24,1920]{1,0:T(8,128)(2,1)S(1)} collective-permute-done((bf16[24,1920]{1,0:T(8,128)(2,1)S(1)}, bf16[24,1920]{1,0:T(8,128)(2,1)S(1)}, u32[]{:S(2)}, u32[]{:S(2)}) %collective-permute-start.14) | collective-permute-done | bytes 92192 | tf_op jit(solution)/shard_map/ppermute | solution.py:25
  48.4 2.0 %collective-permute-done.15.d_ref = bf16[24,1920]{1,0:T(8,128)(2,1)S(1)} collective-permute-done((bf16[24,1920]{1,0:T(8,128)(2,1)S(1)}, bf16[24,1920]{1,0:T(8,128)(2,1)S(1)}, u32[]{:S(2)}, u32[]{:S(2)}) %collective-permute-start.15) | collective-permute-done | bytes 92192 | tf_op jit(solution)/shard_map/ppermute | solution.py:31
  50.5 2.6 %collective-permute-start.16 = (bf16[2,8,1920]{2,1,0:T(8,128)(2,1)S(1)}, bf16[2,8,1920]{2,1,0:T(8,128)(2,1)S(1)}, u32[]{:S(2)}, u32[]{:S(2)}) collective-permute-start(bf16[2,8,1920]{2,1,0:T(8,128)(2,1)S(1)} %get-tuple-element.44), channel_id=1, source_target_pairs={{0,4},{1,5},{2,6},{3,7},{4,0},{5,1},{6,2},{7,3},{8,12},{9,13},{10,... | collective-permute-start | bytes 184328 | tf_op jit(solution)/shard_map/ppermute | solution.py:25
  53.1 1.3 %collective-permute-start.17 = (bf16[2,8,1920]{2,1,0:T(8,128)(2,1)S(1)}, bf16[2,8,1920]{2,1,0:T(8,128)(2,1)S(1)}, u32[]{:S(2)}, u32[]{:S(2)}) collective-permute-start(bf16[2,8,1920]{2,1,0:T(8,128)(2,1)S(1)} %get-tuple-element.45), channel_id=1, source_target_pairs={{0,8},{1,9},{2,10},{3,11},{4,12},{5,13},{6,14},{7,15},{8,0},{9,1},... | collective-permute-start | bytes 184328 | tf_op jit(solution)/shard_map/ppermute | solution.py:25
  54.4 1.1 %collective-permute-start.18 = (bf16[2,8,1920]{2,1,0:T(8,128)(2,1)S(1)}, bf16[2,8,1920]{2,1,0:T(8,128)(2,1)S(1)}, u32[]{:S(2)}, u32[]{:S(2)}) collective-permute-start(bf16[2,8,1920]{2,1,0:T(8,128)(2,1)S(1)} %get-tuple-element.46), channel_id=1, source_target_pairs={{0,12},{1,13},{2,14},{3,15},{4,8},{5,9},{6,10},{7,11},{8,4},{9,5},... | collective-permute-start | bytes 184328 | tf_op jit(solution)/shard_map/ppermute | solution.py:25
  55.5 2.8 %weight_grads.1 = (bf16[1792,512]{1,0:T(8,128)(2,1)}, bf16[1792,512]{1,0:T(8,128)(2,1)}, bf16[1792,512]{1,0:T(8,128)(2,1)}) custom-call(bf16[1792,192]{1,0:T(8,128)(2,1)S(1)} %flip.2.refs_17_.tok_ref, bf16[1792,192]{1,0:T(8,128)(2,1)S(1)} %flip.3.refs_18_.cot_ref, bf16[192,512]{1,0:T(8,128)(2,1)S(1)} %get-tuple-element.49.d_gate, ...), custom_call_target="tpu_custom_call" | custom-call | tf_op jit(solution)/shard_map/weight_grads/pallas_call | solution.py:426
  58.4 0.7 %collective-permute-done.17.refs_2_ = bf16[2,8,1920]{2,1,0:T(8,128)(2,1)S(1)} collective-permute-done((bf16[2,8,1920]{2,1,0:T(8,128)(2,1)S(1)}, bf16[2,8,1920]{2,1,0:T(8,128)(2,1)S(1)}, u32[]{:S(2)}, u32[]{:S(2)}) %collective-permute-start.17) | collective-permute-done | bytes 61472 | tf_op jit(solution)/shard_map/ppermute | solution.py:25
  59.0 1.4 %collective-permute-done.18.refs_3_ = bf16[2,8,1920]{2,1,0:T(8,128)(2,1)S(1)} collective-permute-done((bf16[2,8,1920]{2,1,0:T(8,128)(2,1)S(1)}, bf16[2,8,1920]{2,1,0:T(8,128)(2,1)S(1)}, u32[]{:S(2)}, u32[]{:S(2)}) %collective-permute-start.18) | collective-permute-done | bytes 61472 | tf_op jit(solution)/shard_map/ppermute | solution.py:25
  60.4 1.4 %owner.1 = (bf16[2,4,3584]{2,1,0:T(4,128)(2,1)}, f32[2,2,4]{2,1,0:T(2,128)}) custom-call(s32[2]{0:T(128)S(1)} %pad_add_fusion.where_ref, f32[2,8,256]{2,1,0:T(8,128)S(1)} %get-tuple-element.32.place_ref, bf16[2,8,1920]{2,1,0:T(8,128)(2,1)S(1)} %get-tuple-element.43.refs_0_, bf16[2,8,1920]{2,1,0:T(8,128)(2,1)S(1)} %collective-permute-done.16.refs_1_, ...), custom_call_target="tpu_custom_call" | custom-call | tf_op jit(solution)/shard_map/owner/pallas_call | solution.py:439
  (54 shorter events, 6.1 us)
Async XLA Ops:
  0.6 21.7 %copy-start = (bf16[1792,512]{1,0:T(8,128)(2,1)S(1)}, bf16[1792,512]{1,0:T(8,128)(2,1)}, u32[]{:S(2)}) copy-start(bf16[1792,512]{1,0:T(8,128)(2,1)} %param.13) | copy-start | bytes 5505028
  1.8 5.2 %collective-permute-start = (bf16[16,1920]{1,0:T(8,128)(2,1)S(1)}, bf16[16,1920]{1,0:T(8,128)(2,1)S(1)}, u32[]{:S(2)}, u32[]{:S(2)}) collective-permute-start(bf16[16,1920]{1,0:T(8,128)(2,1)S(1)} %get-tuple-element.61), channel_id=1, source_target_pairs={{0,16},{16,0},{1,17},{17,1},{2,18},{18,2},{3,19},{19,3},{4,20},{20... | collective-permute-start | bytes 184328 | tf_op jit(solution)/shard_map/ppermute | solution.py:25
  8.1 5.6 %collective-permute-start.1 = (bf16[24,1920]{1,0:T(8,128)(2,1)S(1)}, bf16[24,1920]{1,0:T(8,128)(2,1)S(1)}, u32[]{:S(2)}, u32[]{:S(2)}) collective-permute-start(bf16[24,1920]{1,0:T(8,128)(2,1)S(1)} %get-tuple-element.34), channel_id=1, source_target_pairs={{0,4},{1,5},{2,6},{3,7},{4,0},{5,1},{6,2},{7,3},{8,12},{9,13},{10,... | collective-permute-start | bytes 276488 | tf_op jit(solution)/shard_map/ppermute | solution.py:25
  10.3 7.8 %collective-permute-start.5 = (bf16[24,1920]{1,0:T(8,128)(2,1)S(1)}, bf16[24,1920]{1,0:T(8,128)(2,1)S(1)}, u32[]{:S(2)}, u32[]{:S(2)}) collective-permute-start(bf16[24,1920]{1,0:T(8,128)(2,1)S(1)} %get-tuple-element.35), channel_id=1, source_target_pairs={{0,8},{1,9},{2,10},{3,11},{4,12},{5,13},{6,14},{7,15},{8,0},{9,1},... | collective-permute-start | bytes 276488 | tf_op jit(solution)/shard_map/ppermute | solution.py:25
  12.9 6.5 %collective-permute-start.6 = (bf16[24,1920]{1,0:T(8,128)(2,1)S(1)}, bf16[24,1920]{1,0:T(8,128)(2,1)S(1)}, u32[]{:S(2)}, u32[]{:S(2)}) collective-permute-start(bf16[24,1920]{1,0:T(8,128)(2,1)S(1)} %get-tuple-element.36), channel_id=1, source_target_pairs={{0,12},{1,13},{2,14},{3,15},{4,8},{5,9},{6,10},{7,11},{8,4},{9,5},... | collective-permute-start | bytes 276488 | tf_op jit(solution)/shard_map/ppermute | solution.py:25
  13.8 7.5 %copy-start.1 = (bf16[1792,512]{1,0:T(8,128)(2,1)S(1)}, bf16[1792,512]{1,0:T(8,128)(2,1)}, u32[]{:S(2)}) copy-start(bf16[1792,512]{1,0:T(8,128)(2,1)} %weight_ref.3) | copy-start | bytes 5505028
  13.8 5.6 %collective-permute-start.4 = (bf16[2,24,1920]{2,1,0:T(8,128)(2,1)S(1)}, bf16[2,24,1920]{2,1,0:T(8,128)(2,1)S(1)}, u32[]{:S(2)}, u32[]{:S(2)}) collective-permute-start(bf16[2,24,1920]{2,1,0:T(8,128)(2,1)S(1)} %join.2), channel_id=1, source_target_pairs={{0,2},{1,3},{2,0},{3,1},{4,6},{5,7},{6,4},{7,5},{8,10},{9,11},{10,... | collective-permute-start | bytes 552968 | tf_op jit(solution)/shard_map/ppermute | solution.py:25
  15.8 5.5 %collective-permute-start.2 = (bf16[2,24,1920]{2,1,0:T(8,128)(2,1)S(1)}, bf16[2,24,1920]{2,1,0:T(8,128)(2,1)S(1)}, u32[]{:S(2)}, u32[]{:S(2)}) collective-permute-start(bf16[2,24,1920]{2,1,0:T(8,128)(2,1)S(1)} %join.2), channel_id=1, source_target_pairs={{0,1},{1,0},{2,3},{3,2},{4,5},{5,4},{6,7},{7,6},{8,9},{9,8},{10,11... | collective-permute-start | bytes 552968 | tf_op jit(solution)/shard_map/ppermute | solution.py:25
  19.4 2.4 %copy-start.2 = (bf16[1792,512]{1,0:T(8,128)(2,1)S(1)}, bf16[1792,512]{1,0:T(8,128)(2,1)}, u32[]{:S(2)}) copy-start(bf16[1792,512]{1,0:T(8,128)(2,1)} %weight_ref.2) | copy-start | bytes 5505028
  19.4 6.3 %collective-permute-start.9 = (bf16[2,24,1920]{2,1,0:T(8,128)(2,1)S(1)}, bf16[2,24,1920]{2,1,0:T(8,128)(2,1)S(1)}, u32[]{:S(2)}, u32[]{:S(2)}) collective-permute-start(bf16[2,24,1920]{2,1,0:T(8,128)(2,1)S(1)} %tie.2), channel_id=1, source_target_pairs={{0,2},{1,3},{2,0},{3,1},{4,6},{5,7},{6,4},{7,5},{8,10},{9,11},{10,... | collective-permute-start | bytes 552968 | tf_op jit(solution)/shard_map/ppermute | solution.py:25
  22.2 2.1 %collective-permute-start.7 = (bf16[2,48,1920]{2,1,0:T(8,128)(2,1)S(1)}, bf16[2,48,1920]{2,1,0:T(8,128)(2,1)S(1)}, u32[]{:S(2)}, u32[]{:S(2)}) collective-permute-start(bf16[2,48,1920]{2,1,0:T(8,128)(2,1)S(1)} %pad_maximum_fusion), channel_id=1, source_target_pairs={{0,1},{1,0},{2,3},{3,2},{4,5},{5,4},{6,7},{7,6},{8,9},{9,8},{10,11... | collective-permute-start | bytes 1105928 | tf_op jit(solution)/shard_map/ppermute | solution.py:25
  22.8 8.6 %collective-permute-start.3 = (bf16[3,48,512]{2,1,0:T(8,128)(2,1)S(1)}, bf16[3,48,512]{2,1,0:T(8,128)(2,1)S(1)}, u32[]{:S(2)}, u32[]{:S(2)}) collective-permute-start(bf16[3,48,512]{2,1,0:T(8,128)(2,1)S(1)} %pad_maximum_fusion.6), channel_id=1, source_target_pairs={{0,16},{16,0},{1,17},{17,1},{2,18},{18,2},{3,19},{19,3},{4,20},{20... | collective-permute-start | bytes 442376 | tf_op jit(solution)/shard_map/ppermute | solution.py:25
  25.7 1.5 %collective-permute-start.10 = (bf16[2,24,1920]{2,1,0:T(8,128)(2,1)S(1)}, bf16[2,24,1920]{2,1,0:T(8,128)(2,1)S(1)}, u32[]{:S(2)}, u32[]{:S(2)}) collective-permute-start(bf16[2,24,1920]{2,1,0:T(8,128)(2,1)S(1)} %tie.3), channel_id=1, source_target_pairs={{0,1},{1,0},{2,3},{3,2},{4,5},{5,4},{6,7},{7,6},{8,9},{9,8},{10,11... | collective-permute-start | bytes 552968 | tf_op jit(solution)/shard_map/ppermute | solution.py:25
  26.1 9.9 %collective-permute-start.8 = (bf16[3,96,512]{2,1,0:T(8,128)(2,1)S(1)}, bf16[3,96,512]{2,1,0:T(8,128)(2,1)S(1)}, u32[]{:S(2)}, u32[]{:S(2)}) collective-permute-start(bf16[3,96,512]{2,1,0:T(8,128)(2,1)S(1)} %pad_maximum_fusion.3), channel_id=1, source_target_pairs={{0,16},{16,0},{1,17},{17,1},{2,18},{18,2},{3,19},{19,3},{4,20},{20... | collective-permute-start | bytes 884744 | tf_op jit(solution)/shard_map/ppermute | solution.py:25
  28.6 10.0 %collective-permute-start.11 = (bf16[3,48,512]{2,1,0:T(8,128)(2,1)S(1)}, bf16[3,48,512]{2,1,0:T(8,128)(2,1)S(1)}, u32[]{:S(2)}, u32[]{:S(2)}) collective-permute-start(bf16[3,48,512]{2,1,0:T(8,128)(2,1)S(1)} %pad_maximum_fusion.7), channel_id=1, source_target_pairs={{0,16},{16,0},{1,17},{17,1},{2,18},{18,2},{3,19},{19,3},{4,20},{20... | collective-permute-start | bytes 442376 | tf_op jit(solution)/shard_map/ppermute | solution.py:25
  40.5 1.8 %collective-permute-start.12 = (bf16[2,2,24,1920]{3,2,1,0:T(8,128)(2,1)S(1)}, bf16[2,2,24,1920]{3,2,1,0:T(8,128)(2,1)S(1)}, u32[]{:S(2)}, u32[]{:S(2)}) collective-permute-start(bf16[2,2,24,1920]{3,2,1,0:T(8,128)(2,1)S(1)} %get-tuple-element.38), channel_id=1, source_target_pairs={{0,1},{1,0},{2,3},{3,2},{4,5},{5,4},{6,7},{7,6},{8,9},{9,8},{10,11... | collective-permute-start | bytes 1105928 | tf_op jit(solution)/shard_map/ppermute | solution.py:25
  42.3 4.8 %collective-permute-start.13 = (bf16[24,1920]{1,0:T(8,128)(2,1)S(1)}, bf16[24,1920]{1,0:T(8,128)(2,1)S(1)}, u32[]{:S(2)}, u32[]{:S(2)}) collective-permute-start(bf16[24,1920]{1,0:T(8,128)(2,1)S(1)} %get-tuple-element.40), channel_id=1, source_target_pairs={{0,2},{1,3},{2,0},{3,1},{4,6},{5,7},{6,4},{7,5},{8,10},{9,11},{10,... | collective-permute-start | bytes 276488 | tf_op jit(solution)/shard_map/ppermute | solution.py:25
  43.4 5.0 %collective-permute-start.14 = (bf16[24,1920]{1,0:T(8,128)(2,1)S(1)}, bf16[24,1920]{1,0:T(8,128)(2,1)S(1)}, u32[]{:S(2)}, u32[]{:S(2)}) collective-permute-start(bf16[24,1920]{1,0:T(8,128)(2,1)S(1)} %get-tuple-element.41), channel_id=1, source_target_pairs={{0,16},{16,0},{1,17},{17,1},{2,18},{18,2},{3,19},{19,3},{4,20},{20... | collective-permute-start | bytes 276488 | tf_op jit(solution)/shard_map/ppermute | solution.py:25
  44.9 5.5 %collective-permute-start.15 = (bf16[24,1920]{1,0:T(8,128)(2,1)S(1)}, bf16[24,1920]{1,0:T(8,128)(2,1)S(1)}, u32[]{:S(2)}, u32[]{:S(2)}) collective-permute-start(bf16[24,1920]{1,0:T(8,128)(2,1)S(1)} %get-tuple-element.42), channel_id=1, source_target_pairs={{0,18},{1,19},{2,16},{3,17},{4,22},{5,23},{6,20},{7,21},{8,26},{9,... | collective-permute-start | bytes 276488 | tf_op jit(solution)/shard_map/ppermute | solution.py:31
  50.5 7.9 %collective-permute-start.16 = (bf16[2,8,1920]{2,1,0:T(8,128)(2,1)S(1)}, bf16[2,8,1920]{2,1,0:T(8,128)(2,1)S(1)}, u32[]{:S(2)}, u32[]{:S(2)}) collective-permute-start(bf16[2,8,1920]{2,1,0:T(8,128)(2,1)S(1)} %get-tuple-element.44), channel_id=1, source_target_pairs={{0,4},{1,5},{2,6},{3,7},{4,0},{5,1},{6,2},{7,3},{8,12},{9,13},{10,... | collective-permute-start | bytes 184328 | tf_op jit(solution)/shard_map/ppermute | solution.py:25
  53.1 5.9 %collective-permute-start.17 = (bf16[2,8,1920]{2,1,0:T(8,128)(2,1)S(1)}, bf16[2,8,1920]{2,1,0:T(8,128)(2,1)S(1)}, u32[]{:S(2)}, u32[]{:S(2)}) collective-permute-start(bf16[2,8,1920]{2,1,0:T(8,128)(2,1)S(1)} %get-tuple-element.45), channel_id=1, source_target_pairs={{0,8},{1,9},{2,10},{3,11},{4,12},{5,13},{6,14},{7,15},{8,0},{9,1},... | collective-permute-start | bytes 184328 | tf_op jit(solution)/shard_map/ppermute | solution.py:25
  54.4 6.0 %collective-permute-start.18 = (bf16[2,8,1920]{2,1,0:T(8,128)(2,1)S(1)}, bf16[2,8,1920]{2,1,0:T(8,128)(2,1)S(1)}, u32[]{:S(2)}, u32[]{:S(2)}) collective-permute-start(bf16[2,8,1920]{2,1,0:T(8,128)(2,1)S(1)} %get-tuple-element.46), channel_id=1, source_target_pairs={{0,12},{1,13},{2,14},{3,15},{4,8},{5,9},{6,10},{7,11},{8,4},{9,5},... | collective-permute-start | bytes 184328 | tf_op jit(solution)/shard_map/ppermute | solution.py:25

commit v5 on v4

--- a/solution.py
+++ b/solution.py
@@ -15,6 +15,8 @@
 LANES = 128
 ROWS = 8
 PIECES = 3
+SQUARE = EXPERTS * ROWS
+RETURN_ORDER = (0, 2, 3, 1)
 JOIN_COST = dict(flops=4_000_000_000, moved=12_000_000)
 f32, bf16, i32 = jnp.float32, jnp.bfloat16, jnp.int32
 ROWS_BY_ROWS = (((0,), (0,)), ((), ()))
@@ -96,14 +98,18 @@
     base = within // own_rows * slot_count + (device * (own_rows // tok_count) + block) * CAP
     lane = lax.broadcasted_iota(i32, (total, EXPERTS * 2 * slot_count), 1).astype(f32)
     chosen = jnp.zeros(lane.shape, f32)
-    small_lane = lax.broadcasted_iota(i32, (total, LANES), 1).astype(f32)
+    small_lane = lax.broadcasted_iota(i32, (total, LANES), 1)
+    used = own_rows // tok_count * CAP
+    per_row = used // (ROWS - used)
     places = jnp.zeros((total, LANES), f32)
     for k in range(EXPERTS):
         here = routed[:, k : k + 1] > 0.0
         target = (k * 2 * slot_count + base).astype(f32) + position[:, k : k + 1]
         chosen = chosen + jnp.where((lane == target) & here, 1.0, 0.0)
-        local = (k * ROWS + block * CAP).astype(f32) + position[:, k : k + 1]
-        places = places + jnp.where((small_lane == local) & here, 1.0, 0.0)
+        local = block * CAP + position[:, k : k + 1].astype(i32)
+        spare = SQUARE * (1 + local % per_row) + k * ROWS + used + local // per_row
+        at_slot = (small_lane == k * ROWS + local) | (small_lane == spare)
+        places = places + jnp.where(at_slot & here, 1.0, 0.0)
     slots = lax.dot_general(chosen.astype(bf16), rows, ROWS_BY_ROWS, preferred_element_type=f32)
     for k in range(EXPERTS):
         slot_refs[k][...] = slots[2 * k * slot_count : 2 * (k + 1) * slot_count].astype(bf16)
@@ -121,52 +127,68 @@
         out_ref[a] = jnp.concatenate([b[s : s + rows] for s in starts for b in blocks], 0).astype(bf16)
 
 
-def hidden_kernel(d_part, top_count, pipe_size, where_ref, *refs):
-    pieces = [refs[5 * i : 5 * (i + 1)] for i in range(PIECES)]
-    w_gate, w_up = refs[5 * PIECES : 5 * PIECES + 2]
-    d_gate, d_up, scaled, low_back, high_back = refs[-5:]
-    me = where_ref[0].astype(f32)
-    shares, base = [], 0
-    for info, own_g, own_u, own_b, got in pieces:
-        count = own_g.shape[0]
-        extras = info[...].astype(f32)
-        gate = jnp.zeros((count, 1), f32)
-        for k in range(top_count):
-            gate = gate + jnp.where(
-                extras[:, k : k + 1] == me, extras[:, top_count + k : top_count + k + 1], 0.0
-            )
-        pre_gate = own_g[...] + got[0].astype(f32)
-        pre_up = own_u[...] + got[1].astype(f32)
-        back_proj = own_b[...] + got[2].astype(f32)
-        sig = jax.nn.sigmoid(pre_gate)
-        activated = pre_gate * sig
-        hidden = activated * pre_up
-        shares.append(jnp.sum(back_proj * hidden, axis=1, keepdims=True))
-        d_hidden = gate * back_proj
-        here = slice(base, base + count)
-        base += count
-        scaled[here] = (gate * hidden).astype(bf16)
-        d_gate[here] = (d_hidden * pre_up * sig * (1.0 + pre_gate * (1.0 - sig))).astype(bf16)
-        d_up[here] = (d_hidden * activated).astype(bf16)
-    back = jnp.dot(d_gate[...], w_gate[...], preferred_element_type=f32)
-    back = back + jnp.dot(d_up[...], w_up[...], preferred_element_type=f32)
-    share = jnp.concatenate(shares, 0)
+def hidden_gradients(top_count, me, info, own_g, own_u, own_b, got):
+    extras = info[...].astype(f32)
+    gate = jnp.zeros((extras.shape[0], 1), f32)
+    for k in range(top_count):
+        gate = gate + jnp.where(extras[:, k : k + 1] == me, extras[:, top_count + k : top_count + k + 1], 0.0)
+    pre_gate = own_g[...] + got[0].astype(f32)
+    pre_up = own_u[...] + got[1].astype(f32)
+    back_proj = own_b[...] + got[2].astype(f32)
+    sig = jax.nn.sigmoid(pre_gate)
+    activated = pre_gate * sig
+    hidden = activated * pre_up
+    share = jnp.sum(back_proj * hidden, axis=1, keepdims=True)
     high = share.astype(bf16).astype(f32)
     lane = lax.broadcasted_iota(i32, (share.shape[0], LANES), 1)
     tail = jnp.where(lane == 0, high, jnp.where(lane == 1, share - high, 0.0))
-    members = low_back.shape[1] // pipe_size * 2
+    d_hidden = gate * back_proj
+    d_gate = d_hidden * pre_up * sig * (1.0 + pre_gate * (1.0 - sig))
+    return d_gate, d_hidden * activated, gate * hidden, tail
+
+
+def store_halves(values, refs):
+    for value, ref in zip(values, refs):
+        half = value.shape[0] // 2
+        ref[0] = value[:half].astype(bf16)
+        ref[1] = value[half:].astype(bf16)
+
+
+def act_kernel(top_count, where_ref, *refs):
+    store_halves(hidden_gradients(top_count, where_ref[0].astype(f32), *refs[:5]), refs[6:])
+
+
+def back_rows(d_part, pipe_size, where_ref, grads, w_gate, w_up, out_ref):
+    left = [jnp.concatenate([g[i].astype(f32) for g in grads], 0) for i in (0, 1, 3)]
+    back = jnp.dot(left[0].astype(bf16), w_gate[...], preferred_element_type=f32)
+    back = back + jnp.dot(left[1].astype(bf16), w_up[...], preferred_element_type=f32)
+    count = back.shape[0] // 4
+    members = out_ref.shape[1] // pipe_size
     used = count // members // pipe_size
     for h in range(2):
         for member in range(members):
-            ref = low_back if member < members // 2 else high_back
             for p in range(pipe_size):
                 at_p = (member * pipe_size + p) * used
                 between = count + ((2 * member + 1 - h) * pipe_size + p) * used
                 starts = [at_p, between] if h == 0 else [between, 3 * count + at_p]
-                at = member % (members // 2) * pipe_size + (p ^ where_ref[1] if pipe_size == 2 else p)
-                for columns, values in ((slice(0, d_part), back), (slice(d_part, None), tail)):
+                at = member * pipe_size + (p ^ where_ref[1] if pipe_size == 2 else p)
+                for columns, values in ((slice(0, d_part), back), (slice(d_part, None), left[2])):
                     block = jnp.concatenate([values[start : start + used] for start in starts], 0)
-                    ref[h, at, :, columns] = block.astype(bf16)
+                    out_ref[h, at, :, columns] = block.astype(bf16)
+
+
+def last_act_kernel(d_part, top_count, pipe_size, where_ref, *refs):
+    raw, first, middle, (w_gate, w_up), outs = refs[:5], refs[5:9], refs[9:13], refs[13:15], refs[-5:]
+    last = hidden_gradients(top_count, where_ref[0].astype(f32), *raw)
+    store_halves(last, outs[:4])
+    half = last[0].shape[0] // 2
+    grads = [[ref[1] for ref in first], [ref[1] for ref in middle], [value[half:] for value in last]]
+    back_rows(d_part, pipe_size, where_ref, grads, w_gate, w_up, outs[4])
+
+
+def own_back_kernel(d_part, pipe_size, where_ref, *refs):
+    grads = [[ref[0] for ref in refs[4 * i : 4 * i + 4]] for i in range(PIECES)]
+    back_rows(d_part, pipe_size, where_ref, grads, *refs[4 * PIECES : 4 * PIECES + 2], refs[-1])
 
 
 def fold_kernel(a_ref, b_ref, *out_refs):
@@ -175,53 +197,63 @@
         ref[...] = (a_ref[here].astype(f32) + b_ref[here].astype(f32)).astype(bf16)
 
 
-def fold_pairs_kernel(used, a_ref, b_ref, c_ref, d_ref, *out_refs):
-    totals = (
-        a_ref[...].astype(f32) + b_ref[...].astype(f32),
-        c_ref[...].astype(f32) + d_ref[...].astype(f32),
-    )
+def pack_slots(used, columns, tail):
+    main = columns.shape[1] // 4 * 3
+    per_row = used // (ROWS - used)
+    spare = [
+        jnp.concatenate([columns[r * per_row + j : r * per_row + j + 1, main:] for j in range(per_row)], 1)
+        for r in range(ROWS - used)
+    ]
+    rows = jnp.concatenate([columns[:, :main]] + spare, 0)
+    tail = jnp.concatenate([tail, jnp.zeros((ROWS - used, LANES), f32)], 0)
+    return jnp.concatenate([rows, tail], 1)
+
+
+def fold_pairs_kernel(used, d_part, a_ref, b_ref, c_ref, d_ref, *out_refs):
+    here = a_ref[...].astype(f32) + d_ref[...].astype(f32)
+    there = b_ref[...].astype(f32) + c_ref[...].astype(f32)
     for k, ref in enumerate(out_refs):
-        for h, total in enumerate(totals):
-            rows = total[k * used : (k + 1) * used]
-            pad = jnp.zeros((ROWS - used, rows.shape[1]), f32)
-            ref[h] = jnp.concatenate([rows, pad], 0).astype(bf16)
-
-
-def owner_kernel(d_part, where_ref, place_ref, *refs):
+        at = slice(k * used, (k + 1) * used)
+        columns = jnp.concatenate([here[at, :d_part], there[at, :d_part]], 1)
+        ref[...] = pack_slots(used, columns, here[at, d_part:]).astype(bf16)
+
+
+def owner_kernel(d_part, packed, where_ref, place_ref, *refs):
     piece_refs, tok_ref, grad_ref = refs[:EXPERTS], refs[EXPERTS], refs[EXPERTS + 1]
-    micro_count, tok_count = tok_ref.shape[:2]
+    piece_refs = [piece_refs[RETURN_ORDER.index(k)] for k in range(EXPERTS)]
+    micro_count, tok_count, d_model = tok_ref.shape
     top_count = grad_ref.shape[1]
-    pipe_size = piece_refs[0].shape[0]
     mine = place_ref[where_ref[1]]
-    place = mine[:, : EXPERTS * ROWS].astype(bf16)
+    places = mine[:, :LANES].astype(bf16)
+    place = places[:, :SQUARE]
     ids = mine[:, LANES:]
-    halves = []
-    for h in range(pipe_size):
-        rows = jnp.concatenate([ref[h].astype(f32) for ref in piece_refs], 0)
-        halves.append(rows)
-    sums = [jnp.dot(place, h.astype(bf16), preferred_element_type=f32)[:, :d_part] for h in halves]
-    if pipe_size == 2:
+    rows = jnp.concatenate([ref[...].astype(f32) for ref in piece_refs], 0).astype(bf16)
+    wide = rows.shape[1] - LANES
+    out = jnp.dot(place, rows[:, :wide], preferred_element_type=f32)
+    if packed:
+        rest, quarter = 0.0, d_model - wide
+        for j in range(wide // quarter):
+            spare = places[:, (1 + j) * SQUARE : (2 + j) * SQUARE]
+            columns = rows[:, j * quarter : (j + 1) * quarter]
+            rest = rest + jnp.dot(spare, columns, preferred_element_type=f32)
+        out = jnp.concatenate([out, rest], 1)
         first = where_ref[1] == 0
-        sums = [jnp.where(first, sums[0], sums[1]), jnp.where(first, sums[1], sums[0])]
-    tail = halves[0][:, d_part:]
-    shares = tail[:, 0:1] + tail[:, 1:2]
-    slot_lane = lax.broadcasted_iota(i32, place.shape, 1)
+        here, there = out[:, :d_part], out[:, d_part:]
+        out = jnp.concatenate([jnp.where(first, here, there), jnp.where(first, there, here)], 1)
+    for m in range(micro_count):
+        tok_ref[m] = out[m * tok_count : (m + 1) * tok_count].astype(bf16)
+
+    expert_of = ((lax.broadcasted_iota(i32, place.shape, 1) // ROWS) ^ where_ref[0]).astype(f32)
     diagonal = lax.broadcasted_iota(i32, (tok_count, tok_count), 0) == lax.broadcasted_iota(
         i32, (tok_count, tok_count), 1
     )
-    square = EXPERTS * ROWS
-    eye = lax.broadcasted_iota(i32, (square, square), 0) == lax.broadcasted_iota(i32, (square, square), 1)
-    share_row = jnp.sum(jnp.where(eye, jnp.broadcast_to(shares, (square, square)), 0.0), axis=0, keepdims=True)
-    picked = mine[:, : EXPERTS * ROWS] * share_row
-    expert_of = ((slot_lane // ROWS) ^ where_ref[0]).astype(f32)
     for k in range(top_count):
-        grad = jnp.sum(jnp.where(expert_of == ids[:, k : k + 1], picked, 0.0), axis=1, keepdims=True)
+        picked = jnp.where(expert_of == ids[:, k : k + 1], mine[:, :SQUARE], 0.0).astype(bf16)
+        grad = jnp.dot(picked, rows[:, wide:], preferred_element_type=f32)
+        grad = grad[:, 0:1] + grad[:, 1:2]
         for m in range(micro_count):
             part = jnp.broadcast_to(grad[m * tok_count : (m + 1) * tok_count], (tok_count, tok_count))
             grad_ref[m, k : k + 1, :] = jnp.sum(jnp.where(diagonal, part, 0.0), axis=0, keepdims=True)
-    for m in range(micro_count):
-        for p in range(pipe_size):
-            tok_ref[m, :, p * d_part : (p + 1) * d_part] = sums[p][m * tok_count : (m + 1) * tok_count].astype(bf16)
 
 
 def flip_kernel(*refs):
@@ -233,14 +265,17 @@
     out_ref[...] = weight_ref[...].T
 
 
-def weight_kernel(scale, block, tok_ref, cot_ref, d_gate, d_up, scaled, after, *refs):
-    del after
-    out_refs, held, sems = refs[:3], refs[3], refs[4]
+def weight_kernel(scale, block, tok_ref, cot_ref, *refs):
+    pieces, (out_refs, held, sems) = refs[: 3 * PIECES], (refs[-5:-2], refs[-2], refs[-1])
+    rights = []
+    for w in range(3):
+        halves = [ref[h].astype(f32) for ref in pieces[w::3] for h in range(2)]
+        rights.append(jnp.concatenate(halves, 0).astype(bf16))
     copies = []
     for i in range(tok_ref.shape[0] // block):
         here = slice(i * block, (i + 1) * block)
-        for w, (left, right) in enumerate(((tok_ref, d_gate), (tok_ref, d_up), (cot_ref, scaled))):
-            rows = jnp.dot(left[here], right[...], preferred_element_type=f32)
+        for w, left in enumerate((tok_ref, tok_ref, cot_ref)):
+            rows = jnp.dot(left[here], rights[w], preferred_element_type=f32)
             held[w, here] = (rows * scale).astype(bf16)
             copies.append(pltpu.make_async_copy(held.at[w, here], out_refs[w].at[here], sems.at[w, i]))
             copies[-1].start()
@@ -384,16 +419,35 @@
     padded = EXPERTS * slots_here
     half_shape = shape((2, group_size // 4 * pipe_size, padded, out_width), bf16)
     moved = total * (f_part * 24 + d_part * 8) + 4 * d_part * f_part
-    operands = [x for piece in exchanged for x in piece]
-    *grads, low, high = call(
-        functools.partial(hidden_kernel, d_part, top_count, pipe_size),
-        (shape((total, f_part), bf16),) * 3 + (half_shape,) * 2,
-        "s" + "v" * (len(operands) + 2) + "a" * len(flipped),
-        "hidden",
-        mib=min(52, 8 + 2 * moved // (1 << 20)),
-    )(where, *operands, *flipped_weights, *flipped)
-    piece_shapes = [shape((pipe_size, ROWS, out_width), bf16) for _ in range(EXPERTS)]
-    if pipe_size == 2 and group_size == 4:
+    mib = min(52, 8 + 2 * moved // (1 << 20))
+
+    def grad_shapes(piece):
+        rows = piece[0].shape[0] // 2
+        return [shape((2, rows, f_part), bf16)] * 3 + [shape((2, rows, LANES), bf16)]
+
+    grads = [
+        call(functools.partial(act_kernel, top_count), grad_shapes(piece), "svvvvva", "act", mib=mib)(
+            where, *piece, exchanged[-1][3]
+        )
+        for piece in exchanged[:-1]
+    ]
+    *last_grad, high = call(
+        functools.partial(last_act_kernel, d_part, top_count, pipe_size),
+        grad_shapes(exchanged[-1]) + [half_shape],
+        "s" + "v" * 15 + "a" * len(flipped),
+        "last_act",
+        mib=mib,
+    )(where, *exchanged[-1], *grads[0], *grads[1], *flipped_weights, *flipped)
+    grads.append(last_grad)
+    low = call(
+        functools.partial(own_back_kernel, d_part, pipe_size),
+        half_shape,
+        "s" + "v" * (4 * PIECES + 2) + "a",
+        "own_back",
+        mib=mib,
+    )(where, *[x for grad in grads for x in grad], *flipped_weights, high)
+    packed = pipe_size == 2 and group_size == 4
+    if packed:
         parts = call(fold_kernel, [shape((padded, out_width), bf16) for _ in range(4)], "vv", "fold")(
             low, swap(high, "expert", bits[1])
         )
@@ -401,9 +455,12 @@
         got_both = swap_both(parts[3], bits[0])
         got_member = swap(parts[2], "expert", bits[0])
         got_pipe = swap(parts[1], "pipe", 1)
-        contributions = call(functools.partial(fold_pairs_kernel, slots_here), piece_shapes, "vvvv", "fold_pairs")(
-            parts[0], got_member, got_pipe, got_both
-        )
+        contributions = call(
+            functools.partial(fold_pairs_kernel, slots_here, d_part),
+            [shape((ROWS, d_model // 4 * 3 + LANES), bf16) for _ in range(EXPERTS)],
+            "vvvv",
+            "fold_pairs",
+        )(parts[0], got_both, got_pipe, got_member)
     else:
         for bit in reversed(bits[1:]):
             sums = (low.astype(f32) + swap(high, "expert", bit).astype(f32)).astype(bf16)
@@ -411,11 +468,14 @@
         sums = (low.astype(f32) + swap(high, "expert", bits[0]).astype(f32)).astype(bf16)
         after = sums
         if pipe_size == 2:
-            sums = jnp.stack([sums[0], swap(sums[1], "pipe", 1)])
+            got = swap(sums[1], "pipe", 1)
+            sums = jnp.where(pipe == 0, jnp.stack([sums[0], got]), jnp.stack([got, sums[0]]))
         else:
             sums = lax.all_to_all(sums, "pipe", split_axis=0, concat_axis=0, tiled=True)
+        wide = jnp.swapaxes(sums[:, :, :d_part], 0, 1).reshape(padded, d_model)
+        wide = jnp.concatenate([wide, sums[0, :, d_part:]], 1)
         contributions = [
-            jnp.pad(sums[:, k * slots_here : (k + 1) * slots_here], ((0, 0), (0, ROWS - slots_here), (0, 0)))
+            jnp.pad(wide[k * slots_here : (k + 1) * slots_here], ((0, ROWS - slots_here), (0, 0)))
             for k in range(EXPERTS)
         ]
     contributions = [swap(x, "expert", k * group_size) if k else x for k, x in enumerate(contributions)]
@@ -426,7 +486,7 @@
     dw_gate, dw_up, dw_down_t = call(
         functools.partial(weight_kernel, scale, block),
         [shape((d_part, f_part), bf16)] * 3,
-        "vvvvva",
+        "vv" + "v" * (3 * PIECES) + "a",
         "weight_grads",
         mib=min(52, 12 + (d_part * (total * 4 + f_part * 8) >> 20)),
         out_specs=[pl.BlockSpec(memory_space=pl.ANY)] * 3,
@@ -434,14 +494,14 @@
             pltpu.VMEM((3, d_part, f_part), bf16),
             pltpu.SemaphoreType.DMA((3, d_part // block)),
         ],
-    )(*flipped, *grads, after)
+    )(*flipped, *[x for grad in grads for x in grad[:3]], after)
 
     d_tokens, gate_grads = call(
-        functools.partial(owner_kernel, d_part),
+        functools.partial(owner_kernel, d_part, packed),
         (shape(tokens.shape, bf16), shape((micro_count, top_count, tok_count), f32)),
         "sv" + "v" * EXPERTS,
         "owner",
-    )(where, place, *contributions)
+    )(where, place, *[contributions[k] for k in RETURN_ORDER])
     return (d_tokens, jnp.swapaxes(gate_grads, 1, 2), dw_gate, dw_up, dw_down_t)
 
 

time: 61.9 us -> 60.3 us (0.974)
  waiting for transfers between devices: 22 us -> 17.7 us
  Pallas kernels: 10.2 us -> 12.8 us
    ppermute x18, waiting for transfers between devices: 20 us -> 14.8 us  [swap(): lax.ppermute(x, axis, [(i, i ^ bit) for i in range(lax.axis_size(axis))])]
    pallas_call x3 -> x6, Pallas kernels: 3.35 us -> 5.95 us  [the longest x2 1.63 us: on_device(): call(functools.partial(act_kernel, top_count), grad_shapes(piece), 'svvvv...]
    ppermute x18, starting transfers between devices: 23.4 us -> 22.4 us  [swap(): lax.ppermute(x, axis, [(i, i ^ bit) for i in range(lax.axis_size(axis))])]
    ppermute x1, starting transfers between devices: 1.01 us -> 1.97 us  [swap_both(): return lax.ppermute(x, ('pipe', 'expert'), pairs)]
    ppermute x1, waiting for transfers between devices: 1.97 us -> 2.89 us  [swap_both(): return lax.ppermute(x, ('pipe', 'expert'), pairs)]
  transfers between devices with their start and end apart: 19 -> 19, of which waited for: 12 -> 12; matrix products, arithmetic and copies ran while one was open for 7% -> 7% of each run, Pallas kernels for 7% -> 12%
where the time goes in v5:
time: 60.3 us; the launch traced here: 60.2 us
  starting transfers between devices  24.4 us (40%)
  waiting for transfers between devices  17.7 us (29%)
  Pallas kernels  12.8 us (21%)
  matrix products  3.76 us (6%)
  between operations  0.99 us (2%)
    ppermute x18, starting transfers between devices, swap(): lax.ppermute(x, axis, [(i, i ^ bit) for i in range(lax.axis_size(axis))])  22.4 us
    ppermute x18, waiting for transfers between devices, swap(): lax.ppermute(x, axis, [(i, i ^ bit) for i in range(lax.axis_size(axis))])  14.8 us
    dot_general x9, matrix products, project(): own.append(jnp.dot(left, weight, preferred_element_type=f32))  3.76 us
    ppermute x1, waiting for transfers between devices, swap_both(): return lax.ppermute(x, ('pipe', 'expert'), pairs)  2.89 us
    pallas_call x1, Pallas kernels, on_device(): call(functools.partial(weight_kernel, scale, block), [shape((d_part, f_pa...  2.8 us
    ppermute x1, starting transfers between devices, swap_both(): return lax.ppermute(x, ('pipe', 'expert'), pairs)  1.97 us
    pallas_call x2, Pallas kernels, on_device(): call(functools.partial(act_kernel, top_count), grad_shapes(piece), 'svvvv...  1.63 us
    pallas_call x1, Pallas kernels, on_device(): call(functools.partial(owner_kernel, d_part, packed), (shape(tokens.shape...  1.49 us
  transfers between devices with their start and end apart: 19, of which 12 were waited for; matrix products, arithmetic and copies ran while one was open for 7% of the time, Pallas kernels for 12%

profile of v5, /device:TPU:0, one launch (start us, length us, event | category | flops | bytes accessed | tf_op | source)
XLA Modules:
  0.0 60.2 jit_solution(4488706019552311270)
XLA Ops:
  0.7 1.1 %prep.1 = (bf16[16,1920]{1,0:T(8,128)(2,1)S(1)}, bf16[16,1920]{1,0:T(8,128)(2,1)S(1)}) custom-call(bf16[2,4,3584]{2,1,0:T(4,128)(2,1)} %tok_hbm.1, bf16[2,4,3584]{2,1,0:T(4,128)(2,1)} %cot_hbm.1, s32[2,2,4]{2,1,0:T(2,128)} %bitcast.59, bf16[2,2,4]{2,1,0:T(2,128)(2,1)} %bitcast.60), custom_call_target="tpu_custom_call" | custom-call | tf_op jit(solution)/shard_map/prep/pallas_call | solution.py:333
  1.8 3.0 %collective-permute-start = (bf16[16,1920]{1,0:T(8,128)(2,1)S(1)}, bf16[16,1920]{1,0:T(8,128)(2,1)S(1)}, u32[]{:S(2)}, u32[]{:S(2)}) collective-permute-start(bf16[16,1920]{1,0:T(8,128)(2,1)S(1)} %get-tuple-element.75), channel_id=1, source_target_pairs={{0,16},{16,0},{1,17},{17,1},{2,18},{18,2},{3,19},{19,3},{4,20},{20... | collective-permute-start | bytes 184328 | tf_op jit(solution)/shard_map/ppermute | solution.py:27
  4.9 2.1 %collective-permute-done.refs_1_ = bf16[16,1920]{1,0:T(8,128)(2,1)S(1)} collective-permute-done((bf16[16,1920]{1,0:T(8,128)(2,1)S(1)}, bf16[16,1920]{1,0:T(8,128)(2,1)S(1)}, u32[]{:S(2)}, u32[]{:S(2)}) %collective-permute-start) | collective-permute-done | bytes 61472 | tf_op jit(solution)/shard_map/ppermute | solution.py:27
  7.0 1.1 %pack.1 = (bf16[24,1920]{1,0:T(8,128)(2,1)S(1)}, bf16[24,1920]{1,0:T(8,128)(2,1)S(1)}, bf16[24,1920]{1,0:T(8,128)(2,1)S(1)}, bf16[24,1920]{1,0:T(8,128)(2,1)S(1)}, f32[2,8,256]{2,1,0:T(8,128)S(1)}) custom-call(s32[2]{0:T(128)S(1)} %pad_add_fusion.where_ref, bf16[16,1920]{1,0:T(8,128)(2,1)S(1)} %get-tuple-element.76.refs_0_, ...), custom_call_target="tpu_custom_call" | custom-call | tf_op jit(solution)/shard_map/pack/pallas_call | solution.py:353
  8.1 2.2 %collective-permute-start.1 = (bf16[24,1920]{1,0:T(8,128)(2,1)S(1)}, bf16[24,1920]{1,0:T(8,128)(2,1)S(1)}, u32[]{:S(2)}, u32[]{:S(2)}) collective-permute-start(bf16[24,1920]{1,0:T(8,128)(2,1)S(1)} %get-tuple-element.42), channel_id=1, source_target_pairs={{0,4},{1,5},{2,6},{3,7},{4,0},{5,1},{6,2},{7,3},{8,12},{9,13},{10,... | collective-permute-start | bytes 276488 | tf_op jit(solution)/shard_map/ppermute | solution.py:27
  10.3 2.6 %collective-permute-start.4 = (bf16[24,1920]{1,0:T(8,128)(2,1)S(1)}, bf16[24,1920]{1,0:T(8,128)(2,1)S(1)}, u32[]{:S(2)}, u32[]{:S(2)}) collective-permute-start(bf16[24,1920]{1,0:T(8,128)(2,1)S(1)} %get-tuple-element.43), channel_id=1, source_target_pairs={{0,8},{1,9},{2,10},{3,11},{4,12},{5,13},{6,14},{7,15},{8,0},{9,1},... | collective-permute-start | bytes 276488 | tf_op jit(solution)/shard_map/ppermute | solution.py:27
  12.9 0.9 %collective-permute-done.1.refs_1_ = bf16[24,1920]{1,0:T(8,128)(2,1)S(1)} collective-permute-done((bf16[24,1920]{1,0:T(8,128)(2,1)S(1)}, bf16[24,1920]{1,0:T(8,128)(2,1)S(1)}, u32[]{:S(2)}, u32[]{:S(2)}) %collective-permute-start.1) | collective-permute-done | bytes 92192 | tf_op jit(solution)/shard_map/ppermute | solution.py:27
  13.8 1.9 %collective-permute-start.6 = (bf16[2,24,1920]{2,1,0:T(8,128)(2,1)S(1)}, bf16[2,24,1920]{2,1,0:T(8,128)(2,1)S(1)}, u32[]{:S(2)}, u32[]{:S(2)}) collective-permute-start(bf16[2,24,1920]{2,1,0:T(8,128)(2,1)S(1)} %join.2), channel_id=1, source_target_pairs={{0,2},{1,3},{2,0},{3,1},{4,6},{5,7},{6,4},{7,5},{8,10},{9,11},{10,... | collective-permute-start | bytes 552968 | tf_op jit(solution)/shard_map/ppermute | solution.py:27
  15.8 2.3 %collective-permute-done.4.refs_0_ = bf16[24,1920]{1,0:T(8,128)(2,1)S(1)} collective-permute-done((bf16[24,1920]{1,0:T(8,128)(2,1)S(1)}, bf16[24,1920]{1,0:T(8,128)(2,1)S(1)}, u32[]{:S(2)}, u32[]{:S(2)}) %collective-permute-start.4) | collective-permute-done | bytes 92192 | tf_op jit(solution)/shard_map/ppermute | solution.py:27
  18.1 1.2 %collective-permute-done.5.refs_1_ = bf16[24,1920]{1,0:T(8,128)(2,1)S(1)} collective-permute-done((bf16[24,1920]{1,0:T(8,128)(2,1)S(1)}, bf16[24,1920]{1,0:T(8,128)(2,1)S(1)}, u32[]{:S(2)}, u32[]{:S(2)}) %collective-permute-start.5) | collective-permute-done | bytes 92192 | tf_op jit(solution)/shard_map/ppermute | solution.py:27
  19.4 1.9 %collective-permute-start.7 = (bf16[2,24,1920]{2,1,0:T(8,128)(2,1)S(1)}, bf16[2,24,1920]{2,1,0:T(8,128)(2,1)S(1)}, u32[]{:S(2)}, u32[]{:S(2)}) collective-permute-start(bf16[2,24,1920]{2,1,0:T(8,128)(2,1)S(1)} %tie.2), channel_id=1, source_target_pairs={{0,2},{1,3},{2,0},{3,1},{4,6},{5,7},{6,4},{7,5},{8,10},{9,11},{10,... | collective-permute-start | bytes 552968 | tf_op jit(solution)/shard_map/ppermute | solution.py:27
  22.8 1.6 %collective-permute-start.3 = (bf16[3,48,512]{2,1,0:T(8,128)(2,1)S(1)}, bf16[3,48,512]{2,1,0:T(8,128)(2,1)S(1)}, u32[]{:S(2)}, u32[]{:S(2)}) collective-permute-start(bf16[3,48,512]{2,1,0:T(8,128)(2,1)S(1)} %pad_maximum_fusion.5), channel_id=1, source_target_pairs={{0,16},{16,0},{1,17},{17,1},{2,18},{18,2},{3,19},{19,3},{4,20},{20... | collective-permute-start | bytes 442376 | tf_op jit(solution)/shard_map/ppermute | solution.py:27
  26.2 1.1 %collective-permute-start.10 = (bf16[3,96,512]{2,1,0:T(8,128)(2,1)S(1)}, bf16[3,96,512]{2,1,0:T(8,128)(2,1)S(1)}, u32[]{:S(2)}, u32[]{:S(2)}) collective-permute-start(bf16[3,96,512]{2,1,0:T(8,128)(2,1)S(1)} %pad_maximum_fusion.2), channel_id=1, source_target_pairs={{0,16},{16,0},{1,17},{17,1},{2,18},{18,2},{3,19},{19,3},{4,20},{20... | collective-permute-start | bytes 884744 | tf_op jit(solution)/shard_map/ppermute | solution.py:27
  28.7 1.2 %collective-permute-start.11 = (bf16[3,48,512]{2,1,0:T(8,128)(2,1)S(1)}, bf16[3,48,512]{2,1,0:T(8,128)(2,1)S(1)}, u32[]{:S(2)}, u32[]{:S(2)}) collective-permute-start(bf16[3,48,512]{2,1,0:T(8,128)(2,1)S(1)} %pad_maximum_fusion.6), channel_id=1, source_target_pairs={{0,16},{16,0},{1,17},{17,1},{2,18},{18,2},{3,19},{19,3},{4,20},{20... | collective-permute-start | bytes 442376 | tf_op jit(solution)/shard_map/ppermute | solution.py:27
  30.1 0.5 flip_weight.3.refs_14_.refs_13_
  30.7 0.5 flip_weight.2.refs_13_.refs_12_
  31.5 0.8 %act.2 = (bf16[2,24,512]{2,1,0:T(8,128)(2,1)S(1)}, bf16[2,24,512]{2,1,0:T(8,128)(2,1)S(1)}, bf16[2,24,512]{2,1,0:T(8,128)(2,1)S(1)}, bf16[2,24,128]{2,1,0:T(8,128)(2,1)S(1)}) custom-call(s32[2]{0:T(128)S(1)} %pad_add_fusion.where_ref, bf16[48,128]{1,0:T(8,128)(2,1)S(1)} %maximum_bitcast_fusion.3.refs_0_, f32[48,512]{1,0:T(8,128)S(1)} %fusion.7.refs_1_, ...), custom_call_target="tpu_custom_call" | custom-call | tf_op jit(solution)/shard_map/act/pallas_call | solution.py:429
  32.3 3.8 %collective-permute-done.10.refs_4_ = bf16[3,96,512]{2,1,0:T(8,128)(2,1)S(1)} collective-permute-done((bf16[3,96,512]{2,1,0:T(8,128)(2,1)S(1)}, bf16[3,96,512]{2,1,0:T(8,128)(2,1)S(1)}, u32[]{:S(2)}, u32[]{:S(2)}) %collective-permute-start.10) | collective-permute-done | bytes 294944 | tf_op jit(solution)/shard_map/ppermute | solution.py:27
  36.1 0.8 %act.3 = (bf16[2,48,512]{2,1,0:T(8,128)(2,1)S(1)}, bf16[2,48,512]{2,1,0:T(8,128)(2,1)S(1)}, bf16[2,48,512]{2,1,0:T(8,128)(2,1)S(1)}, bf16[2,48,128]{2,1,0:T(8,128)(2,1)S(1)}) custom-call(s32[2]{0:T(128)S(1)} %pad_add_fusion.where_ref, bf16[96,128]{1,0:T(8,128)(2,1)S(1)} %maximum_bitcast_fusion.2.refs_0_, f32[96,512]{1,0:T(8,128)S(1)} %fusion.11.refs_1_, ...), custom_call_target="tpu_custom_call" | custom-call | tf_op jit(solution)/shard_map/act/pallas_call | solution.py:429
  36.9 1.7 %collective-permute-done.11.refs_4_ = bf16[3,48,512]{2,1,0:T(8,128)(2,1)S(1)} collective-permute-done((bf16[3,48,512]{2,1,0:T(8,128)(2,1)S(1)}, bf16[3,48,512]{2,1,0:T(8,128)(2,1)S(1)}, u32[]{:S(2)}, u32[]{:S(2)}) %collective-permute-start.11) | collective-permute-done | bytes 147488 | tf_op jit(solution)/shard_map/ppermute | solution.py:27
  38.6 1.4 %last_act.1 = (bf16[2,24,512]{2,1,0:T(8,128)(2,1)S(1)}, bf16[2,24,512]{2,1,0:T(8,128)(2,1)S(1)}, bf16[2,24,512]{2,1,0:T(8,128)(2,1)S(1)}, bf16[2,24,128]{2,1,0:T(8,128)(2,1)S(1)}, bf16[2,2,24,1920]{3,2,1,0:T(8,128)(2,1)S(1)}) custom-call(s32[2]{0:T(128)S(1)} %pad_add_fusion.where_ref, bf16[48,128]{1,0:T(8,128)(2,1)S(1)} %fusion.5.refs_0_, ...), custom_call_target="tpu_custom_call" | custom-call | tf_op jit(solution)/shard_map/last_act/pallas_call | solution.py:434
  40.1 1.3 %own_back.1.a_ref = bf16[2,2,24,1920]{3,2,1,0:T(8,128)(2,1)S(1)} custom-call(s32[2]{0:T(128)S(1)} %pad_add_fusion.where_ref, bf16[2,24,512]{2,1,0:T(8,128)(2,1)S(1)} %get-tuple-element.45.refs_5_.refs_0_, bf16[2,24,512]{2,1,0:T(8,128)(2,1)S(1)} %get-tuple-element.46.refs_6_.refs_1_, bf16[2,24,512]{2,1,0:T(8,128)(2,1)S(1)} %get-tuple-element.47.refs_7_.refs_2_, ...), custom_call_target="tpu_custom_call" | custom-call | tf_op jit(solution)/shard_map/own_back/pallas_call | solution.py:442
  41.9 2.0 %collective-permute-start.13 = (bf16[24,1920]{1,0:T(8,128)(2,1)S(1)}, bf16[24,1920]{1,0:T(8,128)(2,1)S(1)}, u32[]{:S(2)}, u32[]{:S(2)}) collective-permute-start(bf16[24,1920]{1,0:T(8,128)(2,1)S(1)} %get-tuple-element.59), channel_id=1, source_target_pairs={{0,18},{1,19},{2,16},{3,17},{4,22},{5,23},{6,20},{7,21},{8,26},{9,... | collective-permute-start | bytes 276488 | tf_op jit(solution)/shard_map/ppermute | solution.py:33
  43.9 0.5 collective-permute-start.14
  44.4 1.1 %collective-permute-start.15 = (bf16[24,1920]{1,0:T(8,128)(2,1)S(1)}, bf16[24,1920]{1,0:T(8,128)(2,1)S(1)}, u32[]{:S(2)}, u32[]{:S(2)}) collective-permute-start(bf16[24,1920]{1,0:T(8,128)(2,1)S(1)} %get-tuple-element.61), channel_id=1, source_target_pairs={{0,2},{1,3},{2,0},{3,1},{4,6},{5,7},{6,4},{7,5},{8,10},{9,11},{10,... | collective-permute-start | bytes 276488 | tf_op jit(solution)/shard_map/ppermute | solution.py:27
  45.5 2.9 %collective-permute-done.13.b_ref = bf16[24,1920]{1,0:T(8,128)(2,1)S(1)} collective-permute-done((bf16[24,1920]{1,0:T(8,128)(2,1)S(1)}, bf16[24,1920]{1,0:T(8,128)(2,1)S(1)}, u32[]{:S(2)}, u32[]{:S(2)}) %collective-permute-start.13) | collective-permute-done | bytes 92192 | tf_op jit(solution)/shard_map/ppermute | solution.py:33
  48.3 0.7 %collective-permute-done.14.c_ref = bf16[24,1920]{1,0:T(8,128)(2,1)S(1)} collective-permute-done((bf16[24,1920]{1,0:T(8,128)(2,1)S(1)}, bf16[24,1920]{1,0:T(8,128)(2,1)S(1)}, u32[]{:S(2)}, u32[]{:S(2)}) %collective-permute-start.14) | collective-permute-done | bytes 92192 | tf_op jit(solution)/shard_map/ppermute | solution.py:27
  49.7 2.1 %collective-permute-start.16 = (bf16[8,2816]{1,0:T(8,128)(2,1)S(1)}, bf16[8,2816]{1,0:T(8,128)(2,1)S(1)}, u32[]{:S(2)}, u32[]{:S(2)}) collective-permute-start(bf16[8,2816]{1,0:T(8,128)(2,1)S(1)} %get-tuple-element.63), channel_id=1, source_target_pairs={{0,8},{1,9},{2,10},{3,11},{4,12},{5,13},{6,14},{7,15},{8,0},{9,1},... | collective-permute-start | bytes 135176 | tf_op jit(solution)/shard_map/ppermute | solution.py:27
  51.8 2.9 %collective-permute-start.17 = (bf16[8,2816]{1,0:T(8,128)(2,1)S(1)}, bf16[8,2816]{1,0:T(8,128)(2,1)S(1)}, u32[]{:S(2)}, u32[]{:S(2)}) collective-permute-start(bf16[8,2816]{1,0:T(8,128)(2,1)S(1)} %get-tuple-element.64), channel_id=1, source_target_pairs={{0,12},{1,13},{2,14},{3,15},{4,8},{5,9},{6,10},{7,11},{8,4},{9,5},... | collective-permute-start | bytes 135176 | tf_op jit(solution)/shard_map/ppermute | solution.py:27
  54.7 2.8 %weight_grads.1 = (bf16[1792,512]{1,0:T(8,128)(2,1)}, bf16[1792,512]{1,0:T(8,128)(2,1)}, bf16[1792,512]{1,0:T(8,128)(2,1)}) custom-call(bf16[1792,192]{1,0:T(8,128)(2,1)S(1)} %flip.2.refs_15_.tok_ref, bf16[1792,192]{1,0:T(8,128)(2,1)S(1)} %flip.3.refs_16_.cot_ref, bf16[2,24,512]{2,1,0:T(8,128)(2,1)S(1)} %get-tuple-element.45.refs_5_.refs_0_, ...), custom_call_target="tpu_custom_call" | custom-call | tf_op jit(solution)/shard_map/weight_grads/pallas_call | solution.py:486
  57.7 1.0 %collective-permute-done.18.refs_3_ = bf16[8,2816]{1,0:T(8,128)(2,1)S(1)} collective-permute-done((bf16[8,2816]{1,0:T(8,128)(2,1)S(1)}, bf16[8,2816]{1,0:T(8,128)(2,1)S(1)}, u32[]{:S(2)}, u32[]{:S(2)}) %collective-permute-start.18) | collective-permute-done | bytes 45088 | tf_op jit(solution)/shard_map/ppermute | solution.py:27
  58.7 1.5 %owner.1 = (bf16[2,4,3584]{2,1,0:T(4,128)(2,1)}, f32[2,2,4]{2,1,0:T(2,128)}) custom-call(s32[2]{0:T(128)S(1)} %pad_add_fusion.where_ref, f32[2,8,256]{2,1,0:T(8,128)S(1)} %get-tuple-element.40.place_ref, bf16[8,2816]{1,0:T(8,128)(2,1)S(1)} %get-tuple-element.62.refs_0_, bf16[8,2816]{1,0:T(8,128)(2,1)S(1)} %collective-permute-done.16.refs_1_, ...), custom_call_target="tpu_custom_call" | custom-call | tf_op jit(solution)/shard_map/owner/pallas_call | solution.py:499
  (59 shorter events, 6.7 us)
Async XLA Ops:
  0.6 21.7 %copy-start = (bf16[1792,512]{1,0:T(8,128)(2,1)S(1)}, bf16[1792,512]{1,0:T(8,128)(2,1)}, u32[]{:S(2)}) copy-start(bf16[1792,512]{1,0:T(8,128)(2,1)} %param.13) | copy-start | bytes 5505028
  1.8 5.2 %collective-permute-start = (bf16[16,1920]{1,0:T(8,128)(2,1)S(1)}, bf16[16,1920]{1,0:T(8,128)(2,1)S(1)}, u32[]{:S(2)}, u32[]{:S(2)}) collective-permute-start(bf16[16,1920]{1,0:T(8,128)(2,1)S(1)} %get-tuple-element.75), channel_id=1, source_target_pairs={{0,16},{16,0},{1,17},{17,1},{2,18},{18,2},{3,19},{19,3},{4,20},{20... | collective-permute-start | bytes 184328 | tf_op jit(solution)/shard_map/ppermute | solution.py:27
  8.1 5.6 %collective-permute-start.1 = (bf16[24,1920]{1,0:T(8,128)(2,1)S(1)}, bf16[24,1920]{1,0:T(8,128)(2,1)S(1)}, u32[]{:S(2)}, u32[]{:S(2)}) collective-permute-start(bf16[24,1920]{1,0:T(8,128)(2,1)S(1)} %get-tuple-element.42), channel_id=1, source_target_pairs={{0,4},{1,5},{2,6},{3,7},{4,0},{5,1},{6,2},{7,3},{8,12},{9,13},{10,... | collective-permute-start | bytes 276488 | tf_op jit(solution)/shard_map/ppermute | solution.py:27
  10.3 7.8 %collective-permute-start.4 = (bf16[24,1920]{1,0:T(8,128)(2,1)S(1)}, bf16[24,1920]{1,0:T(8,128)(2,1)S(1)}, u32[]{:S(2)}, u32[]{:S(2)}) collective-permute-start(bf16[24,1920]{1,0:T(8,128)(2,1)S(1)} %get-tuple-element.43), channel_id=1, source_target_pairs={{0,8},{1,9},{2,10},{3,11},{4,12},{5,13},{6,14},{7,15},{8,0},{9,1},... | collective-permute-start | bytes 276488 | tf_op jit(solution)/shard_map/ppermute | solution.py:27
  12.9 6.5 %collective-permute-start.5 = (bf16[24,1920]{1,0:T(8,128)(2,1)S(1)}, bf16[24,1920]{1,0:T(8,128)(2,1)S(1)}, u32[]{:S(2)}, u32[]{:S(2)}) collective-permute-start(bf16[24,1920]{1,0:T(8,128)(2,1)S(1)} %get-tuple-element.44), channel_id=1, source_target_pairs={{0,12},{1,13},{2,14},{3,15},{4,8},{5,9},{6,10},{7,11},{8,4},{9,5},... | collective-permute-start | bytes 276488 | tf_op jit(solution)/shard_map/ppermute | solution.py:27
  13.8 7.5 %copy-start.1 = (bf16[1792,512]{1,0:T(8,128)(2,1)S(1)}, bf16[1792,512]{1,0:T(8,128)(2,1)}, u32[]{:S(2)}) copy-start(bf16[1792,512]{1,0:T(8,128)(2,1)} %weight_ref.3) | copy-start | bytes 5505028
  13.8 5.6 %collective-permute-start.6 = (bf16[2,24,1920]{2,1,0:T(8,128)(2,1)S(1)}, bf16[2,24,1920]{2,1,0:T(8,128)(2,1)S(1)}, u32[]{:S(2)}, u32[]{:S(2)}) collective-permute-start(bf16[2,24,1920]{2,1,0:T(8,128)(2,1)S(1)} %join.2), channel_id=1, source_target_pairs={{0,2},{1,3},{2,0},{3,1},{4,6},{5,7},{6,4},{7,5},{8,10},{9,11},{10,... | collective-permute-start | bytes 552968 | tf_op jit(solution)/shard_map/ppermute | solution.py:27
  15.8 5.5 %collective-permute-start.2 = (bf16[2,24,1920]{2,1,0:T(8,128)(2,1)S(1)}, bf16[2,24,1920]{2,1,0:T(8,128)(2,1)S(1)}, u32[]{:S(2)}, u32[]{:S(2)}) collective-permute-start(bf16[2,24,1920]{2,1,0:T(8,128)(2,1)S(1)} %join.2), channel_id=1, source_target_pairs={{0,1},{1,0},{2,3},{3,2},{4,5},{5,4},{6,7},{7,6},{8,9},{9,8},{10,11... | collective-permute-start | bytes 552968 | tf_op jit(solution)/shard_map/ppermute | solution.py:27
  19.4 2.4 %copy-start.2 = (bf16[1792,512]{1,0:T(8,128)(2,1)S(1)}, bf16[1792,512]{1,0:T(8,128)(2,1)}, u32[]{:S(2)}) copy-start(bf16[1792,512]{1,0:T(8,128)(2,1)} %weight_ref.2) | copy-start | bytes 5505028
  19.4 6.3 %collective-permute-start.7 = (bf16[2,24,1920]{2,1,0:T(8,128)(2,1)S(1)}, bf16[2,24,1920]{2,1,0:T(8,128)(2,1)S(1)}, u32[]{:S(2)}, u32[]{:S(2)}) collective-permute-start(bf16[2,24,1920]{2,1,0:T(8,128)(2,1)S(1)} %tie.2), channel_id=1, source_target_pairs={{0,2},{1,3},{2,0},{3,1},{4,6},{5,7},{6,4},{7,5},{8,10},{9,11},{10,... | collective-permute-start | bytes 552968 | tf_op jit(solution)/shard_map/ppermute | solution.py:27
  22.2 2.1 %collective-permute-start.8 = (bf16[2,48,1920]{2,1,0:T(8,128)(2,1)S(1)}, bf16[2,48,1920]{2,1,0:T(8,128)(2,1)S(1)}, u32[]{:S(2)}, u32[]{:S(2)}) collective-permute-start(bf16[2,48,1920]{2,1,0:T(8,128)(2,1)S(1)} %pad_maximum_fusion.1), channel_id=1, source_target_pairs={{0,1},{1,0},{2,3},{3,2},{4,5},{5,4},{6,7},{7,6},{8,9},{9,8},{10,11... | collective-permute-start | bytes 1105928 | tf_op jit(solution)/shard_map/ppermute | solution.py:27
  22.8 8.7 %collective-permute-start.3 = (bf16[3,48,512]{2,1,0:T(8,128)(2,1)S(1)}, bf16[3,48,512]{2,1,0:T(8,128)(2,1)S(1)}, u32[]{:S(2)}, u32[]{:S(2)}) collective-permute-start(bf16[3,48,512]{2,1,0:T(8,128)(2,1)S(1)} %pad_maximum_fusion.5), channel_id=1, source_target_pairs={{0,16},{16,0},{1,17},{17,1},{2,18},{18,2},{3,19},{19,3},{4,20},{20... | collective-permute-start | bytes 442376 | tf_op jit(solution)/shard_map/ppermute | solution.py:27
  25.8 1.5 %collective-permute-start.9 = (bf16[2,24,1920]{2,1,0:T(8,128)(2,1)S(1)}, bf16[2,24,1920]{2,1,0:T(8,128)(2,1)S(1)}, u32[]{:S(2)}, u32[]{:S(2)}) collective-permute-start(bf16[2,24,1920]{2,1,0:T(8,128)(2,1)S(1)} %tie.3), channel_id=1, source_target_pairs={{0,1},{1,0},{2,3},{3,2},{4,5},{5,4},{6,7},{7,6},{8,9},{9,8},{10,11... | collective-permute-start | bytes 552968 | tf_op jit(solution)/shard_map/ppermute | solution.py:27
  26.2 9.9 %collective-permute-start.10 = (bf16[3,96,512]{2,1,0:T(8,128)(2,1)S(1)}, bf16[3,96,512]{2,1,0:T(8,128)(2,1)S(1)}, u32[]{:S(2)}, u32[]{:S(2)}) collective-permute-start(bf16[3,96,512]{2,1,0:T(8,128)(2,1)S(1)} %pad_maximum_fusion.2), channel_id=1, source_target_pairs={{0,16},{16,0},{1,17},{17,1},{2,18},{18,2},{3,19},{19,3},{4,20},{20... | collective-permute-start | bytes 884744 | tf_op jit(solution)/shard_map/ppermute | solution.py:27
  28.7 9.9 %collective-permute-start.11 = (bf16[3,48,512]{2,1,0:T(8,128)(2,1)S(1)}, bf16[3,48,512]{2,1,0:T(8,128)(2,1)S(1)}, u32[]{:S(2)}, u32[]{:S(2)}) collective-permute-start(bf16[3,48,512]{2,1,0:T(8,128)(2,1)S(1)} %pad_maximum_fusion.6), channel_id=1, source_target_pairs={{0,16},{16,0},{1,17},{17,1},{2,18},{18,2},{3,19},{19,3},{4,20},{20... | collective-permute-start | bytes 442376 | tf_op jit(solution)/shard_map/ppermute | solution.py:27
  40.1 1.8 %collective-permute-start.12 = (bf16[2,2,24,1920]{3,2,1,0:T(8,128)(2,1)S(1)}, bf16[2,2,24,1920]{3,2,1,0:T(8,128)(2,1)S(1)}, u32[]{:S(2)}, u32[]{:S(2)}) collective-permute-start(bf16[2,2,24,1920]{3,2,1,0:T(8,128)(2,1)S(1)} %get-tuple-element.57.refs_14_), channel_id=1, source_target_pairs={{0,1},{1,0},{2,3},{3,2},{4,5},{5,4},{6,7},{7,6},{8,9},{9,8},{10,11... | collective-permute-start | bytes 1105928 | tf_op jit(solution)/shard_map/ppermute | solution.py:27
  41.9 6.4 %collective-permute-start.13 = (bf16[24,1920]{1,0:T(8,128)(2,1)S(1)}, bf16[24,1920]{1,0:T(8,128)(2,1)S(1)}, u32[]{:S(2)}, u32[]{:S(2)}) collective-permute-start(bf16[24,1920]{1,0:T(8,128)(2,1)S(1)} %get-tuple-element.59), channel_id=1, source_target_pairs={{0,18},{1,19},{2,16},{3,17},{4,22},{5,23},{6,20},{7,21},{8,26},{9,... | collective-permute-start | bytes 276488 | tf_op jit(solution)/shard_map/ppermute | solution.py:33
  43.9 5.2 %collective-permute-start.14 = (bf16[24,1920]{1,0:T(8,128)(2,1)S(1)}, bf16[24,1920]{1,0:T(8,128)(2,1)S(1)}, u32[]{:S(2)}, u32[]{:S(2)}) collective-permute-start(bf16[24,1920]{1,0:T(8,128)(2,1)S(1)} %get-tuple-element.60), channel_id=1, source_target_pairs={{0,16},{16,0},{1,17},{17,1},{2,18},{18,2},{3,19},{19,3},{4,20},{20... | collective-permute-start | bytes 276488 | tf_op jit(solution)/shard_map/ppermute | solution.py:27
  44.4 5.1 %collective-permute-start.15 = (bf16[24,1920]{1,0:T(8,128)(2,1)S(1)}, bf16[24,1920]{1,0:T(8,128)(2,1)S(1)}, u32[]{:S(2)}, u32[]{:S(2)}) collective-permute-start(bf16[24,1920]{1,0:T(8,128)(2,1)S(1)} %get-tuple-element.61), channel_id=1, source_target_pairs={{0,2},{1,3},{2,0},{3,1},{4,6},{5,7},{6,4},{7,5},{8,10},{9,11},{10,... | collective-permute-start | bytes 276488 | tf_op jit(solution)/shard_map/ppermute | solution.py:27
  49.7 7.8 %collective-permute-start.16 = (bf16[8,2816]{1,0:T(8,128)(2,1)S(1)}, bf16[8,2816]{1,0:T(8,128)(2,1)S(1)}, u32[]{:S(2)}, u32[]{:S(2)}) collective-permute-start(bf16[8,2816]{1,0:T(8,128)(2,1)S(1)} %get-tuple-element.63), channel_id=1, source_target_pairs={{0,8},{1,9},{2,10},{3,11},{4,12},{5,13},{6,14},{7,15},{8,0},{9,1},... | collective-permute-start | bytes 135176 | tf_op jit(solution)/shard_map/ppermute | solution.py:27
  51.8 5.9 %collective-permute-start.17 = (bf16[8,2816]{1,0:T(8,128)(2,1)S(1)}, bf16[8,2816]{1,0:T(8,128)(2,1)S(1)}, u32[]{:S(2)}, u32[]{:S(2)}) collective-permute-start(bf16[8,2816]{1,0:T(8,128)(2,1)S(1)} %get-tuple-element.64), channel_id=1, source_target_pairs={{0,12},{1,13},{2,14},{3,15},{4,8},{5,9},{6,10},{7,11},{8,4},{9,5},... | collective-permute-start | bytes 135176 | tf_op jit(solution)/shard_map/ppermute | solution.py:27
  54.6 4.0 %collective-permute-start.18 = (bf16[8,2816]{1,0:T(8,128)(2,1)S(1)}, bf16[8,2816]{1,0:T(8,128)(2,1)S(1)}, u32[]{:S(2)}, u32[]{:S(2)}) collective-permute-start(bf16[8,2816]{1,0:T(8,128)(2,1)S(1)} %get-tuple-element.65), channel_id=1, source_target_pairs={{0,4},{1,5},{2,6},{3,7},{4,0},{5,1},{6,2},{7,3},{8,12},{9,13},{10,... | collective-permute-start | bytes 135176 | tf_op jit(solution)/shard_map/ppermute | solution.py:27

commit v6 on v5

--- a/solution.py
+++ b/solution.py
@@ -14,10 +14,12 @@
 PER_GROUP = EXPERTS // GROUPS
 LANES = 128
 ROWS = 8
-PIECES = 3
+PIECES = 4
 SQUARE = EXPERTS * ROWS
 RETURN_ORDER = (0, 2, 3, 1)
-JOIN_COST = dict(flops=4_000_000_000, moved=12_000_000)
+JOIN_COST = dict(flops=4000000000, moved=12000000)
+FILL_A = dict(flops=8000000000, moved=24000000)
+FILL_B = dict(flops=8_000_000_000, moved=24_000_000)
 f32, bf16, i32 = jnp.float32, jnp.bfloat16, jnp.int32
 ROWS_BY_ROWS = (((0,), (0,)), ((), ()))
 shape = jax.ShapeDtypeStruct
@@ -168,9 +170,7 @@
     for h in range(2):
         for member in range(members):
             for p in range(pipe_size):
-                at_p = (member * pipe_size + p) * used
-                between = count + ((2 * member + 1 - h) * pipe_size + p) * used
-                starts = [at_p, between] if h == 0 else [between, 3 * count + at_p]
+                starts = [(2 * g + h) * count + (member * pipe_size + p) * used for g in range(GROUPS)]
                 at = member * pipe_size + (p ^ where_ref[1] if pipe_size == 2 else p)
                 for columns, values in ((slice(0, d_part), back), (slice(d_part, None), left[2])):
                     block = jnp.concatenate([values[start : start + used] for start in starts], 0)
@@ -178,11 +178,13 @@
 
 
 def last_act_kernel(d_part, top_count, pipe_size, where_ref, *refs):
-    raw, first, middle, (w_gate, w_up), outs = refs[:5], refs[5:9], refs[9:13], refs[13:15], refs[-5:]
+    raw, outs = refs[:5], refs[-5:]
+    others = [refs[5 + 4 * i : 9 + 4 * i] for i in range(PIECES - 1)]
+    w_gate, w_up = refs[4 * PIECES + 1 : 4 * PIECES + 3]
     last = hidden_gradients(top_count, where_ref[0].astype(f32), *raw)
     store_halves(last, outs[:4])
     half = last[0].shape[0] // 2
-    grads = [[ref[1] for ref in first], [ref[1] for ref in middle], [value[half:] for value in last]]
+    grads = [[ref[1] for ref in other] for other in others] + [[value[half:] for value in last]]
     back_rows(d_part, pipe_size, where_ref, grads, w_gate, w_up, outs[4])
 
 
@@ -303,7 +305,7 @@
     )
 
 
-def tie(values, after):
+def tie(values, after, **cost):
     return call(
         tie_kernel,
         [shape(v.shape, v.dtype) for v in values],
@@ -311,6 +313,7 @@
         "tie",
         out_specs=[pl.BlockSpec(memory_space=pl.ANY)] * len(values),
         input_output_aliases={i: i for i in range(len(values))},
+        **cost,
     )(*values, after)
 
 
@@ -359,16 +362,14 @@
     )(where, *blocks)
 
     gathered = [slots[0]] + [swap(slots[k], "expert", k * group_size) for k in range(1, EXPERTS)]
-    joined = [
-        call(
+    def join(g, *after, **cost):
+        return call(
             functools.partial(join_kernel, pipe_size),
             shape((2, PER_GROUP * slot_count, width), bf16),
-            "v" * PER_GROUP,
+            "v" * PER_GROUP + "a" * len(after),
             "join",
-            **(JOIN_COST if g else {}),
-        )(*gathered[g * PER_GROUP : (g + 1) * PER_GROUP])
-        for g in range(GROUPS)
-    ]
+            **cost,
+        )(*gathered[g * PER_GROUP : (g + 1) * PER_GROUP], *after)
 
     def spread(rows):
         for bit in bits[1:]:
@@ -391,15 +392,18 @@
         got = swap(jnp.stack([part.astype(bf16) for part in own]), "pipe", 1)
         return [rows[0, :, width - LANES :], *own, got]
 
-    there = swap(joined[0], "expert", bits[0])
-    later = tie([joined[1]], there)[0]
+    first = join(0)
+    there = swap(first, "expert", bits[0])
+    first = spread(first)
+    filler = tie([jnp.zeros((8, LANES), f32) + pipe.astype(f32)], place, **FILL_A)[0]
+    first = tie([first], filler)[0]
+    first_own = project(first)
+    later = join(1, *first_own, **JOIN_COST)
     later_there = swap(later, "expert", bits[0])
-    first = spread(joined[0])
-    first_own = project(first)
-    middle = spread(jnp.concatenate([there, later], 1))
-    middle_own = project(middle)
-    last = spread(tie([later_there], middle_own[2])[0])
-    pieces, owns = [first, middle, last], [first_own, middle_own, project(last)]
+    there, here = spread(there), spread(later)
+    there_own, here_own = project(there), project(here)
+    last = spread(tie([later_there], there_own[2])[0])
+    pieces, owns = [first, there, here, last], [first_own, there_own, here_own, project(last)]
     exchanged = [exchange(rows, own) for rows, own in zip(pieces, owns)]
     total = sum(piece[0].shape[0] for piece in exchanged)
 
@@ -434,10 +438,10 @@
     *last_grad, high = call(
         functools.partial(last_act_kernel, d_part, top_count, pipe_size),
         grad_shapes(exchanged[-1]) + [half_shape],
-        "s" + "v" * 15 + "a" * len(flipped),
+        "s" + "v" * (4 * PIECES + 3) + "a" * len(flipped),
         "last_act",
         mib=mib,
-    )(where, *exchanged[-1], *grads[0], *grads[1], *flipped_weights, *flipped)
+    )(where, *exchanged[-1], *[x for grad in grads for x in grad], *flipped_weights, *flipped)
     grads.append(last_grad)
     low = call(
         functools.partial(own_back_kernel, d_part, pipe_size),

time: 60.3 us -> 59.2 us (0.982)
  waiting for transfers between devices: 17.7 us -> 15.1 us
  starting transfers between devices: 24.4 us -> 23.1 us
  matrix products: 3.76 us -> 4.98 us
  Pallas kernels: 12.8 us -> 13.6 us
  local copies, waits for them, and re-layouts: 0.06 us -> 0.79 us
    ppermute x18 -> x20, waiting for transfers between devices: 14.8 us -> 12.2 us  [swap(): lax.ppermute(x, axis, [(i, i ^ bit) for i in range(lax.axis_size(axis))])]
    dot_general x9 -> x12, matrix products: 3.76 us -> 4.98 us  [project(): own.append(jnp.dot(left, weight, preferred_element_type=f32))]
    ppermute x1, starting transfers between devices: 1.97 us -> 1.16 us  [swap_both(): return lax.ppermute(x, ('pipe', 'expert'), pairs)]
    pallas_call x2 -> x3, Pallas kernels: 1.63 us -> 2.37 us  [on_device(): call(functools.partial(act_kernel, top_count), grad_shapes(piece), 'svvvv...]
    unnamed x6 -> x7, local copies, waits for them, and re-layouts: 0.03 us -> 0.7 us
    ppermute x18 -> x20, starting transfers between devices: 22.4 us -> 22 us  [swap(): lax.ppermute(x, axis, [(i, i ^ bit) for i in range(lax.axis_size(axis))])]
  transfers between devices with their start and end apart: 19 -> 21, of which waited for: 12 -> 13; matrix products, arithmetic and copies ran while one was open for 7% -> 9% of each run, Pallas kernels for 12% -> 14%
where the time goes in v6:
time: 59.2 us; the launch traced here: 59 us
  starting transfers between devices  23.1 us (39%)
  waiting for transfers between devices  15.1 us (26%)
  Pallas kernels  13.6 us (23%)
  matrix products  4.98 us (8%)
  between operations  1.04 us (2%)
  local copies, waits for them, and re-layouts  0.79 us (1%)
    ppermute x20, starting transfers between devices, swap(): lax.ppermute(x, axis, [(i, i ^ bit) for i in range(lax.axis_size(axis))])  22 us
    ppermute x20, waiting for transfers between devices, swap(): lax.ppermute(x, axis, [(i, i ^ bit) for i in range(lax.axis_size(axis))])  12.2 us
    dot_general x12, matrix products, project(): own.append(jnp.dot(left, weight, preferred_element_type=f32))  4.98 us
    ppermute x1, waiting for transfers between devices, swap_both(): return lax.ppermute(x, ('pipe', 'expert'), pairs)  2.91 us
    pallas_call x1, Pallas kernels, on_device(): call(functools.partial(weight_kernel, scale, block), [shape((d_part, f_pa...  2.8 us
    pallas_call x3, Pallas kernels, on_device(): call(functools.partial(act_kernel, top_count), grad_shapes(piece), 'svvvv...  2.37 us
    pallas_call x1, Pallas kernels, on_device(): call(functools.partial(owner_kernel, d_part, packed), (shape(tokens.shape...  1.49 us
    pallas_call x1, Pallas kernels, on_device(): call(functools.partial(last_act_kernel, d_part, top_count, pipe_size), gr...  1.44 us
  transfers between devices with their start and end apart: 21, of which 13 were waited for; matrix products, arithmetic and copies ran while one was open for 9% of the time, Pallas kernels for 14%

profile of v6, /device:TPU:0, one launch (start us, length us, event | category | flops | bytes accessed | tf_op | source)
XLA Modules:
  0.0 59.0 jit_solution(3388924933163243142)
XLA Ops:
  0.7 1.1 %prep.1 = (bf16[16,1920]{1,0:T(8,128)(2,1)S(1)}, bf16[16,1920]{1,0:T(8,128)(2,1)S(1)}) custom-call(bf16[2,4,3584]{2,1,0:T(4,128)(2,1)} %tok_hbm.1, bf16[2,4,3584]{2,1,0:T(4,128)(2,1)} %cot_hbm.1, s32[2,2,4]{2,1,0:T(2,128)} %bitcast.77, bf16[2,2,4]{2,1,0:T(2,128)(2,1)} %bitcast.78), custom_call_target="tpu_custom_call" | custom-call | tf_op jit(solution)/shard_map/prep/pallas_call | solution.py:336
  1.8 3.0 %collective-permute-start = (bf16[16,1920]{1,0:T(8,128)(2,1)S(1)}, bf16[16,1920]{1,0:T(8,128)(2,1)S(1)}, u32[]{:S(2)}, u32[]{:S(2)}) collective-permute-start(bf16[16,1920]{1,0:T(8,128)(2,1)S(1)} %get-tuple-element.87), channel_id=1, source_target_pairs={{0,16},{16,0},{1,17},{17,1},{2,18},{18,2},{3,19},{19,3},{4,20},{20... | collective-permute-start | bytes 184328 | tf_op jit(solution)/shard_map/ppermute | solution.py:29
  4.9 2.1 %collective-permute-done.refs_1_ = bf16[16,1920]{1,0:T(8,128)(2,1)S(1)} collective-permute-done((bf16[16,1920]{1,0:T(8,128)(2,1)S(1)}, bf16[16,1920]{1,0:T(8,128)(2,1)S(1)}, u32[]{:S(2)}, u32[]{:S(2)}) %collective-permute-start) | collective-permute-done | bytes 61472 | tf_op jit(solution)/shard_map/ppermute | solution.py:29
  7.0 1.1 %pack.1 = (bf16[24,1920]{1,0:T(8,128)(2,1)S(1)}, bf16[24,1920]{1,0:T(8,128)(2,1)S(1)}, bf16[24,1920]{1,0:T(8,128)(2,1)S(1)}, bf16[24,1920]{1,0:T(8,128)(2,1)S(1)}, f32[2,8,256]{2,1,0:T(8,128)S(1)}) custom-call(s32[2]{0:T(128)S(1)} %pad_add_fusion.where_ref, bf16[16,1920]{1,0:T(8,128)(2,1)S(1)} %get-tuple-element.88.refs_0_, ...), custom_call_target="tpu_custom_call" | custom-call | tf_op jit(solution)/shard_map/pack/pallas_call | solution.py:356
  8.1 2.2 %collective-permute-start.1 = (bf16[24,1920]{1,0:T(8,128)(2,1)S(1)}, bf16[24,1920]{1,0:T(8,128)(2,1)S(1)}, u32[]{:S(2)}, u32[]{:S(2)}) collective-permute-start(bf16[24,1920]{1,0:T(8,128)(2,1)S(1)} %get-tuple-element.46), channel_id=1, source_target_pairs={{0,4},{1,5},{2,6},{3,7},{4,0},{5,1},{6,2},{7,3},{8,12},{9,13},{10,... | collective-permute-start | bytes 276488 | tf_op jit(solution)/shard_map/ppermute | solution.py:29
  10.3 2.6 %collective-permute-start.4 = (bf16[24,1920]{1,0:T(8,128)(2,1)S(1)}, bf16[24,1920]{1,0:T(8,128)(2,1)S(1)}, u32[]{:S(2)}, u32[]{:S(2)}) collective-permute-start(bf16[24,1920]{1,0:T(8,128)(2,1)S(1)} %get-tuple-element.47), channel_id=1, source_target_pairs={{0,8},{1,9},{2,10},{3,11},{4,12},{5,13},{6,14},{7,15},{8,0},{9,1},... | collective-permute-start | bytes 276488 | tf_op jit(solution)/shard_map/ppermute | solution.py:29
  12.9 0.9 %collective-permute-done.1.refs_1_ = bf16[24,1920]{1,0:T(8,128)(2,1)S(1)} collective-permute-done((bf16[24,1920]{1,0:T(8,128)(2,1)S(1)}, bf16[24,1920]{1,0:T(8,128)(2,1)S(1)}, u32[]{:S(2)}, u32[]{:S(2)}) %collective-permute-start.1) | collective-permute-done | bytes 92192 | tf_op jit(solution)/shard_map/ppermute | solution.py:29
  13.9 1.9 %collective-permute-start.7 = (bf16[2,24,1920]{2,1,0:T(8,128)(2,1)S(1)}, bf16[2,24,1920]{2,1,0:T(8,128)(2,1)S(1)}, u32[]{:S(2)}, u32[]{:S(2)}) collective-permute-start(bf16[2,24,1920]{2,1,0:T(8,128)(2,1)S(1)} %join.2), channel_id=1, source_target_pairs={{0,2},{1,3},{2,0},{3,1},{4,6},{5,7},{6,4},{7,5},{8,10},{9,11},{10,... | collective-permute-start | bytes 552968 | tf_op jit(solution)/shard_map/ppermute | solution.py:29
  16.8 0.7 %copy-done.2 = bf16[1792,512]{1,0:T(8,128)(2,1)S(1)} copy-done((bf16[1792,512]{1,0:T(8,128)(2,1)S(1)}, bf16[1792,512]{1,0:T(8,128)(2,1)}, u32[]{:S(2)}) %copy-start.2) | copy-done | bytes 1835032
  18.1 1.2 %collective-permute-done.5.refs_1_ = bf16[24,1920]{1,0:T(8,128)(2,1)S(1)} collective-permute-done((bf16[24,1920]{1,0:T(8,128)(2,1)S(1)}, bf16[24,1920]{1,0:T(8,128)(2,1)S(1)}, u32[]{:S(2)}, u32[]{:S(2)}) %collective-permute-start.5) | collective-permute-done | bytes 92192 | tf_op jit(solution)/shard_map/ppermute | solution.py:29
  19.5 1.6 %collective-permute-start.6 = (bf16[2,24,1920]{2,1,0:T(8,128)(2,1)S(1)}, bf16[2,24,1920]{2,1,0:T(8,128)(2,1)S(1)}, u32[]{:S(2)}, u32[]{:S(2)}) collective-permute-start(bf16[2,24,1920]{2,1,0:T(8,128)(2,1)S(1)} %join.3), channel_id=1, source_target_pairs={{0,2},{1,3},{2,0},{3,1},{4,6},{5,7},{6,4},{7,5},{8,10},{9,11},{10,... | collective-permute-start | bytes 552968 | tf_op jit(solution)/shard_map/ppermute | solution.py:29
  21.1 1.6 %collective-permute-start.3 = (bf16[3,48,512]{2,1,0:T(8,128)(2,1)S(1)}, bf16[3,48,512]{2,1,0:T(8,128)(2,1)S(1)}, u32[]{:S(2)}, u32[]{:S(2)}) collective-permute-start(bf16[3,48,512]{2,1,0:T(8,128)(2,1)S(1)} %pad_maximum_fusion.3), channel_id=1, source_target_pairs={{0,16},{16,0},{1,17},{17,1},{2,18},{18,2},{3,19},{19,3},{4,20},{20... | collective-permute-start | bytes 442376 | tf_op jit(solution)/shard_map/ppermute | solution.py:29
  26.6 1.6 %collective-permute-start.10 = (bf16[3,48,512]{2,1,0:T(8,128)(2,1)S(1)}, bf16[3,48,512]{2,1,0:T(8,128)(2,1)S(1)}, u32[]{:S(2)}, u32[]{:S(2)}) collective-permute-start(bf16[3,48,512]{2,1,0:T(8,128)(2,1)S(1)} %pad_maximum_fusion.4), channel_id=1, source_target_pairs={{0,16},{16,0},{1,17},{17,1},{2,18},{18,2},{3,19},{19,3},{4,20},{20... | collective-permute-start | bytes 442376 | tf_op jit(solution)/shard_map/ppermute | solution.py:29
  28.1 1.4 %collective-permute-done.9 = bf16[2,24,1920]{2,1,0:T(8,128)(2,1)S(1)} collective-permute-done((bf16[2,24,1920]{2,1,0:T(8,128)(2,1)S(1)}, bf16[2,24,1920]{2,1,0:T(8,128)(2,1)S(1)}, u32[]{:S(2)}, u32[]{:S(2)}) %collective-permute-start.9) | collective-permute-done | bytes 184352 | tf_op jit(solution)/shard_map/ppermute | solution.py:29
  30.9 0.6 %collective-permute-start.13 = (bf16[3,48,512]{2,1,0:T(8,128)(2,1)S(1)}, bf16[3,48,512]{2,1,0:T(8,128)(2,1)S(1)}, u32[]{:S(2)}, u32[]{:S(2)}) collective-permute-start(bf16[3,48,512]{2,1,0:T(8,128)(2,1)S(1)} %pad_maximum_fusion.6), channel_id=1, source_target_pairs={{0,16},{16,0},{1,17},{17,1},{2,18},{18,2},{3,19},{19,3},{4,20},{20... | collective-permute-start | bytes 442376 | tf_op jit(solution)/shard_map/ppermute | solution.py:29
  33.2 0.8 %act.5 = (bf16[2,24,512]{2,1,0:T(8,128)(2,1)S(1)}, bf16[2,24,512]{2,1,0:T(8,128)(2,1)S(1)}, bf16[2,24,512]{2,1,0:T(8,128)(2,1)S(1)}, bf16[2,24,128]{2,1,0:T(8,128)(2,1)S(1)}) custom-call(s32[2]{0:T(128)S(1)} %pad_add_fusion.where_ref, bf16[48,128]{1,0:T(8,128)(2,1)S(1)} %maximum_bitcast_fusion.1.refs_0_, f32[48,512]{1,0:T(8,128)S(1)} %fusion.13.refs_1_, ...), custom_call_target="tpu_custom_call" | custom-call | tf_op jit(solution)/shard_map/act/pallas_call | solution.py:433
  34.0 1.8 %collective-permute-done.10.refs_4_ = bf16[3,48,512]{2,1,0:T(8,128)(2,1)S(1)} collective-permute-done((bf16[3,48,512]{2,1,0:T(8,128)(2,1)S(1)}, bf16[3,48,512]{2,1,0:T(8,128)(2,1)S(1)}, u32[]{:S(2)}, u32[]{:S(2)}) %collective-permute-start.10) | collective-permute-done | bytes 147488 | tf_op jit(solution)/shard_map/ppermute | solution.py:29
  35.8 0.8 %act.4 = (bf16[2,24,512]{2,1,0:T(8,128)(2,1)S(1)}, bf16[2,24,512]{2,1,0:T(8,128)(2,1)S(1)}, bf16[2,24,512]{2,1,0:T(8,128)(2,1)S(1)}, bf16[2,24,128]{2,1,0:T(8,128)(2,1)S(1)}) custom-call(s32[2]{0:T(128)S(1)} %pad_add_fusion.where_ref, bf16[48,128]{1,0:T(8,128)(2,1)S(1)} %slice_bitcast_fusion.4.refs_0_, f32[48,512]{1,0:T(8,128)S(1)} %fusion.11.refs_1_, ...), custom_call_target="tpu_custom_call" | custom-call | tf_op jit(solution)/shard_map/act/pallas_call | solution.py:433
  36.6 0.8 %act.3 = (bf16[2,24,512]{2,1,0:T(8,128)(2,1)S(1)}, bf16[2,24,512]{2,1,0:T(8,128)(2,1)S(1)}, bf16[2,24,512]{2,1,0:T(8,128)(2,1)S(1)}, bf16[2,24,128]{2,1,0:T(8,128)(2,1)S(1)}) custom-call(s32[2]{0:T(128)S(1)} %pad_add_fusion.where_ref, bf16[48,128]{1,0:T(8,128)(2,1)S(1)} %slice_bitcast_fusion.5.refs_0_, f32[48,512]{1,0:T(8,128)S(1)} %fusion.9.refs_2_.refs_1_, ...), custom_call_target="tpu_custom_call" | custom-call | tf_op jit(solution)/shard_map/act/pallas_call | solution.py:433
  37.4 0.7 %collective-permute-done.13.refs_4_ = bf16[3,48,512]{2,1,0:T(8,128)(2,1)S(1)} collective-permute-done((bf16[3,48,512]{2,1,0:T(8,128)(2,1)S(1)}, bf16[3,48,512]{2,1,0:T(8,128)(2,1)S(1)}, u32[]{:S(2)}, u32[]{:S(2)}) %collective-permute-start.13) | collective-permute-done | bytes 147488 | tf_op jit(solution)/shard_map/ppermute | solution.py:29
  38.2 1.4 %last_act.1 = (bf16[2,24,512]{2,1,0:T(8,128)(2,1)S(1)}, bf16[2,24,512]{2,1,0:T(8,128)(2,1)S(1)}, bf16[2,24,512]{2,1,0:T(8,128)(2,1)S(1)}, bf16[2,24,128]{2,1,0:T(8,128)(2,1)S(1)}, bf16[2,2,24,1920]{3,2,1,0:T(8,128)(2,1)S(1)}) custom-call(s32[2]{0:T(128)S(1)} %pad_add_fusion.where_ref, bf16[48,128]{1,0:T(8,128)(2,1)S(1)} %fusion.5.refs_0_, ...), custom_call_target="tpu_custom_call" | custom-call | tf_op jit(solution)/shard_map/last_act/pallas_call | solution.py:438
  39.7 1.3 %own_back.1.a_ref = bf16[2,2,24,1920]{3,2,1,0:T(8,128)(2,1)S(1)} custom-call(s32[2]{0:T(128)S(1)} %pad_add_fusion.where_ref, bf16[2,24,512]{2,1,0:T(8,128)(2,1)S(1)} %get-tuple-element.49.refs_5_.refs_0_, bf16[2,24,512]{2,1,0:T(8,128)(2,1)S(1)} %get-tuple-element.50.refs_6_.refs_1_, bf16[2,24,512]{2,1,0:T(8,128)(2,1)S(1)} %get-tuple-element.51.refs_7_.refs_2_, ...), custom_call_target="tpu_custom_call" | custom-call | tf_op jit(solution)/shard_map/own_back/pallas_call | solution.py:446
  41.5 1.2 %collective-permute-start.15 = (bf16[24,1920]{1,0:T(8,128)(2,1)S(1)}, bf16[24,1920]{1,0:T(8,128)(2,1)S(1)}, u32[]{:S(2)}, u32[]{:S(2)}) collective-permute-start(bf16[24,1920]{1,0:T(8,128)(2,1)S(1)} %get-tuple-element.67), channel_id=1, source_target_pairs={{0,18},{1,19},{2,16},{3,17},{4,22},{5,23},{6,20},{7,21},{8,26},{9,... | collective-permute-start | bytes 276488 | tf_op jit(solution)/shard_map/ppermute | solution.py:35
  42.6 0.9 %collective-permute-start.16 = (bf16[24,1920]{1,0:T(8,128)(2,1)S(1)}, bf16[24,1920]{1,0:T(8,128)(2,1)S(1)}, u32[]{:S(2)}, u32[]{:S(2)}) collective-permute-start(bf16[24,1920]{1,0:T(8,128)(2,1)S(1)} %get-tuple-element.68), channel_id=1, source_target_pairs={{0,16},{16,0},{1,17},{17,1},{2,18},{18,2},{3,19},{19,3},{4,20},{20... | collective-permute-start | bytes 276488 | tf_op jit(solution)/shard_map/ppermute | solution.py:29
  43.5 1.5 %collective-permute-start.17 = (bf16[24,1920]{1,0:T(8,128)(2,1)S(1)}, bf16[24,1920]{1,0:T(8,128)(2,1)S(1)}, u32[]{:S(2)}, u32[]{:S(2)}) collective-permute-start(bf16[24,1920]{1,0:T(8,128)(2,1)S(1)} %get-tuple-element.69), channel_id=1, source_target_pairs={{0,2},{1,3},{2,0},{3,1},{4,6},{5,7},{6,4},{7,5},{8,10},{9,11},{10,... | collective-permute-start | bytes 276488 | tf_op jit(solution)/shard_map/ppermute | solution.py:29
  45.0 2.9 %collective-permute-done.15.b_ref = bf16[24,1920]{1,0:T(8,128)(2,1)S(1)} collective-permute-done((bf16[24,1920]{1,0:T(8,128)(2,1)S(1)}, bf16[24,1920]{1,0:T(8,128)(2,1)S(1)}, u32[]{:S(2)}, u32[]{:S(2)}) %collective-permute-start.15) | collective-permute-done | bytes 92192 | tf_op jit(solution)/shard_map/ppermute | solution.py:35
  48.2 1.0 %collective-permute-done.17.d_ref = bf16[24,1920]{1,0:T(8,128)(2,1)S(1)} collective-permute-done((bf16[24,1920]{1,0:T(8,128)(2,1)S(1)}, bf16[24,1920]{1,0:T(8,128)(2,1)S(1)}, u32[]{:S(2)}, u32[]{:S(2)}) %collective-permute-start.17) | collective-permute-done | bytes 92192 | tf_op jit(solution)/shard_map/ppermute | solution.py:29
  49.2 2.4 %collective-permute-start.18 = (bf16[8,2816]{1,0:T(8,128)(2,1)S(1)}, bf16[8,2816]{1,0:T(8,128)(2,1)S(1)}, u32[]{:S(2)}, u32[]{:S(2)}) collective-permute-start(bf16[8,2816]{1,0:T(8,128)(2,1)S(1)} %get-tuple-element.71), channel_id=1, source_target_pairs={{0,8},{1,9},{2,10},{3,11},{4,12},{5,13},{6,14},{7,15},{8,0},{9,1},... | collective-permute-start | bytes 135176 | tf_op jit(solution)/shard_map/ppermute | solution.py:29
  51.6 1.3 %collective-permute-start.19 = (bf16[8,2816]{1,0:T(8,128)(2,1)S(1)}, bf16[8,2816]{1,0:T(8,128)(2,1)S(1)}, u32[]{:S(2)}, u32[]{:S(2)}) collective-permute-start(bf16[8,2816]{1,0:T(8,128)(2,1)S(1)} %get-tuple-element.72), channel_id=1, source_target_pairs={{0,12},{1,13},{2,14},{3,15},{4,8},{5,9},{6,10},{7,11},{8,4},{9,5},... | collective-permute-start | bytes 135176 | tf_op jit(solution)/shard_map/ppermute | solution.py:29
  53.0 2.8 %weight_grads.1 = (bf16[1792,512]{1,0:T(8,128)(2,1)}, bf16[1792,512]{1,0:T(8,128)(2,1)}, bf16[1792,512]{1,0:T(8,128)(2,1)}) custom-call(bf16[1792,192]{1,0:T(8,128)(2,1)S(1)} %flip.2.refs_19_.tok_ref, bf16[1792,192]{1,0:T(8,128)(2,1)S(1)} %flip.3.refs_20_.cot_ref, bf16[2,24,512]{2,1,0:T(8,128)(2,1)S(1)} %get-tuple-element.49.refs_5_.refs_0_, ...), custom_call_target="tpu_custom_call" | custom-call | tf_op jit(solution)/shard_map/weight_grads/pallas_call | solution.py:490
  55.8 1.7 %collective-permute-done.19.refs_2_ = bf16[8,2816]{1,0:T(8,128)(2,1)S(1)} collective-permute-done((bf16[8,2816]{1,0:T(8,128)(2,1)S(1)}, bf16[8,2816]{1,0:T(8,128)(2,1)S(1)}, u32[]{:S(2)}, u32[]{:S(2)}) %collective-permute-start.19) | collective-permute-done | bytes 45088 | tf_op jit(solution)/shard_map/ppermute | solution.py:29
  57.5 1.5 %owner.1 = (bf16[2,4,3584]{2,1,0:T(4,128)(2,1)}, f32[2,2,4]{2,1,0:T(2,128)}) custom-call(s32[2]{0:T(128)S(1)} %pad_add_fusion.where_ref, f32[2,8,256]{2,1,0:T(8,128)S(1)} %get-tuple-element.44.refs_1_.place_ref, bf16[8,2816]{1,0:T(8,128)(2,1)S(1)} %get-tuple-element.70.refs_0_, bf16[8,2816]{1,0:T(8,128)(2,1)S(1)} %collective-permute-done.18.refs_1_, ...), custom_call_target="tpu_custom_call" | custom-call | tf_op jit(solution)/shard_map/owner/pallas_call | solution.py:503
  (74 shorter events, 9.7 us)
Async XLA Ops:
  0.6 15.8 %copy-start = (bf16[1792,512]{1,0:T(8,128)(2,1)S(1)}, bf16[1792,512]{1,0:T(8,128)(2,1)}, u32[]{:S(2)}) copy-start(bf16[1792,512]{1,0:T(8,128)(2,1)} %param.13) | copy-start | bytes 5505028
  1.8 5.2 %collective-permute-start = (bf16[16,1920]{1,0:T(8,128)(2,1)S(1)}, bf16[16,1920]{1,0:T(8,128)(2,1)S(1)}, u32[]{:S(2)}, u32[]{:S(2)}) collective-permute-start(bf16[16,1920]{1,0:T(8,128)(2,1)S(1)} %get-tuple-element.87), channel_id=1, source_target_pairs={{0,16},{16,0},{1,17},{17,1},{2,18},{18,2},{3,19},{19,3},{4,20},{20... | collective-permute-start | bytes 184328 | tf_op jit(solution)/shard_map/ppermute | solution.py:29
  8.1 5.6 %collective-permute-start.1 = (bf16[24,1920]{1,0:T(8,128)(2,1)S(1)}, bf16[24,1920]{1,0:T(8,128)(2,1)S(1)}, u32[]{:S(2)}, u32[]{:S(2)}) collective-permute-start(bf16[24,1920]{1,0:T(8,128)(2,1)S(1)} %get-tuple-element.46), channel_id=1, source_target_pairs={{0,4},{1,5},{2,6},{3,7},{4,0},{5,1},{6,2},{7,3},{8,12},{9,13},{10,... | collective-permute-start | bytes 276488 | tf_op jit(solution)/shard_map/ppermute | solution.py:29
  10.3 7.8 %collective-permute-start.4 = (bf16[24,1920]{1,0:T(8,128)(2,1)S(1)}, bf16[24,1920]{1,0:T(8,128)(2,1)S(1)}, u32[]{:S(2)}, u32[]{:S(2)}) collective-permute-start(bf16[24,1920]{1,0:T(8,128)(2,1)S(1)} %get-tuple-element.47), channel_id=1, source_target_pairs={{0,8},{1,9},{2,10},{3,11},{4,12},{5,13},{6,14},{7,15},{8,0},{9,1},... | collective-permute-start | bytes 276488 | tf_op jit(solution)/shard_map/ppermute | solution.py:29
  12.9 6.5 %collective-permute-start.5 = (bf16[24,1920]{1,0:T(8,128)(2,1)S(1)}, bf16[24,1920]{1,0:T(8,128)(2,1)S(1)}, u32[]{:S(2)}, u32[]{:S(2)}) collective-permute-start(bf16[24,1920]{1,0:T(8,128)(2,1)S(1)} %get-tuple-element.48), channel_id=1, source_target_pairs={{0,12},{1,13},{2,14},{3,15},{4,8},{5,9},{6,10},{7,11},{8,4},{9,5},... | collective-permute-start | bytes 276488 | tf_op jit(solution)/shard_map/ppermute | solution.py:29
  13.8 2.1 %collective-permute-start.2 = (bf16[2,24,1920]{2,1,0:T(8,128)(2,1)S(1)}, bf16[2,24,1920]{2,1,0:T(8,128)(2,1)S(1)}, u32[]{:S(2)}, u32[]{:S(2)}) collective-permute-start(bf16[2,24,1920]{2,1,0:T(8,128)(2,1)S(1)} %join.2), channel_id=1, source_target_pairs={{0,1},{1,0},{2,3},{3,2},{4,5},{5,4},{6,7},{7,6},{8,9},{9,8},{10,11... | collective-permute-start | bytes 552968 | tf_op jit(solution)/shard_map/ppermute | solution.py:29
  13.9 2.0 %copy-start.1 = (bf16[1792,512]{1,0:T(8,128)(2,1)S(1)}, bf16[1792,512]{1,0:T(8,128)(2,1)}, u32[]{:S(2)}) copy-start(bf16[1792,512]{1,0:T(8,128)(2,1)} %weight_ref.3) | copy-start | bytes 5505028
  13.9 8.7 %collective-permute-start.7 = (bf16[2,24,1920]{2,1,0:T(8,128)(2,1)S(1)}, bf16[2,24,1920]{2,1,0:T(8,128)(2,1)S(1)}, u32[]{:S(2)}, u32[]{:S(2)}) collective-permute-start(bf16[2,24,1920]{2,1,0:T(8,128)(2,1)S(1)} %join.2), channel_id=1, source_target_pairs={{0,2},{1,3},{2,0},{3,1},{4,6},{5,7},{6,4},{7,5},{8,10},{9,11},{10,... | collective-permute-start | bytes 552968 | tf_op jit(solution)/shard_map/ppermute | solution.py:29
  16.0 1.5 %copy-start.2 = (bf16[1792,512]{1,0:T(8,128)(2,1)S(1)}, bf16[1792,512]{1,0:T(8,128)(2,1)}, u32[]{:S(2)}) copy-start(bf16[1792,512]{1,0:T(8,128)(2,1)} %weight_ref.2) | copy-start | bytes 5505028
  19.4 3.3 %collective-permute-start.11 = (bf16[2,24,1920]{2,1,0:T(8,128)(2,1)S(1)}, bf16[2,24,1920]{2,1,0:T(8,128)(2,1)S(1)}, u32[]{:S(2)}, u32[]{:S(2)}) collective-permute-start(bf16[2,24,1920]{2,1,0:T(8,128)(2,1)S(1)} %join.3), channel_id=1, source_target_pairs={{0,1},{1,0},{2,3},{3,2},{4,5},{5,4},{6,7},{7,6},{8,9},{9,8},{10,11... | collective-permute-start | bytes 552968 | tf_op jit(solution)/shard_map/ppermute | solution.py:29
  19.5 8.6 %collective-permute-start.6 = (bf16[2,24,1920]{2,1,0:T(8,128)(2,1)S(1)}, bf16[2,24,1920]{2,1,0:T(8,128)(2,1)S(1)}, u32[]{:S(2)}, u32[]{:S(2)}) collective-permute-start(bf16[2,24,1920]{2,1,0:T(8,128)(2,1)S(1)} %join.3), channel_id=1, source_target_pairs={{0,2},{1,3},{2,0},{3,1},{4,6},{5,7},{6,4},{7,5},{8,10},{9,11},{10,... | collective-permute-start | bytes 552968 | tf_op jit(solution)/shard_map/ppermute | solution.py:29
  21.1 15.5 %collective-permute-start.3 = (bf16[3,48,512]{2,1,0:T(8,128)(2,1)S(1)}, bf16[3,48,512]{2,1,0:T(8,128)(2,1)S(1)}, u32[]{:S(2)}, u32[]{:S(2)}) collective-permute-start(bf16[3,48,512]{2,1,0:T(8,128)(2,1)S(1)} %pad_maximum_fusion.3), channel_id=1, source_target_pairs={{0,16},{16,0},{1,17},{17,1},{2,18},{18,2},{3,19},{19,3},{4,20},{20... | collective-permute-start | bytes 442376 | tf_op jit(solution)/shard_map/ppermute | solution.py:29
  22.7 1.4 %collective-permute-start.8 = (bf16[2,24,1920]{2,1,0:T(8,128)(2,1)S(1)}, bf16[2,24,1920]{2,1,0:T(8,128)(2,1)S(1)}, u32[]{:S(2)}, u32[]{:S(2)}) collective-permute-start(bf16[2,24,1920]{2,1,0:T(8,128)(2,1)S(1)} %collective-permute-done.7), channel_id=1, source_target_pairs={{0,1},{1,0},{2,3},{3,2},{4,5},{5,4},{6,7},{7,6},{8,9},{9,8},{10,11... | collective-permute-start | bytes 552968 | tf_op jit(solution)/shard_map/ppermute | solution.py:29
  25.9 7.3 %collective-permute-start.12 = (bf16[3,48,512]{2,1,0:T(8,128)(2,1)S(1)}, bf16[3,48,512]{2,1,0:T(8,128)(2,1)S(1)}, u32[]{:S(2)}, u32[]{:S(2)}) collective-permute-start(bf16[3,48,512]{2,1,0:T(8,128)(2,1)S(1)} %pad_maximum_fusion.5), channel_id=1, source_target_pairs={{0,16},{16,0},{1,17},{17,1},{2,18},{18,2},{3,19},{19,3},{4,20},{20... | collective-permute-start | bytes 442376 | tf_op jit(solution)/shard_map/ppermute | solution.py:29
  26.6 9.3 %collective-permute-start.10 = (bf16[3,48,512]{2,1,0:T(8,128)(2,1)S(1)}, bf16[3,48,512]{2,1,0:T(8,128)(2,1)S(1)}, u32[]{:S(2)}, u32[]{:S(2)}) collective-permute-start(bf16[3,48,512]{2,1,0:T(8,128)(2,1)S(1)} %pad_maximum_fusion.4), channel_id=1, source_target_pairs={{0,16},{16,0},{1,17},{17,1},{2,18},{18,2},{3,19},{19,3},{4,20},{20... | collective-permute-start | bytes 442376 | tf_op jit(solution)/shard_map/ppermute | solution.py:29
  28.1 1.4 %collective-permute-start.9 = (bf16[2,24,1920]{2,1,0:T(8,128)(2,1)S(1)}, bf16[2,24,1920]{2,1,0:T(8,128)(2,1)S(1)}, u32[]{:S(2)}, u32[]{:S(2)}) collective-permute-start(bf16[2,24,1920]{2,1,0:T(8,128)(2,1)S(1)} %tie.5), channel_id=1, source_target_pairs={{0,1},{1,0},{2,3},{3,2},{4,5},{5,4},{6,7},{7,6},{8,9},{9,8},{10,11... | collective-permute-start | bytes 552968 | tf_op jit(solution)/shard_map/ppermute | solution.py:29
  30.9 7.3 %collective-permute-start.13 = (bf16[3,48,512]{2,1,0:T(8,128)(2,1)S(1)}, bf16[3,48,512]{2,1,0:T(8,128)(2,1)S(1)}, u32[]{:S(2)}, u32[]{:S(2)}) collective-permute-start(bf16[3,48,512]{2,1,0:T(8,128)(2,1)S(1)} %pad_maximum_fusion.6), channel_id=1, source_target_pairs={{0,16},{16,0},{1,17},{17,1},{2,18},{18,2},{3,19},{19,3},{4,20},{20... | collective-permute-start | bytes 442376 | tf_op jit(solution)/shard_map/ppermute | solution.py:29
  39.6 1.8 %collective-permute-start.14 = (bf16[2,2,24,1920]{3,2,1,0:T(8,128)(2,1)S(1)}, bf16[2,2,24,1920]{3,2,1,0:T(8,128)(2,1)S(1)}, u32[]{:S(2)}, u32[]{:S(2)}) collective-permute-start(bf16[2,2,24,1920]{3,2,1,0:T(8,128)(2,1)S(1)} %get-tuple-element.65.refs_18_), channel_id=1, source_target_pairs={{0,1},{1,0},{2,3},{3,2},{4,5},{5,4},{6,7},{7,6},{8,9},{9,8},{10,11... | collective-permute-start | bytes 1105928 | tf_op jit(solution)/shard_map/ppermute | solution.py:29
  41.5 6.5 %collective-permute-start.15 = (bf16[24,1920]{1,0:T(8,128)(2,1)S(1)}, bf16[24,1920]{1,0:T(8,128)(2,1)S(1)}, u32[]{:S(2)}, u32[]{:S(2)}) collective-permute-start(bf16[24,1920]{1,0:T(8,128)(2,1)S(1)} %get-tuple-element.67), channel_id=1, source_target_pairs={{0,18},{1,19},{2,16},{3,17},{4,22},{5,23},{6,20},{7,21},{8,26},{9,... | collective-permute-start | bytes 276488 | tf_op jit(solution)/shard_map/ppermute | solution.py:35
  42.6 5.5 %collective-permute-start.16 = (bf16[24,1920]{1,0:T(8,128)(2,1)S(1)}, bf16[24,1920]{1,0:T(8,128)(2,1)S(1)}, u32[]{:S(2)}, u32[]{:S(2)}) collective-permute-start(bf16[24,1920]{1,0:T(8,128)(2,1)S(1)} %get-tuple-element.68), channel_id=1, source_target_pairs={{0,16},{16,0},{1,17},{17,1},{2,18},{18,2},{3,19},{19,3},{4,20},{20... | collective-permute-start | bytes 276488 | tf_op jit(solution)/shard_map/ppermute | solution.py:29
  43.5 5.6 %collective-permute-start.17 = (bf16[24,1920]{1,0:T(8,128)(2,1)S(1)}, bf16[24,1920]{1,0:T(8,128)(2,1)S(1)}, u32[]{:S(2)}, u32[]{:S(2)}) collective-permute-start(bf16[24,1920]{1,0:T(8,128)(2,1)S(1)} %get-tuple-element.69), channel_id=1, source_target_pairs={{0,2},{1,3},{2,0},{3,1},{4,6},{5,7},{6,4},{7,5},{8,10},{9,11},{10,... | collective-permute-start | bytes 276488 | tf_op jit(solution)/shard_map/ppermute | solution.py:29
  49.2 6.6 %collective-permute-start.18 = (bf16[8,2816]{1,0:T(8,128)(2,1)S(1)}, bf16[8,2816]{1,0:T(8,128)(2,1)S(1)}, u32[]{:S(2)}, u32[]{:S(2)}) collective-permute-start(bf16[8,2816]{1,0:T(8,128)(2,1)S(1)} %get-tuple-element.71), channel_id=1, source_target_pairs={{0,8},{1,9},{2,10},{3,11},{4,12},{5,13},{6,14},{7,15},{8,0},{9,1},... | collective-permute-start | bytes 135176 | tf_op jit(solution)/shard_map/ppermute | solution.py:29
  51.6 5.9 %collective-permute-start.19 = (bf16[8,2816]{1,0:T(8,128)(2,1)S(1)}, bf16[8,2816]{1,0:T(8,128)(2,1)S(1)}, u32[]{:S(2)}, u32[]{:S(2)}) collective-permute-start(bf16[8,2816]{1,0:T(8,128)(2,1)S(1)} %get-tuple-element.72), channel_id=1, source_target_pairs={{0,12},{1,13},{2,14},{3,15},{4,8},{5,9},{6,10},{7,11},{8,4},{9,5},... | collective-permute-start | bytes 135176 | tf_op jit(solution)/shard_map/ppermute | solution.py:29
  53.0 4.5 %collective-permute-start.20 = (bf16[8,2816]{1,0:T(8,128)(2,1)S(1)}, bf16[8,2816]{1,0:T(8,128)(2,1)S(1)}, u32[]{:S(2)}, u32[]{:S(2)}) collective-permute-start(bf16[8,2816]{1,0:T(8,128)(2,1)S(1)} %get-tuple-element.73), channel_id=1, source_target_pairs={{0,4},{1,5},{2,6},{3,7},{4,0},{5,1},{6,2},{7,3},{8,12},{9,13},{10,... | collective-permute-start | bytes 135176 | tf_op jit(solution)/shard_map/ppermute | solution.py:29

commit v7 on v6

--- a/solution.py
+++ b/solution.py
@@ -85,14 +85,14 @@
         blocks = [jnp.where(first, blocks[0], blocks[1]), jnp.where(first, blocks[1], blocks[0])]
     rows = jnp.concatenate(blocks, 0)
     extras = rows[:, width - LANES :].astype(f32)
-    row = lax.broadcasted_iota(i32, (total, total), 0)
-    other = lax.broadcasted_iota(i32, (total, total), 1)
-    earlier = ((other < row) & (other // tok_count == row // tok_count)).astype(bf16)
     at = (lax.broadcasted_iota(i32, (total, LANES), 1) ^ me).astype(f32)
     routed = jnp.zeros((total, LANES), f32)
     for k in range(top_count):
         routed = jnp.where(extras[:, k : k + 1] == at, 1.0, routed)
-    position = jnp.dot(earlier, routed.astype(bf16), preferred_element_type=f32)
+    at_row = lax.broadcasted_iota(i32, (total, LANES), 0) % tok_count
+    position = jnp.zeros((total, LANES), f32)
+    for d in range(1, tok_count):
+        position = position + jnp.where(at_row >= d, pltpu.roll(routed, d, 0), 0.0)
     index = lax.broadcasted_iota(i32, (total, 1), 0)
     within = index % both_rows
     block = within % own_rows // tok_count
@@ -195,7 +195,7 @@
 
 def fold_kernel(a_ref, b_ref, *out_refs):
     for i, ref in enumerate(out_refs):
-        here = i // a_ref.shape[1], i % a_ref.shape[1]
+        here = i // a_ref.shape[1], i % a_ref.shape[1], slice(None), slice(0, ref.shape[1])
         ref[...] = (a_ref[here].astype(f32) + b_ref[here].astype(f32)).astype(bf16)
 
 
@@ -398,10 +398,13 @@
     filler = tie([jnp.zeros((8, LANES), f32) + pipe.astype(f32)], place, **FILL_A)[0]
     first = tie([first], filler)[0]
     first_own = project(first)
-    later = join(1, *first_own, **JOIN_COST)
+    first_sent = jnp.stack([part.astype(bf16) for part in first_own])
+    later = join(1, *first_own, first_sent, **JOIN_COST)
     later_there = swap(later, "expert", bits[0])
-    there, here = spread(there), spread(later)
-    there_own, here_own = project(there), project(here)
+    here = spread(later)
+    here_own = project(here)
+    there = spread(tie([there], here_own[2])[0])
+    there_own = project(there)
     last = spread(tie([later_there], there_own[2])[0])
     pieces, owns = [first, there, here, last], [first_own, there_own, here_own, project(last)]
     exchanged = [exchange(rows, own) for rows, own in zip(pieces, owns)]
@@ -452,7 +455,7 @@
     )(where, *[x for grad in grads for x in grad], *flipped_weights, high)
     packed = pipe_size == 2 and group_size == 4
     if packed:
-        parts = call(fold_kernel, [shape((padded, out_width), bf16) for _ in range(4)], "vv", "fold")(
+        parts = call(fold_kernel, [shape((padded, w), bf16) for w in (out_width, d_part) * 2], "vv", "fold")(
             low, swap(high, "expert", bits[1])
         )
         after = parts[0]

time: 59.2 us -> 57.5 us (0.971)
  waiting for transfers between devices: 15.1 us -> 11.7 us
  starting transfers between devices: 23.1 us -> 25 us
    ppermute x20, waiting for transfers between devices: 12.2 us -> 7.65 us  [swap(): lax.ppermute(x, axis, [(i, i ^ bit) for i in range(lax.axis_size(axis))])]
    ppermute x20, starting transfers between devices: 22 us -> 23.6 us  [swap(): lax.ppermute(x, axis, [(i, i ^ bit) for i in range(lax.axis_size(axis))])]
    ppermute x1, waiting for transfers between devices: 2.91 us -> 4.03 us  [swap_both(): return lax.ppermute(x, ('pipe', 'expert'), pairs)]
  transfers between devices with their start and end apart: 21 -> 21, of which waited for: 13 -> 10; matrix products, arithmetic and copies ran while one was open for 9% -> 10% of each run, Pallas kernels for 14% -> 14%
where the time goes in v7:
time: 57.5 us; the launch traced here: 57.4 us
  starting transfers between devices  25 us (43%)
  Pallas kernels  13.5 us (23%)
  waiting for transfers between devices  11.7 us (20%)
  matrix products  5 us (9%)
  between operations  1.05 us (2%)
  local copies, waits for them, and re-layouts  0.71 us (1%)
    ppermute x20, starting transfers between devices, swap(): lax.ppermute(x, axis, [(i, i ^ bit) for i in range(lax.axis_size(axis))])  23.6 us
    ppermute x20, waiting for transfers between devices, swap(): lax.ppermute(x, axis, [(i, i ^ bit) for i in range(lax.axis_size(axis))])  7.65 us
    dot_general x12, matrix products, project(): own.append(jnp.dot(left, weight, preferred_element_type=f32))  5 us
    ppermute x1, waiting for transfers between devices, swap_both(): return lax.ppermute(x, ('pipe', 'expert'), pairs)  4.03 us
    pallas_call x1, Pallas kernels, on_device(): call(functools.partial(weight_kernel, scale, block), [shape((d_part, f_pa...  2.8 us
    pallas_call x3, Pallas kernels, on_device(): call(functools.partial(act_kernel, top_count), grad_shapes(piece), 'svvvv...  2.37 us
    pallas_call x1, Pallas kernels, on_device(): call(functools.partial(owner_kernel, d_part, packed), (shape(tokens.shape...  1.49 us
    pallas_call x1, Pallas kernels, on_device(): call(functools.partial(last_act_kernel, d_part, top_count, pipe_size), gr...  1.45 us
  transfers between devices with their start and end apart: 21, of which 10 were waited for; matrix products, arithmetic and copies ran while one was open for 10% of the time, Pallas kernels for 14%

profile of v7, /device:TPU:0, one launch (start us, length us, event | category | flops | bytes accessed | tf_op | source)
XLA Modules:
  0.0 57.4 jit_solution(11114229666610123181)
XLA Ops:
  0.7 1.1 %prep.1 = (bf16[16,1920]{1,0:T(8,128)(2,1)S(1)}, bf16[16,1920]{1,0:T(8,128)(2,1)S(1)}) custom-call(bf16[2,4,3584]{2,1,0:T(4,128)(2,1)} %tok_hbm.1, bf16[2,4,3584]{2,1,0:T(4,128)(2,1)} %cot_hbm.1, s32[2,2,4]{2,1,0:T(2,128)} %bitcast.77, bf16[2,2,4]{2,1,0:T(2,128)(2,1)} %bitcast.78), custom_call_target="tpu_custom_call" | custom-call | tf_op jit(solution)/shard_map/prep/pallas_call | solution.py:336
  1.8 3.0 %collective-permute-start = (bf16[16,1920]{1,0:T(8,128)(2,1)S(1)}, bf16[16,1920]{1,0:T(8,128)(2,1)S(1)}, u32[]{:S(2)}, u32[]{:S(2)}) collective-permute-start(bf16[16,1920]{1,0:T(8,128)(2,1)S(1)} %get-tuple-element.87), channel_id=1, source_target_pairs={{0,16},{16,0},{1,17},{17,1},{2,18},{18,2},{3,19},{19,3},{4,20},{20... | collective-permute-start | bytes 184328 | tf_op jit(solution)/shard_map/ppermute | solution.py:29
  4.9 2.1 %collective-permute-done.refs_1_ = bf16[16,1920]{1,0:T(8,128)(2,1)S(1)} collective-permute-done((bf16[16,1920]{1,0:T(8,128)(2,1)S(1)}, bf16[16,1920]{1,0:T(8,128)(2,1)S(1)}, u32[]{:S(2)}, u32[]{:S(2)}) %collective-permute-start) | collective-permute-done | bytes 61472 | tf_op jit(solution)/shard_map/ppermute | solution.py:29
  7.0 1.0 %pack.1 = (bf16[24,1920]{1,0:T(8,128)(2,1)S(1)}, bf16[24,1920]{1,0:T(8,128)(2,1)S(1)}, bf16[24,1920]{1,0:T(8,128)(2,1)S(1)}, bf16[24,1920]{1,0:T(8,128)(2,1)S(1)}, f32[2,8,256]{2,1,0:T(8,128)S(1)}) custom-call(s32[2]{0:T(128)S(1)} %pad_add_fusion.where_ref, bf16[16,1920]{1,0:T(8,128)(2,1)S(1)} %get-tuple-element.88.refs_0_, ...), custom_call_target="tpu_custom_call" | custom-call | tf_op jit(solution)/shard_map/pack/pallas_call | solution.py:356
  8.0 2.2 %collective-permute-start.1 = (bf16[24,1920]{1,0:T(8,128)(2,1)S(1)}, bf16[24,1920]{1,0:T(8,128)(2,1)S(1)}, u32[]{:S(2)}, u32[]{:S(2)}) collective-permute-start(bf16[24,1920]{1,0:T(8,128)(2,1)S(1)} %get-tuple-element.46), channel_id=1, source_target_pairs={{0,4},{1,5},{2,6},{3,7},{4,0},{5,1},{6,2},{7,3},{8,12},{9,13},{10,... | collective-permute-start | bytes 276488 | tf_op jit(solution)/shard_map/ppermute | solution.py:29
  10.2 2.6 %collective-permute-start.4 = (bf16[24,1920]{1,0:T(8,128)(2,1)S(1)}, bf16[24,1920]{1,0:T(8,128)(2,1)S(1)}, u32[]{:S(2)}, u32[]{:S(2)}) collective-permute-start(bf16[24,1920]{1,0:T(8,128)(2,1)S(1)} %get-tuple-element.47), channel_id=1, source_target_pairs={{0,8},{1,9},{2,10},{3,11},{4,12},{5,13},{6,14},{7,15},{8,0},{9,1},... | collective-permute-start | bytes 276488 | tf_op jit(solution)/shard_map/ppermute | solution.py:29
  12.8 0.9 %collective-permute-done.1.refs_1_ = bf16[24,1920]{1,0:T(8,128)(2,1)S(1)} collective-permute-done((bf16[24,1920]{1,0:T(8,128)(2,1)S(1)}, bf16[24,1920]{1,0:T(8,128)(2,1)S(1)}, u32[]{:S(2)}, u32[]{:S(2)}) %collective-permute-start.1) | collective-permute-done | bytes 92192 | tf_op jit(solution)/shard_map/ppermute | solution.py:29
  13.8 1.9 %collective-permute-start.7 = (bf16[2,24,1920]{2,1,0:T(8,128)(2,1)S(1)}, bf16[2,24,1920]{2,1,0:T(8,128)(2,1)S(1)}, u32[]{:S(2)}, u32[]{:S(2)}) collective-permute-start(bf16[2,24,1920]{2,1,0:T(8,128)(2,1)S(1)} %join.2), channel_id=1, source_target_pairs={{0,2},{1,3},{2,0},{3,1},{4,6},{5,7},{6,4},{7,5},{8,10},{9,11},{10,... | collective-permute-start | bytes 552968 | tf_op jit(solution)/shard_map/ppermute | solution.py:29
  16.7 0.7 %copy-done.2 = bf16[1792,512]{1,0:T(8,128)(2,1)S(1)} copy-done((bf16[1792,512]{1,0:T(8,128)(2,1)S(1)}, bf16[1792,512]{1,0:T(8,128)(2,1)}, u32[]{:S(2)}) %copy-start.2) | copy-done | bytes 1835032
  17.8 1.6 %collective-permute-start.3 = (bf16[3,48,512]{2,1,0:T(8,128)(2,1)S(1)}, bf16[3,48,512]{2,1,0:T(8,128)(2,1)S(1)}, u32[]{:S(2)}, u32[]{:S(2)}) collective-permute-start(bf16[3,48,512]{2,1,0:T(8,128)(2,1)S(1)} %pad_maximum_fusion.4.refs_5_), channel_id=1, source_target_pairs={{0,16},{16,0},{1,17},{17,1},{2,18},{18,2},{3,19},{19,3},{4,20},{20... | collective-permute-start | bytes 442376 | tf_op jit(solution)/shard_map/ppermute | solution.py:29
  19.6 1.5 %collective-permute-start.6 = (bf16[2,24,1920]{2,1,0:T(8,128)(2,1)S(1)}, bf16[2,24,1920]{2,1,0:T(8,128)(2,1)S(1)}, u32[]{:S(2)}, u32[]{:S(2)}) collective-permute-start(bf16[2,24,1920]{2,1,0:T(8,128)(2,1)S(1)} %join.3), channel_id=1, source_target_pairs={{0,2},{1,3},{2,0},{3,1},{4,6},{5,7},{6,4},{7,5},{8,10},{9,11},{10,... | collective-permute-start | bytes 552968 | tf_op jit(solution)/shard_map/ppermute | solution.py:29
  22.6 1.6 %collective-permute-start.12 = (bf16[3,48,512]{2,1,0:T(8,128)(2,1)S(1)}, bf16[3,48,512]{2,1,0:T(8,128)(2,1)S(1)}, u32[]{:S(2)}, u32[]{:S(2)}) collective-permute-start(bf16[3,48,512]{2,1,0:T(8,128)(2,1)S(1)} %pad_maximum_fusion.6), channel_id=1, source_target_pairs={{0,16},{16,0},{1,17},{17,1},{2,18},{18,2},{3,19},{19,3},{4,20},{20... | collective-permute-start | bytes 442376 | tf_op jit(solution)/shard_map/ppermute | solution.py:29
  25.5 1.1 %collective-permute-done.6.refs_0_ = bf16[2,24,1920]{2,1,0:T(8,128)(2,1)S(1)} collective-permute-done((bf16[2,24,1920]{2,1,0:T(8,128)(2,1)S(1)}, bf16[2,24,1920]{2,1,0:T(8,128)(2,1)S(1)}, u32[]{:S(2)}, u32[]{:S(2)}) %collective-permute-start.6) | collective-permute-done | bytes 184352 | tf_op jit(solution)/shard_map/ppermute | solution.py:29
  26.7 1.4 %collective-permute-start.11 = (bf16[3,48,512]{2,1,0:T(8,128)(2,1)S(1)}, bf16[3,48,512]{2,1,0:T(8,128)(2,1)S(1)}, u32[]{:S(2)}, u32[]{:S(2)}) collective-permute-start(bf16[3,48,512]{2,1,0:T(8,128)(2,1)S(1)} %pad_maximum_fusion.5), channel_id=1, source_target_pairs={{0,16},{16,0},{1,17},{17,1},{2,18},{18,2},{3,19},{19,3},{4,20},{20... | collective-permute-start | bytes 442376 | tf_op jit(solution)/shard_map/ppermute | solution.py:29
  29.4 1.4 %collective-permute-start.13 = (bf16[3,48,512]{2,1,0:T(8,128)(2,1)S(1)}, bf16[3,48,512]{2,1,0:T(8,128)(2,1)S(1)}, u32[]{:S(2)}, u32[]{:S(2)}) collective-permute-start(bf16[3,48,512]{2,1,0:T(8,128)(2,1)S(1)} %pad_maximum_fusion.7), channel_id=1, source_target_pairs={{0,16},{16,0},{1,17},{17,1},{2,18},{18,2},{3,19},{19,3},{4,20},{20... | collective-permute-start | bytes 442376 | tf_op jit(solution)/shard_map/ppermute | solution.py:29
  30.8 0.5 flip_weight.3.refs_18_.refs_17_
  31.3 0.5 flip_weight.2.refs_17_.refs_16_
  32.5 0.8 %act.5 = (bf16[2,24,512]{2,1,0:T(8,128)(2,1)S(1)}, bf16[2,24,512]{2,1,0:T(8,128)(2,1)S(1)}, bf16[2,24,512]{2,1,0:T(8,128)(2,1)S(1)}, bf16[2,24,128]{2,1,0:T(8,128)(2,1)S(1)}) custom-call(s32[2]{0:T(128)S(1)} %pad_add_fusion.where_ref, bf16[48,128]{1,0:T(8,128)(2,1)S(1)} %fusion.12.refs_0_, f32[48,512]{1,0:T(8,128)S(1)} %fusion.23.refs_1_, ...), custom_call_target="tpu_custom_call" | custom-call | tf_op jit(solution)/shard_map/act/pallas_call | solution.py:436
  33.4 0.8 %act.4 = (bf16[2,24,512]{2,1,0:T(8,128)(2,1)S(1)}, bf16[2,24,512]{2,1,0:T(8,128)(2,1)S(1)}, bf16[2,24,512]{2,1,0:T(8,128)(2,1)S(1)}, bf16[2,24,128]{2,1,0:T(8,128)(2,1)S(1)}) custom-call(s32[2]{0:T(128)S(1)} %pad_add_fusion.where_ref, bf16[48,128]{1,0:T(8,128)(2,1)S(1)} %fusion.13.refs_0_, f32[48,512]{1,0:T(8,128)S(1)} %fusion.21.refs_1_, ...), custom_call_target="tpu_custom_call" | custom-call | tf_op jit(solution)/shard_map/act/pallas_call | solution.py:436
  34.2 0.8 %act.3 = (bf16[2,24,512]{2,1,0:T(8,128)(2,1)S(1)}, bf16[2,24,512]{2,1,0:T(8,128)(2,1)S(1)}, bf16[2,24,512]{2,1,0:T(8,128)(2,1)S(1)}, bf16[2,24,128]{2,1,0:T(8,128)(2,1)S(1)}) custom-call(s32[2]{0:T(128)S(1)} %pad_add_fusion.where_ref, bf16[48,128]{1,0:T(8,128)(2,1)S(1)} %slice_bitcast_fusion.2.refs_0_, f32[48,512]{1,0:T(8,128)S(1)} %fusion.17.refs_2_.refs_1_, ...), custom_call_target="tpu_custom_call" | custom-call | tf_op jit(solution)/shard_map/act/pallas_call | solution.py:436
  35.0 1.2 %collective-permute-done.13.refs_4_ = bf16[3,48,512]{2,1,0:T(8,128)(2,1)S(1)} collective-permute-done((bf16[3,48,512]{2,1,0:T(8,128)(2,1)S(1)}, bf16[3,48,512]{2,1,0:T(8,128)(2,1)S(1)}, u32[]{:S(2)}, u32[]{:S(2)}) %collective-permute-start.13) | collective-permute-done | bytes 147488 | tf_op jit(solution)/shard_map/ppermute | solution.py:29
  36.1 1.4 %last_act.1 = (bf16[2,24,512]{2,1,0:T(8,128)(2,1)S(1)}, bf16[2,24,512]{2,1,0:T(8,128)(2,1)S(1)}, bf16[2,24,512]{2,1,0:T(8,128)(2,1)S(1)}, bf16[2,24,128]{2,1,0:T(8,128)(2,1)S(1)}, bf16[2,2,24,1920]{3,2,1,0:T(8,128)(2,1)S(1)}) custom-call(s32[2]{0:T(128)S(1)} %pad_add_fusion.where_ref, bf16[48,128]{1,0:T(8,128)(2,1)S(1)} %fusion.14.refs_0_, ...), custom_call_target="tpu_custom_call" | custom-call | tf_op jit(solution)/shard_map/last_act/pallas_call | solution.py:441
  37.7 1.3 %own_back.1.a_ref = bf16[2,2,24,1920]{3,2,1,0:T(8,128)(2,1)S(1)} custom-call(s32[2]{0:T(128)S(1)} %pad_add_fusion.where_ref, bf16[2,24,512]{2,1,0:T(8,128)(2,1)S(1)} %get-tuple-element.49.refs_5_.refs_0_, bf16[2,24,512]{2,1,0:T(8,128)(2,1)S(1)} %get-tuple-element.50.refs_6_.refs_1_, bf16[2,24,512]{2,1,0:T(8,128)(2,1)S(1)} %get-tuple-element.51.refs_7_.refs_2_, ...), custom_call_target="tpu_custom_call" | custom-call | tf_op jit(solution)/shard_map/own_back/pallas_call | solution.py:449
  39.4 1.4 %collective-permute-start.17 = (bf16[24,1920]{1,0:T(8,128)(2,1)S(1)}, bf16[24,1920]{1,0:T(8,128)(2,1)S(1)}, u32[]{:S(2)}, u32[]{:S(2)}) collective-permute-start(bf16[24,1920]{1,0:T(8,128)(2,1)S(1)} %get-tuple-element.69), channel_id=1, source_target_pairs={{0,2},{1,3},{2,0},{3,1},{4,6},{5,7},{6,4},{7,5},{8,10},{9,11},{10,... | collective-permute-start | bytes 276488 | tf_op jit(solution)/shard_map/ppermute | solution.py:29
  40.8 1.4 %collective-permute-start.15 = (bf16[24,1792]{1,0:T(8,128)(2,1)S(1)}, bf16[24,1792]{1,0:T(8,128)(2,1)S(1)}, u32[]{:S(2)}, u32[]{:S(2)}) collective-permute-start(bf16[24,1792]{1,0:T(8,128)(2,1)S(1)} %get-tuple-element.67), channel_id=1, source_target_pairs={{0,18},{1,19},{2,16},{3,17},{4,22},{5,23},{6,20},{7,21},{8,26},{9,... | collective-permute-start | bytes 258056 | tf_op jit(solution)/shard_map/ppermute | solution.py:35
  42.3 0.7 %collective-permute-start.16 = (bf16[24,1792]{1,0:T(8,128)(2,1)S(1)}, bf16[24,1792]{1,0:T(8,128)(2,1)S(1)}, u32[]{:S(2)}, u32[]{:S(2)}) collective-permute-start(bf16[24,1792]{1,0:T(8,128)(2,1)S(1)} %get-tuple-element.68), channel_id=1, source_target_pairs={{0,16},{16,0},{1,17},{17,1},{2,18},{18,2},{3,19},{19,3},{4,20},{20... | collective-permute-start | bytes 258056 | tf_op jit(solution)/shard_map/ppermute | solution.py:29
  43.0 4.0 %collective-permute-done.15.b_ref = bf16[24,1792]{1,0:T(8,128)(2,1)S(1)} collective-permute-done((bf16[24,1792]{1,0:T(8,128)(2,1)S(1)}, bf16[24,1792]{1,0:T(8,128)(2,1)S(1)}, u32[]{:S(2)}, u32[]{:S(2)}) %collective-permute-start.15) | collective-permute-done | bytes 86048 | tf_op jit(solution)/shard_map/ppermute | solution.py:35
  47.3 2.3 %collective-permute-start.18 = (bf16[8,2816]{1,0:T(8,128)(2,1)S(1)}, bf16[8,2816]{1,0:T(8,128)(2,1)S(1)}, u32[]{:S(2)}, u32[]{:S(2)}) collective-permute-start(bf16[8,2816]{1,0:T(8,128)(2,1)S(1)} %get-tuple-element.71), channel_id=1, source_target_pairs={{0,8},{1,9},{2,10},{3,11},{4,12},{5,13},{6,14},{7,15},{8,0},{9,1},... | collective-permute-start | bytes 135176 | tf_op jit(solution)/shard_map/ppermute | solution.py:29
  49.6 1.7 %collective-permute-start.19 = (bf16[8,2816]{1,0:T(8,128)(2,1)S(1)}, bf16[8,2816]{1,0:T(8,128)(2,1)S(1)}, u32[]{:S(2)}, u32[]{:S(2)}) collective-permute-start(bf16[8,2816]{1,0:T(8,128)(2,1)S(1)} %get-tuple-element.72), channel_id=1, source_target_pairs={{0,12},{1,13},{2,14},{3,15},{4,8},{5,9},{6,10},{7,11},{8,4},{9,5},... | collective-permute-start | bytes 135176 | tf_op jit(solution)/shard_map/ppermute | solution.py:29
  51.4 2.8 %weight_grads.1 = (bf16[1792,512]{1,0:T(8,128)(2,1)}, bf16[1792,512]{1,0:T(8,128)(2,1)}, bf16[1792,512]{1,0:T(8,128)(2,1)}) custom-call(bf16[1792,192]{1,0:T(8,128)(2,1)S(1)} %flip.2.refs_19_.tok_ref, bf16[1792,192]{1,0:T(8,128)(2,1)S(1)} %flip.3.refs_20_.cot_ref, bf16[2,24,512]{2,1,0:T(8,128)(2,1)S(1)} %get-tuple-element.49.refs_5_.refs_0_, ...), custom_call_target="tpu_custom_call" | custom-call | tf_op jit(solution)/shard_map/weight_grads/pallas_call | solution.py:493
  54.2 1.4 %collective-permute-done.19.refs_2_ = bf16[8,2816]{1,0:T(8,128)(2,1)S(1)} collective-permute-done((bf16[8,2816]{1,0:T(8,128)(2,1)S(1)}, bf16[8,2816]{1,0:T(8,128)(2,1)S(1)}, u32[]{:S(2)}, u32[]{:S(2)}) %collective-permute-start.19) | collective-permute-done | bytes 45088 | tf_op jit(solution)/shard_map/ppermute | solution.py:29
  55.9 1.5 %owner.1 = (bf16[2,4,3584]{2,1,0:T(4,128)(2,1)}, f32[2,2,4]{2,1,0:T(2,128)}) custom-call(s32[2]{0:T(128)S(1)} %pad_add_fusion.where_ref, f32[2,8,256]{2,1,0:T(8,128)S(1)} %get-tuple-element.44.refs_1_.place_ref, bf16[8,2816]{1,0:T(8,128)(2,1)S(1)} %get-tuple-element.70.refs_0_, bf16[8,2816]{1,0:T(8,128)(2,1)S(1)} %collective-permute-done.18.refs_1_, ...), custom_call_target="tpu_custom_call" | custom-call | tf_op jit(solution)/shard_map/owner/pallas_call | solution.py:506
  (76 shorter events, 7.8 us)
Async XLA Ops:
  0.6 15.7 %copy-start = (bf16[1792,512]{1,0:T(8,128)(2,1)S(1)}, bf16[1792,512]{1,0:T(8,128)(2,1)}, u32[]{:S(2)}) copy-start(bf16[1792,512]{1,0:T(8,128)(2,1)} %param.13) | copy-start | bytes 5505028
  1.8 5.2 %collective-permute-start = (bf16[16,1920]{1,0:T(8,128)(2,1)S(1)}, bf16[16,1920]{1,0:T(8,128)(2,1)S(1)}, u32[]{:S(2)}, u32[]{:S(2)}) collective-permute-start(bf16[16,1920]{1,0:T(8,128)(2,1)S(1)} %get-tuple-element.87), channel_id=1, source_target_pairs={{0,16},{16,0},{1,17},{17,1},{2,18},{18,2},{3,19},{19,3},{4,20},{20... | collective-permute-start | bytes 184328 | tf_op jit(solution)/shard_map/ppermute | solution.py:29
  8.0 5.6 %collective-permute-start.1 = (bf16[24,1920]{1,0:T(8,128)(2,1)S(1)}, bf16[24,1920]{1,0:T(8,128)(2,1)S(1)}, u32[]{:S(2)}, u32[]{:S(2)}) collective-permute-start(bf16[24,1920]{1,0:T(8,128)(2,1)S(1)} %get-tuple-element.46), channel_id=1, source_target_pairs={{0,4},{1,5},{2,6},{3,7},{4,0},{5,1},{6,2},{7,3},{8,12},{9,13},{10,... | collective-permute-start | bytes 276488 | tf_op jit(solution)/shard_map/ppermute | solution.py:29
  10.2 9.2 %collective-permute-start.4 = (bf16[24,1920]{1,0:T(8,128)(2,1)S(1)}, bf16[24,1920]{1,0:T(8,128)(2,1)S(1)}, u32[]{:S(2)}, u32[]{:S(2)}) collective-permute-start(bf16[24,1920]{1,0:T(8,128)(2,1)S(1)} %get-tuple-element.47), channel_id=1, source_target_pairs={{0,8},{1,9},{2,10},{3,11},{4,12},{5,13},{6,14},{7,15},{8,0},{9,1},... | collective-permute-start | bytes 276488 | tf_op jit(solution)/shard_map/ppermute | solution.py:29
  12.8 6.6 %collective-permute-start.5 = (bf16[24,1920]{1,0:T(8,128)(2,1)S(1)}, bf16[24,1920]{1,0:T(8,128)(2,1)S(1)}, u32[]{:S(2)}, u32[]{:S(2)}) collective-permute-start(bf16[24,1920]{1,0:T(8,128)(2,1)S(1)} %get-tuple-element.48), channel_id=1, source_target_pairs={{0,12},{1,13},{2,14},{3,15},{4,8},{5,9},{6,10},{7,11},{8,4},{9,5},... | collective-permute-start | bytes 276488 | tf_op jit(solution)/shard_map/ppermute | solution.py:29
  13.7 2.1 %collective-permute-start.2 = (bf16[2,24,1920]{2,1,0:T(8,128)(2,1)S(1)}, bf16[2,24,1920]{2,1,0:T(8,128)(2,1)S(1)}, u32[]{:S(2)}, u32[]{:S(2)}) collective-permute-start(bf16[2,24,1920]{2,1,0:T(8,128)(2,1)S(1)} %join.2), channel_id=1, source_target_pairs={{0,1},{1,0},{2,3},{3,2},{4,5},{5,4},{6,7},{7,6},{8,9},{9,8},{10,11... | collective-permute-start | bytes 552968 | tf_op jit(solution)/shard_map/ppermute | solution.py:29
  13.8 2.0 %copy-start.1 = (bf16[1792,512]{1,0:T(8,128)(2,1)S(1)}, bf16[1792,512]{1,0:T(8,128)(2,1)}, u32[]{:S(2)}) copy-start(bf16[1792,512]{1,0:T(8,128)(2,1)} %weight_ref.3) | copy-start | bytes 5505028
  13.8 8.6 %collective-permute-start.7 = (bf16[2,24,1920]{2,1,0:T(8,128)(2,1)S(1)}, bf16[2,24,1920]{2,1,0:T(8,128)(2,1)S(1)}, u32[]{:S(2)}, u32[]{:S(2)}) collective-permute-start(bf16[2,24,1920]{2,1,0:T(8,128)(2,1)S(1)} %join.2), channel_id=1, source_target_pairs={{0,2},{1,3},{2,0},{3,1},{4,6},{5,7},{6,4},{7,5},{8,10},{9,11},{10,... | collective-permute-start | bytes 552968 | tf_op jit(solution)/shard_map/ppermute | solution.py:29
  15.9 1.5 %copy-start.2 = (bf16[1792,512]{1,0:T(8,128)(2,1)S(1)}, bf16[1792,512]{1,0:T(8,128)(2,1)}, u32[]{:S(2)}) copy-start(bf16[1792,512]{1,0:T(8,128)(2,1)} %weight_ref.2) | copy-start | bytes 5505028
  17.8 16.3 %collective-permute-start.3 = (bf16[3,48,512]{2,1,0:T(8,128)(2,1)S(1)}, bf16[3,48,512]{2,1,0:T(8,128)(2,1)S(1)}, u32[]{:S(2)}, u32[]{:S(2)}) collective-permute-start(bf16[3,48,512]{2,1,0:T(8,128)(2,1)S(1)} %pad_maximum_fusion.4.refs_5_), channel_id=1, source_target_pairs={{0,16},{16,0},{1,17},{17,1},{2,18},{18,2},{3,19},{19,3},{4,20},{20... | collective-permute-start | bytes 442376 | tf_op jit(solution)/shard_map/ppermute | solution.py:29
  19.5 1.6 %collective-permute-start.8 = (bf16[2,24,1920]{2,1,0:T(8,128)(2,1)S(1)}, bf16[2,24,1920]{2,1,0:T(8,128)(2,1)S(1)}, u32[]{:S(2)}, u32[]{:S(2)}) collective-permute-start(bf16[2,24,1920]{2,1,0:T(8,128)(2,1)S(1)} %join.3), channel_id=1, source_target_pairs={{0,1},{1,0},{2,3},{3,2},{4,5},{5,4},{6,7},{7,6},{8,9},{9,8},{10,11... | collective-permute-start | bytes 552968 | tf_op jit(solution)/shard_map/ppermute | solution.py:29
  19.6 7.1 %collective-permute-start.6 = (bf16[2,24,1920]{2,1,0:T(8,128)(2,1)S(1)}, bf16[2,24,1920]{2,1,0:T(8,128)(2,1)S(1)}, u32[]{:S(2)}, u32[]{:S(2)}) collective-permute-start(bf16[2,24,1920]{2,1,0:T(8,128)(2,1)S(1)} %join.3), channel_id=1, source_target_pairs={{0,2},{1,3},{2,0},{3,1},{4,6},{5,7},{6,4},{7,5},{8,10},{9,11},{10,... | collective-permute-start | bytes 552968 | tf_op jit(solution)/shard_map/ppermute | solution.py:29
  22.5 1.7 %collective-permute-start.9 = (bf16[2,24,1920]{2,1,0:T(8,128)(2,1)S(1)}, bf16[2,24,1920]{2,1,0:T(8,128)(2,1)S(1)}, u32[]{:S(2)}, u32[]{:S(2)}) collective-permute-start(bf16[2,24,1920]{2,1,0:T(8,128)(2,1)S(1)} %tie.6), channel_id=1, source_target_pairs={{0,1},{1,0},{2,3},{3,2},{4,5},{5,4},{6,7},{7,6},{8,9},{9,8},{10,11... | collective-permute-start | bytes 552968 | tf_op jit(solution)/shard_map/ppermute | solution.py:29
  22.6 9.9 %collective-permute-start.12 = (bf16[3,48,512]{2,1,0:T(8,128)(2,1)S(1)}, bf16[3,48,512]{2,1,0:T(8,128)(2,1)S(1)}, u32[]{:S(2)}, u32[]{:S(2)}) collective-permute-start(bf16[3,48,512]{2,1,0:T(8,128)(2,1)S(1)} %pad_maximum_fusion.6), channel_id=1, source_target_pairs={{0,16},{16,0},{1,17},{17,1},{2,18},{18,2},{3,19},{19,3},{4,20},{20... | collective-permute-start | bytes 442376 | tf_op jit(solution)/shard_map/ppermute | solution.py:29
  26.6 1.4 %collective-permute-start.10 = (bf16[2,24,1920]{2,1,0:T(8,128)(2,1)S(1)}, bf16[2,24,1920]{2,1,0:T(8,128)(2,1)S(1)}, u32[]{:S(2)}, u32[]{:S(2)}) collective-permute-start(bf16[2,24,1920]{2,1,0:T(8,128)(2,1)S(1)} %tie.7), channel_id=1, source_target_pairs={{0,1},{1,0},{2,3},{3,2},{4,5},{5,4},{6,7},{7,6},{8,9},{9,8},{10,11... | collective-permute-start | bytes 552968 | tf_op jit(solution)/shard_map/ppermute | solution.py:29
  26.7 6.7 %collective-permute-start.11 = (bf16[3,48,512]{2,1,0:T(8,128)(2,1)S(1)}, bf16[3,48,512]{2,1,0:T(8,128)(2,1)S(1)}, u32[]{:S(2)}, u32[]{:S(2)}) collective-permute-start(bf16[3,48,512]{2,1,0:T(8,128)(2,1)S(1)} %pad_maximum_fusion.5), channel_id=1, source_target_pairs={{0,16},{16,0},{1,17},{17,1},{2,18},{18,2},{3,19},{19,3},{4,20},{20... | collective-permute-start | bytes 442376 | tf_op jit(solution)/shard_map/ppermute | solution.py:29
  29.4 6.7 %collective-permute-start.13 = (bf16[3,48,512]{2,1,0:T(8,128)(2,1)S(1)}, bf16[3,48,512]{2,1,0:T(8,128)(2,1)S(1)}, u32[]{:S(2)}, u32[]{:S(2)}) collective-permute-start(bf16[3,48,512]{2,1,0:T(8,128)(2,1)S(1)} %pad_maximum_fusion.7), channel_id=1, source_target_pairs={{0,16},{16,0},{1,17},{17,1},{2,18},{18,2},{3,19},{19,3},{4,20},{20... | collective-permute-start | bytes 442376 | tf_op jit(solution)/shard_map/ppermute | solution.py:29
  37.6 1.8 %collective-permute-start.14 = (bf16[2,2,24,1920]{3,2,1,0:T(8,128)(2,1)S(1)}, bf16[2,2,24,1920]{3,2,1,0:T(8,128)(2,1)S(1)}, u32[]{:S(2)}, u32[]{:S(2)}) collective-permute-start(bf16[2,2,24,1920]{3,2,1,0:T(8,128)(2,1)S(1)} %get-tuple-element.65.refs_18_), channel_id=1, source_target_pairs={{0,1},{1,0},{2,3},{3,2},{4,5},{5,4},{6,7},{7,6},{8,9},{9,8},{10,11... | collective-permute-start | bytes 1105928 | tf_op jit(solution)/shard_map/ppermute | solution.py:29
  39.4 7.8 %collective-permute-start.17 = (bf16[24,1920]{1,0:T(8,128)(2,1)S(1)}, bf16[24,1920]{1,0:T(8,128)(2,1)S(1)}, u32[]{:S(2)}, u32[]{:S(2)}) collective-permute-start(bf16[24,1920]{1,0:T(8,128)(2,1)S(1)} %get-tuple-element.69), channel_id=1, source_target_pairs={{0,2},{1,3},{2,0},{3,1},{4,6},{5,7},{6,4},{7,5},{8,10},{9,11},{10,... | collective-permute-start | bytes 276488 | tf_op jit(solution)/shard_map/ppermute | solution.py:29
  40.8 6.2 %collective-permute-start.15 = (bf16[24,1792]{1,0:T(8,128)(2,1)S(1)}, bf16[24,1792]{1,0:T(8,128)(2,1)S(1)}, u32[]{:S(2)}, u32[]{:S(2)}) collective-permute-start(bf16[24,1792]{1,0:T(8,128)(2,1)S(1)} %get-tuple-element.67), channel_id=1, source_target_pairs={{0,18},{1,19},{2,16},{3,17},{4,22},{5,23},{6,20},{7,21},{8,26},{9,... | collective-permute-start | bytes 258056 | tf_op jit(solution)/shard_map/ppermute | solution.py:35
  42.3 4.9 %collective-permute-start.16 = (bf16[24,1792]{1,0:T(8,128)(2,1)S(1)}, bf16[24,1792]{1,0:T(8,128)(2,1)S(1)}, u32[]{:S(2)}, u32[]{:S(2)}) collective-permute-start(bf16[24,1792]{1,0:T(8,128)(2,1)S(1)} %get-tuple-element.68), channel_id=1, source_target_pairs={{0,16},{16,0},{1,17},{17,1},{2,18},{18,2},{3,19},{19,3},{4,20},{20... | collective-permute-start | bytes 258056 | tf_op jit(solution)/shard_map/ppermute | solution.py:29
  47.3 6.8 %collective-permute-start.18 = (bf16[8,2816]{1,0:T(8,128)(2,1)S(1)}, bf16[8,2816]{1,0:T(8,128)(2,1)S(1)}, u32[]{:S(2)}, u32[]{:S(2)}) collective-permute-start(bf16[8,2816]{1,0:T(8,128)(2,1)S(1)} %get-tuple-element.71), channel_id=1, source_target_pairs={{0,8},{1,9},{2,10},{3,11},{4,12},{5,13},{6,14},{7,15},{8,0},{9,1},... | collective-permute-start | bytes 135176 | tf_op jit(solution)/shard_map/ppermute | solution.py:29
  49.6 6.0 %collective-permute-start.19 = (bf16[8,2816]{1,0:T(8,128)(2,1)S(1)}, bf16[8,2816]{1,0:T(8,128)(2,1)S(1)}, u32[]{:S(2)}, u32[]{:S(2)}) collective-permute-start(bf16[8,2816]{1,0:T(8,128)(2,1)S(1)} %get-tuple-element.72), channel_id=1, source_target_pairs={{0,12},{1,13},{2,14},{3,15},{4,8},{5,9},{6,10},{7,11},{8,4},{9,5},... | collective-permute-start | bytes 135176 | tf_op jit(solution)/shard_map/ppermute | solution.py:29
  51.4 4.5 %collective-permute-start.20 = (bf16[8,2816]{1,0:T(8,128)(2,1)S(1)}, bf16[8,2816]{1,0:T(8,128)(2,1)S(1)}, u32[]{:S(2)}, u32[]{:S(2)}) collective-permute-start(bf16[8,2816]{1,0:T(8,128)(2,1)S(1)} %get-tuple-element.73), channel_id=1, source_target_pairs={{0,4},{1,5},{2,6},{3,7},{4,0},{5,1},{6,2},{7,3},{8,12},{9,13},{10,... | collective-permute-start | bytes 135176 | tf_op jit(solution)/shard_map/ppermute | solution.py:29

commit v8 on v7

--- a/solution.py
+++ b/solution.py
@@ -35,14 +35,7 @@
     return lax.ppermute(x, ("pipe", "expert"), pairs)
 
 
-def prep_kernel(d_part, tok_hbm, cot_hbm, ids_hbm, gate_hbm, *refs):
-    out_refs, (tok_ref, cot_ref, ids_ref, gate_ref, sems) = refs[:-5], refs[-5:]
-    pairs = ((tok_hbm, tok_ref), (cot_hbm, cot_ref), (ids_hbm, ids_ref), (gate_hbm, gate_ref))
-    copies = [pltpu.make_async_copy(src, dst, sems.at[i]) for i, (src, dst) in enumerate(pairs)]
-    for copy in copies:
-        copy.start()
-    for copy in copies:
-        copy.wait()
+def prep_kernel(d_part, tok_ref, cot_ref, ids_ref, gate_ref, *out_refs):
     micro_count, tok_count = tok_ref.shape[:2]
     top_count = ids_ref.shape[1]
     seg = out_refs[0].shape[-1] - LANES
@@ -289,15 +282,14 @@
     del refs
 
 
-def call(kernel, out_shape, in_specs, name, mib=8, flops=0, moved=0, **more):
+def call(kernel, out_shape, operands, name, mib=8, flops=0, moved=0, **more):
     specs = {"s": pl.BlockSpec(memory_space=pltpu.SMEM), "v": pl.BlockSpec(memory_space=pltpu.VMEM)}
     specs["a"] = pl.BlockSpec(memory_space=pl.ANY)
-    specs["h"] = pl.BlockSpec(memory_space=pltpu.HBM)
+    more.setdefault("in_specs", [specs[c] for c in operands])
     more.setdefault("out_specs", jax.tree.map(lambda _: specs["v"], out_shape))
     return pl.pallas_call(
         kernel,
         out_shape=out_shape,
-        in_specs=[specs[c] for c in in_specs],
         compiler_params=pltpu.CompilerParams(vmem_limit_bytes=mib << 20),
         cost_estimate=pl.CostEstimate(flops=flops, bytes_accessed=moved, transcendentals=0),
         name=name,
@@ -338,13 +330,8 @@
         [shape((2 * own_rows, width), bf16) for _ in range(pipe_size)],
         "aaaa",
         "prep",
-        scratch_shapes=[
-            pltpu.VMEM(tokens.shape, bf16),
-            pltpu.VMEM(tokens.shape, bf16),
-            pltpu.VMEM((micro_count, top_count, tok_count), i32),
-            pltpu.VMEM((micro_count, top_count, tok_count), bf16),
-            pltpu.SemaphoreType.DMA((4,)),
-        ],
+        grid=(1,),
+        in_specs=[pl.BlockSpec(x.shape, lambda i: (0, 0, 0)) for x in inputs],
     )(*[pltpu.with_memory_space_constraint(x, pltpu.HBM) for x in inputs])
     if pipe_size == 2:
         first = pipe == 0

time: 57.5 us -> 57.5 us (level)
  no operation moved by 1% of the time
where the time goes in v8:
time: 57.5 us; the launch traced here: 57.3 us
  starting transfers between devices  25 us (43%)
  Pallas kernels  13.4 us (23%)
  waiting for transfers between devices  11.7 us (20%)
  matrix products  5 us (9%)
  between operations  1.04 us (2%)
  local copies, waits for them, and re-layouts  0.71 us (1%)
    ppermute x20, starting transfers between devices, swap(): lax.ppermute(x, axis, [(i, i ^ bit) for i in range(lax.axis_size(axis))])  23.6 us
    ppermute x20, waiting for transfers between devices, swap(): lax.ppermute(x, axis, [(i, i ^ bit) for i in range(lax.axis_size(axis))])  7.64 us
    dot_general x12, matrix products, project(): own.append(jnp.dot(left, weight, preferred_element_type=f32))  5 us
    ppermute x1, waiting for transfers between devices, swap_both(): return lax.ppermute(x, ('pipe', 'expert'), pairs)  4.03 us
    pallas_call x1, Pallas kernels, on_device(): call(functools.partial(weight_kernel, scale, block), [shape((d_part, f_pa...  2.81 us
    pallas_call x3, Pallas kernels, on_device(): call(functools.partial(act_kernel, top_count), grad_shapes(piece), 'svvvv...  2.37 us
    pallas_call x1, Pallas kernels, on_device(): call(functools.partial(owner_kernel, d_part, packed), (shape(tokens.shape...  1.49 us
    ppermute x1, starting transfers between devices, swap_both(): return lax.ppermute(x, ('pipe', 'expert'), pairs)  1.45 us
  transfers between devices with their start and end apart: 21, of which 10 were waited for; matrix products, arithmetic and copies ran while one was open for 10% of the time, Pallas kernels for 14%

profile of v8, /device:TPU:0, one launch (start us, length us, event | category | flops | bytes accessed | tf_op | source)
XLA Modules:
  0.0 57.3 jit_solution(308123765759862726)
XLA Ops:
  0.7 1.1 %prep.1 = (bf16[16,1920]{1,0:T(8,128)(2,1)S(1)}, bf16[16,1920]{1,0:T(8,128)(2,1)S(1)}) custom-call(bf16[2,4,3584]{2,1,0:T(4,128)(2,1)} %tok_ref.1, bf16[2,4,3584]{2,1,0:T(4,128)(2,1)} %cot_ref.1, s32[2,2,4]{2,1,0:T(2,128)} %bitcast.77, bf16[2,2,4]{2,1,0:T(2,128)(2,1)} %bitcast.78), custom_call_target="tpu_custom_call" | custom-call | tf_op jit(solution)/shard_map/prep/pallas_call | solution.py:328
  1.8 3.0 %collective-permute-start = (bf16[16,1920]{1,0:T(8,128)(2,1)S(1)}, bf16[16,1920]{1,0:T(8,128)(2,1)S(1)}, u32[]{:S(2)}, u32[]{:S(2)}) collective-permute-start(bf16[16,1920]{1,0:T(8,128)(2,1)S(1)} %get-tuple-element.87), channel_id=1, source_target_pairs={{0,16},{16,0},{1,17},{17,1},{2,18},{18,2},{3,19},{19,3},{4,20},{20... | collective-permute-start | bytes 184328 | tf_op jit(solution)/shard_map/ppermute | solution.py:29
  4.8 2.1 %collective-permute-done.refs_1_ = bf16[16,1920]{1,0:T(8,128)(2,1)S(1)} collective-permute-done((bf16[16,1920]{1,0:T(8,128)(2,1)S(1)}, bf16[16,1920]{1,0:T(8,128)(2,1)S(1)}, u32[]{:S(2)}, u32[]{:S(2)}) %collective-permute-start) | collective-permute-done | bytes 61472 | tf_op jit(solution)/shard_map/ppermute | solution.py:29
  7.0 1.0 %pack.1 = (bf16[24,1920]{1,0:T(8,128)(2,1)S(1)}, bf16[24,1920]{1,0:T(8,128)(2,1)S(1)}, bf16[24,1920]{1,0:T(8,128)(2,1)S(1)}, bf16[24,1920]{1,0:T(8,128)(2,1)S(1)}, f32[2,8,256]{2,1,0:T(8,128)S(1)}) custom-call(s32[2]{0:T(128)S(1)} %pad_add_fusion.where_ref, bf16[16,1920]{1,0:T(8,128)(2,1)S(1)} %get-tuple-element.88.refs_0_, ...), custom_call_target="tpu_custom_call" | custom-call | tf_op jit(solution)/shard_map/pack/pallas_call | solution.py:343
  8.0 2.2 %collective-permute-start.1 = (bf16[24,1920]{1,0:T(8,128)(2,1)S(1)}, bf16[24,1920]{1,0:T(8,128)(2,1)S(1)}, u32[]{:S(2)}, u32[]{:S(2)}) collective-permute-start(bf16[24,1920]{1,0:T(8,128)(2,1)S(1)} %get-tuple-element.46), channel_id=1, source_target_pairs={{0,4},{1,5},{2,6},{3,7},{4,0},{5,1},{6,2},{7,3},{8,12},{9,13},{10,... | collective-permute-start | bytes 276488 | tf_op jit(solution)/shard_map/ppermute | solution.py:29
  10.2 2.6 %collective-permute-start.4 = (bf16[24,1920]{1,0:T(8,128)(2,1)S(1)}, bf16[24,1920]{1,0:T(8,128)(2,1)S(1)}, u32[]{:S(2)}, u32[]{:S(2)}) collective-permute-start(bf16[24,1920]{1,0:T(8,128)(2,1)S(1)} %get-tuple-element.47), channel_id=1, source_target_pairs={{0,8},{1,9},{2,10},{3,11},{4,12},{5,13},{6,14},{7,15},{8,0},{9,1},... | collective-permute-start | bytes 276488 | tf_op jit(solution)/shard_map/ppermute | solution.py:29
  12.7 0.9 %collective-permute-done.1.refs_1_ = bf16[24,1920]{1,0:T(8,128)(2,1)S(1)} collective-permute-done((bf16[24,1920]{1,0:T(8,128)(2,1)S(1)}, bf16[24,1920]{1,0:T(8,128)(2,1)S(1)}, u32[]{:S(2)}, u32[]{:S(2)}) %collective-permute-start.1) | collective-permute-done | bytes 92192 | tf_op jit(solution)/shard_map/ppermute | solution.py:29
  13.8 1.9 %collective-permute-start.7 = (bf16[2,24,1920]{2,1,0:T(8,128)(2,1)S(1)}, bf16[2,24,1920]{2,1,0:T(8,128)(2,1)S(1)}, u32[]{:S(2)}, u32[]{:S(2)}) collective-permute-start(bf16[2,24,1920]{2,1,0:T(8,128)(2,1)S(1)} %join.2), channel_id=1, source_target_pairs={{0,2},{1,3},{2,0},{3,1},{4,6},{5,7},{6,4},{7,5},{8,10},{9,11},{10,... | collective-permute-start | bytes 552968 | tf_op jit(solution)/shard_map/ppermute | solution.py:29
  16.7 0.7 %copy-done.2 = bf16[1792,512]{1,0:T(8,128)(2,1)S(1)} copy-done((bf16[1792,512]{1,0:T(8,128)(2,1)S(1)}, bf16[1792,512]{1,0:T(8,128)(2,1)}, u32[]{:S(2)}) %copy-start.2) | copy-done | bytes 1835032
  17.8 1.6 %collective-permute-start.3 = (bf16[3,48,512]{2,1,0:T(8,128)(2,1)S(1)}, bf16[3,48,512]{2,1,0:T(8,128)(2,1)S(1)}, u32[]{:S(2)}, u32[]{:S(2)}) collective-permute-start(bf16[3,48,512]{2,1,0:T(8,128)(2,1)S(1)} %pad_maximum_fusion.4.refs_5_), channel_id=1, source_target_pairs={{0,16},{16,0},{1,17},{17,1},{2,18},{18,2},{3,19},{19,3},{4,20},{20... | collective-permute-start | bytes 442376 | tf_op jit(solution)/shard_map/ppermute | solution.py:29
  19.5 1.5 %collective-permute-start.6 = (bf16[2,24,1920]{2,1,0:T(8,128)(2,1)S(1)}, bf16[2,24,1920]{2,1,0:T(8,128)(2,1)S(1)}, u32[]{:S(2)}, u32[]{:S(2)}) collective-permute-start(bf16[2,24,1920]{2,1,0:T(8,128)(2,1)S(1)} %join.3), channel_id=1, source_target_pairs={{0,2},{1,3},{2,0},{3,1},{4,6},{5,7},{6,4},{7,5},{8,10},{9,11},{10,... | collective-permute-start | bytes 552968 | tf_op jit(solution)/shard_map/ppermute | solution.py:29
  22.5 1.6 %collective-permute-start.12 = (bf16[3,48,512]{2,1,0:T(8,128)(2,1)S(1)}, bf16[3,48,512]{2,1,0:T(8,128)(2,1)S(1)}, u32[]{:S(2)}, u32[]{:S(2)}) collective-permute-start(bf16[3,48,512]{2,1,0:T(8,128)(2,1)S(1)} %pad_maximum_fusion.6), channel_id=1, source_target_pairs={{0,16},{16,0},{1,17},{17,1},{2,18},{18,2},{3,19},{19,3},{4,20},{20... | collective-permute-start | bytes 442376 | tf_op jit(solution)/shard_map/ppermute | solution.py:29
  25.5 1.1 %collective-permute-done.6.refs_0_ = bf16[2,24,1920]{2,1,0:T(8,128)(2,1)S(1)} collective-permute-done((bf16[2,24,1920]{2,1,0:T(8,128)(2,1)S(1)}, bf16[2,24,1920]{2,1,0:T(8,128)(2,1)S(1)}, u32[]{:S(2)}, u32[]{:S(2)}) %collective-permute-start.6) | collective-permute-done | bytes 184352 | tf_op jit(solution)/shard_map/ppermute | solution.py:29
  26.6 1.4 %collective-permute-start.11 = (bf16[3,48,512]{2,1,0:T(8,128)(2,1)S(1)}, bf16[3,48,512]{2,1,0:T(8,128)(2,1)S(1)}, u32[]{:S(2)}, u32[]{:S(2)}) collective-permute-start(bf16[3,48,512]{2,1,0:T(8,128)(2,1)S(1)} %pad_maximum_fusion.5), channel_id=1, source_target_pairs={{0,16},{16,0},{1,17},{17,1},{2,18},{18,2},{3,19},{19,3},{4,20},{20... | collective-permute-start | bytes 442376 | tf_op jit(solution)/shard_map/ppermute | solution.py:29
  29.4 1.4 %collective-permute-start.13 = (bf16[3,48,512]{2,1,0:T(8,128)(2,1)S(1)}, bf16[3,48,512]{2,1,0:T(8,128)(2,1)S(1)}, u32[]{:S(2)}, u32[]{:S(2)}) collective-permute-start(bf16[3,48,512]{2,1,0:T(8,128)(2,1)S(1)} %pad_maximum_fusion.7), channel_id=1, source_target_pairs={{0,16},{16,0},{1,17},{17,1},{2,18},{18,2},{3,19},{19,3},{4,20},{20... | collective-permute-start | bytes 442376 | tf_op jit(solution)/shard_map/ppermute | solution.py:29
  30.8 0.5 flip_weight.3.refs_18_.refs_17_
  31.3 0.5 flip_weight.2.refs_17_.refs_16_
  32.4 0.8 %act.5 = (bf16[2,24,512]{2,1,0:T(8,128)(2,1)S(1)}, bf16[2,24,512]{2,1,0:T(8,128)(2,1)S(1)}, bf16[2,24,512]{2,1,0:T(8,128)(2,1)S(1)}, bf16[2,24,128]{2,1,0:T(8,128)(2,1)S(1)}) custom-call(s32[2]{0:T(128)S(1)} %pad_add_fusion.where_ref, bf16[48,128]{1,0:T(8,128)(2,1)S(1)} %fusion.12.refs_0_, f32[48,512]{1,0:T(8,128)S(1)} %fusion.23.refs_1_, ...), custom_call_target="tpu_custom_call" | custom-call | tf_op jit(solution)/shard_map/act/pallas_call | solution.py:423
  33.3 0.8 %act.4 = (bf16[2,24,512]{2,1,0:T(8,128)(2,1)S(1)}, bf16[2,24,512]{2,1,0:T(8,128)(2,1)S(1)}, bf16[2,24,512]{2,1,0:T(8,128)(2,1)S(1)}, bf16[2,24,128]{2,1,0:T(8,128)(2,1)S(1)}) custom-call(s32[2]{0:T(128)S(1)} %pad_add_fusion.where_ref, bf16[48,128]{1,0:T(8,128)(2,1)S(1)} %fusion.13.refs_0_, f32[48,512]{1,0:T(8,128)S(1)} %fusion.21.refs_1_, ...), custom_call_target="tpu_custom_call" | custom-call | tf_op jit(solution)/shard_map/act/pallas_call | solution.py:423
  34.1 0.8 %act.3 = (bf16[2,24,512]{2,1,0:T(8,128)(2,1)S(1)}, bf16[2,24,512]{2,1,0:T(8,128)(2,1)S(1)}, bf16[2,24,512]{2,1,0:T(8,128)(2,1)S(1)}, bf16[2,24,128]{2,1,0:T(8,128)(2,1)S(1)}) custom-call(s32[2]{0:T(128)S(1)} %pad_add_fusion.where_ref, bf16[48,128]{1,0:T(8,128)(2,1)S(1)} %slice_bitcast_fusion.2.refs_0_, f32[48,512]{1,0:T(8,128)S(1)} %fusion.17.refs_2_.refs_1_, ...), custom_call_target="tpu_custom_call" | custom-call | tf_op jit(solution)/shard_map/act/pallas_call | solution.py:423
  34.9 1.2 %collective-permute-done.13.refs_4_ = bf16[3,48,512]{2,1,0:T(8,128)(2,1)S(1)} collective-permute-done((bf16[3,48,512]{2,1,0:T(8,128)(2,1)S(1)}, bf16[3,48,512]{2,1,0:T(8,128)(2,1)S(1)}, u32[]{:S(2)}, u32[]{:S(2)}) %collective-permute-start.13) | collective-permute-done | bytes 147488 | tf_op jit(solution)/shard_map/ppermute | solution.py:29
  36.1 1.4 %last_act.1 = (bf16[2,24,512]{2,1,0:T(8,128)(2,1)S(1)}, bf16[2,24,512]{2,1,0:T(8,128)(2,1)S(1)}, bf16[2,24,512]{2,1,0:T(8,128)(2,1)S(1)}, bf16[2,24,128]{2,1,0:T(8,128)(2,1)S(1)}, bf16[2,2,24,1920]{3,2,1,0:T(8,128)(2,1)S(1)}) custom-call(s32[2]{0:T(128)S(1)} %pad_add_fusion.where_ref, bf16[48,128]{1,0:T(8,128)(2,1)S(1)} %fusion.14.refs_0_, ...), custom_call_target="tpu_custom_call" | custom-call | tf_op jit(solution)/shard_map/last_act/pallas_call | solution.py:428
  37.6 1.3 %own_back.1.a_ref = bf16[2,2,24,1920]{3,2,1,0:T(8,128)(2,1)S(1)} custom-call(s32[2]{0:T(128)S(1)} %pad_add_fusion.where_ref, bf16[2,24,512]{2,1,0:T(8,128)(2,1)S(1)} %get-tuple-element.49.refs_5_.refs_0_, bf16[2,24,512]{2,1,0:T(8,128)(2,1)S(1)} %get-tuple-element.50.refs_6_.refs_1_, bf16[2,24,512]{2,1,0:T(8,128)(2,1)S(1)} %get-tuple-element.51.refs_7_.refs_2_, ...), custom_call_target="tpu_custom_call" | custom-call | tf_op jit(solution)/shard_map/own_back/pallas_call | solution.py:436
  39.4 1.4 %collective-permute-start.17 = (bf16[24,1920]{1,0:T(8,128)(2,1)S(1)}, bf16[24,1920]{1,0:T(8,128)(2,1)S(1)}, u32[]{:S(2)}, u32[]{:S(2)}) collective-permute-start(bf16[24,1920]{1,0:T(8,128)(2,1)S(1)} %get-tuple-element.69), channel_id=1, source_target_pairs={{0,2},{1,3},{2,0},{3,1},{4,6},{5,7},{6,4},{7,5},{8,10},{9,11},{10,... | collective-permute-start | bytes 276488 | tf_op jit(solution)/shard_map/ppermute | solution.py:29
  40.8 1.4 %collective-permute-start.15 = (bf16[24,1792]{1,0:T(8,128)(2,1)S(1)}, bf16[24,1792]{1,0:T(8,128)(2,1)S(1)}, u32[]{:S(2)}, u32[]{:S(2)}) collective-permute-start(bf16[24,1792]{1,0:T(8,128)(2,1)S(1)} %get-tuple-element.67), channel_id=1, source_target_pairs={{0,18},{1,19},{2,16},{3,17},{4,22},{5,23},{6,20},{7,21},{8,26},{9,... | collective-permute-start | bytes 258056 | tf_op jit(solution)/shard_map/ppermute | solution.py:35
  42.2 0.7 %collective-permute-start.16 = (bf16[24,1792]{1,0:T(8,128)(2,1)S(1)}, bf16[24,1792]{1,0:T(8,128)(2,1)S(1)}, u32[]{:S(2)}, u32[]{:S(2)}) collective-permute-start(bf16[24,1792]{1,0:T(8,128)(2,1)S(1)} %get-tuple-element.68), channel_id=1, source_target_pairs={{0,16},{16,0},{1,17},{17,1},{2,18},{18,2},{3,19},{19,3},{4,20},{20... | collective-permute-start | bytes 258056 | tf_op jit(solution)/shard_map/ppermute | solution.py:29
  42.9 4.0 %collective-permute-done.15.b_ref = bf16[24,1792]{1,0:T(8,128)(2,1)S(1)} collective-permute-done((bf16[24,1792]{1,0:T(8,128)(2,1)S(1)}, bf16[24,1792]{1,0:T(8,128)(2,1)S(1)}, u32[]{:S(2)}, u32[]{:S(2)}) %collective-permute-start.15) | collective-permute-done | bytes 86048 | tf_op jit(solution)/shard_map/ppermute | solution.py:35
  47.3 2.3 %collective-permute-start.18 = (bf16[8,2816]{1,0:T(8,128)(2,1)S(1)}, bf16[8,2816]{1,0:T(8,128)(2,1)S(1)}, u32[]{:S(2)}, u32[]{:S(2)}) collective-permute-start(bf16[8,2816]{1,0:T(8,128)(2,1)S(1)} %get-tuple-element.71), channel_id=1, source_target_pairs={{0,8},{1,9},{2,10},{3,11},{4,12},{5,13},{6,14},{7,15},{8,0},{9,1},... | collective-permute-start | bytes 135176 | tf_op jit(solution)/shard_map/ppermute | solution.py:29
  49.6 1.7 %collective-permute-start.19 = (bf16[8,2816]{1,0:T(8,128)(2,1)S(1)}, bf16[8,2816]{1,0:T(8,128)(2,1)S(1)}, u32[]{:S(2)}, u32[]{:S(2)}) collective-permute-start(bf16[8,2816]{1,0:T(8,128)(2,1)S(1)} %get-tuple-element.72), channel_id=1, source_target_pairs={{0,12},{1,13},{2,14},{3,15},{4,8},{5,9},{6,10},{7,11},{8,4},{9,5},... | collective-permute-start | bytes 135176 | tf_op jit(solution)/shard_map/ppermute | solution.py:29
  51.3 2.8 %weight_grads.1 = (bf16[1792,512]{1,0:T(8,128)(2,1)}, bf16[1792,512]{1,0:T(8,128)(2,1)}, bf16[1792,512]{1,0:T(8,128)(2,1)}) custom-call(bf16[1792,192]{1,0:T(8,128)(2,1)S(1)} %flip.2.refs_19_.tok_ref, bf16[1792,192]{1,0:T(8,128)(2,1)S(1)} %flip.3.refs_20_.cot_ref, bf16[2,24,512]{2,1,0:T(8,128)(2,1)S(1)} %get-tuple-element.49.refs_5_.refs_0_, ...), custom_call_target="tpu_custom_call" | custom-call | tf_op jit(solution)/shard_map/weight_grads/pallas_call | solution.py:480
  54.1 1.4 %collective-permute-done.19.refs_2_ = bf16[8,2816]{1,0:T(8,128)(2,1)S(1)} collective-permute-done((bf16[8,2816]{1,0:T(8,128)(2,1)S(1)}, bf16[8,2816]{1,0:T(8,128)(2,1)S(1)}, u32[]{:S(2)}, u32[]{:S(2)}) %collective-permute-start.19) | collective-permute-done | bytes 45088 | tf_op jit(solution)/shard_map/ppermute | solution.py:29
  55.8 1.5 %owner.1 = (bf16[2,4,3584]{2,1,0:T(4,128)(2,1)}, f32[2,2,4]{2,1,0:T(2,128)}) custom-call(s32[2]{0:T(128)S(1)} %pad_add_fusion.where_ref, f32[2,8,256]{2,1,0:T(8,128)S(1)} %get-tuple-element.44.refs_1_.place_ref, bf16[8,2816]{1,0:T(8,128)(2,1)S(1)} %get-tuple-element.70.refs_0_, bf16[8,2816]{1,0:T(8,128)(2,1)S(1)} %collective-permute-done.18.refs_1_, ...), custom_call_target="tpu_custom_call" | custom-call | tf_op jit(solution)/shard_map/owner/pallas_call | solution.py:493
  (76 shorter events, 7.8 us)
Async XLA Ops:
  0.6 15.6 %copy-start = (bf16[1792,512]{1,0:T(8,128)(2,1)S(1)}, bf16[1792,512]{1,0:T(8,128)(2,1)}, u32[]{:S(2)}) copy-start(bf16[1792,512]{1,0:T(8,128)(2,1)} %param.13) | copy-start | bytes 5505028
  1.8 5.2 %collective-permute-start = (bf16[16,1920]{1,0:T(8,128)(2,1)S(1)}, bf16[16,1920]{1,0:T(8,128)(2,1)S(1)}, u32[]{:S(2)}, u32[]{:S(2)}) collective-permute-start(bf16[16,1920]{1,0:T(8,128)(2,1)S(1)} %get-tuple-element.87), channel_id=1, source_target_pairs={{0,16},{16,0},{1,17},{17,1},{2,18},{18,2},{3,19},{19,3},{4,20},{20... | collective-permute-start | bytes 184328 | tf_op jit(solution)/shard_map/ppermute | solution.py:29
  8.0 5.6 %collective-permute-start.1 = (bf16[24,1920]{1,0:T(8,128)(2,1)S(1)}, bf16[24,1920]{1,0:T(8,128)(2,1)S(1)}, u32[]{:S(2)}, u32[]{:S(2)}) collective-permute-start(bf16[24,1920]{1,0:T(8,128)(2,1)S(1)} %get-tuple-element.46), channel_id=1, source_target_pairs={{0,4},{1,5},{2,6},{3,7},{4,0},{5,1},{6,2},{7,3},{8,12},{9,13},{10,... | collective-permute-start | bytes 276488 | tf_op jit(solution)/shard_map/ppermute | solution.py:29
  10.2 9.2 %collective-permute-start.4 = (bf16[24,1920]{1,0:T(8,128)(2,1)S(1)}, bf16[24,1920]{1,0:T(8,128)(2,1)S(1)}, u32[]{:S(2)}, u32[]{:S(2)}) collective-permute-start(bf16[24,1920]{1,0:T(8,128)(2,1)S(1)} %get-tuple-element.47), channel_id=1, source_target_pairs={{0,8},{1,9},{2,10},{3,11},{4,12},{5,13},{6,14},{7,15},{8,0},{9,1},... | collective-permute-start | bytes 276488 | tf_op jit(solution)/shard_map/ppermute | solution.py:29
  12.7 6.6 %collective-permute-start.5 = (bf16[24,1920]{1,0:T(8,128)(2,1)S(1)}, bf16[24,1920]{1,0:T(8,128)(2,1)S(1)}, u32[]{:S(2)}, u32[]{:S(2)}) collective-permute-start(bf16[24,1920]{1,0:T(8,128)(2,1)S(1)} %get-tuple-element.48), channel_id=1, source_target_pairs={{0,12},{1,13},{2,14},{3,15},{4,8},{5,9},{6,10},{7,11},{8,4},{9,5},... | collective-permute-start | bytes 276488 | tf_op jit(solution)/shard_map/ppermute | solution.py:29
  13.7 2.1 %collective-permute-start.2 = (bf16[2,24,1920]{2,1,0:T(8,128)(2,1)S(1)}, bf16[2,24,1920]{2,1,0:T(8,128)(2,1)S(1)}, u32[]{:S(2)}, u32[]{:S(2)}) collective-permute-start(bf16[2,24,1920]{2,1,0:T(8,128)(2,1)S(1)} %join.2), channel_id=1, source_target_pairs={{0,1},{1,0},{2,3},{3,2},{4,5},{5,4},{6,7},{7,6},{8,9},{9,8},{10,11... | collective-permute-start | bytes 552968 | tf_op jit(solution)/shard_map/ppermute | solution.py:29
  13.8 2.0 %copy-start.1 = (bf16[1792,512]{1,0:T(8,128)(2,1)S(1)}, bf16[1792,512]{1,0:T(8,128)(2,1)}, u32[]{:S(2)}) copy-start(bf16[1792,512]{1,0:T(8,128)(2,1)} %weight_ref.3) | copy-start | bytes 5505028
  13.8 8.6 %collective-permute-start.7 = (bf16[2,24,1920]{2,1,0:T(8,128)(2,1)S(1)}, bf16[2,24,1920]{2,1,0:T(8,128)(2,1)S(1)}, u32[]{:S(2)}, u32[]{:S(2)}) collective-permute-start(bf16[2,24,1920]{2,1,0:T(8,128)(2,1)S(1)} %join.2), channel_id=1, source_target_pairs={{0,2},{1,3},{2,0},{3,1},{4,6},{5,7},{6,4},{7,5},{8,10},{9,11},{10,... | collective-permute-start | bytes 552968 | tf_op jit(solution)/shard_map/ppermute | solution.py:29
  15.8 1.5 %copy-start.2 = (bf16[1792,512]{1,0:T(8,128)(2,1)S(1)}, bf16[1792,512]{1,0:T(8,128)(2,1)}, u32[]{:S(2)}) copy-start(bf16[1792,512]{1,0:T(8,128)(2,1)} %weight_ref.2) | copy-start | bytes 5505028
  17.8 16.3 %collective-permute-start.3 = (bf16[3,48,512]{2,1,0:T(8,128)(2,1)S(1)}, bf16[3,48,512]{2,1,0:T(8,128)(2,1)S(1)}, u32[]{:S(2)}, u32[]{:S(2)}) collective-permute-start(bf16[3,48,512]{2,1,0:T(8,128)(2,1)S(1)} %pad_maximum_fusion.4.refs_5_), channel_id=1, source_target_pairs={{0,16},{16,0},{1,17},{17,1},{2,18},{18,2},{3,19},{19,3},{4,20},{20... | collective-permute-start | bytes 442376 | tf_op jit(solution)/shard_map/ppermute | solution.py:29
  19.4 1.6 %collective-permute-start.8 = (bf16[2,24,1920]{2,1,0:T(8,128)(2,1)S(1)}, bf16[2,24,1920]{2,1,0:T(8,128)(2,1)S(1)}, u32[]{:S(2)}, u32[]{:S(2)}) collective-permute-start(bf16[2,24,1920]{2,1,0:T(8,128)(2,1)S(1)} %join.3), channel_id=1, source_target_pairs={{0,1},{1,0},{2,3},{3,2},{4,5},{5,4},{6,7},{7,6},{8,9},{9,8},{10,11... | collective-permute-start | bytes 552968 | tf_op jit(solution)/shard_map/ppermute | solution.py:29
  19.5 7.1 %collective-permute-start.6 = (bf16[2,24,1920]{2,1,0:T(8,128)(2,1)S(1)}, bf16[2,24,1920]{2,1,0:T(8,128)(2,1)S(1)}, u32[]{:S(2)}, u32[]{:S(2)}) collective-permute-start(bf16[2,24,1920]{2,1,0:T(8,128)(2,1)S(1)} %join.3), channel_id=1, source_target_pairs={{0,2},{1,3},{2,0},{3,1},{4,6},{5,7},{6,4},{7,5},{8,10},{9,11},{10,... | collective-permute-start | bytes 552968 | tf_op jit(solution)/shard_map/ppermute | solution.py:29
  22.4 1.7 %collective-permute-start.9 = (bf16[2,24,1920]{2,1,0:T(8,128)(2,1)S(1)}, bf16[2,24,1920]{2,1,0:T(8,128)(2,1)S(1)}, u32[]{:S(2)}, u32[]{:S(2)}) collective-permute-start(bf16[2,24,1920]{2,1,0:T(8,128)(2,1)S(1)} %tie.6), channel_id=1, source_target_pairs={{0,1},{1,0},{2,3},{3,2},{4,5},{5,4},{6,7},{7,6},{8,9},{9,8},{10,11... | collective-permute-start | bytes 552968 | tf_op jit(solution)/shard_map/ppermute | solution.py:29
  22.5 9.9 %collective-permute-start.12 = (bf16[3,48,512]{2,1,0:T(8,128)(2,1)S(1)}, bf16[3,48,512]{2,1,0:T(8,128)(2,1)S(1)}, u32[]{:S(2)}, u32[]{:S(2)}) collective-permute-start(bf16[3,48,512]{2,1,0:T(8,128)(2,1)S(1)} %pad_maximum_fusion.6), channel_id=1, source_target_pairs={{0,16},{16,0},{1,17},{17,1},{2,18},{18,2},{3,19},{19,3},{4,20},{20... | collective-permute-start | bytes 442376 | tf_op jit(solution)/shard_map/ppermute | solution.py:29
  26.6 1.4 %collective-permute-start.10 = (bf16[2,24,1920]{2,1,0:T(8,128)(2,1)S(1)}, bf16[2,24,1920]{2,1,0:T(8,128)(2,1)S(1)}, u32[]{:S(2)}, u32[]{:S(2)}) collective-permute-start(bf16[2,24,1920]{2,1,0:T(8,128)(2,1)S(1)} %tie.7), channel_id=1, source_target_pairs={{0,1},{1,0},{2,3},{3,2},{4,5},{5,4},{6,7},{7,6},{8,9},{9,8},{10,11... | collective-permute-start | bytes 552968 | tf_op jit(solution)/shard_map/ppermute | solution.py:29
  26.6 6.7 %collective-permute-start.11 = (bf16[3,48,512]{2,1,0:T(8,128)(2,1)S(1)}, bf16[3,48,512]{2,1,0:T(8,128)(2,1)S(1)}, u32[]{:S(2)}, u32[]{:S(2)}) collective-permute-start(bf16[3,48,512]{2,1,0:T(8,128)(2,1)S(1)} %pad_maximum_fusion.5), channel_id=1, source_target_pairs={{0,16},{16,0},{1,17},{17,1},{2,18},{18,2},{3,19},{19,3},{4,20},{20... | collective-permute-start | bytes 442376 | tf_op jit(solution)/shard_map/ppermute | solution.py:29
  29.4 6.7 %collective-permute-start.13 = (bf16[3,48,512]{2,1,0:T(8,128)(2,1)S(1)}, bf16[3,48,512]{2,1,0:T(8,128)(2,1)S(1)}, u32[]{:S(2)}, u32[]{:S(2)}) collective-permute-start(bf16[3,48,512]{2,1,0:T(8,128)(2,1)S(1)} %pad_maximum_fusion.7), channel_id=1, source_target_pairs={{0,16},{16,0},{1,17},{17,1},{2,18},{18,2},{3,19},{19,3},{4,20},{20... | collective-permute-start | bytes 442376 | tf_op jit(solution)/shard_map/ppermute | solution.py:29
  37.6 1.8 %collective-permute-start.14 = (bf16[2,2,24,1920]{3,2,1,0:T(8,128)(2,1)S(1)}, bf16[2,2,24,1920]{3,2,1,0:T(8,128)(2,1)S(1)}, u32[]{:S(2)}, u32[]{:S(2)}) collective-permute-start(bf16[2,2,24,1920]{3,2,1,0:T(8,128)(2,1)S(1)} %get-tuple-element.65.refs_18_), channel_id=1, source_target_pairs={{0,1},{1,0},{2,3},{3,2},{4,5},{5,4},{6,7},{7,6},{8,9},{9,8},{10,11... | collective-permute-start | bytes 1105928 | tf_op jit(solution)/shard_map/ppermute | solution.py:29
  39.4 7.8 %collective-permute-start.17 = (bf16[24,1920]{1,0:T(8,128)(2,1)S(1)}, bf16[24,1920]{1,0:T(8,128)(2,1)S(1)}, u32[]{:S(2)}, u32[]{:S(2)}) collective-permute-start(bf16[24,1920]{1,0:T(8,128)(2,1)S(1)} %get-tuple-element.69), channel_id=1, source_target_pairs={{0,2},{1,3},{2,0},{3,1},{4,6},{5,7},{6,4},{7,5},{8,10},{9,11},{10,... | collective-permute-start | bytes 276488 | tf_op jit(solution)/shard_map/ppermute | solution.py:29
  40.8 6.2 %collective-permute-start.15 = (bf16[24,1792]{1,0:T(8,128)(2,1)S(1)}, bf16[24,1792]{1,0:T(8,128)(2,1)S(1)}, u32[]{:S(2)}, u32[]{:S(2)}) collective-permute-start(bf16[24,1792]{1,0:T(8,128)(2,1)S(1)} %get-tuple-element.67), channel_id=1, source_target_pairs={{0,18},{1,19},{2,16},{3,17},{4,22},{5,23},{6,20},{7,21},{8,26},{9,... | collective-permute-start | bytes 258056 | tf_op jit(solution)/shard_map/ppermute | solution.py:35
  42.2 4.9 %collective-permute-start.16 = (bf16[24,1792]{1,0:T(8,128)(2,1)S(1)}, bf16[24,1792]{1,0:T(8,128)(2,1)S(1)}, u32[]{:S(2)}, u32[]{:S(2)}) collective-permute-start(bf16[24,1792]{1,0:T(8,128)(2,1)S(1)} %get-tuple-element.68), channel_id=1, source_target_pairs={{0,16},{16,0},{1,17},{17,1},{2,18},{18,2},{3,19},{19,3},{4,20},{20... | collective-permute-start | bytes 258056 | tf_op jit(solution)/shard_map/ppermute | solution.py:29
  47.3 6.8 %collective-permute-start.18 = (bf16[8,2816]{1,0:T(8,128)(2,1)S(1)}, bf16[8,2816]{1,0:T(8,128)(2,1)S(1)}, u32[]{:S(2)}, u32[]{:S(2)}) collective-permute-start(bf16[8,2816]{1,0:T(8,128)(2,1)S(1)} %get-tuple-element.71), channel_id=1, source_target_pairs={{0,8},{1,9},{2,10},{3,11},{4,12},{5,13},{6,14},{7,15},{8,0},{9,1},... | collective-permute-start | bytes 135176 | tf_op jit(solution)/shard_map/ppermute | solution.py:29
  49.6 6.0 %collective-permute-start.19 = (bf16[8,2816]{1,0:T(8,128)(2,1)S(1)}, bf16[8,2816]{1,0:T(8,128)(2,1)S(1)}, u32[]{:S(2)}, u32[]{:S(2)}) collective-permute-start(bf16[8,2816]{1,0:T(8,128)(2,1)S(1)} %get-tuple-element.72), channel_id=1, source_target_pairs={{0,12},{1,13},{2,14},{3,15},{4,8},{5,9},{6,10},{7,11},{8,4},{9,5},... | collective-permute-start | bytes 135176 | tf_op jit(solution)/shard_map/ppermute | solution.py:29
  51.3 4.5 %collective-permute-start.20 = (bf16[8,2816]{1,0:T(8,128)(2,1)S(1)}, bf16[8,2816]{1,0:T(8,128)(2,1)S(1)}, u32[]{:S(2)}, u32[]{:S(2)}) collective-permute-start(bf16[8,2816]{1,0:T(8,128)(2,1)S(1)} %get-tuple-element.73), channel_id=1, source_target_pairs={{0,4},{1,5},{2,6},{3,7},{4,0},{5,1},{6,2},{7,3},{8,12},{9,13},{10,... | collective-permute-start | bytes 135176 | tf_op jit(solution)/shard_map/ppermute | solution.py:29

commit v9 on v8

--- a/solution.py
+++ b/solution.py
@@ -16,7 +16,7 @@
 ROWS = 8
 PIECES = 4
 SQUARE = EXPERTS * ROWS
-RETURN_ORDER = (0, 2, 3, 1)
+RETURN_ORDER = (0, 3, 2, 1)
 JOIN_COST = dict(flops=4000000000, moved=12000000)
 FILL_A = dict(flops=8000000000, moved=24000000)
 FILL_B = dict(flops=8_000_000_000, moved=24_000_000)

time: 57.5 us -> 56.7 us (0.986)
  waiting for transfers between devices: 11.7 us -> 10.4 us
    ppermute x20, waiting for transfers between devices: 7.64 us -> 6.38 us  [swap(): lax.ppermute(x, axis, [(i, i ^ bit) for i in range(lax.axis_size(axis))])]
  transfers between devices with their start and end apart: 21 -> 21, of which waited for: 10 -> 9; matrix products, arithmetic and copies ran while one was open for 10% -> 10% of each run, Pallas kernels for 14% -> 15%
where the time goes in v9:
time: 56.7 us; the launch traced here: 56.5 us
  starting transfers between devices  25.4 us (45%)
  Pallas kernels  13.4 us (24%)
  waiting for transfers between devices  10.4 us (18%)
  matrix products  5 us (9%)
  between operations  1.04 us (2%)
  local copies, waits for them, and re-layouts  0.71 us (1%)
    ppermute x20, starting transfers between devices, swap(): lax.ppermute(x, axis, [(i, i ^ bit) for i in range(lax.axis_size(axis))])  24 us
    ppermute x20, waiting for transfers between devices, swap(): lax.ppermute(x, axis, [(i, i ^ bit) for i in range(lax.axis_size(axis))])  6.38 us
    dot_general x12, matrix products, project(): own.append(jnp.dot(left, weight, preferred_element_type=f32))  5 us
    ppermute x1, waiting for transfers between devices, swap_both(): return lax.ppermute(x, ('pipe', 'expert'), pairs)  4.03 us
    pallas_call x1, Pallas kernels, on_device(): call(functools.partial(weight_kernel, scale, block), [shape((d_part, f_pa...  2.81 us
    pallas_call x3, Pallas kernels, on_device(): call(functools.partial(act_kernel, top_count), grad_shapes(piece), 'svvvv...  2.37 us
    pallas_call x1, Pallas kernels, on_device(): call(functools.partial(owner_kernel, d_part, packed), (shape(tokens.shape...  1.49 us
    ppermute x1, starting transfers between devices, swap_both(): return lax.ppermute(x, ('pipe', 'expert'), pairs)  1.45 us
  transfers between devices with their start and end apart: 21, of which 9 were waited for; matrix products, arithmetic and copies ran while one was open for 10% of the time, Pallas kernels for 15%

profile of v9, /device:TPU:0, one launch (start us, length us, event | category | flops | bytes accessed | tf_op | source)
XLA Modules:
  0.0 56.5 jit_solution(6022845928077082417)
XLA Ops:
  0.7 1.1 %prep.1 = (bf16[16,1920]{1,0:T(8,128)(2,1)S(1)}, bf16[16,1920]{1,0:T(8,128)(2,1)S(1)}) custom-call(bf16[2,4,3584]{2,1,0:T(4,128)(2,1)} %tok_ref.1, bf16[2,4,3584]{2,1,0:T(4,128)(2,1)} %cot_ref.1, s32[2,2,4]{2,1,0:T(2,128)} %bitcast.77, bf16[2,2,4]{2,1,0:T(2,128)(2,1)} %bitcast.78), custom_call_target="tpu_custom_call" | custom-call | tf_op jit(solution)/shard_map/prep/pallas_call | solution.py:328
  1.8 3.0 %collective-permute-start = (bf16[16,1920]{1,0:T(8,128)(2,1)S(1)}, bf16[16,1920]{1,0:T(8,128)(2,1)S(1)}, u32[]{:S(2)}, u32[]{:S(2)}) collective-permute-start(bf16[16,1920]{1,0:T(8,128)(2,1)S(1)} %get-tuple-element.87), channel_id=1, source_target_pairs={{0,16},{16,0},{1,17},{17,1},{2,18},{18,2},{3,19},{19,3},{4,20},{20... | collective-permute-start | bytes 184328 | tf_op jit(solution)/shard_map/ppermute | solution.py:29
  4.8 2.1 %collective-permute-done.refs_1_ = bf16[16,1920]{1,0:T(8,128)(2,1)S(1)} collective-permute-done((bf16[16,1920]{1,0:T(8,128)(2,1)S(1)}, bf16[16,1920]{1,0:T(8,128)(2,1)S(1)}, u32[]{:S(2)}, u32[]{:S(2)}) %collective-permute-start) | collective-permute-done | bytes 61472 | tf_op jit(solution)/shard_map/ppermute | solution.py:29
  7.0 1.0 %pack.1 = (bf16[24,1920]{1,0:T(8,128)(2,1)S(1)}, bf16[24,1920]{1,0:T(8,128)(2,1)S(1)}, bf16[24,1920]{1,0:T(8,128)(2,1)S(1)}, bf16[24,1920]{1,0:T(8,128)(2,1)S(1)}, f32[2,8,256]{2,1,0:T(8,128)S(1)}) custom-call(s32[2]{0:T(128)S(1)} %pad_add_fusion.where_ref, bf16[16,1920]{1,0:T(8,128)(2,1)S(1)} %get-tuple-element.88.refs_0_, ...), custom_call_target="tpu_custom_call" | custom-call | tf_op jit(solution)/shard_map/pack/pallas_call | solution.py:343
  8.0 2.2 %collective-permute-start.1 = (bf16[24,1920]{1,0:T(8,128)(2,1)S(1)}, bf16[24,1920]{1,0:T(8,128)(2,1)S(1)}, u32[]{:S(2)}, u32[]{:S(2)}) collective-permute-start(bf16[24,1920]{1,0:T(8,128)(2,1)S(1)} %get-tuple-element.46), channel_id=1, source_target_pairs={{0,4},{1,5},{2,6},{3,7},{4,0},{5,1},{6,2},{7,3},{8,12},{9,13},{10,... | collective-permute-start | bytes 276488 | tf_op jit(solution)/shard_map/ppermute | solution.py:29
  10.2 2.6 %collective-permute-start.4 = (bf16[24,1920]{1,0:T(8,128)(2,1)S(1)}, bf16[24,1920]{1,0:T(8,128)(2,1)S(1)}, u32[]{:S(2)}, u32[]{:S(2)}) collective-permute-start(bf16[24,1920]{1,0:T(8,128)(2,1)S(1)} %get-tuple-element.47), channel_id=1, source_target_pairs={{0,8},{1,9},{2,10},{3,11},{4,12},{5,13},{6,14},{7,15},{8,0},{9,1},... | collective-permute-start | bytes 276488 | tf_op jit(solution)/shard_map/ppermute | solution.py:29
  12.7 0.9 %collective-permute-done.1.refs_1_ = bf16[24,1920]{1,0:T(8,128)(2,1)S(1)} collective-permute-done((bf16[24,1920]{1,0:T(8,128)(2,1)S(1)}, bf16[24,1920]{1,0:T(8,128)(2,1)S(1)}, u32[]{:S(2)}, u32[]{:S(2)}) %collective-permute-start.1) | collective-permute-done | bytes 92192 | tf_op jit(solution)/shard_map/ppermute | solution.py:29
  13.8 1.9 %collective-permute-start.7 = (bf16[2,24,1920]{2,1,0:T(8,128)(2,1)S(1)}, bf16[2,24,1920]{2,1,0:T(8,128)(2,1)S(1)}, u32[]{:S(2)}, u32[]{:S(2)}) collective-permute-start(bf16[2,24,1920]{2,1,0:T(8,128)(2,1)S(1)} %join.2), channel_id=1, source_target_pairs={{0,2},{1,3},{2,0},{3,1},{4,6},{5,7},{6,4},{7,5},{8,10},{9,11},{10,... | collective-permute-start | bytes 552968 | tf_op jit(solution)/shard_map/ppermute | solution.py:29
  16.7 0.7 %copy-done.2 = bf16[1792,512]{1,0:T(8,128)(2,1)S(1)} copy-done((bf16[1792,512]{1,0:T(8,128)(2,1)S(1)}, bf16[1792,512]{1,0:T(8,128)(2,1)}, u32[]{:S(2)}) %copy-start.2) | copy-done | bytes 1835032
  17.8 1.6 %collective-permute-start.3 = (bf16[3,48,512]{2,1,0:T(8,128)(2,1)S(1)}, bf16[3,48,512]{2,1,0:T(8,128)(2,1)S(1)}, u32[]{:S(2)}, u32[]{:S(2)}) collective-permute-start(bf16[3,48,512]{2,1,0:T(8,128)(2,1)S(1)} %pad_maximum_fusion.4.refs_5_), channel_id=1, source_target_pairs={{0,16},{16,0},{1,17},{17,1},{2,18},{18,2},{3,19},{19,3},{4,20},{20... | collective-permute-start | bytes 442376 | tf_op jit(solution)/shard_map/ppermute | solution.py:29
  19.5 1.5 %collective-permute-start.6 = (bf16[2,24,1920]{2,1,0:T(8,128)(2,1)S(1)}, bf16[2,24,1920]{2,1,0:T(8,128)(2,1)S(1)}, u32[]{:S(2)}, u32[]{:S(2)}) collective-permute-start(bf16[2,24,1920]{2,1,0:T(8,128)(2,1)S(1)} %join.3), channel_id=1, source_target_pairs={{0,2},{1,3},{2,0},{3,1},{4,6},{5,7},{6,4},{7,5},{8,10},{9,11},{10,... | collective-permute-start | bytes 552968 | tf_op jit(solution)/shard_map/ppermute | solution.py:29
  22.5 1.6 %collective-permute-start.12 = (bf16[3,48,512]{2,1,0:T(8,128)(2,1)S(1)}, bf16[3,48,512]{2,1,0:T(8,128)(2,1)S(1)}, u32[]{:S(2)}, u32[]{:S(2)}) collective-permute-start(bf16[3,48,512]{2,1,0:T(8,128)(2,1)S(1)} %pad_maximum_fusion.6), channel_id=1, source_target_pairs={{0,16},{16,0},{1,17},{17,1},{2,18},{18,2},{3,19},{19,3},{4,20},{20... | collective-permute-start | bytes 442376 | tf_op jit(solution)/shard_map/ppermute | solution.py:29
  25.5 1.1 %collective-permute-done.6.refs_0_ = bf16[2,24,1920]{2,1,0:T(8,128)(2,1)S(1)} collective-permute-done((bf16[2,24,1920]{2,1,0:T(8,128)(2,1)S(1)}, bf16[2,24,1920]{2,1,0:T(8,128)(2,1)S(1)}, u32[]{:S(2)}, u32[]{:S(2)}) %collective-permute-start.6) | collective-permute-done | bytes 184352 | tf_op jit(solution)/shard_map/ppermute | solution.py:29
  26.6 1.4 %collective-permute-start.11 = (bf16[3,48,512]{2,1,0:T(8,128)(2,1)S(1)}, bf16[3,48,512]{2,1,0:T(8,128)(2,1)S(1)}, u32[]{:S(2)}, u32[]{:S(2)}) collective-permute-start(bf16[3,48,512]{2,1,0:T(8,128)(2,1)S(1)} %pad_maximum_fusion.5), channel_id=1, source_target_pairs={{0,16},{16,0},{1,17},{17,1},{2,18},{18,2},{3,19},{19,3},{4,20},{20... | collective-permute-start | bytes 442376 | tf_op jit(solution)/shard_map/ppermute | solution.py:29
  29.4 1.4 %collective-permute-start.13 = (bf16[3,48,512]{2,1,0:T(8,128)(2,1)S(1)}, bf16[3,48,512]{2,1,0:T(8,128)(2,1)S(1)}, u32[]{:S(2)}, u32[]{:S(2)}) collective-permute-start(bf16[3,48,512]{2,1,0:T(8,128)(2,1)S(1)} %pad_maximum_fusion.7), channel_id=1, source_target_pairs={{0,16},{16,0},{1,17},{17,1},{2,18},{18,2},{3,19},{19,3},{4,20},{20... | collective-permute-start | bytes 442376 | tf_op jit(solution)/shard_map/ppermute | solution.py:29
  30.8 0.5 flip_weight.3.refs_18_.refs_17_
  31.3 0.5 flip_weight.2.refs_17_.refs_16_
  32.4 0.8 %act.5 = (bf16[2,24,512]{2,1,0:T(8,128)(2,1)S(1)}, bf16[2,24,512]{2,1,0:T(8,128)(2,1)S(1)}, bf16[2,24,512]{2,1,0:T(8,128)(2,1)S(1)}, bf16[2,24,128]{2,1,0:T(8,128)(2,1)S(1)}) custom-call(s32[2]{0:T(128)S(1)} %pad_add_fusion.where_ref, bf16[48,128]{1,0:T(8,128)(2,1)S(1)} %fusion.12.refs_0_, f32[48,512]{1,0:T(8,128)S(1)} %fusion.23.refs_1_, ...), custom_call_target="tpu_custom_call" | custom-call | tf_op jit(solution)/shard_map/act/pallas_call | solution.py:423
  33.3 0.8 %act.4 = (bf16[2,24,512]{2,1,0:T(8,128)(2,1)S(1)}, bf16[2,24,512]{2,1,0:T(8,128)(2,1)S(1)}, bf16[2,24,512]{2,1,0:T(8,128)(2,1)S(1)}, bf16[2,24,128]{2,1,0:T(8,128)(2,1)S(1)}) custom-call(s32[2]{0:T(128)S(1)} %pad_add_fusion.where_ref, bf16[48,128]{1,0:T(8,128)(2,1)S(1)} %fusion.13.refs_0_, f32[48,512]{1,0:T(8,128)S(1)} %fusion.21.refs_1_, ...), custom_call_target="tpu_custom_call" | custom-call | tf_op jit(solution)/shard_map/act/pallas_call | solution.py:423
  34.1 0.8 %act.3 = (bf16[2,24,512]{2,1,0:T(8,128)(2,1)S(1)}, bf16[2,24,512]{2,1,0:T(8,128)(2,1)S(1)}, bf16[2,24,512]{2,1,0:T(8,128)(2,1)S(1)}, bf16[2,24,128]{2,1,0:T(8,128)(2,1)S(1)}) custom-call(s32[2]{0:T(128)S(1)} %pad_add_fusion.where_ref, bf16[48,128]{1,0:T(8,128)(2,1)S(1)} %slice_bitcast_fusion.2.refs_0_, f32[48,512]{1,0:T(8,128)S(1)} %fusion.17.refs_2_.refs_1_, ...), custom_call_target="tpu_custom_call" | custom-call | tf_op jit(solution)/shard_map/act/pallas_call | solution.py:423
  34.9 1.2 %collective-permute-done.13.refs_4_ = bf16[3,48,512]{2,1,0:T(8,128)(2,1)S(1)} collective-permute-done((bf16[3,48,512]{2,1,0:T(8,128)(2,1)S(1)}, bf16[3,48,512]{2,1,0:T(8,128)(2,1)S(1)}, u32[]{:S(2)}, u32[]{:S(2)}) %collective-permute-start.13) | collective-permute-done | bytes 147488 | tf_op jit(solution)/shard_map/ppermute | solution.py:29
  36.1 1.4 %last_act.1 = (bf16[2,24,512]{2,1,0:T(8,128)(2,1)S(1)}, bf16[2,24,512]{2,1,0:T(8,128)(2,1)S(1)}, bf16[2,24,512]{2,1,0:T(8,128)(2,1)S(1)}, bf16[2,24,128]{2,1,0:T(8,128)(2,1)S(1)}, bf16[2,2,24,1920]{3,2,1,0:T(8,128)(2,1)S(1)}) custom-call(s32[2]{0:T(128)S(1)} %pad_add_fusion.where_ref, bf16[48,128]{1,0:T(8,128)(2,1)S(1)} %fusion.14.refs_0_, ...), custom_call_target="tpu_custom_call" | custom-call | tf_op jit(solution)/shard_map/last_act/pallas_call | solution.py:428
  37.6 1.3 %own_back.1.a_ref = bf16[2,2,24,1920]{3,2,1,0:T(8,128)(2,1)S(1)} custom-call(s32[2]{0:T(128)S(1)} %pad_add_fusion.where_ref, bf16[2,24,512]{2,1,0:T(8,128)(2,1)S(1)} %get-tuple-element.49.refs_5_.refs_0_, bf16[2,24,512]{2,1,0:T(8,128)(2,1)S(1)} %get-tuple-element.50.refs_6_.refs_1_, bf16[2,24,512]{2,1,0:T(8,128)(2,1)S(1)} %get-tuple-element.51.refs_7_.refs_2_, ...), custom_call_target="tpu_custom_call" | custom-call | tf_op jit(solution)/shard_map/own_back/pallas_call | solution.py:436
  39.4 1.4 %collective-permute-start.17 = (bf16[24,1920]{1,0:T(8,128)(2,1)S(1)}, bf16[24,1920]{1,0:T(8,128)(2,1)S(1)}, u32[]{:S(2)}, u32[]{:S(2)}) collective-permute-start(bf16[24,1920]{1,0:T(8,128)(2,1)S(1)} %get-tuple-element.69), channel_id=1, source_target_pairs={{0,2},{1,3},{2,0},{3,1},{4,6},{5,7},{6,4},{7,5},{8,10},{9,11},{10,... | collective-permute-start | bytes 276488 | tf_op jit(solution)/shard_map/ppermute | solution.py:29
  40.8 1.4 %collective-permute-start.15 = (bf16[24,1792]{1,0:T(8,128)(2,1)S(1)}, bf16[24,1792]{1,0:T(8,128)(2,1)S(1)}, u32[]{:S(2)}, u32[]{:S(2)}) collective-permute-start(bf16[24,1792]{1,0:T(8,128)(2,1)S(1)} %get-tuple-element.67), channel_id=1, source_target_pairs={{0,18},{1,19},{2,16},{3,17},{4,22},{5,23},{6,20},{7,21},{8,26},{9,... | collective-permute-start | bytes 258056 | tf_op jit(solution)/shard_map/ppermute | solution.py:35
  42.2 0.7 %collective-permute-start.16 = (bf16[24,1792]{1,0:T(8,128)(2,1)S(1)}, bf16[24,1792]{1,0:T(8,128)(2,1)S(1)}, u32[]{:S(2)}, u32[]{:S(2)}) collective-permute-start(bf16[24,1792]{1,0:T(8,128)(2,1)S(1)} %get-tuple-element.68), channel_id=1, source_target_pairs={{0,16},{16,0},{1,17},{17,1},{2,18},{18,2},{3,19},{19,3},{4,20},{20... | collective-permute-start | bytes 258056 | tf_op jit(solution)/shard_map/ppermute | solution.py:29
  42.9 4.0 %collective-permute-done.15.b_ref = bf16[24,1792]{1,0:T(8,128)(2,1)S(1)} collective-permute-done((bf16[24,1792]{1,0:T(8,128)(2,1)S(1)}, bf16[24,1792]{1,0:T(8,128)(2,1)S(1)}, u32[]{:S(2)}, u32[]{:S(2)}) %collective-permute-start.15) | collective-permute-done | bytes 86048 | tf_op jit(solution)/shard_map/ppermute | solution.py:35
  47.3 2.7 %collective-permute-start.18 = (bf16[8,2816]{1,0:T(8,128)(2,1)S(1)}, bf16[8,2816]{1,0:T(8,128)(2,1)S(1)}, u32[]{:S(2)}, u32[]{:S(2)}) collective-permute-start(bf16[8,2816]{1,0:T(8,128)(2,1)S(1)} %get-tuple-element.71), channel_id=1, source_target_pairs={{0,12},{1,13},{2,14},{3,15},{4,8},{5,9},{6,10},{7,11},{8,4},{9,5},... | collective-permute-start | bytes 135176 | tf_op jit(solution)/shard_map/ppermute | solution.py:29
  50.4 1.3 %collective-permute-start.20 = (bf16[8,2816]{1,0:T(8,128)(2,1)S(1)}, bf16[8,2816]{1,0:T(8,128)(2,1)S(1)}, u32[]{:S(2)}, u32[]{:S(2)}) collective-permute-start(bf16[8,2816]{1,0:T(8,128)(2,1)S(1)} %get-tuple-element.73), channel_id=1, source_target_pairs={{0,4},{1,5},{2,6},{3,7},{4,0},{5,1},{6,2},{7,3},{8,12},{9,13},{10,... | collective-permute-start | bytes 135176 | tf_op jit(solution)/shard_map/ppermute | solution.py:29
  51.8 2.8 %weight_grads.1 = (bf16[1792,512]{1,0:T(8,128)(2,1)}, bf16[1792,512]{1,0:T(8,128)(2,1)}, bf16[1792,512]{1,0:T(8,128)(2,1)}) custom-call(bf16[1792,192]{1,0:T(8,128)(2,1)S(1)} %flip.2.refs_19_.tok_ref, bf16[1792,192]{1,0:T(8,128)(2,1)S(1)} %flip.3.refs_20_.cot_ref, bf16[2,24,512]{2,1,0:T(8,128)(2,1)S(1)} %get-tuple-element.49.refs_5_.refs_0_, ...), custom_call_target="tpu_custom_call" | custom-call | tf_op jit(solution)/shard_map/weight_grads/pallas_call | solution.py:480
  54.6 0.4 collective-permute-done.19.refs_2_
  55.0 1.5 %owner.1 = (bf16[2,4,3584]{2,1,0:T(4,128)(2,1)}, f32[2,2,4]{2,1,0:T(2,128)}) custom-call(s32[2]{0:T(128)S(1)} %pad_add_fusion.where_ref, f32[2,8,256]{2,1,0:T(8,128)S(1)} %get-tuple-element.44.refs_1_.place_ref, bf16[8,2816]{1,0:T(8,128)(2,1)S(1)} %get-tuple-element.70.refs_0_, bf16[8,2816]{1,0:T(8,128)(2,1)S(1)} %collective-permute-done.18.refs_1_, ...), custom_call_target="tpu_custom_call" | custom-call | tf_op jit(solution)/shard_map/owner/pallas_call | solution.py:493
  (76 shorter events, 7.9 us)
Async XLA Ops:
  0.6 15.6 %copy-start = (bf16[1792,512]{1,0:T(8,128)(2,1)S(1)}, bf16[1792,512]{1,0:T(8,128)(2,1)}, u32[]{:S(2)}) copy-start(bf16[1792,512]{1,0:T(8,128)(2,1)} %param.13) | copy-start | bytes 5505028
  1.8 5.2 %collective-permute-start = (bf16[16,1920]{1,0:T(8,128)(2,1)S(1)}, bf16[16,1920]{1,0:T(8,128)(2,1)S(1)}, u32[]{:S(2)}, u32[]{:S(2)}) collective-permute-start(bf16[16,1920]{1,0:T(8,128)(2,1)S(1)} %get-tuple-element.87), channel_id=1, source_target_pairs={{0,16},{16,0},{1,17},{17,1},{2,18},{18,2},{3,19},{19,3},{4,20},{20... | collective-permute-start | bytes 184328 | tf_op jit(solution)/shard_map/ppermute | solution.py:29
  8.0 5.6 %collective-permute-start.1 = (bf16[24,1920]{1,0:T(8,128)(2,1)S(1)}, bf16[24,1920]{1,0:T(8,128)(2,1)S(1)}, u32[]{:S(2)}, u32[]{:S(2)}) collective-permute-start(bf16[24,1920]{1,0:T(8,128)(2,1)S(1)} %get-tuple-element.46), channel_id=1, source_target_pairs={{0,4},{1,5},{2,6},{3,7},{4,0},{5,1},{6,2},{7,3},{8,12},{9,13},{10,... | collective-permute-start | bytes 276488 | tf_op jit(solution)/shard_map/ppermute | solution.py:29
  10.2 9.2 %collective-permute-start.4 = (bf16[24,1920]{1,0:T(8,128)(2,1)S(1)}, bf16[24,1920]{1,0:T(8,128)(2,1)S(1)}, u32[]{:S(2)}, u32[]{:S(2)}) collective-permute-start(bf16[24,1920]{1,0:T(8,128)(2,1)S(1)} %get-tuple-element.47), channel_id=1, source_target_pairs={{0,8},{1,9},{2,10},{3,11},{4,12},{5,13},{6,14},{7,15},{8,0},{9,1},... | collective-permute-start | bytes 276488 | tf_op jit(solution)/shard_map/ppermute | solution.py:29
  12.7 6.6 %collective-permute-start.5 = (bf16[24,1920]{1,0:T(8,128)(2,1)S(1)}, bf16[24,1920]{1,0:T(8,128)(2,1)S(1)}, u32[]{:S(2)}, u32[]{:S(2)}) collective-permute-start(bf16[24,1920]{1,0:T(8,128)(2,1)S(1)} %get-tuple-element.48), channel_id=1, source_target_pairs={{0,12},{1,13},{2,14},{3,15},{4,8},{5,9},{6,10},{7,11},{8,4},{9,5},... | collective-permute-start | bytes 276488 | tf_op jit(solution)/shard_map/ppermute | solution.py:29
  13.7 2.1 %collective-permute-start.2 = (bf16[2,24,1920]{2,1,0:T(8,128)(2,1)S(1)}, bf16[2,24,1920]{2,1,0:T(8,128)(2,1)S(1)}, u32[]{:S(2)}, u32[]{:S(2)}) collective-permute-start(bf16[2,24,1920]{2,1,0:T(8,128)(2,1)S(1)} %join.2), channel_id=1, source_target_pairs={{0,1},{1,0},{2,3},{3,2},{4,5},{5,4},{6,7},{7,6},{8,9},{9,8},{10,11... | collective-permute-start | bytes 552968 | tf_op jit(solution)/shard_map/ppermute | solution.py:29
  13.8 2.0 %copy-start.1 = (bf16[1792,512]{1,0:T(8,128)(2,1)S(1)}, bf16[1792,512]{1,0:T(8,128)(2,1)}, u32[]{:S(2)}) copy-start(bf16[1792,512]{1,0:T(8,128)(2,1)} %weight_ref.3) | copy-start | bytes 5505028
  13.8 8.6 %collective-permute-start.7 = (bf16[2,24,1920]{2,1,0:T(8,128)(2,1)S(1)}, bf16[2,24,1920]{2,1,0:T(8,128)(2,1)S(1)}, u32[]{:S(2)}, u32[]{:S(2)}) collective-permute-start(bf16[2,24,1920]{2,1,0:T(8,128)(2,1)S(1)} %join.2), channel_id=1, source_target_pairs={{0,2},{1,3},{2,0},{3,1},{4,6},{5,7},{6,4},{7,5},{8,10},{9,11},{10,... | collective-permute-start | bytes 552968 | tf_op jit(solution)/shard_map/ppermute | solution.py:29
  15.8 1.5 %copy-start.2 = (bf16[1792,512]{1,0:T(8,128)(2,1)S(1)}, bf16[1792,512]{1,0:T(8,128)(2,1)}, u32[]{:S(2)}) copy-start(bf16[1792,512]{1,0:T(8,128)(2,1)} %weight_ref.2) | copy-start | bytes 5505028
  17.8 16.3 %collective-permute-start.3 = (bf16[3,48,512]{2,1,0:T(8,128)(2,1)S(1)}, bf16[3,48,512]{2,1,0:T(8,128)(2,1)S(1)}, u32[]{:S(2)}, u32[]{:S(2)}) collective-permute-start(bf16[3,48,512]{2,1,0:T(8,128)(2,1)S(1)} %pad_maximum_fusion.4.refs_5_), channel_id=1, source_target_pairs={{0,16},{16,0},{1,17},{17,1},{2,18},{18,2},{3,19},{19,3},{4,20},{20... | collective-permute-start | bytes 442376 | tf_op jit(solution)/shard_map/ppermute | solution.py:29
  19.4 1.6 %collective-permute-start.8 = (bf16[2,24,1920]{2,1,0:T(8,128)(2,1)S(1)}, bf16[2,24,1920]{2,1,0:T(8,128)(2,1)S(1)}, u32[]{:S(2)}, u32[]{:S(2)}) collective-permute-start(bf16[2,24,1920]{2,1,0:T(8,128)(2,1)S(1)} %join.3), channel_id=1, source_target_pairs={{0,1},{1,0},{2,3},{3,2},{4,5},{5,4},{6,7},{7,6},{8,9},{9,8},{10,11... | collective-permute-start | bytes 552968 | tf_op jit(solution)/shard_map/ppermute | solution.py:29
  19.5 7.1 %collective-permute-start.6 = (bf16[2,24,1920]{2,1,0:T(8,128)(2,1)S(1)}, bf16[2,24,1920]{2,1,0:T(8,128)(2,1)S(1)}, u32[]{:S(2)}, u32[]{:S(2)}) collective-permute-start(bf16[2,24,1920]{2,1,0:T(8,128)(2,1)S(1)} %join.3), channel_id=1, source_target_pairs={{0,2},{1,3},{2,0},{3,1},{4,6},{5,7},{6,4},{7,5},{8,10},{9,11},{10,... | collective-permute-start | bytes 552968 | tf_op jit(solution)/shard_map/ppermute | solution.py:29
  22.4 1.7 %collective-permute-start.9 = (bf16[2,24,1920]{2,1,0:T(8,128)(2,1)S(1)}, bf16[2,24,1920]{2,1,0:T(8,128)(2,1)S(1)}, u32[]{:S(2)}, u32[]{:S(2)}) collective-permute-start(bf16[2,24,1920]{2,1,0:T(8,128)(2,1)S(1)} %tie.6), channel_id=1, source_target_pairs={{0,1},{1,0},{2,3},{3,2},{4,5},{5,4},{6,7},{7,6},{8,9},{9,8},{10,11... | collective-permute-start | bytes 552968 | tf_op jit(solution)/shard_map/ppermute | solution.py:29
  22.5 9.9 %collective-permute-start.12 = (bf16[3,48,512]{2,1,0:T(8,128)(2,1)S(1)}, bf16[3,48,512]{2,1,0:T(8,128)(2,1)S(1)}, u32[]{:S(2)}, u32[]{:S(2)}) collective-permute-start(bf16[3,48,512]{2,1,0:T(8,128)(2,1)S(1)} %pad_maximum_fusion.6), channel_id=1, source_target_pairs={{0,16},{16,0},{1,17},{17,1},{2,18},{18,2},{3,19},{19,3},{4,20},{20... | collective-permute-start | bytes 442376 | tf_op jit(solution)/shard_map/ppermute | solution.py:29
  26.6 1.4 %collective-permute-start.10 = (bf16[2,24,1920]{2,1,0:T(8,128)(2,1)S(1)}, bf16[2,24,1920]{2,1,0:T(8,128)(2,1)S(1)}, u32[]{:S(2)}, u32[]{:S(2)}) collective-permute-start(bf16[2,24,1920]{2,1,0:T(8,128)(2,1)S(1)} %tie.7), channel_id=1, source_target_pairs={{0,1},{1,0},{2,3},{3,2},{4,5},{5,4},{6,7},{7,6},{8,9},{9,8},{10,11... | collective-permute-start | bytes 552968 | tf_op jit(solution)/shard_map/ppermute | solution.py:29
  26.6 6.7 %collective-permute-start.11 = (bf16[3,48,512]{2,1,0:T(8,128)(2,1)S(1)}, bf16[3,48,512]{2,1,0:T(8,128)(2,1)S(1)}, u32[]{:S(2)}, u32[]{:S(2)}) collective-permute-start(bf16[3,48,512]{2,1,0:T(8,128)(2,1)S(1)} %pad_maximum_fusion.5), channel_id=1, source_target_pairs={{0,16},{16,0},{1,17},{17,1},{2,18},{18,2},{3,19},{19,3},{4,20},{20... | collective-permute-start | bytes 442376 | tf_op jit(solution)/shard_map/ppermute | solution.py:29
  29.4 6.7 %collective-permute-start.13 = (bf16[3,48,512]{2,1,0:T(8,128)(2,1)S(1)}, bf16[3,48,512]{2,1,0:T(8,128)(2,1)S(1)}, u32[]{:S(2)}, u32[]{:S(2)}) collective-permute-start(bf16[3,48,512]{2,1,0:T(8,128)(2,1)S(1)} %pad_maximum_fusion.7), channel_id=1, source_target_pairs={{0,16},{16,0},{1,17},{17,1},{2,18},{18,2},{3,19},{19,3},{4,20},{20... | collective-permute-start | bytes 442376 | tf_op jit(solution)/shard_map/ppermute | solution.py:29
  37.6 1.8 %collective-permute-start.14 = (bf16[2,2,24,1920]{3,2,1,0:T(8,128)(2,1)S(1)}, bf16[2,2,24,1920]{3,2,1,0:T(8,128)(2,1)S(1)}, u32[]{:S(2)}, u32[]{:S(2)}) collective-permute-start(bf16[2,2,24,1920]{3,2,1,0:T(8,128)(2,1)S(1)} %get-tuple-element.65.refs_18_), channel_id=1, source_target_pairs={{0,1},{1,0},{2,3},{3,2},{4,5},{5,4},{6,7},{7,6},{8,9},{9,8},{10,11... | collective-permute-start | bytes 1105928 | tf_op jit(solution)/shard_map/ppermute | solution.py:29
  39.4 7.8 %collective-permute-start.17 = (bf16[24,1920]{1,0:T(8,128)(2,1)S(1)}, bf16[24,1920]{1,0:T(8,128)(2,1)S(1)}, u32[]{:S(2)}, u32[]{:S(2)}) collective-permute-start(bf16[24,1920]{1,0:T(8,128)(2,1)S(1)} %get-tuple-element.69), channel_id=1, source_target_pairs={{0,2},{1,3},{2,0},{3,1},{4,6},{5,7},{6,4},{7,5},{8,10},{9,11},{10,... | collective-permute-start | bytes 276488 | tf_op jit(solution)/shard_map/ppermute | solution.py:29
  40.8 6.2 %collective-permute-start.15 = (bf16[24,1792]{1,0:T(8,128)(2,1)S(1)}, bf16[24,1792]{1,0:T(8,128)(2,1)S(1)}, u32[]{:S(2)}, u32[]{:S(2)}) collective-permute-start(bf16[24,1792]{1,0:T(8,128)(2,1)S(1)} %get-tuple-element.67), channel_id=1, source_target_pairs={{0,18},{1,19},{2,16},{3,17},{4,22},{5,23},{6,20},{7,21},{8,26},{9,... | collective-permute-start | bytes 258056 | tf_op jit(solution)/shard_map/ppermute | solution.py:35
  42.2 4.9 %collective-permute-start.16 = (bf16[24,1792]{1,0:T(8,128)(2,1)S(1)}, bf16[24,1792]{1,0:T(8,128)(2,1)S(1)}, u32[]{:S(2)}, u32[]{:S(2)}) collective-permute-start(bf16[24,1792]{1,0:T(8,128)(2,1)S(1)} %get-tuple-element.68), channel_id=1, source_target_pairs={{0,16},{16,0},{1,17},{17,1},{2,18},{18,2},{3,19},{19,3},{4,20},{20... | collective-permute-start | bytes 258056 | tf_op jit(solution)/shard_map/ppermute | solution.py:29
  47.3 7.3 %collective-permute-start.18 = (bf16[8,2816]{1,0:T(8,128)(2,1)S(1)}, bf16[8,2816]{1,0:T(8,128)(2,1)S(1)}, u32[]{:S(2)}, u32[]{:S(2)}) collective-permute-start(bf16[8,2816]{1,0:T(8,128)(2,1)S(1)} %get-tuple-element.71), channel_id=1, source_target_pairs={{0,12},{1,13},{2,14},{3,15},{4,8},{5,9},{6,10},{7,11},{8,4},{9,5},... | collective-permute-start | bytes 135176 | tf_op jit(solution)/shard_map/ppermute | solution.py:29
  50.0 5.0 %collective-permute-start.19 = (bf16[8,2816]{1,0:T(8,128)(2,1)S(1)}, bf16[8,2816]{1,0:T(8,128)(2,1)S(1)}, u32[]{:S(2)}, u32[]{:S(2)}) collective-permute-start(bf16[8,2816]{1,0:T(8,128)(2,1)S(1)} %get-tuple-element.72), channel_id=1, source_target_pairs={{0,8},{1,9},{2,10},{3,11},{4,12},{5,13},{6,14},{7,15},{8,0},{9,1},... | collective-permute-start | bytes 135176 | tf_op jit(solution)/shard_map/ppermute | solution.py:29
  50.4 4.6 %collective-permute-start.20 = (bf16[8,2816]{1,0:T(8,128)(2,1)S(1)}, bf16[8,2816]{1,0:T(8,128)(2,1)S(1)}, u32[]{:S(2)}, u32[]{:S(2)}) collective-permute-start(bf16[8,2816]{1,0:T(8,128)(2,1)S(1)} %get-tuple-element.73), channel_id=1, source_target_pairs={{0,4},{1,5},{2,6},{3,7},{4,0},{5,1},{6,2},{7,3},{8,12},{9,13},{10,... | collective-permute-start | bytes 135176 | tf_op jit(solution)/shard_map/ppermute | solution.py:29

commit v10 on v9

--- a/solution.py
+++ b/solution.py
@@ -33,6 +33,10 @@
     count = lax.axis_size("expert")
     pairs = [(p * count + e, (p ^ 1) * count + (e ^ bit)) for p in range(2) for e in range(count)]
     return lax.ppermute(x, ("pipe", "expert"), pairs)
+
+
+def scalar(ref, lane):
+    return ref[...][0, lane]
 
 
 def prep_kernel(d_part, tok_ref, cot_ref, ids_ref, gate_ref, *out_refs):
@@ -72,9 +76,9 @@
     own_rows = both_rows // 2
     total = pipe_size * both_rows
     slot_count = slot_refs[0].shape[0] // 2
-    me = where_ref[0]
+    me = scalar(where_ref, 0)
     if pipe_size == 2:
-        first = where_ref[1] == 0
+        first = scalar(where_ref, 1) == 0
         blocks = [jnp.where(first, blocks[0], blocks[1]), jnp.where(first, blocks[1], blocks[0])]
     rows = jnp.concatenate(blocks, 0)
     extras = rows[:, width - LANES :].astype(f32)
@@ -150,7 +154,7 @@
 
 
 def act_kernel(top_count, where_ref, *refs):
-    store_halves(hidden_gradients(top_count, where_ref[0].astype(f32), *refs[:5]), refs[6:])
+    store_halves(hidden_gradients(top_count, scalar(where_ref, 0).astype(f32), *refs[:5]), refs[6:])
 
 
 def back_rows(d_part, pipe_size, where_ref, grads, w_gate, w_up, out_ref):
@@ -164,7 +168,7 @@
         for member in range(members):
             for p in range(pipe_size):
                 starts = [(2 * g + h) * count + (member * pipe_size + p) * used for g in range(GROUPS)]
-                at = member * pipe_size + (p ^ where_ref[1] if pipe_size == 2 else p)
+                at = member * pipe_size + (p ^ scalar(where_ref, 1) if pipe_size == 2 else p)
                 for columns, values in ((slice(0, d_part), back), (slice(d_part, None), left[2])):
                     block = jnp.concatenate([values[start : start + used] for start in starts], 0)
                     out_ref[h, at, :, columns] = block.astype(bf16)
@@ -174,7 +178,7 @@
     raw, outs = refs[:5], refs[-5:]
     others = [refs[5 + 4 * i : 9 + 4 * i] for i in range(PIECES - 1)]
     w_gate, w_up = refs[4 * PIECES + 1 : 4 * PIECES + 3]
-    last = hidden_gradients(top_count, where_ref[0].astype(f32), *raw)
+    last = hidden_gradients(top_count, scalar(where_ref, 0).astype(f32), *raw)
     store_halves(last, outs[:4])
     half = last[0].shape[0] // 2
     grads = [[ref[1] for ref in other] for other in others] + [[value[half:] for value in last]]
@@ -218,7 +222,7 @@
     piece_refs = [piece_refs[RETURN_ORDER.index(k)] for k in range(EXPERTS)]
     micro_count, tok_count, d_model = tok_ref.shape
     top_count = grad_ref.shape[1]
-    mine = place_ref[where_ref[1]]
+    mine = place_ref[scalar(where_ref, 1)]
     places = mine[:, :LANES].astype(bf16)
     place = places[:, :SQUARE]
     ids = mine[:, LANES:]
@@ -232,13 +236,13 @@
             columns = rows[:, j * quarter : (j + 1) * quarter]
             rest = rest + jnp.dot(spare, columns, preferred_element_type=f32)
         out = jnp.concatenate([out, rest], 1)
-        first = where_ref[1] == 0
+        first = scalar(where_ref, 1) == 0
         here, there = out[:, :d_part], out[:, d_part:]
         out = jnp.concatenate([jnp.where(first, here, there), jnp.where(first, there, here)], 1)
     for m in range(micro_count):
         tok_ref[m] = out[m * tok_count : (m + 1) * tok_count].astype(bf16)
 
-    expert_of = ((lax.broadcasted_iota(i32, place.shape, 1) // ROWS) ^ where_ref[0]).astype(f32)
+    expert_of = ((lax.broadcasted_iota(i32, place.shape, 1) // ROWS) ^ scalar(where_ref, 0)).astype(f32)
     diagonal = lax.broadcasted_iota(i32, (tok_count, tok_count), 0) == lax.broadcasted_iota(
         i32, (tok_count, tok_count), 1
     )
@@ -283,7 +287,7 @@
 
 
 def call(kernel, out_shape, operands, name, mib=8, flops=0, moved=0, **more):
-    specs = {"s": pl.BlockSpec(memory_space=pltpu.SMEM), "v": pl.BlockSpec(memory_space=pltpu.VMEM)}
+    specs = {"v": pl.BlockSpec(memory_space=pltpu.VMEM)}
     specs["a"] = pl.BlockSpec(memory_space=pl.ANY)
     more.setdefault("in_specs", [specs[c] for c in operands])
     more.setdefault("out_specs", jax.tree.map(lambda _: specs["v"], out_shape))
@@ -322,7 +326,8 @@
     slots_here = micro_count * CAP
     slot_count = pipe_size * slots_here
     pipe = lax.axis_index("pipe")
-    where = jnp.stack([lax.axis_index("expert") // group_size, pipe]).astype(i32)
+    lanes = lax.broadcasted_iota(i32, (ROWS, LANES), 1)
+    where = jnp.where(lanes == 0, (lax.axis_index("expert") // group_size).astype(i32), pipe.astype(i32))
 
     inputs = (tokens, cotangent, jnp.swapaxes(expert_ids, 1, 2), jnp.swapaxes(gate_values, 1, 2))
     blocks = call(
@@ -344,7 +349,7 @@
         functools.partial(pack_kernel, tok_count, top_count, pipe_size),
         tuple(shape((2 * slot_count, width), bf16) for _ in range(EXPERTS))
         + (shape((pipe_size, own_rows, 2 * LANES), f32),),
-        "s" + "v" * pipe_size,
+        "v" + "v" * pipe_size,
         "pack",
     )(where, *blocks)
 
@@ -420,7 +425,7 @@
         return [shape((2, rows, f_part), bf16)] * 3 + [shape((2, rows, LANES), bf16)]
 
     grads = [
-        call(functools.partial(act_kernel, top_count), grad_shapes(piece), "svvvvva", "act", mib=mib)(
+        call(functools.partial(act_kernel, top_count), grad_shapes(piece), "vvvvvva", "act", mib=mib)(
             where, *piece, exchanged[-1][3]
         )
         for piece in exchanged[:-1]
@@ -428,7 +433,7 @@
     *last_grad, high = call(
         functools.partial(last_act_kernel, d_part, top_count, pipe_size),
         grad_shapes(exchanged[-1]) + [half_shape],
-        "s" + "v" * (4 * PIECES + 3) + "a" * len(flipped),
+        "v" + "v" * (4 * PIECES + 3) + "a" * len(flipped),
         "last_act",
         mib=mib,
     )(where, *exchanged[-1], *[x for grad in grads for x in grad], *flipped_weights, *flipped)
@@ -436,7 +441,7 @@
     low = call(
         functools.partial(own_back_kernel, d_part, pipe_size),
         half_shape,
-        "s" + "v" * (4 * PIECES + 2) + "a",
+        "v" + "v" * (4 * PIECES + 2) + "a",
         "own_back",
         mib=mib,
     )(where, *[x for grad in grads for x in grad], *flipped_weights, high)
@@ -493,7 +498,7 @@
     d_tokens, gate_grads = call(
         functools.partial(owner_kernel, d_part, packed),
         (shape(tokens.shape, bf16), shape((micro_count, top_count, tok_count), f32)),
-        "sv" + "v" * EXPERTS,
+        "vv" + "v" * EXPERTS,
         "owner",
     )(where, place, *[contributions[k] for k in RETURN_ORDER])
     return (d_tokens, jnp.swapaxes(gate_grads, 1, 2), dw_gate, dw_up, dw_down_t)

time: 56.7 us -> 55.3 us (0.975)
  Pallas kernels: 13.4 us -> 9.86 us
  waiting for transfers between devices: 10.4 us -> 12.7 us
    ppermute x20, waiting for transfers between devices: 6.38 us -> 8.63 us  [swap(): lax.ppermute(x, axis, [(i, i ^ bit) for i in range(lax.axis_size(axis))])]
    pallas_call x3, Pallas kernels: 2.37 us -> 0.75 us  [on_device(): call(functools.partial(act_kernel, top_count), grad_shapes(piece), 'vvvvv...]
  transfers between devices with their start and end apart: 21 -> 21, of which waited for: 9 -> 9; matrix products, arithmetic and copies ran while one was open for 10% -> 10% of each run, Pallas kernels for 15% -> 11%
where the time goes in v10:
time: 55.3 us; the launch traced here: 55.1 us
  starting transfers between devices  25.4 us (46%)
  waiting for transfers between devices  12.7 us (23%)
  Pallas kernels  9.86 us (18%)
  matrix products  5 us (9%)
  between operations  1.04 us (2%)
  local copies, waits for them, and re-layouts  0.72 us (1%)
    ppermute x20, starting transfers between devices, swap(): lax.ppermute(x, axis, [(i, i ^ bit) for i in range(lax.axis_size(axis))])  24 us
    ppermute x20, waiting for transfers between devices, swap(): lax.ppermute(x, axis, [(i, i ^ bit) for i in range(lax.axis_size(axis))])  8.63 us
    dot_general x12, matrix products, project(): own.append(jnp.dot(left, weight, preferred_element_type=f32))  5 us
    ppermute x1, waiting for transfers between devices, swap_both(): return lax.ppermute(x, ('pipe', 'expert'), pairs)  4.03 us
    pallas_call x1, Pallas kernels, on_device(): call(functools.partial(weight_kernel, scale, block), [shape((d_part, f_pa...  2.8 us
    ppermute x1, starting transfers between devices, swap_both(): return lax.ppermute(x, ('pipe', 'expert'), pairs)  1.45 us
  transfers between devices with their start and end apart: 21, of which 9 were waited for; matrix products, arithmetic and copies ran while one was open for 10% of the time, Pallas kernels for 11%

profile of v10, /device:TPU:0, one launch (start us, length us, event | category | flops | bytes accessed | tf_op | source)
XLA Modules:
  0.0 55.1 jit_solution(15636550961173957075)
XLA Ops:
  0.7 1.1 %prep.1 = (bf16[16,1920]{1,0:T(8,128)(2,1)S(1)}, bf16[16,1920]{1,0:T(8,128)(2,1)S(1)}) custom-call(bf16[2,4,3584]{2,1,0:T(4,128)(2,1)} %tok_ref.1, bf16[2,4,3584]{2,1,0:T(4,128)(2,1)} %cot_ref.1, s32[2,2,4]{2,1,0:T(2,128)} %bitcast.75, bf16[2,2,4]{2,1,0:T(2,128)(2,1)} %bitcast.76), custom_call_target="tpu_custom_call" | custom-call | tf_op jit(solution)/shard_map/prep/pallas_call | solution.py:333
  1.8 3.0 %collective-permute-start = (bf16[16,1920]{1,0:T(8,128)(2,1)S(1)}, bf16[16,1920]{1,0:T(8,128)(2,1)S(1)}, u32[]{:S(2)}, u32[]{:S(2)}) collective-permute-start(bf16[16,1920]{1,0:T(8,128)(2,1)S(1)} %get-tuple-element.87), channel_id=1, source_target_pairs={{0,16},{16,0},{1,17},{17,1},{2,18},{18,2},{3,19},{19,3},{4,20},{20... | collective-permute-start | bytes 184328 | tf_op jit(solution)/shard_map/ppermute | solution.py:29
  4.8 2.2 %collective-permute-done.refs_1_ = bf16[16,1920]{1,0:T(8,128)(2,1)S(1)} collective-permute-done((bf16[16,1920]{1,0:T(8,128)(2,1)S(1)}, bf16[16,1920]{1,0:T(8,128)(2,1)S(1)}, u32[]{:S(2)}, u32[]{:S(2)}) %collective-permute-start) | collective-permute-done | bytes 61472 | tf_op jit(solution)/shard_map/ppermute | solution.py:29
  7.0 0.6 %pack.1 = (bf16[24,1920]{1,0:T(8,128)(2,1)S(1)}, bf16[24,1920]{1,0:T(8,128)(2,1)S(1)}, bf16[24,1920]{1,0:T(8,128)(2,1)S(1)}, bf16[24,1920]{1,0:T(8,128)(2,1)S(1)}, f32[2,8,256]{2,1,0:T(8,128)S(1)}) custom-call(s32[8,128]{1,0:T(8,128)S(1)} %iota.7.where_ref, bf16[16,1920]{1,0:T(8,128)(2,1)S(1)} %get-tuple-element.88.refs_0_, ...), custom_call_target="tpu_custom_call" | custom-call | tf_op jit(solution)/shard_map/pack/pallas_call | solution.py:348
  7.5 2.2 %collective-permute-start.1 = (bf16[24,1920]{1,0:T(8,128)(2,1)S(1)}, bf16[24,1920]{1,0:T(8,128)(2,1)S(1)}, u32[]{:S(2)}, u32[]{:S(2)}) collective-permute-start(bf16[24,1920]{1,0:T(8,128)(2,1)S(1)} %get-tuple-element.46), channel_id=1, source_target_pairs={{0,4},{1,5},{2,6},{3,7},{4,0},{5,1},{6,2},{7,3},{8,12},{9,13},{10,... | collective-permute-start | bytes 276488 | tf_op jit(solution)/shard_map/ppermute | solution.py:29
  9.7 2.6 %collective-permute-start.4 = (bf16[24,1920]{1,0:T(8,128)(2,1)S(1)}, bf16[24,1920]{1,0:T(8,128)(2,1)S(1)}, u32[]{:S(2)}, u32[]{:S(2)}) collective-permute-start(bf16[24,1920]{1,0:T(8,128)(2,1)S(1)} %get-tuple-element.47), channel_id=1, source_target_pairs={{0,8},{1,9},{2,10},{3,11},{4,12},{5,13},{6,14},{7,15},{8,0},{9,1},... | collective-permute-start | bytes 276488 | tf_op jit(solution)/shard_map/ppermute | solution.py:29
  12.3 0.9 %collective-permute-done.1.refs_1_ = bf16[24,1920]{1,0:T(8,128)(2,1)S(1)} collective-permute-done((bf16[24,1920]{1,0:T(8,128)(2,1)S(1)}, bf16[24,1920]{1,0:T(8,128)(2,1)S(1)}, u32[]{:S(2)}, u32[]{:S(2)}) %collective-permute-start.1) | collective-permute-done | bytes 92192 | tf_op jit(solution)/shard_map/ppermute | solution.py:29
  13.3 1.9 %collective-permute-start.7 = (bf16[2,24,1920]{2,1,0:T(8,128)(2,1)S(1)}, bf16[2,24,1920]{2,1,0:T(8,128)(2,1)S(1)}, u32[]{:S(2)}, u32[]{:S(2)}) collective-permute-start(bf16[2,24,1920]{2,1,0:T(8,128)(2,1)S(1)} %join.2), channel_id=1, source_target_pairs={{0,2},{1,3},{2,0},{3,1},{4,6},{5,7},{6,4},{7,5},{8,10},{9,11},{10,... | collective-permute-start | bytes 552968 | tf_op jit(solution)/shard_map/ppermute | solution.py:29
  16.2 0.7 %copy-done.2 = bf16[1792,512]{1,0:T(8,128)(2,1)S(1)} copy-done((bf16[1792,512]{1,0:T(8,128)(2,1)S(1)}, bf16[1792,512]{1,0:T(8,128)(2,1)}, u32[]{:S(2)}) %copy-start.2) | copy-done | bytes 1835032
  17.4 1.6 %collective-permute-start.3 = (bf16[3,48,512]{2,1,0:T(8,128)(2,1)S(1)}, bf16[3,48,512]{2,1,0:T(8,128)(2,1)S(1)}, u32[]{:S(2)}, u32[]{:S(2)}) collective-permute-start(bf16[3,48,512]{2,1,0:T(8,128)(2,1)S(1)} %pad_maximum_fusion.4.refs_5_), channel_id=1, source_target_pairs={{0,16},{16,0},{1,17},{17,1},{2,18},{18,2},{3,19},{19,3},{4,20},{20... | collective-permute-start | bytes 442376 | tf_op jit(solution)/shard_map/ppermute | solution.py:29
  19.1 1.5 %collective-permute-start.6 = (bf16[2,24,1920]{2,1,0:T(8,128)(2,1)S(1)}, bf16[2,24,1920]{2,1,0:T(8,128)(2,1)S(1)}, u32[]{:S(2)}, u32[]{:S(2)}) collective-permute-start(bf16[2,24,1920]{2,1,0:T(8,128)(2,1)S(1)} %join.3), channel_id=1, source_target_pairs={{0,2},{1,3},{2,0},{3,1},{4,6},{5,7},{6,4},{7,5},{8,10},{9,11},{10,... | collective-permute-start | bytes 552968 | tf_op jit(solution)/shard_map/ppermute | solution.py:29
  22.1 1.6 %collective-permute-start.12 = (bf16[3,48,512]{2,1,0:T(8,128)(2,1)S(1)}, bf16[3,48,512]{2,1,0:T(8,128)(2,1)S(1)}, u32[]{:S(2)}, u32[]{:S(2)}) collective-permute-start(bf16[3,48,512]{2,1,0:T(8,128)(2,1)S(1)} %pad_maximum_fusion.6), channel_id=1, source_target_pairs={{0,16},{16,0},{1,17},{17,1},{2,18},{18,2},{3,19},{19,3},{4,20},{20... | collective-permute-start | bytes 442376 | tf_op jit(solution)/shard_map/ppermute | solution.py:29
  24.1 0.4 fusion.21.refs_1_
  25.0 1.1 %collective-permute-done.6.refs_0_ = bf16[2,24,1920]{2,1,0:T(8,128)(2,1)S(1)} collective-permute-done((bf16[2,24,1920]{2,1,0:T(8,128)(2,1)S(1)}, bf16[2,24,1920]{2,1,0:T(8,128)(2,1)S(1)}, u32[]{:S(2)}, u32[]{:S(2)}) %collective-permute-start.6) | collective-permute-done | bytes 184352 | tf_op jit(solution)/shard_map/ppermute | solution.py:29
  26.2 1.4 %collective-permute-start.11 = (bf16[3,48,512]{2,1,0:T(8,128)(2,1)S(1)}, bf16[3,48,512]{2,1,0:T(8,128)(2,1)S(1)}, u32[]{:S(2)}, u32[]{:S(2)}) collective-permute-start(bf16[3,48,512]{2,1,0:T(8,128)(2,1)S(1)} %pad_maximum_fusion.5), channel_id=1, source_target_pairs={{0,16},{16,0},{1,17},{17,1},{2,18},{18,2},{3,19},{19,3},{4,20},{20... | collective-permute-start | bytes 442376 | tf_op jit(solution)/shard_map/ppermute | solution.py:29
  29.0 1.4 %collective-permute-start.13 = (bf16[3,48,512]{2,1,0:T(8,128)(2,1)S(1)}, bf16[3,48,512]{2,1,0:T(8,128)(2,1)S(1)}, u32[]{:S(2)}, u32[]{:S(2)}) collective-permute-start(bf16[3,48,512]{2,1,0:T(8,128)(2,1)S(1)} %pad_maximum_fusion.7), channel_id=1, source_target_pairs={{0,16},{16,0},{1,17},{17,1},{2,18},{18,2},{3,19},{19,3},{4,20},{20... | collective-permute-start | bytes 442376 | tf_op jit(solution)/shard_map/ppermute | solution.py:29
  30.3 0.5 flip_weight.3.refs_18_.refs_17_
  30.9 0.5 flip_weight.2.refs_17_.refs_16_
  32.3 0.6 %collective-permute-done.11.refs_4_ = bf16[3,48,512]{2,1,0:T(8,128)(2,1)S(1)} collective-permute-done((bf16[3,48,512]{2,1,0:T(8,128)(2,1)S(1)}, bf16[3,48,512]{2,1,0:T(8,128)(2,1)S(1)}, u32[]{:S(2)}, u32[]{:S(2)}) %collective-permute-start.11) | collective-permute-done | bytes 147488 | tf_op jit(solution)/shard_map/ppermute | solution.py:29
  33.4 2.2 %collective-permute-done.13.refs_4_ = bf16[3,48,512]{2,1,0:T(8,128)(2,1)S(1)} collective-permute-done((bf16[3,48,512]{2,1,0:T(8,128)(2,1)S(1)}, bf16[3,48,512]{2,1,0:T(8,128)(2,1)S(1)}, u32[]{:S(2)}, u32[]{:S(2)}) %collective-permute-start.13) | collective-permute-done | bytes 147488 | tf_op jit(solution)/shard_map/ppermute | solution.py:29
  35.7 0.9 %last_act.1 = (bf16[2,24,512]{2,1,0:T(8,128)(2,1)S(1)}, bf16[2,24,512]{2,1,0:T(8,128)(2,1)S(1)}, bf16[2,24,512]{2,1,0:T(8,128)(2,1)S(1)}, bf16[2,24,128]{2,1,0:T(8,128)(2,1)S(1)}, bf16[2,2,24,1920]{3,2,1,0:T(8,128)(2,1)S(1)}) custom-call(s32[8,128]{1,0:T(8,128)S(1)} %iota.7.where_ref, bf16[48,128]{1,0:T(8,128)(2,1)S(1)} %fusion.14.refs_0_, ...), custom_call_target="tpu_custom_call" | custom-call | tf_op jit(solution)/shard_map/last_act/pallas_call | solution.py:433
  36.7 0.7 %own_back.1.a_ref = bf16[2,2,24,1920]{3,2,1,0:T(8,128)(2,1)S(1)} custom-call(s32[8,128]{1,0:T(8,128)S(1)} %iota.7.where_ref, bf16[2,24,512]{2,1,0:T(8,128)(2,1)S(1)} %get-tuple-element.49.refs_5_.refs_0_, bf16[2,24,512]{2,1,0:T(8,128)(2,1)S(1)} %get-tuple-element.50.refs_6_.refs_1_, bf16[2,24,512]{2,1,0:T(8,128)(2,1)S(1)} %get-tuple-element.51.refs_7_.refs_2_, ...), custom_call_target="tpu_custom_call" | custom-call | tf_op jit(solution)/shard_map/own_back/pallas_call | solution.py:441
  37.4 0.9 %collective-permute-done.14.b_ref = bf16[2,2,24,1920]{3,2,1,0:T(8,128)(2,1)S(1)} collective-permute-done((bf16[2,2,24,1920]{3,2,1,0:T(8,128)(2,1)S(1)}, bf16[2,2,24,1920]{3,2,1,0:T(8,128)(2,1)S(1)}, u32[]{:S(2)}, u32[]{:S(2)}) %collective-permute-start.14) | collective-permute-done | bytes 368672 | tf_op jit(solution)/shard_map/ppermute | solution.py:29
  38.4 1.4 %collective-permute-start.17 = (bf16[24,1920]{1,0:T(8,128)(2,1)S(1)}, bf16[24,1920]{1,0:T(8,128)(2,1)S(1)}, u32[]{:S(2)}, u32[]{:S(2)}) collective-permute-start(bf16[24,1920]{1,0:T(8,128)(2,1)S(1)} %get-tuple-element.69), channel_id=1, source_target_pairs={{0,2},{1,3},{2,0},{3,1},{4,6},{5,7},{6,4},{7,5},{8,10},{9,11},{10,... | collective-permute-start | bytes 276488 | tf_op jit(solution)/shard_map/ppermute | solution.py:29
  39.8 1.4 %collective-permute-start.15 = (bf16[24,1792]{1,0:T(8,128)(2,1)S(1)}, bf16[24,1792]{1,0:T(8,128)(2,1)S(1)}, u32[]{:S(2)}, u32[]{:S(2)}) collective-permute-start(bf16[24,1792]{1,0:T(8,128)(2,1)S(1)} %get-tuple-element.67), channel_id=1, source_target_pairs={{0,18},{1,19},{2,16},{3,17},{4,22},{5,23},{6,20},{7,21},{8,26},{9,... | collective-permute-start | bytes 258056 | tf_op jit(solution)/shard_map/ppermute | solution.py:35
  41.3 0.7 %collective-permute-start.16 = (bf16[24,1792]{1,0:T(8,128)(2,1)S(1)}, bf16[24,1792]{1,0:T(8,128)(2,1)S(1)}, u32[]{:S(2)}, u32[]{:S(2)}) collective-permute-start(bf16[24,1792]{1,0:T(8,128)(2,1)S(1)} %get-tuple-element.68), channel_id=1, source_target_pairs={{0,16},{16,0},{1,17},{17,1},{2,18},{18,2},{3,19},{19,3},{4,20},{20... | collective-permute-start | bytes 258056 | tf_op jit(solution)/shard_map/ppermute | solution.py:29
  42.0 4.0 %collective-permute-done.15.b_ref = bf16[24,1792]{1,0:T(8,128)(2,1)S(1)} collective-permute-done((bf16[24,1792]{1,0:T(8,128)(2,1)S(1)}, bf16[24,1792]{1,0:T(8,128)(2,1)S(1)}, u32[]{:S(2)}, u32[]{:S(2)}) %collective-permute-start.15) | collective-permute-done | bytes 86048 | tf_op jit(solution)/shard_map/ppermute | solution.py:35
  46.3 2.7 %collective-permute-start.18 = (bf16[8,2816]{1,0:T(8,128)(2,1)S(1)}, bf16[8,2816]{1,0:T(8,128)(2,1)S(1)}, u32[]{:S(2)}, u32[]{:S(2)}) collective-permute-start(bf16[8,2816]{1,0:T(8,128)(2,1)S(1)} %get-tuple-element.71), channel_id=1, source_target_pairs={{0,12},{1,13},{2,14},{3,15},{4,8},{5,9},{6,10},{7,11},{8,4},{9,5},... | collective-permute-start | bytes 135176 | tf_op jit(solution)/shard_map/ppermute | solution.py:29
  49.4 1.3 %collective-permute-start.20 = (bf16[8,2816]{1,0:T(8,128)(2,1)S(1)}, bf16[8,2816]{1,0:T(8,128)(2,1)S(1)}, u32[]{:S(2)}, u32[]{:S(2)}) collective-permute-start(bf16[8,2816]{1,0:T(8,128)(2,1)S(1)} %get-tuple-element.73), channel_id=1, source_target_pairs={{0,4},{1,5},{2,6},{3,7},{4,0},{5,1},{6,2},{7,3},{8,12},{9,13},{10,... | collective-permute-start | bytes 135176 | tf_op jit(solution)/shard_map/ppermute | solution.py:29
  50.8 2.8 %weight_grads.1 = (bf16[1792,512]{1,0:T(8,128)(2,1)}, bf16[1792,512]{1,0:T(8,128)(2,1)}, bf16[1792,512]{1,0:T(8,128)(2,1)}) custom-call(bf16[1792,192]{1,0:T(8,128)(2,1)S(1)} %flip.2.refs_19_.tok_ref, bf16[1792,192]{1,0:T(8,128)(2,1)S(1)} %flip.3.refs_20_.cot_ref, bf16[2,24,512]{2,1,0:T(8,128)(2,1)S(1)} %get-tuple-element.49.refs_5_.refs_0_, ...), custom_call_target="tpu_custom_call" | custom-call | tf_op jit(solution)/shard_map/weight_grads/pallas_call | solution.py:485
  53.6 0.4 collective-permute-done.19.refs_2_
  54.1 1.0 %owner.1 = (bf16[2,4,3584]{2,1,0:T(4,128)(2,1)}, f32[2,2,4]{2,1,0:T(2,128)}) custom-call(s32[8,128]{1,0:T(8,128)S(1)} %iota.7.where_ref, f32[2,8,256]{2,1,0:T(8,128)S(1)} %get-tuple-element.44.refs_1_.place_ref, bf16[8,2816]{1,0:T(8,128)(2,1)S(1)} %get-tuple-element.70.refs_0_, bf16[8,2816]{1,0:T(8,128)(2,1)S(1)} %collective-permute-done.18.refs_1_, ...), custom_call_target="tpu_custom_call" | custom-call | tf_op jit(solution)/shard_map/owner/pallas_call | solution.py:498
  (77 shorter events, 7.6 us)
Async XLA Ops:
  0.6 15.2 %copy-start = (bf16[1792,512]{1,0:T(8,128)(2,1)S(1)}, bf16[1792,512]{1,0:T(8,128)(2,1)}, u32[]{:S(2)}) copy-start(bf16[1792,512]{1,0:T(8,128)(2,1)} %param.13) | copy-start | bytes 5505028
  1.8 5.2 %collective-permute-start = (bf16[16,1920]{1,0:T(8,128)(2,1)S(1)}, bf16[16,1920]{1,0:T(8,128)(2,1)S(1)}, u32[]{:S(2)}, u32[]{:S(2)}) collective-permute-start(bf16[16,1920]{1,0:T(8,128)(2,1)S(1)} %get-tuple-element.87), channel_id=1, source_target_pairs={{0,16},{16,0},{1,17},{17,1},{2,18},{18,2},{3,19},{19,3},{4,20},{20... | collective-permute-start | bytes 184328 | tf_op jit(solution)/shard_map/ppermute | solution.py:29
  7.5 5.6 %collective-permute-start.1 = (bf16[24,1920]{1,0:T(8,128)(2,1)S(1)}, bf16[24,1920]{1,0:T(8,128)(2,1)S(1)}, u32[]{:S(2)}, u32[]{:S(2)}) collective-permute-start(bf16[24,1920]{1,0:T(8,128)(2,1)S(1)} %get-tuple-element.46), channel_id=1, source_target_pairs={{0,4},{1,5},{2,6},{3,7},{4,0},{5,1},{6,2},{7,3},{8,12},{9,13},{10,... | collective-permute-start | bytes 276488 | tf_op jit(solution)/shard_map/ppermute | solution.py:29
  9.7 9.2 %collective-permute-start.4 = (bf16[24,1920]{1,0:T(8,128)(2,1)S(1)}, bf16[24,1920]{1,0:T(8,128)(2,1)S(1)}, u32[]{:S(2)}, u32[]{:S(2)}) collective-permute-start(bf16[24,1920]{1,0:T(8,128)(2,1)S(1)} %get-tuple-element.47), channel_id=1, source_target_pairs={{0,8},{1,9},{2,10},{3,11},{4,12},{5,13},{6,14},{7,15},{8,0},{9,1},... | collective-permute-start | bytes 276488 | tf_op jit(solution)/shard_map/ppermute | solution.py:29
  12.3 6.6 %collective-permute-start.5 = (bf16[24,1920]{1,0:T(8,128)(2,1)S(1)}, bf16[24,1920]{1,0:T(8,128)(2,1)S(1)}, u32[]{:S(2)}, u32[]{:S(2)}) collective-permute-start(bf16[24,1920]{1,0:T(8,128)(2,1)S(1)} %get-tuple-element.48), channel_id=1, source_target_pairs={{0,12},{1,13},{2,14},{3,15},{4,8},{5,9},{6,10},{7,11},{8,4},{9,5},... | collective-permute-start | bytes 276488 | tf_op jit(solution)/shard_map/ppermute | solution.py:29
  13.2 2.1 %collective-permute-start.2 = (bf16[2,24,1920]{2,1,0:T(8,128)(2,1)S(1)}, bf16[2,24,1920]{2,1,0:T(8,128)(2,1)S(1)}, u32[]{:S(2)}, u32[]{:S(2)}) collective-permute-start(bf16[2,24,1920]{2,1,0:T(8,128)(2,1)S(1)} %join.2), channel_id=1, source_target_pairs={{0,1},{1,0},{2,3},{3,2},{4,5},{5,4},{6,7},{7,6},{8,9},{9,8},{10,11... | collective-permute-start | bytes 552968 | tf_op jit(solution)/shard_map/ppermute | solution.py:29
  13.3 2.0 %copy-start.1 = (bf16[1792,512]{1,0:T(8,128)(2,1)S(1)}, bf16[1792,512]{1,0:T(8,128)(2,1)}, u32[]{:S(2)}) copy-start(bf16[1792,512]{1,0:T(8,128)(2,1)} %weight_ref.3) | copy-start | bytes 5505028
  13.3 8.6 %collective-permute-start.7 = (bf16[2,24,1920]{2,1,0:T(8,128)(2,1)S(1)}, bf16[2,24,1920]{2,1,0:T(8,128)(2,1)S(1)}, u32[]{:S(2)}, u32[]{:S(2)}) collective-permute-start(bf16[2,24,1920]{2,1,0:T(8,128)(2,1)S(1)} %join.2), channel_id=1, source_target_pairs={{0,2},{1,3},{2,0},{3,1},{4,6},{5,7},{6,4},{7,5},{8,10},{9,11},{10,... | collective-permute-start | bytes 552968 | tf_op jit(solution)/shard_map/ppermute | solution.py:29
  15.4 1.5 %copy-start.2 = (bf16[1792,512]{1,0:T(8,128)(2,1)S(1)}, bf16[1792,512]{1,0:T(8,128)(2,1)}, u32[]{:S(2)}) copy-start(bf16[1792,512]{1,0:T(8,128)(2,1)} %weight_ref.2) | copy-start | bytes 5505028
  17.4 15.8 %collective-permute-start.3 = (bf16[3,48,512]{2,1,0:T(8,128)(2,1)S(1)}, bf16[3,48,512]{2,1,0:T(8,128)(2,1)S(1)}, u32[]{:S(2)}, u32[]{:S(2)}) collective-permute-start(bf16[3,48,512]{2,1,0:T(8,128)(2,1)S(1)} %pad_maximum_fusion.4.refs_5_), channel_id=1, source_target_pairs={{0,16},{16,0},{1,17},{17,1},{2,18},{18,2},{3,19},{19,3},{4,20},{20... | collective-permute-start | bytes 442376 | tf_op jit(solution)/shard_map/ppermute | solution.py:29
  19.0 1.6 %collective-permute-start.8 = (bf16[2,24,1920]{2,1,0:T(8,128)(2,1)S(1)}, bf16[2,24,1920]{2,1,0:T(8,128)(2,1)S(1)}, u32[]{:S(2)}, u32[]{:S(2)}) collective-permute-start(bf16[2,24,1920]{2,1,0:T(8,128)(2,1)S(1)} %join.3), channel_id=1, source_target_pairs={{0,1},{1,0},{2,3},{3,2},{4,5},{5,4},{6,7},{7,6},{8,9},{9,8},{10,11... | collective-permute-start | bytes 552968 | tf_op jit(solution)/shard_map/ppermute | solution.py:29
  19.1 7.1 %collective-permute-start.6 = (bf16[2,24,1920]{2,1,0:T(8,128)(2,1)S(1)}, bf16[2,24,1920]{2,1,0:T(8,128)(2,1)S(1)}, u32[]{:S(2)}, u32[]{:S(2)}) collective-permute-start(bf16[2,24,1920]{2,1,0:T(8,128)(2,1)S(1)} %join.3), channel_id=1, source_target_pairs={{0,2},{1,3},{2,0},{3,1},{4,6},{5,7},{6,4},{7,5},{8,10},{9,11},{10,... | collective-permute-start | bytes 552968 | tf_op jit(solution)/shard_map/ppermute | solution.py:29
  22.0 1.7 %collective-permute-start.9 = (bf16[2,24,1920]{2,1,0:T(8,128)(2,1)S(1)}, bf16[2,24,1920]{2,1,0:T(8,128)(2,1)S(1)}, u32[]{:S(2)}, u32[]{:S(2)}) collective-permute-start(bf16[2,24,1920]{2,1,0:T(8,128)(2,1)S(1)} %tie.6), channel_id=1, source_target_pairs={{0,1},{1,0},{2,3},{3,2},{4,5},{5,4},{6,7},{7,6},{8,9},{9,8},{10,11... | collective-permute-start | bytes 552968 | tf_op jit(solution)/shard_map/ppermute | solution.py:29
  22.1 9.9 %collective-permute-start.12 = (bf16[3,48,512]{2,1,0:T(8,128)(2,1)S(1)}, bf16[3,48,512]{2,1,0:T(8,128)(2,1)S(1)}, u32[]{:S(2)}, u32[]{:S(2)}) collective-permute-start(bf16[3,48,512]{2,1,0:T(8,128)(2,1)S(1)} %pad_maximum_fusion.6), channel_id=1, source_target_pairs={{0,16},{16,0},{1,17},{17,1},{2,18},{18,2},{3,19},{19,3},{4,20},{20... | collective-permute-start | bytes 442376 | tf_op jit(solution)/shard_map/ppermute | solution.py:29
  26.1 1.4 %collective-permute-start.10 = (bf16[2,24,1920]{2,1,0:T(8,128)(2,1)S(1)}, bf16[2,24,1920]{2,1,0:T(8,128)(2,1)S(1)}, u32[]{:S(2)}, u32[]{:S(2)}) collective-permute-start(bf16[2,24,1920]{2,1,0:T(8,128)(2,1)S(1)} %tie.7), channel_id=1, source_target_pairs={{0,1},{1,0},{2,3},{3,2},{4,5},{5,4},{6,7},{7,6},{8,9},{9,8},{10,11... | collective-permute-start | bytes 552968 | tf_op jit(solution)/shard_map/ppermute | solution.py:29
  26.2 6.7 %collective-permute-start.11 = (bf16[3,48,512]{2,1,0:T(8,128)(2,1)S(1)}, bf16[3,48,512]{2,1,0:T(8,128)(2,1)S(1)}, u32[]{:S(2)}, u32[]{:S(2)}) collective-permute-start(bf16[3,48,512]{2,1,0:T(8,128)(2,1)S(1)} %pad_maximum_fusion.5), channel_id=1, source_target_pairs={{0,16},{16,0},{1,17},{17,1},{2,18},{18,2},{3,19},{19,3},{4,20},{20... | collective-permute-start | bytes 442376 | tf_op jit(solution)/shard_map/ppermute | solution.py:29
  29.0 6.7 %collective-permute-start.13 = (bf16[3,48,512]{2,1,0:T(8,128)(2,1)S(1)}, bf16[3,48,512]{2,1,0:T(8,128)(2,1)S(1)}, u32[]{:S(2)}, u32[]{:S(2)}) collective-permute-start(bf16[3,48,512]{2,1,0:T(8,128)(2,1)S(1)} %pad_maximum_fusion.7), channel_id=1, source_target_pairs={{0,16},{16,0},{1,17},{17,1},{2,18},{18,2},{3,19},{19,3},{4,20},{20... | collective-permute-start | bytes 442376 | tf_op jit(solution)/shard_map/ppermute | solution.py:29
  36.6 1.8 %collective-permute-start.14 = (bf16[2,2,24,1920]{3,2,1,0:T(8,128)(2,1)S(1)}, bf16[2,2,24,1920]{3,2,1,0:T(8,128)(2,1)S(1)}, u32[]{:S(2)}, u32[]{:S(2)}) collective-permute-start(bf16[2,2,24,1920]{3,2,1,0:T(8,128)(2,1)S(1)} %get-tuple-element.65.refs_18_), channel_id=1, source_target_pairs={{0,1},{1,0},{2,3},{3,2},{4,5},{5,4},{6,7},{7,6},{8,9},{9,8},{10,11... | collective-permute-start | bytes 1105928 | tf_op jit(solution)/shard_map/ppermute | solution.py:29
  38.4 7.8 %collective-permute-start.17 = (bf16[24,1920]{1,0:T(8,128)(2,1)S(1)}, bf16[24,1920]{1,0:T(8,128)(2,1)S(1)}, u32[]{:S(2)}, u32[]{:S(2)}) collective-permute-start(bf16[24,1920]{1,0:T(8,128)(2,1)S(1)} %get-tuple-element.69), channel_id=1, source_target_pairs={{0,2},{1,3},{2,0},{3,1},{4,6},{5,7},{6,4},{7,5},{8,10},{9,11},{10,... | collective-permute-start | bytes 276488 | tf_op jit(solution)/shard_map/ppermute | solution.py:29
  39.8 6.2 %collective-permute-start.15 = (bf16[24,1792]{1,0:T(8,128)(2,1)S(1)}, bf16[24,1792]{1,0:T(8,128)(2,1)S(1)}, u32[]{:S(2)}, u32[]{:S(2)}) collective-permute-start(bf16[24,1792]{1,0:T(8,128)(2,1)S(1)} %get-tuple-element.67), channel_id=1, source_target_pairs={{0,18},{1,19},{2,16},{3,17},{4,22},{5,23},{6,20},{7,21},{8,26},{9,... | collective-permute-start | bytes 258056 | tf_op jit(solution)/shard_map/ppermute | solution.py:35
  41.3 4.9 %collective-permute-start.16 = (bf16[24,1792]{1,0:T(8,128)(2,1)S(1)}, bf16[24,1792]{1,0:T(8,128)(2,1)S(1)}, u32[]{:S(2)}, u32[]{:S(2)}) collective-permute-start(bf16[24,1792]{1,0:T(8,128)(2,1)S(1)} %get-tuple-element.68), channel_id=1, source_target_pairs={{0,16},{16,0},{1,17},{17,1},{2,18},{18,2},{3,19},{19,3},{4,20},{20... | collective-permute-start | bytes 258056 | tf_op jit(solution)/shard_map/ppermute | solution.py:29
  46.3 7.3 %collective-permute-start.18 = (bf16[8,2816]{1,0:T(8,128)(2,1)S(1)}, bf16[8,2816]{1,0:T(8,128)(2,1)S(1)}, u32[]{:S(2)}, u32[]{:S(2)}) collective-permute-start(bf16[8,2816]{1,0:T(8,128)(2,1)S(1)} %get-tuple-element.71), channel_id=1, source_target_pairs={{0,12},{1,13},{2,14},{3,15},{4,8},{5,9},{6,10},{7,11},{8,4},{9,5},... | collective-permute-start | bytes 135176 | tf_op jit(solution)/shard_map/ppermute | solution.py:29
  49.0 5.0 %collective-permute-start.19 = (bf16[8,2816]{1,0:T(8,128)(2,1)S(1)}, bf16[8,2816]{1,0:T(8,128)(2,1)S(1)}, u32[]{:S(2)}, u32[]{:S(2)}) collective-permute-start(bf16[8,2816]{1,0:T(8,128)(2,1)S(1)} %get-tuple-element.72), channel_id=1, source_target_pairs={{0,8},{1,9},{2,10},{3,11},{4,12},{5,13},{6,14},{7,15},{8,0},{9,1},... | collective-permute-start | bytes 135176 | tf_op jit(solution)/shard_map/ppermute | solution.py:29
  49.4 4.6 %collective-permute-start.20 = (bf16[8,2816]{1,0:T(8,128)(2,1)S(1)}, bf16[8,2816]{1,0:T(8,128)(2,1)S(1)}, u32[]{:S(2)}, u32[]{:S(2)}) collective-permute-start(bf16[8,2816]{1,0:T(8,128)(2,1)S(1)} %get-tuple-element.73), channel_id=1, source_target_pairs={{0,4},{1,5},{2,6},{3,7},{4,0},{5,1},{6,2},{7,3},{8,12},{9,13},{10,... | collective-permute-start | bytes 135176 | tf_op jit(solution)/shard_map/ppermute | solution.py:29

commit v11 on v10

--- a/solution.py
+++ b/solution.py
@@ -16,7 +16,7 @@
 ROWS = 8
 PIECES = 4
 SQUARE = EXPERTS * ROWS
-RETURN_ORDER = (0, 3, 2, 1)
+RETURN_ORDER = (0, 3, 1, 2)
 JOIN_COST = dict(flops=4000000000, moved=12000000)
 FILL_A = dict(flops=8000000000, moved=24000000)
 FILL_B = dict(flops=8_000_000_000, moved=24_000_000)

time: 55.3 us -> 55.3 us (level)
  no operation moved by 1% of the time
where the time goes in v11:
time: 55.3 us; the launch traced here: 55.2 us
  starting transfers between devices  25.4 us (46%)
  waiting for transfers between devices  12.7 us (23%)
  Pallas kernels  9.86 us (18%)
  matrix products  5 us (9%)
  between operations  1.05 us (2%)
  local copies, waits for them, and re-layouts  0.72 us (1%)
    ppermute x20, starting transfers between devices, swap(): lax.ppermute(x, axis, [(i, i ^ bit) for i in range(lax.axis_size(axis))])  24 us
    ppermute x20, waiting for transfers between devices, swap(): lax.ppermute(x, axis, [(i, i ^ bit) for i in range(lax.axis_size(axis))])  8.7 us
    dot_general x12, matrix products, project(): own.append(jnp.dot(left, weight, preferred_element_type=f32))  5 us
    ppermute x1, waiting for transfers between devices, swap_both(): return lax.ppermute(x, ('pipe', 'expert'), pairs)  4.03 us
    pallas_call x1, Pallas kernels, on_device(): call(functools.partial(weight_kernel, scale, block), [shape((d_part, f_pa...  2.8 us
    ppermute x1, starting transfers between devices, swap_both(): return lax.ppermute(x, ('pipe', 'expert'), pairs)  1.45 us
  transfers between devices with their start and end apart: 21, of which 9 were waited for; matrix products, arithmetic and copies ran while one was open for 10% of the time, Pallas kernels for 11%

profile of v11, /device:TPU:0, one launch (start us, length us, event | category | flops | bytes accessed | tf_op | source)
XLA Modules:
  0.0 55.2 jit_solution(10274540167115215762)
XLA Ops:
  0.7 1.1 %prep.1 = (bf16[16,1920]{1,0:T(8,128)(2,1)S(1)}, bf16[16,1920]{1,0:T(8,128)(2,1)S(1)}) custom-call(bf16[2,4,3584]{2,1,0:T(4,128)(2,1)} %tok_ref.1, bf16[2,4,3584]{2,1,0:T(4,128)(2,1)} %cot_ref.1, s32[2,2,4]{2,1,0:T(2,128)} %bitcast.75, bf16[2,2,4]{2,1,0:T(2,128)(2,1)} %bitcast.76), custom_call_target="tpu_custom_call" | custom-call | tf_op jit(solution)/shard_map/prep/pallas_call | solution.py:333
  1.8 3.0 %collective-permute-start = (bf16[16,1920]{1,0:T(8,128)(2,1)S(1)}, bf16[16,1920]{1,0:T(8,128)(2,1)S(1)}, u32[]{:S(2)}, u32[]{:S(2)}) collective-permute-start(bf16[16,1920]{1,0:T(8,128)(2,1)S(1)} %get-tuple-element.87), channel_id=1, source_target_pairs={{0,16},{16,0},{1,17},{17,1},{2,18},{18,2},{3,19},{19,3},{4,20},{20... | collective-permute-start | bytes 184328 | tf_op jit(solution)/shard_map/ppermute | solution.py:29
  4.8 2.2 %collective-permute-done.refs_1_ = bf16[16,1920]{1,0:T(8,128)(2,1)S(1)} collective-permute-done((bf16[16,1920]{1,0:T(8,128)(2,1)S(1)}, bf16[16,1920]{1,0:T(8,128)(2,1)S(1)}, u32[]{:S(2)}, u32[]{:S(2)}) %collective-permute-start) | collective-permute-done | bytes 61472 | tf_op jit(solution)/shard_map/ppermute | solution.py:29
  7.0 0.6 %pack.1 = (bf16[24,1920]{1,0:T(8,128)(2,1)S(1)}, bf16[24,1920]{1,0:T(8,128)(2,1)S(1)}, bf16[24,1920]{1,0:T(8,128)(2,1)S(1)}, bf16[24,1920]{1,0:T(8,128)(2,1)S(1)}, f32[2,8,256]{2,1,0:T(8,128)S(1)}) custom-call(s32[8,128]{1,0:T(8,128)S(1)} %iota.7.where_ref, bf16[16,1920]{1,0:T(8,128)(2,1)S(1)} %get-tuple-element.88.refs_0_, ...), custom_call_target="tpu_custom_call" | custom-call | tf_op jit(solution)/shard_map/pack/pallas_call | solution.py:348
  7.5 2.2 %collective-permute-start.1 = (bf16[24,1920]{1,0:T(8,128)(2,1)S(1)}, bf16[24,1920]{1,0:T(8,128)(2,1)S(1)}, u32[]{:S(2)}, u32[]{:S(2)}) collective-permute-start(bf16[24,1920]{1,0:T(8,128)(2,1)S(1)} %get-tuple-element.46), channel_id=1, source_target_pairs={{0,4},{1,5},{2,6},{3,7},{4,0},{5,1},{6,2},{7,3},{8,12},{9,13},{10,... | collective-permute-start | bytes 276488 | tf_op jit(solution)/shard_map/ppermute | solution.py:29
  9.7 2.6 %collective-permute-start.4 = (bf16[24,1920]{1,0:T(8,128)(2,1)S(1)}, bf16[24,1920]{1,0:T(8,128)(2,1)S(1)}, u32[]{:S(2)}, u32[]{:S(2)}) collective-permute-start(bf16[24,1920]{1,0:T(8,128)(2,1)S(1)} %get-tuple-element.47), channel_id=1, source_target_pairs={{0,8},{1,9},{2,10},{3,11},{4,12},{5,13},{6,14},{7,15},{8,0},{9,1},... | collective-permute-start | bytes 276488 | tf_op jit(solution)/shard_map/ppermute | solution.py:29
  12.3 0.9 %collective-permute-done.1.refs_1_ = bf16[24,1920]{1,0:T(8,128)(2,1)S(1)} collective-permute-done((bf16[24,1920]{1,0:T(8,128)(2,1)S(1)}, bf16[24,1920]{1,0:T(8,128)(2,1)S(1)}, u32[]{:S(2)}, u32[]{:S(2)}) %collective-permute-start.1) | collective-permute-done | bytes 92192 | tf_op jit(solution)/shard_map/ppermute | solution.py:29
  13.3 1.9 %collective-permute-start.7 = (bf16[2,24,1920]{2,1,0:T(8,128)(2,1)S(1)}, bf16[2,24,1920]{2,1,0:T(8,128)(2,1)S(1)}, u32[]{:S(2)}, u32[]{:S(2)}) collective-permute-start(bf16[2,24,1920]{2,1,0:T(8,128)(2,1)S(1)} %join.2), channel_id=1, source_target_pairs={{0,2},{1,3},{2,0},{3,1},{4,6},{5,7},{6,4},{7,5},{8,10},{9,11},{10,... | collective-permute-start | bytes 552968 | tf_op jit(solution)/shard_map/ppermute | solution.py:29
  16.2 0.7 %copy-done.2 = bf16[1792,512]{1,0:T(8,128)(2,1)S(1)} copy-done((bf16[1792,512]{1,0:T(8,128)(2,1)S(1)}, bf16[1792,512]{1,0:T(8,128)(2,1)}, u32[]{:S(2)}) %copy-start.2) | copy-done | bytes 1835032
  17.4 1.6 %collective-permute-start.3 = (bf16[3,48,512]{2,1,0:T(8,128)(2,1)S(1)}, bf16[3,48,512]{2,1,0:T(8,128)(2,1)S(1)}, u32[]{:S(2)}, u32[]{:S(2)}) collective-permute-start(bf16[3,48,512]{2,1,0:T(8,128)(2,1)S(1)} %pad_maximum_fusion.4.refs_5_), channel_id=1, source_target_pairs={{0,16},{16,0},{1,17},{17,1},{2,18},{18,2},{3,19},{19,3},{4,20},{20... | collective-permute-start | bytes 442376 | tf_op jit(solution)/shard_map/ppermute | solution.py:29
  19.1 1.5 %collective-permute-start.6 = (bf16[2,24,1920]{2,1,0:T(8,128)(2,1)S(1)}, bf16[2,24,1920]{2,1,0:T(8,128)(2,1)S(1)}, u32[]{:S(2)}, u32[]{:S(2)}) collective-permute-start(bf16[2,24,1920]{2,1,0:T(8,128)(2,1)S(1)} %join.3), channel_id=1, source_target_pairs={{0,2},{1,3},{2,0},{3,1},{4,6},{5,7},{6,4},{7,5},{8,10},{9,11},{10,... | collective-permute-start | bytes 552968 | tf_op jit(solution)/shard_map/ppermute | solution.py:29
  22.1 1.6 %collective-permute-start.12 = (bf16[3,48,512]{2,1,0:T(8,128)(2,1)S(1)}, bf16[3,48,512]{2,1,0:T(8,128)(2,1)S(1)}, u32[]{:S(2)}, u32[]{:S(2)}) collective-permute-start(bf16[3,48,512]{2,1,0:T(8,128)(2,1)S(1)} %pad_maximum_fusion.6), channel_id=1, source_target_pairs={{0,16},{16,0},{1,17},{17,1},{2,18},{18,2},{3,19},{19,3},{4,20},{20... | collective-permute-start | bytes 442376 | tf_op jit(solution)/shard_map/ppermute | solution.py:29
  24.1 0.4 fusion.21.refs_1_
  25.0 1.1 %collective-permute-done.6.refs_0_ = bf16[2,24,1920]{2,1,0:T(8,128)(2,1)S(1)} collective-permute-done((bf16[2,24,1920]{2,1,0:T(8,128)(2,1)S(1)}, bf16[2,24,1920]{2,1,0:T(8,128)(2,1)S(1)}, u32[]{:S(2)}, u32[]{:S(2)}) %collective-permute-start.6) | collective-permute-done | bytes 184352 | tf_op jit(solution)/shard_map/ppermute | solution.py:29
  26.2 1.4 %collective-permute-start.11 = (bf16[3,48,512]{2,1,0:T(8,128)(2,1)S(1)}, bf16[3,48,512]{2,1,0:T(8,128)(2,1)S(1)}, u32[]{:S(2)}, u32[]{:S(2)}) collective-permute-start(bf16[3,48,512]{2,1,0:T(8,128)(2,1)S(1)} %pad_maximum_fusion.5), channel_id=1, source_target_pairs={{0,16},{16,0},{1,17},{17,1},{2,18},{18,2},{3,19},{19,3},{4,20},{20... | collective-permute-start | bytes 442376 | tf_op jit(solution)/shard_map/ppermute | solution.py:29
  29.0 1.4 %collective-permute-start.13 = (bf16[3,48,512]{2,1,0:T(8,128)(2,1)S(1)}, bf16[3,48,512]{2,1,0:T(8,128)(2,1)S(1)}, u32[]{:S(2)}, u32[]{:S(2)}) collective-permute-start(bf16[3,48,512]{2,1,0:T(8,128)(2,1)S(1)} %pad_maximum_fusion.7), channel_id=1, source_target_pairs={{0,16},{16,0},{1,17},{17,1},{2,18},{18,2},{3,19},{19,3},{4,20},{20... | collective-permute-start | bytes 442376 | tf_op jit(solution)/shard_map/ppermute | solution.py:29
  30.3 0.5 flip_weight.3.refs_18_.refs_17_
  30.9 0.5 flip_weight.2.refs_17_.refs_16_
  32.3 0.6 %collective-permute-done.11.refs_4_ = bf16[3,48,512]{2,1,0:T(8,128)(2,1)S(1)} collective-permute-done((bf16[3,48,512]{2,1,0:T(8,128)(2,1)S(1)}, bf16[3,48,512]{2,1,0:T(8,128)(2,1)S(1)}, u32[]{:S(2)}, u32[]{:S(2)}) %collective-permute-start.11) | collective-permute-done | bytes 147488 | tf_op jit(solution)/shard_map/ppermute | solution.py:29
  33.4 2.2 %collective-permute-done.13.refs_4_ = bf16[3,48,512]{2,1,0:T(8,128)(2,1)S(1)} collective-permute-done((bf16[3,48,512]{2,1,0:T(8,128)(2,1)S(1)}, bf16[3,48,512]{2,1,0:T(8,128)(2,1)S(1)}, u32[]{:S(2)}, u32[]{:S(2)}) %collective-permute-start.13) | collective-permute-done | bytes 147488 | tf_op jit(solution)/shard_map/ppermute | solution.py:29
  35.7 0.9 %last_act.1 = (bf16[2,24,512]{2,1,0:T(8,128)(2,1)S(1)}, bf16[2,24,512]{2,1,0:T(8,128)(2,1)S(1)}, bf16[2,24,512]{2,1,0:T(8,128)(2,1)S(1)}, bf16[2,24,128]{2,1,0:T(8,128)(2,1)S(1)}, bf16[2,2,24,1920]{3,2,1,0:T(8,128)(2,1)S(1)}) custom-call(s32[8,128]{1,0:T(8,128)S(1)} %iota.7.where_ref, bf16[48,128]{1,0:T(8,128)(2,1)S(1)} %fusion.14.refs_0_, ...), custom_call_target="tpu_custom_call" | custom-call | tf_op jit(solution)/shard_map/last_act/pallas_call | solution.py:433
  36.7 0.7 %own_back.1.a_ref = bf16[2,2,24,1920]{3,2,1,0:T(8,128)(2,1)S(1)} custom-call(s32[8,128]{1,0:T(8,128)S(1)} %iota.7.where_ref, bf16[2,24,512]{2,1,0:T(8,128)(2,1)S(1)} %get-tuple-element.49.refs_5_.refs_0_, bf16[2,24,512]{2,1,0:T(8,128)(2,1)S(1)} %get-tuple-element.50.refs_6_.refs_1_, bf16[2,24,512]{2,1,0:T(8,128)(2,1)S(1)} %get-tuple-element.51.refs_7_.refs_2_, ...), custom_call_target="tpu_custom_call" | custom-call | tf_op jit(solution)/shard_map/own_back/pallas_call | solution.py:441
  37.4 0.9 %collective-permute-done.14.b_ref = bf16[2,2,24,1920]{3,2,1,0:T(8,128)(2,1)S(1)} collective-permute-done((bf16[2,2,24,1920]{3,2,1,0:T(8,128)(2,1)S(1)}, bf16[2,2,24,1920]{3,2,1,0:T(8,128)(2,1)S(1)}, u32[]{:S(2)}, u32[]{:S(2)}) %collective-permute-start.14) | collective-permute-done | bytes 368672 | tf_op jit(solution)/shard_map/ppermute | solution.py:29
  38.4 1.4 %collective-permute-start.17 = (bf16[24,1920]{1,0:T(8,128)(2,1)S(1)}, bf16[24,1920]{1,0:T(8,128)(2,1)S(1)}, u32[]{:S(2)}, u32[]{:S(2)}) collective-permute-start(bf16[24,1920]{1,0:T(8,128)(2,1)S(1)} %get-tuple-element.69), channel_id=1, source_target_pairs={{0,2},{1,3},{2,0},{3,1},{4,6},{5,7},{6,4},{7,5},{8,10},{9,11},{10,... | collective-permute-start | bytes 276488 | tf_op jit(solution)/shard_map/ppermute | solution.py:29
  39.8 1.4 %collective-permute-start.15 = (bf16[24,1792]{1,0:T(8,128)(2,1)S(1)}, bf16[24,1792]{1,0:T(8,128)(2,1)S(1)}, u32[]{:S(2)}, u32[]{:S(2)}) collective-permute-start(bf16[24,1792]{1,0:T(8,128)(2,1)S(1)} %get-tuple-element.67), channel_id=1, source_target_pairs={{0,18},{1,19},{2,16},{3,17},{4,22},{5,23},{6,20},{7,21},{8,26},{9,... | collective-permute-start | bytes 258056 | tf_op jit(solution)/shard_map/ppermute | solution.py:35
  41.3 0.7 %collective-permute-start.16 = (bf16[24,1792]{1,0:T(8,128)(2,1)S(1)}, bf16[24,1792]{1,0:T(8,128)(2,1)S(1)}, u32[]{:S(2)}, u32[]{:S(2)}) collective-permute-start(bf16[24,1792]{1,0:T(8,128)(2,1)S(1)} %get-tuple-element.68), channel_id=1, source_target_pairs={{0,16},{16,0},{1,17},{17,1},{2,18},{18,2},{3,19},{19,3},{4,20},{20... | collective-permute-start | bytes 258056 | tf_op jit(solution)/shard_map/ppermute | solution.py:29
  42.0 4.0 %collective-permute-done.15.b_ref = bf16[24,1792]{1,0:T(8,128)(2,1)S(1)} collective-permute-done((bf16[24,1792]{1,0:T(8,128)(2,1)S(1)}, bf16[24,1792]{1,0:T(8,128)(2,1)S(1)}, u32[]{:S(2)}, u32[]{:S(2)}) %collective-permute-start.15) | collective-permute-done | bytes 86048 | tf_op jit(solution)/shard_map/ppermute | solution.py:35
  46.3 2.7 %collective-permute-start.18 = (bf16[8,2816]{1,0:T(8,128)(2,1)S(1)}, bf16[8,2816]{1,0:T(8,128)(2,1)S(1)}, u32[]{:S(2)}, u32[]{:S(2)}) collective-permute-start(bf16[8,2816]{1,0:T(8,128)(2,1)S(1)} %get-tuple-element.71), channel_id=1, source_target_pairs={{0,12},{1,13},{2,14},{3,15},{4,8},{5,9},{6,10},{7,11},{8,4},{9,5},... | collective-permute-start | bytes 135176 | tf_op jit(solution)/shard_map/ppermute | solution.py:29
  49.2 1.6 %collective-permute-start.20 = (bf16[8,2816]{1,0:T(8,128)(2,1)S(1)}, bf16[8,2816]{1,0:T(8,128)(2,1)S(1)}, u32[]{:S(2)}, u32[]{:S(2)}) collective-permute-start(bf16[8,2816]{1,0:T(8,128)(2,1)S(1)} %get-tuple-element.73), channel_id=1, source_target_pairs={{0,8},{1,9},{2,10},{3,11},{4,12},{5,13},{6,14},{7,15},{8,0},{9,1},... | collective-permute-start | bytes 135176 | tf_op jit(solution)/shard_map/ppermute | solution.py:29
  50.8 2.8 %weight_grads.1 = (bf16[1792,512]{1,0:T(8,128)(2,1)}, bf16[1792,512]{1,0:T(8,128)(2,1)}, bf16[1792,512]{1,0:T(8,128)(2,1)}) custom-call(bf16[1792,192]{1,0:T(8,128)(2,1)S(1)} %flip.2.refs_19_.tok_ref, bf16[1792,192]{1,0:T(8,128)(2,1)S(1)} %flip.3.refs_20_.cot_ref, bf16[2,24,512]{2,1,0:T(8,128)(2,1)S(1)} %get-tuple-element.49.refs_5_.refs_0_, ...), custom_call_target="tpu_custom_call" | custom-call | tf_op jit(solution)/shard_map/weight_grads/pallas_call | solution.py:485
  53.6 0.5 collective-permute-done.20.refs_3_
  54.1 1.0 %owner.1 = (bf16[2,4,3584]{2,1,0:T(4,128)(2,1)}, f32[2,2,4]{2,1,0:T(2,128)}) custom-call(s32[8,128]{1,0:T(8,128)S(1)} %iota.7.where_ref, f32[2,8,256]{2,1,0:T(8,128)S(1)} %get-tuple-element.44.refs_1_.place_ref, bf16[8,2816]{1,0:T(8,128)(2,1)S(1)} %get-tuple-element.70.refs_0_, bf16[8,2816]{1,0:T(8,128)(2,1)S(1)} %collective-permute-done.18.refs_1_, ...), custom_call_target="tpu_custom_call" | custom-call | tf_op jit(solution)/shard_map/owner/pallas_call | solution.py:498
  (77 shorter events, 7.4 us)
Async XLA Ops:
  0.6 15.2 %copy-start = (bf16[1792,512]{1,0:T(8,128)(2,1)S(1)}, bf16[1792,512]{1,0:T(8,128)(2,1)}, u32[]{:S(2)}) copy-start(bf16[1792,512]{1,0:T(8,128)(2,1)} %param.13) | copy-start | bytes 5505028
  1.8 5.2 %collective-permute-start = (bf16[16,1920]{1,0:T(8,128)(2,1)S(1)}, bf16[16,1920]{1,0:T(8,128)(2,1)S(1)}, u32[]{:S(2)}, u32[]{:S(2)}) collective-permute-start(bf16[16,1920]{1,0:T(8,128)(2,1)S(1)} %get-tuple-element.87), channel_id=1, source_target_pairs={{0,16},{16,0},{1,17},{17,1},{2,18},{18,2},{3,19},{19,3},{4,20},{20... | collective-permute-start | bytes 184328 | tf_op jit(solution)/shard_map/ppermute | solution.py:29
  7.5 5.6 %collective-permute-start.1 = (bf16[24,1920]{1,0:T(8,128)(2,1)S(1)}, bf16[24,1920]{1,0:T(8,128)(2,1)S(1)}, u32[]{:S(2)}, u32[]{:S(2)}) collective-permute-start(bf16[24,1920]{1,0:T(8,128)(2,1)S(1)} %get-tuple-element.46), channel_id=1, source_target_pairs={{0,4},{1,5},{2,6},{3,7},{4,0},{5,1},{6,2},{7,3},{8,12},{9,13},{10,... | collective-permute-start | bytes 276488 | tf_op jit(solution)/shard_map/ppermute | solution.py:29
  9.7 9.2 %collective-permute-start.4 = (bf16[24,1920]{1,0:T(8,128)(2,1)S(1)}, bf16[24,1920]{1,0:T(8,128)(2,1)S(1)}, u32[]{:S(2)}, u32[]{:S(2)}) collective-permute-start(bf16[24,1920]{1,0:T(8,128)(2,1)S(1)} %get-tuple-element.47), channel_id=1, source_target_pairs={{0,8},{1,9},{2,10},{3,11},{4,12},{5,13},{6,14},{7,15},{8,0},{9,1},... | collective-permute-start | bytes 276488 | tf_op jit(solution)/shard_map/ppermute | solution.py:29
  12.3 6.6 %collective-permute-start.5 = (bf16[24,1920]{1,0:T(8,128)(2,1)S(1)}, bf16[24,1920]{1,0:T(8,128)(2,1)S(1)}, u32[]{:S(2)}, u32[]{:S(2)}) collective-permute-start(bf16[24,1920]{1,0:T(8,128)(2,1)S(1)} %get-tuple-element.48), channel_id=1, source_target_pairs={{0,12},{1,13},{2,14},{3,15},{4,8},{5,9},{6,10},{7,11},{8,4},{9,5},... | collective-permute-start | bytes 276488 | tf_op jit(solution)/shard_map/ppermute | solution.py:29
  13.2 2.1 %collective-permute-start.2 = (bf16[2,24,1920]{2,1,0:T(8,128)(2,1)S(1)}, bf16[2,24,1920]{2,1,0:T(8,128)(2,1)S(1)}, u32[]{:S(2)}, u32[]{:S(2)}) collective-permute-start(bf16[2,24,1920]{2,1,0:T(8,128)(2,1)S(1)} %join.2), channel_id=1, source_target_pairs={{0,1},{1,0},{2,3},{3,2},{4,5},{5,4},{6,7},{7,6},{8,9},{9,8},{10,11... | collective-permute-start | bytes 552968 | tf_op jit(solution)/shard_map/ppermute | solution.py:29
  13.3 2.0 %copy-start.1 = (bf16[1792,512]{1,0:T(8,128)(2,1)S(1)}, bf16[1792,512]{1,0:T(8,128)(2,1)}, u32[]{:S(2)}) copy-start(bf16[1792,512]{1,0:T(8,128)(2,1)} %weight_ref.3) | copy-start | bytes 5505028
  13.3 8.6 %collective-permute-start.7 = (bf16[2,24,1920]{2,1,0:T(8,128)(2,1)S(1)}, bf16[2,24,1920]{2,1,0:T(8,128)(2,1)S(1)}, u32[]{:S(2)}, u32[]{:S(2)}) collective-permute-start(bf16[2,24,1920]{2,1,0:T(8,128)(2,1)S(1)} %join.2), channel_id=1, source_target_pairs={{0,2},{1,3},{2,0},{3,1},{4,6},{5,7},{6,4},{7,5},{8,10},{9,11},{10,... | collective-permute-start | bytes 552968 | tf_op jit(solution)/shard_map/ppermute | solution.py:29
  15.4 1.5 %copy-start.2 = (bf16[1792,512]{1,0:T(8,128)(2,1)S(1)}, bf16[1792,512]{1,0:T(8,128)(2,1)}, u32[]{:S(2)}) copy-start(bf16[1792,512]{1,0:T(8,128)(2,1)} %weight_ref.2) | copy-start | bytes 5505028
  17.4 15.8 %collective-permute-start.3 = (bf16[3,48,512]{2,1,0:T(8,128)(2,1)S(1)}, bf16[3,48,512]{2,1,0:T(8,128)(2,1)S(1)}, u32[]{:S(2)}, u32[]{:S(2)}) collective-permute-start(bf16[3,48,512]{2,1,0:T(8,128)(2,1)S(1)} %pad_maximum_fusion.4.refs_5_), channel_id=1, source_target_pairs={{0,16},{16,0},{1,17},{17,1},{2,18},{18,2},{3,19},{19,3},{4,20},{20... | collective-permute-start | bytes 442376 | tf_op jit(solution)/shard_map/ppermute | solution.py:29
  19.0 1.6 %collective-permute-start.8 = (bf16[2,24,1920]{2,1,0:T(8,128)(2,1)S(1)}, bf16[2,24,1920]{2,1,0:T(8,128)(2,1)S(1)}, u32[]{:S(2)}, u32[]{:S(2)}) collective-permute-start(bf16[2,24,1920]{2,1,0:T(8,128)(2,1)S(1)} %join.3), channel_id=1, source_target_pairs={{0,1},{1,0},{2,3},{3,2},{4,5},{5,4},{6,7},{7,6},{8,9},{9,8},{10,11... | collective-permute-start | bytes 552968 | tf_op jit(solution)/shard_map/ppermute | solution.py:29
  19.1 7.1 %collective-permute-start.6 = (bf16[2,24,1920]{2,1,0:T(8,128)(2,1)S(1)}, bf16[2,24,1920]{2,1,0:T(8,128)(2,1)S(1)}, u32[]{:S(2)}, u32[]{:S(2)}) collective-permute-start(bf16[2,24,1920]{2,1,0:T(8,128)(2,1)S(1)} %join.3), channel_id=1, source_target_pairs={{0,2},{1,3},{2,0},{3,1},{4,6},{5,7},{6,4},{7,5},{8,10},{9,11},{10,... | collective-permute-start | bytes 552968 | tf_op jit(solution)/shard_map/ppermute | solution.py:29
  22.0 1.7 %collective-permute-start.9 = (bf16[2,24,1920]{2,1,0:T(8,128)(2,1)S(1)}, bf16[2,24,1920]{2,1,0:T(8,128)(2,1)S(1)}, u32[]{:S(2)}, u32[]{:S(2)}) collective-permute-start(bf16[2,24,1920]{2,1,0:T(8,128)(2,1)S(1)} %tie.6), channel_id=1, source_target_pairs={{0,1},{1,0},{2,3},{3,2},{4,5},{5,4},{6,7},{7,6},{8,9},{9,8},{10,11... | collective-permute-start | bytes 552968 | tf_op jit(solution)/shard_map/ppermute | solution.py:29
  22.1 9.9 %collective-permute-start.12 = (bf16[3,48,512]{2,1,0:T(8,128)(2,1)S(1)}, bf16[3,48,512]{2,1,0:T(8,128)(2,1)S(1)}, u32[]{:S(2)}, u32[]{:S(2)}) collective-permute-start(bf16[3,48,512]{2,1,0:T(8,128)(2,1)S(1)} %pad_maximum_fusion.6), channel_id=1, source_target_pairs={{0,16},{16,0},{1,17},{17,1},{2,18},{18,2},{3,19},{19,3},{4,20},{20... | collective-permute-start | bytes 442376 | tf_op jit(solution)/shard_map/ppermute | solution.py:29
  26.1 1.4 %collective-permute-start.10 = (bf16[2,24,1920]{2,1,0:T(8,128)(2,1)S(1)}, bf16[2,24,1920]{2,1,0:T(8,128)(2,1)S(1)}, u32[]{:S(2)}, u32[]{:S(2)}) collective-permute-start(bf16[2,24,1920]{2,1,0:T(8,128)(2,1)S(1)} %tie.7), channel_id=1, source_target_pairs={{0,1},{1,0},{2,3},{3,2},{4,5},{5,4},{6,7},{7,6},{8,9},{9,8},{10,11... | collective-permute-start | bytes 552968 | tf_op jit(solution)/shard_map/ppermute | solution.py:29
  26.2 6.7 %collective-permute-start.11 = (bf16[3,48,512]{2,1,0:T(8,128)(2,1)S(1)}, bf16[3,48,512]{2,1,0:T(8,128)(2,1)S(1)}, u32[]{:S(2)}, u32[]{:S(2)}) collective-permute-start(bf16[3,48,512]{2,1,0:T(8,128)(2,1)S(1)} %pad_maximum_fusion.5), channel_id=1, source_target_pairs={{0,16},{16,0},{1,17},{17,1},{2,18},{18,2},{3,19},{19,3},{4,20},{20... | collective-permute-start | bytes 442376 | tf_op jit(solution)/shard_map/ppermute | solution.py:29
  29.0 6.7 %collective-permute-start.13 = (bf16[3,48,512]{2,1,0:T(8,128)(2,1)S(1)}, bf16[3,48,512]{2,1,0:T(8,128)(2,1)S(1)}, u32[]{:S(2)}, u32[]{:S(2)}) collective-permute-start(bf16[3,48,512]{2,1,0:T(8,128)(2,1)S(1)} %pad_maximum_fusion.7), channel_id=1, source_target_pairs={{0,16},{16,0},{1,17},{17,1},{2,18},{18,2},{3,19},{19,3},{4,20},{20... | collective-permute-start | bytes 442376 | tf_op jit(solution)/shard_map/ppermute | solution.py:29
  36.6 1.8 %collective-permute-start.14 = (bf16[2,2,24,1920]{3,2,1,0:T(8,128)(2,1)S(1)}, bf16[2,2,24,1920]{3,2,1,0:T(8,128)(2,1)S(1)}, u32[]{:S(2)}, u32[]{:S(2)}) collective-permute-start(bf16[2,2,24,1920]{3,2,1,0:T(8,128)(2,1)S(1)} %get-tuple-element.65.refs_18_), channel_id=1, source_target_pairs={{0,1},{1,0},{2,3},{3,2},{4,5},{5,4},{6,7},{7,6},{8,9},{9,8},{10,11... | collective-permute-start | bytes 1105928 | tf_op jit(solution)/shard_map/ppermute | solution.py:29
  38.4 7.8 %collective-permute-start.17 = (bf16[24,1920]{1,0:T(8,128)(2,1)S(1)}, bf16[24,1920]{1,0:T(8,128)(2,1)S(1)}, u32[]{:S(2)}, u32[]{:S(2)}) collective-permute-start(bf16[24,1920]{1,0:T(8,128)(2,1)S(1)} %get-tuple-element.69), channel_id=1, source_target_pairs={{0,2},{1,3},{2,0},{3,1},{4,6},{5,7},{6,4},{7,5},{8,10},{9,11},{10,... | collective-permute-start | bytes 276488 | tf_op jit(solution)/shard_map/ppermute | solution.py:29
  39.8 6.2 %collective-permute-start.15 = (bf16[24,1792]{1,0:T(8,128)(2,1)S(1)}, bf16[24,1792]{1,0:T(8,128)(2,1)S(1)}, u32[]{:S(2)}, u32[]{:S(2)}) collective-permute-start(bf16[24,1792]{1,0:T(8,128)(2,1)S(1)} %get-tuple-element.67), channel_id=1, source_target_pairs={{0,18},{1,19},{2,16},{3,17},{4,22},{5,23},{6,20},{7,21},{8,26},{9,... | collective-permute-start | bytes 258056 | tf_op jit(solution)/shard_map/ppermute | solution.py:35
  41.3 4.9 %collective-permute-start.16 = (bf16[24,1792]{1,0:T(8,128)(2,1)S(1)}, bf16[24,1792]{1,0:T(8,128)(2,1)S(1)}, u32[]{:S(2)}, u32[]{:S(2)}) collective-permute-start(bf16[24,1792]{1,0:T(8,128)(2,1)S(1)} %get-tuple-element.68), channel_id=1, source_target_pairs={{0,16},{16,0},{1,17},{17,1},{2,18},{18,2},{3,19},{19,3},{4,20},{20... | collective-permute-start | bytes 258056 | tf_op jit(solution)/shard_map/ppermute | solution.py:29
  46.3 7.3 %collective-permute-start.18 = (bf16[8,2816]{1,0:T(8,128)(2,1)S(1)}, bf16[8,2816]{1,0:T(8,128)(2,1)S(1)}, u32[]{:S(2)}, u32[]{:S(2)}) collective-permute-start(bf16[8,2816]{1,0:T(8,128)(2,1)S(1)} %get-tuple-element.71), channel_id=1, source_target_pairs={{0,12},{1,13},{2,14},{3,15},{4,8},{5,9},{6,10},{7,11},{8,4},{9,5},... | collective-permute-start | bytes 135176 | tf_op jit(solution)/shard_map/ppermute | solution.py:29
  49.0 4.6 %collective-permute-start.19 = (bf16[8,2816]{1,0:T(8,128)(2,1)S(1)}, bf16[8,2816]{1,0:T(8,128)(2,1)S(1)}, u32[]{:S(2)}, u32[]{:S(2)}) collective-permute-start(bf16[8,2816]{1,0:T(8,128)(2,1)S(1)} %get-tuple-element.72), channel_id=1, source_target_pairs={{0,4},{1,5},{2,6},{3,7},{4,0},{5,1},{6,2},{7,3},{8,12},{9,13},{10,... | collective-permute-start | bytes 135176 | tf_op jit(solution)/shard_map/ppermute | solution.py:29
  49.2 4.9 %collective-permute-start.20 = (bf16[8,2816]{1,0:T(8,128)(2,1)S(1)}, bf16[8,2816]{1,0:T(8,128)(2,1)S(1)}, u32[]{:S(2)}, u32[]{:S(2)}) collective-permute-start(bf16[8,2816]{1,0:T(8,128)(2,1)S(1)} %get-tuple-element.73), channel_id=1, source_target_pairs={{0,8},{1,9},{2,10},{3,11},{4,12},{5,13},{6,14},{7,15},{8,0},{9,1},... | collective-permute-start | bytes 135176 | tf_op jit(solution)/shard_map/ppermute | solution.py:29
